TPU v7x, 256 devices: a whole 4x4x8 slice. The times are simulated.
256 devices in a mesh: heads: 4 (over x), seq: 64 (over z, y, core).
Axes of the slice: x: 4, y: 4, z: 8, core: 2. Of those that a mesh axis runs over, the one named last changes fastest.
Arguments:
- queries: bfloat16 [49152, 2048], P('seq', 'heads'), may hold values from -6 to 6
- key_vectors: bfloat16 [49152, 2048], P('seq', 'heads'), may hold values from -10 to 10
- value_vectors: bfloat16 [49152, 2048], P('seq', 'heads'), may hold values from -6 to 6
- random_blocks: int32 [16, 768, 3], P('heads', 'seq'), may hold values from 0 to 767, as said below
- global_blocks: int32 [2], replicated, may hold values from 0 to 767, as said below
- out_weight: bfloat16 [2048, 4096], P('heads'), may hold values from -0.1875 to 0.1875
Outputs:
- layer_out: bfloat16 [49152, 4096], P('seq', 'heads')
Inputs may be any that keep to these rules, and one draw needn't show every extreme that they name: `random_blocks`: entries are block numbers. Of the entries with heads of one group of 4 and query blocks of one run of 12 blocks, at most 4 lie in any one run of key blocks s * 12 to (s + 1) * 12 - 1, and exactly 4 lie in one such run. Entries may repeat. `global_blocks`: Distinct; the last entry is the last block, 767.
All inputs are finite; a program needn't handle non-finite values.
Results may differ from a plain program's by a relative error of at most 0.0095.
Values may be sent and summed in bfloat16 or wider, within the bound.
No kernel may reach another device: no remote copies, remote signals or barrier semaphores. Data moves between devices by JAX's collectives and lax.ppermute only.
A program may use at most 128 MiB of HBM per device.

v0:
```python
import jax
import jax.numpy as jnp
from jax import lax
from jax.sharding import Mesh
from jax.sharding import PartitionSpec as P

DH = 128
BLOCK = 64
RANDOM = 3
GLOBAL = 2
SEQ = ("seq_0", "seq_1", "seq_2")


def extended(shard, sides, width):
    for axis, dim in sides:
        peers, length = (lax.axis_size(axis), shard.shape[dim])
        up = [(i, (i + 1) % peers) for i in range(peers - 1)]
        down = [(j, i) for i, j in up]
        last = lax.slice_in_dim(shard, length - width, length, axis=dim)
        leading = lax.slice_in_dim(shard, 0, width, axis=dim)
        before = lax.ppermute(last, axis, up)
        after = lax.ppermute(leading, axis, down)
        shard = jnp.concatenate([before, shard, after], axis=dim)
    return shard


def filled_up(lines, peers):
    spare = -len(lines) % peers
    return jnp.pad(lines, [(0, spare)] + [(0, 0)] * (lines.ndim - 1))


def sum_in_order(parts, axes, turns):
    inside = parts.shape[1:]
    parts = parts.reshape(*(lax.axis_size(a) for a in axes), *inside)
    parts = jnp.moveaxis(parts, turns, range(len(axes))).reshape(-1, *inside)
    for k in turns:
        parts = lax.psum_scatter(parts, axes[k], scatter_dimension=0, tiled=True)
    return parts[0]


def gather_in_order(shard, axes, turns):
    parts = shard[None]
    for k in turns:
        parts = lax.all_gather(parts, axes[k], axis=0, tiled=True)
    held = [lax.axis_size(axes[k]) for k in reversed(turns)]
    parts = parts.reshape(*held, *shard.shape)
    turned = sorted(range(len(turns)), key=lambda place: turns[len(turns) - 1 - place])
    return parts.transpose(*turned, *range(len(turns), parts.ndim)).reshape(-1, *shard.shape)


def total_of(shard, axes, turns):
    peers, lines = (lax.axis_size(axes), shard.reshape(-1, *shard.shape[1:][-1:]))
    parts = filled_up(lines, peers).reshape(peers, -1, *lines.shape[1:])
    own = sum_in_order(parts, axes, turns)
    whole = gather_in_order(own, axes, turns[::-1]).reshape(-1, *lines.shape[1:])
    return whole[: len(lines)].reshape(shard.shape)


def collected_together(shard, axis):
    leaves = jax.tree.leaves(shard)
    turns = sorted(range(len(leaves)), key=lambda k: -leaves[k].size)
    width = (1, *leaves[turns[0]].shape)[-1]
    lines = [
        jnp.pad(leaves[k].reshape(-1), (0, -leaves[k].size % width)).reshape(-1, width)
        for k in turns
    ]
    both, at, found = (lax.all_gather(jnp.concatenate(lines), axis), 0, {})
    for k, line in zip(turns, lines):
        piece = both[:, at : at + len(line)].reshape(len(both), -1)
        found[k] = piece[:, : leaves[k].size].reshape(-1, *leaves[k].shape)
        at += len(line)
    numbers = iter(range(len(leaves)))
    return jax.tree.map(lambda _: found[next(numbers)], shard)


def combined_by_axis(shard, axes, combine):
    for axis in axes:
        pieces = collected_together(
            jax.tree.map(
                lambda part, kind: part.astype(kind),
                shard,
                (jnp.bfloat16, jnp.bfloat16, jnp.bfloat16),
            ),
            axis,
        )
        widened = [
            jax.tree.map(lambda part, own: part[k].astype(own.dtype), pieces, shard)
            for k in range(lax.axis_size(axis))
        ]
        shard = widened[0]
        for other in widened[1:]:
            shard = combine(shard, other)
    return shard


def in_blocks(shard, dim, peers):
    before, after = (shard.shape[:dim], shard.shape[dim + 1 :])
    return jnp.moveaxis(shard.reshape(*before, peers, -1, *after), dim, 0)


def sent_and_summed(shard, axis, dim):
    parts = in_blocks(shard, dim, lax.axis_size(axis))
    arrived = lax.all_to_all(parts, axis, split_axis=0, concat_axis=0, tiled=True)
    return arrived.astype(jnp.float32).sum(axis=0)


def combine_parts(first, second):
    top_first, total_first, out_first = first
    top_second, total_second, out_second = second
    highest = jnp.maximum(top_first, top_second)
    scale_first = jnp.exp(top_first - highest)
    scale_second = jnp.exp(top_second - highest)
    return (
        highest,
        total_first * scale_first + total_second * scale_second,
        out_first * scale_first[..., None] + out_second * scale_second[..., None],
    )


def on_device(queries, key_vectors, value_vectors, random_blocks, global_blocks, out_weight):
    shards = lax.axis_size(SEQ)
    my_index = lax.axis_index(SEQ)
    tok_rows, features = queries.shape
    heads_here = features // DH
    blocks_here = tok_rows // BLOCK
    requests = heads_here * blocks_here * RANDOM
    capacity = max(2, 3 * requests // (2 * shards) + 1)
    score_multiplier = DH ** (-0.5)
    query_block_tiles = queries.reshape(blocks_here, BLOCK, heads_here, DH).transpose(2, 0, 1, 3)
    stacked = jnp.concatenate([key_vectors, value_vectors], axis=1)
    padded = extended(stacked, ((SEQ, 0),), BLOCK)
    kv_tiles = padded.reshape(blocks_here + 2, BLOCK, 2, heads_here, DH).transpose(3, 0, 1, 2, 4)
    own_tiles = kv_tiles[:, 1:-1]
    table = own_tiles.reshape(heads_here * blocks_here, BLOCK, 2, DH)
    flat_lists = random_blocks.reshape(requests)
    head_of = jnp.arange(requests, dtype=jnp.int32) // (blocks_here * RANDOM)
    code_flat = head_of * blocks_here + flat_lists % blocks_here
    holders = flat_lists // blocks_here
    onehot = (holders[:, None] == jnp.arange(shards, dtype=jnp.int32)[None, :]).astype(jnp.int32)
    rank_flat = jnp.sum((jnp.cumsum(onehot, axis=0) - onehot) * onehot, axis=1)
    slot_flat = holders * capacity + rank_flat
    asked = (
        jnp.zeros((shards * capacity,), jnp.int32)
        .at[slot_flat]
        .set(code_flat)
        .reshape(shards, capacity)
    )
    arrived = lax.all_to_all(
        table[lax.all_to_all(asked, SEQ, split_axis=0, concat_axis=0, tiled=True)],
        SEQ,
        split_axis=0,
        concat_axis=0,
        tiled=True,
    )
    fetched = arrived.reshape(shards * capacity, BLOCK, 2, DH)[slot_flat]
    fetched = fetched.reshape(heads_here, blocks_here, RANDOM, BLOCK, 2, DH)
    holder_glob = global_blocks // blocks_here
    place_glob = global_blocks % blocks_here
    mine_glob = holder_glob == my_index
    global_q_local = query_block_tiles[:, place_glob]
    global_kv_local = own_tiles[:, place_glob]
    owned_mask = mine_glob.astype(jnp.float32)
    summed_query, summed_pairs = (
        total_of(
            global_q_local.astype(jnp.float32) * owned_mask[None, :, None, None], SEQ, (0, 1, 2)
        ),
        total_of(
            global_kv_local.astype(jnp.float32) * owned_mask[None, :, None, None, None],
            SEQ,
            (0, 1, 2),
        ),
    )
    global_query = summed_query.astype(jnp.bfloat16)
    global_pairs = summed_pairs.astype(jnp.bfloat16)
    window = jnp.stack([kv_tiles[:, :-2], kv_tiles[:, 1:-1], kv_tiles[:, 2:]], axis=2)
    spread_global = jnp.broadcast_to(
        global_pairs[:, None], (heads_here, blocks_here, GLOBAL, BLOCK, 2, DH)
    )
    listed = jnp.concatenate([window, fetched, spread_global], axis=2).reshape(
        heads_here, blocks_here, -1, 2, DH
    )
    window_key_rows = listed[:, :, :, 0]
    window_value_rows = listed[:, :, :, 1]
    logit_scores = (
        jnp.einsum(
            "hbqd,hbkd->hbqk",
            query_block_tiles,
            window_key_rows,
            preferred_element_type=jnp.float32,
        )
        * score_multiplier
    )
    column_block = jnp.arange(window_key_rows.shape[2]) // BLOCK
    row_global = my_index * blocks_here + jnp.arange(blocks_here)
    valid_keys = jnp.where(
        column_block[None, :] == 0,
        row_global[:, None] > 0,
        jnp.where(column_block[None, :] == 2, row_global[:, None] < shards * blocks_here - 1, True),
    )
    logit_scores = jnp.where(valid_keys[None, :, None, :], logit_scores, -jnp.inf)
    row_peak = jnp.max(logit_scores, axis=-1, keepdims=True)
    exponent = jnp.exp(logit_scores - row_peak)
    softmax_divisor = jnp.sum(exponent, axis=-1, keepdims=True)
    sparse_result = (
        jnp.einsum(
            "hbqk,hbkd->hbqd",
            exponent.astype(jnp.bfloat16),
            window_value_rows,
            preferred_element_type=jnp.float32,
        )
        / softmax_divisor
    )
    sparse_result = sparse_result.astype(jnp.bfloat16)
    local_keys = own_tiles[:, :, :, 0].reshape(heads_here, tok_rows, DH)
    local_values = own_tiles[:, :, :, 1].reshape(heads_here, tok_rows, DH).astype(jnp.float32)
    global_rows_q = global_query.reshape(heads_here, GLOBAL * BLOCK, DH)
    global_scores = (
        jnp.einsum("hqd,hkd->hqk", global_rows_q, local_keys, preferred_element_type=jnp.float32)
        * score_multiplier
    )
    local_top = jnp.max(global_scores, axis=-1)
    global_exp = jnp.exp(global_scores - local_top[..., None])
    top_all, total_all, out_all = combined_by_axis(
        (
            local_top,
            jnp.sum(global_exp, axis=-1),
            jnp.einsum("hqk,hkd->hqd", global_exp, local_values, precision=lax.Precision.HIGHEST),
        ),
        SEQ,
        combine_parts,
    )
    global_out = (
        (out_all / total_all[..., None]).astype(jnp.bfloat16).reshape(heads_here, GLOBAL, BLOCK, DH)
    )
    block_ids = jnp.arange(blocks_here)
    for glob_index in range(GLOBAL):
        replace_mask = mine_glob[glob_index] & (block_ids == place_glob[glob_index])
        sparse_result = jnp.where(
            replace_mask[None, :, None, None], global_out[:, glob_index][:, None], sparse_result
        )
    attention = sparse_result.transpose(1, 2, 0, 3).reshape(tok_rows, features)
    partial_out = jnp.dot(attention, out_weight, preferred_element_type=jnp.float32)
    return sent_and_summed(partial_out.astype(jnp.bfloat16), "heads", 1).astype(jnp.bfloat16)


def solution(mesh):
    torus = Mesh(
        mesh.devices.reshape(mesh.shape["heads"], 8, 4, 2), ("heads", "seq_0", "seq_1", "seq_2")
    )
    in_specs = (
        P(SEQ, "heads"),
        P(SEQ, "heads"),
        P(SEQ, "heads"),
        P("heads", SEQ, None),
        P(),
        P("heads", None),
    )
    out_specs = P(SEQ, "heads")
    return jax.shard_map(
        on_device, mesh=torus, in_specs=in_specs, out_specs=out_specs, check_vma=False
    )
```

profile of v0, /device:TPU:32, one launch (start us, length us, event | category | flops | bytes accessed | tf_op | source)
XLA Modules:
  0.0 506.1 jit_solution(17802183879058602323)
XLA Ops:
  6.5 1.3 constant_dynamic-update-slice_fusion.1
  7.8 1.2 constant_dynamic-update-slice_fusion
  9.1 3.9 collective-permute-start.1
  13.0 1.9 collective-permute-start
  17.2 1.0 scatter_custom_fusion
  18.2 0.7 all_to_all.14
  18.9 12.9 %all-to-all-start = ((s32[64,1,4]{2,1,0:T(1,128)}), s32[64,1,4]{2,1,0:T(1,128)S(1)}, u32[]{:S(2)}, u32[]{:S(2)}) async-start(s32[64,1,4]{2,1,0:T(1,128)} %bitcast.76), calls=%async_computation.2 | async-start | bytes 65536 | tf_op jit(solution)/shard_map/all_to_all | solution.py:149
  32.4 8.0 %all-to-all-done = s32[64,1,4]{2,1,0:T(1,128)S(1)} async-done(((s32[64,1,4]{2,1,0:T(1,128)}), s32[64,1,4]{2,1,0:T(1,128)S(1)}, u32[]{:S(2)}, u32[]{:S(2)}) %all-to-all-start) | async-done | bytes 1056 | tf_op jit(solution)/shard_map/all_to_all | solution.py:149
  40.5 1.1 pad_maximum_fusion
  41.6 2.3 reshape.870
  43.9 2.0 copy.99
  45.9 3.1 fusion.195
  49.0 8.5 %gather_fusion.1 = bf16[256,64,2,128]{3,1,2,0:T(8,128)(2,1)} fusion(bf16[48,64,2,128]{3,1,2,0:T(8,128)(2,1)S(1)} %bitcast.858, s32[1024]{0:T(1024)S(1)} %get-tuple-element.68), kind=kCustom, calls=%fused_computation.1 | custom fusion | bytes 16778240 | tf_op jit(solution)/shard_map/gather | solution.py:149
  57.5 6.7 %all-to-all-start.1 = ((bf16[64,4,64,2,128]{4,2,3,1,0:T(8,128)(2,1)}), bf16[64,4,64,2,128]{4,2,3,1,0:T(8,128)(2,1)}, u32[]{:S(2)}, u32[]{:S(2)}) async-start(bf16[64,4,64,2,128]{4,2,3,1,0:T(8,128)(2,1)} %bitcast.861), calls=%async_computation.3 | async-start | bytes 16777216 | tf_op jit(solution)/shard_map/all_to_all | solution.py:148
  64.3 2.5 reshape.869
  66.7 2.2 copy.100
  69.0 0.7 mul.343
  69.7 1.7 gather_fusion
  71.5 1.6 broadcast_multiply_fusion.1
  73.2 0.8 mul.419
  73.9 1.1 mul.420
  75.0 1.3 gather_fusion.3
  76.3 1.0 convert_bitcast_fusion
  77.7 39.7 %reduce-scatter.6.cloned.1.call-done = f32[8,8,128]{2,1,0:T(8,128)} async-done(((f32[64,8,128]{2,1,0:T(8,128)}), f32[8,8,128]{2,1,0:T(8,128)}) %reduce-scatter.6.cloned.1.call-update) | async-done | bytes 32784 | tf_op jit(solution)/shard_map/reduce_scatter | solution.py:37
  117.4 1.0 broadcast_multiply_fusion
  118.5 1.3 dynamic-slice
  119.8 1.0 fusion.194
  120.9 36.8 %reduce-scatter.8.cloned.1.call-done = f32[2,8,128]{2,1,0:T(8,128)} async-done(((f32[8,8,128]{2,1,0:T(8,128)}), f32[2,8,128]{2,1,0:T(8,128)}) %reduce-scatter.8.cloned.1.call-update) | async-done | bytes 8208 | tf_op jit(solution)/shard_map/reduce_scatter | solution.py:37
  157.6 2.6 all-reduce.1
  160.9 1.8 all_gather.36
  162.6 12.2 %all_gather.37 = bf16[8,8,128]{2,1,0:T(8,128)(2,1)S(1)} all-gather(bf16[2,8,128]{2,1,0:T(8,128)(2,1)S(1)} %all_gather.36), channel_id=1, replica_groups=mesh['heads'=4,'seq_0'=8,'seq_1'=4,'seq_2'=2] {'seq_1'}, dimensions={0}, use_global_device_ids=true | all-gather | bytes 20480 | tf_op jit(solution)/shard_map/all_gather | solution.py:44
  174.8 98.1 %all_gather.38 = bf16[64,8,128]{2,1,0:T(8,128)(2,1)S(1)} all-gather(bf16[8,8,128]{2,1,0:T(8,128)(2,1)S(1)} %all_gather.37), channel_id=1, replica_groups=mesh['heads'=4,'seq_0'=8,'seq_1'=4,'seq_2'=2] {'seq_0'}, dimensions={0}, use_global_device_ids=true | all-gather | bytes 147456 | tf_op jit(solution)/shard_map/all_gather | solution.py:44
  273.4 2.3 fusion.15
  276.2 23.5 %reduce-scatter.12.cloned.1.call-done = f32[2,16,128]{2,1,0:T(8,128)} async-done(((f32[8,16,128]{2,1,0:T(8,128)}), f32[2,16,128]{2,1,0:T(8,128)}) %reduce-scatter.12.cloned.1.call-update) | async-done | bytes 16400 | tf_op jit(solution)/shard_map/reduce_scatter | solution.py:37
  299.8 0.7 pad_maximum_fusion.1
  300.5 0.6 fusion.198
  301.2 0.6 fusion.199
  301.8 2.5 compare_and_fusion.1
  304.4 3.0 copy_dynamic-update-slice_fusion.3
  307.4 1.5 copy_dynamic-update-slice_fusion.2
  308.9 1.5 copy_dynamic-update-slice_fusion.1
  310.5 4.0 reduce-scatter.14.cloned.1.call-done
  314.5 2.0 all_gather.45
  316.5 12.2 %all_gather.46 = f32[8,16,128]{2,1,0:T(8,128)S(1)} all-gather(f32[2,16,128]{2,1,0:T(8,128)S(1)} %all_gather.45), channel_id=1, replica_groups=mesh['heads'=4,'seq_0'=8,'seq_1'=4,'seq_2'=2] {'seq_1'}, dimensions={0}, use_global_device_ids=true | all-gather | bytes 81920 | tf_op jit(solution)/shard_map/all_gather | solution.py:44
  328.7 26.6 %all_gather.47 = f32[64,16,128]{2,1,0:T(8,128)S(1)} all-gather(f32[8,16,128]{2,1,0:T(8,128)S(1)} %all_gather.46), channel_id=1, replica_groups=mesh['heads'=4,'seq_0'=8,'seq_1'=4,'seq_2'=2] {'seq_0'}, dimensions={0}, use_global_device_ids=true | all-gather | bytes 589824 | tf_op jit(solution)/shard_map/all_gather | solution.py:44
  355.4 1.6 all-gather.5.cloned.1.call-done
  357.0 0.8 fusion.107
  357.9 0.7 fusion.97
  358.6 0.7 fusion.112
  359.3 0.7 fusion.133
  360.0 0.7 fusion.139
  360.7 2.2 fusion.35
  362.9 12.9 %all-gather.1 = bf16[2080,128]{1,0:T(8,128)(2,1)S(1)} all-gather(bf16[520,128]{1,0:T(8,128)(2,1)S(1)} %pad_maximum_fusion.2), channel_id=3, replica_groups=mesh['heads'=4,'seq_0'=8,'seq_1'=4,'seq_2'=2] {'seq_1'}, dimensions={0}, use_global_device_ids=true | all-gather | bytes 665600 | tf_op jit(solution)/shard_map/all_gather | solution.py:67
  376.4 2.0 all-gather.2
  379.1 11.0 %gather_fusion.2 = bf16[144,64,2,128]{3,1,2,0:T(8,128)(2,1)} fusion(bf16[256,64,2,128]{3,1,2,0:T(8,128)(2,1)} %bitcast.79, s32[1024]{0:T(1024)S(1)} %pad_clamp_fusion), kind=kCustom, calls=%fused_computation.2 | custom fusion | bytes 9437760 | tf_op jit(solution)/shard_map/gather | solution.py:155
  390.1 6.1 %copy_dynamic-update-slice_fusion = bf16[4,12,8,64,2,128]{5,3,2,1,0,4:T(8,128)(2,1)} fusion(bf16[4,12,8,64,2,128]{5,3,2,1,0,4:T(8,128)(2,1)} %copy_dynamic-update-slice_fusion.1, bf16[4,12,3,64,2,128]{5,3,4,2,1,0:T(8,128)(2,1)} %bitcast.863), kind=kLoop, calls=%fused_computation.17 | loop fusion | bytes 9437184
  396.2 2.5 broadcast_dynamic-update-slice_fusion
  398.7 5.2 %bitcast_reduce_fusion = (f32[4,12,64]{2,1,0:T(8,128)S(1)}, f32[4,12,512,64]{2,3,1,0:T(8,128)S(1)}) fusion(pred[12,512]{1,0:T(8,128)(4,1)S(1)} %select_select_fusion, bf16[12,64,4,128]{3,2,1,0:T(4,128)(2,1)S(1)} %copy-done.2, bf16[4,12,512,2,128]{4,2,1,0,3:T(8,128)(2,1)} %bitcast.84), kind=kOutput, calls=%fused_computation.12 | convolution fusion | flops 407368704 | bytes 13387776 | tf_op jit(solution)/shard_map/hbqd,hbkd->hbqk/dot_general | solution.py:185
  404.0 1.8 fusion.3
  405.8 4.4 fusion.19
  410.9 5.9 %convolution_convert_fusion = bf16[768,4096]{1,0:T(8,128)(2,1)S(1)} fusion(bf16[512,4096]{1,0:T(8,128)(2,1)} %param.11, bf16[96,8,4,128]{3,2,1,0:T(4,128)(2,1)S(1)} %bitcast.882), kind=kOutput, calls=%fused_computation.5 | convolution fusion | flops 3224371200 | bytes 11272192 | tf_op jit(solution)/shard_map/dot_general | solution.py:242
  416.7 1.0 copy.98
  417.7 75.6 %all_to_all.22 = bf16[4,768,1024]{2,1,0:T(8,128)(2,1)} all-to-all(bf16[4,768,1024]{2,1,0:T(8,128)(2,1)S(1)} %bitcast.862), channel_id=1, replica_groups=mesh['heads'=4,'seq_0'=8,'seq_1'=4,'seq_2'=2] {'heads'}, dimensions={0} | all-to-all | bytes 12582912 | tf_op jit(solution)/shard_map/all_to_all | solution.py:103
  493.3 5.9 %reduce_sum.45 = bf16[768,1024]{1,0:T(8,128)(2,1)} reduce(bf16[4,768,1024]{2,1,0:T(8,128)(2,1)} %all_to_all.22, bf16[]{:T(256)} %constant.104.clone.1), dimensions={0}, to_apply=%region_14.15 | reduce | flops 2359296 | bytes 7864322 | tf_op jit(solution)/shard_map/reduce_sum | solution.py:104
  (86 shorter events, 7.2 us)
Async XLA Ops:
  6.5 8.4 %copy-start.3 = (s32[4,12,3]{1,0,2:T(4,128)S(1)}, s32[4,12,3]{1,0,2:T(4,128)}, u32[]{:S(2)}) copy-start(s32[4,12,3]{1,0,2:T(4,128)} %param.9) | copy-start | bytes 1732
  6.5 25.3 %copy-start.5 = (s32[2]{0:T(128)S(1)}, s32[2]{0:T(128)}, u32[]{:S(2)}) copy-start(s32[2]{0:T(128)} %param.10) | copy-start | bytes 28
  9.1 31.4 %collective-permute-start.1 = (bf16[64,1024]{1,0:T(8,128)(2,1)S(1)}, bf16[64,1024]{1,0:T(8,128)(2,1)S(1)}, u32[]{:S(2)}, u32[]{:S(2)}) collective-permute-start(bf16[64,1024]{1,0:T(8,128)(2,1)S(1)} %get-tuple-element.25), channel_id=1, source_target_pairs={{1,0},{2,1},{3,2},{4,3},{5,4},{6,5},{7,6},{8,7},{9,8},{10,9},{11,1... | collective-permute-start | bytes 393224 | tf_op jit(solution)/shard_map/ppermute | solution.py:22
  13.0 27.5 %collective-permute-start = (bf16[64,1024]{1,0:T(8,128)(2,1)S(1)}, bf16[64,1024]{1,0:T(8,128)(2,1)}, u32[]{:S(2)}, u32[]{:S(2)}) collective-permute-start(bf16[64,1024]{1,0:T(8,128)(2,1)S(1)} %get-tuple-element.24), channel_id=1, source_target_pairs={{0,1},{1,2},{2,3},{3,4},{4,5},{5,6},{6,7},{7,8},{8,9},{9,10},{10,1... | collective-permute-start | bytes 393224 | tf_op jit(solution)/shard_map/ppermute | solution.py:21
  18.9 21.4 %all-to-all-start = ((s32[64,1,4]{2,1,0:T(1,128)}), s32[64,1,4]{2,1,0:T(1,128)S(1)}, u32[]{:S(2)}, u32[]{:S(2)}) async-start(s32[64,1,4]{2,1,0:T(1,128)} %bitcast.76), calls=%async_computation.2 | async-start | bytes 65536 | tf_op jit(solution)/shard_map/all_to_all | solution.py:149
  57.5 11.5 %copy-start.6 = (s32[2]{0:T(128)S(1)}, s32[2]{0:T(128)}, u32[]{:S(2)}) copy-start(s32[2]{0:T(128)} %param.10) | copy-start | bytes 28
  57.5 321.6 %all-to-all-start.1 = ((bf16[64,4,64,2,128]{4,2,3,1,0:T(8,128)(2,1)}), bf16[64,4,64,2,128]{4,2,3,1,0:T(8,128)(2,1)}, u32[]{:S(2)}, u32[]{:S(2)}) async-start(bf16[64,4,64,2,128]{4,2,3,1,0:T(8,128)(2,1)} %bitcast.861), calls=%async_computation.3 | async-start | bytes 16777216 | tf_op jit(solution)/shard_map/all_to_all | solution.py:148
  64.2 53.2 %reduce-scatter.6.cloned.1.call-start = ((), (), s32[]{:S(2)}) async-start(), calls=%async_computation.8 | async-start | bytes 294912 | tf_op jit(solution)/shard_map/reduce_scatter | solution.py:37
  73.1 84.5 %reduce-scatter.8.cloned.1.call-start = ((), (), s32[]{:S(2)}) async-start(), calls=%async_computation.9 | async-start | bytes 40960 | tf_op jit(solution)/shard_map/reduce_scatter | solution.py:37
  117.4 158.3 %reduce-scatter.10.cloned.1.call-start = ((), (), s32[]{:S(2)}) async-start(), calls=%async_computation.10 | async-start | bytes 589824 | tf_op jit(solution)/shard_map/reduce_scatter | solution.py:37
  118.5 181.3 %reduce-scatter.12.cloned.1.call-start = ((), (), s32[]{:S(2)}) async-start(), calls=%async_computation.11 | async-start | bytes 81920 | tf_op jit(solution)/shard_map/reduce_scatter | solution.py:37
  120.9 179.6 %copy-start.4 = (s32[2]{0:T(128)S(1)}, s32[2]{0:T(128)}, u32[]{:S(2)}) copy-start(s32[2]{0:T(128)} %get-tuple-element.15) | copy-start | bytes 28
  273.4 34.0 %copy-start.1 = (bf16[4,12,1,64,2,128]{5,3,4,1,0,2:T(8,128)(2,1)S(1)}, bf16[4,12,1,64,2,128]{5,3,4,1,0,2:T(8,128)(2,1)}, u32[]{:S(2)}) copy-start(bf16[4,12,1,64,2,128]{5,3,4,1,0,2:T(8,128)(2,1)} %get-tuple-element.21) | copy-start | bytes 4718596
  275.7 38.8 %reduce-scatter.14.cloned.1.call-start = ((), (), s32[]{:S(2)}) async-start(), calls=%async_computation.12 | async-start | bytes 24576 | tf_op jit(solution)/shard_map/reduce_scatter | solution.py:37
  276.2 32.7 %copy-start = (bf16[4,12,1,64,2,128]{5,3,4,1,0,2:T(8,128)(2,1)S(1)}, bf16[4,12,1,64,2,128]{5,3,4,1,0,2:T(8,128)(2,1)}, u32[]{:S(2)}) copy-start(bf16[4,12,1,64,2,128]{5,3,4,1,0,2:T(8,128)(2,1)} %get-tuple-element.22) | copy-start | bytes 4718596
  299.8 57.3 %all-gather.5.cloned.1.call-start = ((), (), s32[]{:S(2)}) async-start(), calls=%async_computation.13 | async-start | bytes 1198080 | tf_op jit(solution)/shard_map/all_gather | solution.py:67
  390.1 8.7 %copy-start.2 = (bf16[12,64,4,128]{3,2,1,0:T(4,128)(2,1)S(1)}, bf16[12,64,4,128]{3,2,1,0:T(4,128)(2,1)}, u32[]{:S(2)}) copy-start(bf16[12,64,4,128]{3,2,1,0:T(4,128)(2,1)} %reshape.869) | copy-start | bytes 2359300
Sparse Core Ops, SparseCore 0:
  73.2 44.0 reduce-scatter.5
  120.0 37.5 reduce-scatter.7
  160.2 49.1 reduce-scatter.9
  275.8 23.8 reduce-scatter.11
  302.0 12.4 reduce-scatter.13
  316.2 40.8 all-gather.4
where the time goes:
time: 508 us; the launch traced here: 506 us
  blocking collectives  246 us (48%)
  waiting for transfers between devices  114 us (22%)
  local copies, waits for them, and re-layouts  64.3 us (13%)
  starting transfers between devices  25.6 us (5%)
  other arithmetic  24.2 us (5%)
  matrix products  18.3 us (4%)
  between operations  13.9 us (3%)
    all_gather x6, blocking collectives, gather_in_order(): parts = lax.all_gather(parts, axes[k], axis=0, tiled=True)  153 us
    reduce_scatter x5, waiting for transfers between devices, sum_in_order(): parts = lax.psum_scatter(parts, axes[k], scatter_dimension=0, tiled=True)  104 us
    all_to_all x1, blocking collectives, sent_and_summed(): lax.all_to_all(parts, axis, split_axis=0, concat_axis=0, tiled=True)  75.6 us
    unnamed x21, local copies, waits for them, and re-layouts  15.4 us
    all_gather x2, blocking collectives, collected_together(): both, at, found = (lax.all_gather(jnp.concatenate(lines), axis), 0, {})  14.9 us
    all_to_all x1, starting transfers between devices, on_device(): lax.all_to_all(asked, SEQ, split_axis=0, concat_axis=0, tiled=True)  12.9 us
    gather x1, local copies, waits for them, and re-layouts, on_device(): fetched = arrived.reshape(shards * capacity, BLOCK, 2, DH)[slot_flat]  11 us
  transfers between devices with their start and end apart: 10, of which 6 were waited for; matrix products, arithmetic and copies ran while one was open for 8% of the time, Pallas kernels for 0%

commit v1 on v0

v1 whole, which is shorter than its diff:
```python
import jax
import jax.numpy as jnp
from jax import lax
from jax.experimental import pallas as pl
from jax.experimental.pallas import tpu as pltpu
from jax.sharding import Mesh
from jax.sharding import PartitionSpec as P

DH = 128
BLOCK = 64
RANDOM = 3
GLOBAL = 2
CAP = 4
PLANES = 8
INPLANE = 8
SEQ = ("seq_0", "seq_1", "seq_2")
PLANE = ("seq_1", "seq_2")
VMEM_LIMIT = 56 * 2**20


def ring_step(shard, step):
    peers = lax.axis_size("seq_0")
    return lax.ppermute(shard, "seq_0", [(i, (i + step) % peers) for i in range(peers)])


def pick_kernel(n, first, codes, *refs):
    keys, values, out, sem = refs[:n], refs[n : 2 * n], refs[2 * n], refs[2 * n + 1]

    def one_peer(peer, carry):
        for run in range(n):
            for rank in range(CAP):
                code = codes[(peer * PLANES + first + run) * CAP + rank]
                rows = pl.ds(pl.multiple_of((code & 15) * BLOCK, BLOCK), BLOCK)
                cols = pl.ds(pl.multiple_of((code >> 4) * DH, DH), DH)
                for side, source in enumerate((keys[run], values[run])):
                    pltpu.make_async_copy(
                        source.at[rows, cols], out.at[peer, run, rank, side], sem
                    ).start()
        return carry

    lax.fori_loop(0, INPLANE, one_peer, 0)
    pltpu.make_async_copy(out, out, sem).wait()


def picked(codes, first, keys, values):
    n = len(keys)
    shape = (INPLANE, n, CAP, 2, BLOCK, DH)
    size = 2 * INPLANE * n * CAP * 2 * BLOCK * DH * 2
    return pl.pallas_call(
        lambda *refs: pick_kernel(n, first, *refs),
        out_shape=jax.ShapeDtypeStruct(shape, jnp.bfloat16),
        in_specs=[pl.BlockSpec(memory_space=pltpu.SMEM)]
        + [pl.BlockSpec(memory_space=pl.ANY)] * (2 * n),
        out_specs=pl.BlockSpec(memory_space=pl.ANY),
        scratch_shapes=[pltpu.SemaphoreType.DMA],
        cost_estimate=pl.CostEstimate(flops=0, bytes_accessed=size, transcendentals=0),
        name="pick_blocks",
    )(codes, *keys, *values)


def attend_kernel(
    counts, slots, place, q, k, v, kb, vb, ka, va, glob, gout, *refs
):
    n = len(counts)
    arrived, out, held, sems = refs[:n], refs[n], refs[n + 1], refs[n + 2]
    kpad, vpad = refs[n + 3], refs[n + 4]
    copies = []
    at = 0
    for part, count in enumerate(counts):
        copies.append(
            pltpu.make_async_copy(
                arrived[part], held.at[:, pl.ds(at, count)], sems.at[part]
            )
        )
        copies[-1].start()
        at += count
    heads = q.shape[1] // DH
    blocks = q.shape[0] // BLOCK
    rows = q.shape[0]
    for pad, before, own, after in ((kpad, kb, k, ka), (vpad, vb, v, va)):
        pad[0:BLOCK] = before[...]
        pad[BLOCK : BLOCK + rows] = own[...]
        pad[BLOCK + rows :] = after[...]
    for copy in copies:
        copy.wait()
    scale = DH ** (-0.5)
    col = lax.broadcasted_iota(jnp.int32, (BLOCK, (3 + RANDOM + GLOBAL) * BLOCK), 1)

    def one_block(b, carry):
        at_rows = pl.ds(pl.multiple_of(b * BLOCK, BLOCK), BLOCK)
        win_rows = pl.ds(pl.multiple_of(b * BLOCK, BLOCK), 3 * BLOCK)
        number = place[0] + b
        low = jnp.where(number == 0, BLOCK, 0)
        high = jnp.where(number == place[1] - 1, 2 * BLOCK, 3 * BLOCK)
        valid = (col >= low) & ((col < high) | (col >= 3 * BLOCK))
        for h in range(heads):
            hs = slice(h * DH, (h + 1) * DH)
            picks = []
            for r in range(RANDOM):
                slot = slots[(h * blocks + b) * RANDOM + r]
                picks.append((slot >> 5, (slot >> 2) & 7, slot & 3))
            keys = jnp.concatenate(
                [kpad[win_rows, hs]]
                + [held[p[0], p[1], p[2], 0] for p in picks]
                + [glob[g, 1, :, hs] for g in range(GLOBAL)],
                axis=0,
            )
            values = jnp.concatenate(
                [vpad[win_rows, hs]]
                + [held[p[0], p[1], p[2], 1] for p in picks]
                + [glob[g, 2, :, hs] for g in range(GLOBAL)],
                axis=0,
            )
            scores = lax.dot_general(
                q[at_rows, hs], keys, (((1,), (1,)), ((), ())),
                preferred_element_type=jnp.float32,
            ) * scale
            scores = jnp.where(valid, scores, -jnp.inf)
            peak = jnp.max(scores, axis=1, keepdims=True)
            weights = jnp.exp(scores - peak)
            total = jnp.sum(weights, axis=1, keepdims=True)
            summed = jnp.dot(
                weights.astype(jnp.bfloat16), values, preferred_element_type=jnp.float32
            )
            out[at_rows, hs] = (summed / total).astype(jnp.bfloat16)
        return carry

    lax.fori_loop(0, blocks, one_block, 0)
    for g in range(GLOBAL):

        @pl.when(place[2 + g] >= 0)
        def _():
            at_rows = pl.ds(pl.multiple_of(place[2 + g] * BLOCK, BLOCK), BLOCK)
            for h in range(heads):
                out[at_rows, h * DH : (h + 1) * DH] = gout[h, g * BLOCK : (g + 1) * BLOCK]


def attended(slots, place, q, k, v, kb, vb, ka, va, glob, gout, arrived):
    rows, features = q.shape
    counts = tuple(a.shape[1] for a in arrived)
    vmem = pl.BlockSpec(memory_space=pltpu.VMEM)
    smem = pl.BlockSpec(memory_space=pltpu.SMEM)
    return pl.pallas_call(
        lambda *refs: attend_kernel(counts, *refs),
        out_shape=jax.ShapeDtypeStruct((rows, features), jnp.bfloat16),
        in_specs=[smem, smem]
        + [vmem] * 9
        + [pl.BlockSpec(memory_space=pl.ANY)] * len(arrived),
        out_specs=vmem,
        scratch_shapes=[
            pltpu.VMEM((INPLANE, PLANES, CAP, 2, BLOCK, DH), jnp.bfloat16),
            pltpu.SemaphoreType.DMA((len(arrived),)),
            pltpu.VMEM((rows + 2 * BLOCK, features), jnp.bfloat16),
            pltpu.VMEM((rows + 2 * BLOCK, features), jnp.bfloat16),
        ],
        compiler_params=pltpu.CompilerParams(vmem_limit_bytes=VMEM_LIMIT),
        cost_estimate=pl.CostEstimate(
            flops=4 * rows * features * 512, bytes_accessed=12 * 2**20, transcendentals=rows * 4 * 512
        ),
        name="attend",
    )(slots, place, q, k, v, kb, vb, ka, va, glob, gout, *arrived)


def on_device(queries, key_vectors, value_vectors, random_blocks, global_blocks, out_weight):
    shards = lax.axis_size(SEQ)
    my_index = lax.axis_index(SEQ)
    my_plane = lax.axis_index("seq_0")
    rows, features = queries.shape
    heads = features // DH
    blocks = rows // BLOCK
    requests = heads * blocks * RANDOM

    flat = random_blocks.reshape(requests)
    holders = flat // blocks
    number = jnp.arange(requests, dtype=jnp.int32)
    codes = (number // (blocks * RANDOM)) * 16 + flat % blocks
    earlier = (holders[:, None] == holders[None, :]) & (number[None, :] < number[:, None])
    rank = jnp.sum(earlier.astype(jnp.int32), axis=1)
    apart = (holders // INPLANE - my_plane) % PLANES
    order = jnp.where(apart <= PLANES // 2, jnp.minimum(2 * apart, PLANES - 1), 2 * PLANES - 1 - 2 * apart)
    slots = ((holders % INPLANE) * PLANES + order) * CAP + rank
    every = jnp.arange(INPLANE * PLANES * CAP, dtype=jnp.int32)
    asked = jnp.sum(jnp.where(slots[None, :] == every[:, None], codes[None, :], 0), axis=1)
    asked = asked.reshape(INPLANE, PLANES * CAP)
    asked = lax.all_to_all(asked, PLANE, split_axis=0, concat_axis=0, tiled=True).reshape(-1)

    peers = [(i, i + 1) for i in range(shards - 1)]
    back = [(j, i) for i, j in peers]
    kb = lax.ppermute(key_vectors[rows - BLOCK :], SEQ, peers)
    vb = lax.ppermute(value_vectors[rows - BLOCK :], SEQ, peers)
    ka = lax.ppermute(key_vectors[:BLOCK], SEQ, back)
    va = lax.ppermute(value_vectors[:BLOCK], SEQ, back)

    up_k, up_v, down_k, down_v = key_vectors, value_vectors, key_vectors, value_vectors
    keys, values = [key_vectors], [value_vectors]
    arrived = []
    first = 0
    for step in range(1, PLANES // 2 + 1):
        last = step == PLANES // 2
        up_k = ring_step(up_k, 1)
        down_v = ring_step(down_v, -1)
        if last:
            keys.append(up_k)
            values.append(down_v)
        else:
            up_v = ring_step(up_v, 1)
            down_k = ring_step(down_k, -1)
            keys += [up_k, down_k]
            values += [up_v, down_v]
        picks = picked(asked, first, keys, values)
        first += len(keys)
        arrived.append(lax.all_to_all(picks, PLANE, split_axis=0, concat_axis=0, tiled=True))
        keys, values = [], []

    holder = global_blocks // blocks
    spot = global_blocks % blocks
    mine = holder == my_index
    own = []
    for g in range(GLOBAL):
        for source in (queries, key_vectors, value_vectors):
            piece = lax.dynamic_slice_in_dim(source, spot[g] * BLOCK, BLOCK, axis=0)
            own.append(jnp.where(mine[g], piece, jnp.zeros_like(piece)))
    glob = lax.psum(jnp.stack(own), SEQ).reshape(GLOBAL, 3, BLOCK, features)

    global_q = glob[:, 0].reshape(GLOBAL * BLOCK, heads, DH)
    scores = jnp.einsum(
        "qhd,khd->hqk", global_q, key_vectors.reshape(rows, heads, DH),
        preferred_element_type=jnp.float32,
    ) * (DH ** (-0.5))
    top = lax.pmax(jnp.max(scores, axis=-1), SEQ)
    weights = jnp.exp(scores - top[..., None])
    part = jnp.einsum(
        "hqk,khd->hqd", weights, value_vectors.reshape(rows, heads, DH).astype(jnp.float32),
        precision=lax.Precision.HIGHEST,
    )
    both = lax.psum(
        jnp.concatenate([part.reshape(-1, DH), jnp.sum(weights, axis=-1).reshape(-1, DH)]), SEQ
    )
    many = heads * GLOBAL * BLOCK
    totals = both[many:].reshape(heads, GLOBAL * BLOCK, 1)
    gout = (both[:many].reshape(heads, GLOBAL * BLOCK, DH) / totals).astype(jnp.bfloat16)

    place = jnp.concatenate(
        [
            jnp.stack([my_index * blocks, jnp.int32(shards * blocks)]).astype(jnp.int32),
            jnp.where(mine, spot, -1).astype(jnp.int32),
        ]
    )
    attention = attended(
        slots, place, queries, key_vectors, value_vectors, kb, vb, ka, va, glob, gout, arrived
    )
    weight = lax.all_to_all(out_weight, "heads", split_axis=1, concat_axis=0, tiled=True)
    whole = lax.all_gather(attention, "heads", axis=1, tiled=True)
    return jnp.dot(whole, weight, preferred_element_type=jnp.float32).astype(jnp.bfloat16)


def solution(mesh):
    torus = Mesh(
        mesh.devices.reshape(mesh.shape["heads"], 8, 4, 2), ("heads", "seq_0", "seq_1", "seq_2")
    )
    in_specs = (
        P(SEQ, "heads"),
        P(SEQ, "heads"),
        P(SEQ, "heads"),
        P("heads", SEQ, None),
        P(),
        P("heads", None),
    )
    out_specs = P(SEQ, "heads")
    return jax.shard_map(
        on_device, mesh=torus, in_specs=in_specs, out_specs=out_specs, check_vma=False
    )
```

time: 508 us -> 1050 us (2.07)
  waiting for transfers between devices: 114 us -> 452 us
  Pallas kernels: 0 us -> 281 us
  blocking collectives: 246 us -> 202 us
  local copies, waits for them, and re-layouts: 64.3 us -> 22.3 us
  starting transfers between devices: 25.6 us -> 54.1 us
  other arithmetic: 24.2 us -> 11.9 us
    psum x0 -> x2, waiting for transfers between devices: none -> 359 us  [the longest x1 184 us: on_device(): glob = lax.psum(jnp.stack(own), SEQ).reshape(GLOBAL, 3, BLOCK, features)]
    pallas_call x0 -> x5, Pallas kernels: none -> 281 us  [the longest x4 261 us: picked(): pl.pallas_call(lambda *refs: pick_kernel(n, first, *refs), out_shape=jax....]
    all_gather x8 -> x0, blocking collectives: 168 us -> none  [the longest x6 153 us: gather_in_order(): parts = lax.all_gather(parts, axes[k], axis=0, tiled=True)]
    pmax x0 -> x1, blocking collectives: none -> 112 us  [on_device(): top = lax.pmax(jnp.max(scores, axis=-1), SEQ)]
    reduce_scatter x5 -> x0, waiting for transfers between devices: 104 us -> none  [sum_in_order(): parts = lax.psum_scatter(parts, axes[k], scatter_dimension=0, tiled=True)]
    ppermute x2 -> x18, waiting for transfers between devices: 0.01 us -> 92.8 us  [the longest x14 92.8 us: ring_step(): lax.ppermute(shard, 'seq_0', [(i, (i + step) % peers) for i in range(peer...]
    ppermute x2 -> x18, starting transfers between devices: 5.83 us -> 35.9 us  [the longest x14 22.1 us: ring_step(): lax.ppermute(shard, 'seq_0', [(i, (i + step) % peers) for i in range(peer...]
    gather x4 -> x0, local copies, waits for them, and re-layouts: 22.5 us -> none  [the longest x1 11 us: on_device(): fetched = arrived.reshape(shards * capacity, BLOCK, 2, DH)[slot_flat]]
  transfers between devices with their start and end apart: 10 -> 25, of which waited for: 6 -> 13; matrix products, arithmetic and copies ran while one was open for 8% -> 3% of each run, Pallas kernels for 0% -> 19%
where the time goes in v1:
time: 1050 us
  waiting for transfers between devices  452 us (43%)
  Pallas kernels  281 us (27%)
  blocking collectives  202 us (19%)
  starting transfers between devices  54.1 us (5%)
  local copies, waits for them, and re-layouts  22.3 us (2%)
  between operations  14.8 us (1%)
  other arithmetic  11.9 us (1%)
    pallas_call x4, Pallas kernels, picked(): pl.pallas_call(lambda *refs: pick_kernel(n, first, *refs), out_shape=jax....  261 us
    psum x1, waiting for transfers between devices, on_device(): glob = lax.psum(jnp.stack(own), SEQ).reshape(GLOBAL, 3, BLOCK, features)  184 us
    psum x1, waiting for transfers between devices, on_device(): lax.psum(jnp.concatenate([part.reshape(-1, DH), jnp.sum(weights, axis=-1)...  175 us
    pmax x1, blocking collectives, on_device(): top = lax.pmax(jnp.max(scores, axis=-1), SEQ)  112 us
    ppermute x14, waiting for transfers between devices, ring_step(): lax.ppermute(shard, 'seq_0', [(i, (i + step) % peers) for i in range(peer...  92.8 us
    all_to_all x1, blocking collectives, on_device(): lax.all_to_all(out_weight, 'heads', split_axis=1, concat_axis=0, tiled=True)  80.6 us
    ppermute x14, starting transfers between devices, ring_step(): lax.ppermute(shard, 'seq_0', [(i, (i + step) % peers) for i in range(peer...  22.1 us
  transfers between devices with their start and end apart: 25, of which 13 were waited for; matrix products, arithmetic and copies ran while one was open for 3% of the time, Pallas kernels for 19%

profile of v1, /device:TPU:32, one launch (start us, length us, event | category | flops | bytes accessed | tf_op | source)
XLA Modules:
  0.0 1047.9 jit_solution(2065145207916089993)
XLA Ops:
  6.5 1.9 collective-permute-start.4
  8.6 1.9 collective-permute-start.6
  10.5 2.0 collective-permute-start.7
  12.5 0.7 broadcast_remainder_fusion
  13.2 14.0 %collective-permute-done.4.refs_2_ = bf16[768,512]{1,0:T(8,128)(2,1)S(1)} collective-permute-done((bf16[768,512]{1,0:T(8,128)(2,1)}, bf16[768,512]{1,0:T(8,128)(2,1)S(1)}, u32[]{:S(2)}, u32[]{:S(2)}) %collective-permute-start.4) | collective-permute-done | bytes 786464 | tf_op jit(solution)/shard_map/ppermute | solution.py:23
  27.2 1.9 collective-permute-start.8
  29.1 2.1 collective-permute-start.9
  31.2 12.8 %collective-permute-done.6.refs_5_ = bf16[768,512]{1,0:T(8,128)(2,1)S(1)} collective-permute-done((bf16[768,512]{1,0:T(8,128)(2,1)}, bf16[768,512]{1,0:T(8,128)(2,1)S(1)}, u32[]{:S(2)}, u32[]{:S(2)}) %collective-permute-start.6) | collective-permute-done | bytes 786464 | tf_op jit(solution)/shard_map/ppermute | solution.py:23
  44.0 1.9 collective-permute-start.10
  46.1 2.0 collective-permute-start.11
  48.0 0.7 sign_compare_fusion
  49.9 9.5 all_to_all.48
  60.0 0.6 reduce.3
  60.6 0.6 reshape.160.refs_0_
  61.2 1.7 collective-permute-done.9.refs_2_
  62.9 13.8 %collective-permute-done.10.refs_3_ = bf16[768,512]{1,0:T(8,128)(2,1)} collective-permute-done((bf16[768,512]{1,0:T(8,128)(2,1)S(1)}, bf16[768,512]{1,0:T(8,128)(2,1)}, u32[]{:S(2)}, u32[]{:S(2)}) %collective-permute-start.10) | collective-permute-done | bytes 786464 | tf_op jit(solution)/shard_map/ppermute | solution.py:23
  76.7 1.8 collective-permute-done.11.refs_4_
  78.5 65.3 %pick_blocks.5 = bf16[8,2,4,2,64,128]{5,4,3,2,1,0:T(8,128)(2,1)} custom-call(s32[256]{0:T(256)} %reshape.160.refs_0_, bf16[768,512]{1,0:T(8,128)(2,1)} %collective-permute-done.8.refs_1_, bf16[768,512]{1,0:T(8,128)(2,1)} %collective-permute-done.9.refs_2_, bf16[768,512]{1,0:T(8,128)(2,1)} %collective-permute-done.10.refs_3_, ...), custom_call_target="tpu_custom_call" | custom-call | bytes 4194304 | tf_op jit(solution)/shard_map/pick_blocks/pallas_call | solution.py:49
  143.9 4.5 all-to-all-start.2
  148.4 97.1 %pick_blocks.4 = bf16[8,3,4,2,64,128]{5,4,3,2,1,0:T(8,128)(2,1)} custom-call(s32[256]{0:T(256)} %reshape.160.refs_0_, bf16[768,512]{1,0:T(8,128)(2,1)} %refs_3_.1, bf16[768,512]{1,0:T(8,128)(2,1)} %copy-done.4, bf16[768,512]{1,0:T(8,128)(2,1)} %copy-done.5, bf16[768,512]{1,0:T(8,128)(2,1)} %refs_4_.3, bf16[768,512]{1,0:T(8,128)(2,1)} %copy-done.6, ...), custom_call_target="tpu_custom_call" | custom-call | bytes 6291456 | tf_op jit(solution)/shard_map/pick_blocks/pallas_call | solution.py:49
  245.5 1.3 copy-done.3
  246.9 4.8 all-to-all-start.1
  251.7 3.2 collective-permute-start.12
  254.9 17.7 %collective-permute-done.12.refs_1_ = bf16[768,512]{1,0:T(8,128)(2,1)S(1)} collective-permute-done((bf16[768,512]{1,0:T(8,128)(2,1)}, bf16[768,512]{1,0:T(8,128)(2,1)S(1)}, u32[]{:S(2)}, u32[]{:S(2)}) %collective-permute-start.12) | collective-permute-done | bytes 786464 | tf_op jit(solution)/shard_map/ppermute | solution.py:23
  272.6 1.0 copy-done.7
  273.6 2.9 collective-permute-start.16
  276.5 17.4 %collective-permute-done.16.refs_1_ = bf16[768,512]{1,0:T(8,128)(2,1)} collective-permute-done((bf16[768,512]{1,0:T(8,128)(2,1)S(1)}, bf16[768,512]{1,0:T(8,128)(2,1)}, u32[]{:S(2)}, u32[]{:S(2)}) %collective-permute-start.16) | collective-permute-done | bytes 786464 | tf_op jit(solution)/shard_map/ppermute | solution.py:23
  293.9 2.2 collective-permute-done.17.refs_2_
  296.0 33.6 %pick_blocks.7 = bf16[8,1,4,2,64,128]{5,4,3,2,1,0:T(8,128)(2,1)} custom-call(s32[256]{0:T(256)} %reshape.160.refs_0_, bf16[768,512]{1,0:T(8,128)(2,1)} %collective-permute-done.16.refs_1_, bf16[768,512]{1,0:T(8,128)(2,1)} %collective-permute-done.17.refs_2_), custom_call_target="tpu_custom_call" | custom-call | bytes 2097152 | tf_op jit(solution)/shard_map/pick_blocks/pallas_call | solution.py:49
  329.6 4.3 all-to-all-start.4
  333.9 0.9 collective-permute-start.13
  334.8 1.2 collective-permute-start.14
  336.0 0.7 fusion.19
  338.0 0.6 fusion.18
  338.5 1.5 bitcast_dynamic-update-slice_fusion.5
  340.0 1.5 bitcast_dynamic-update-slice_fusion.4
  341.5 1.5 bitcast_dynamic-update-slice_fusion.3
  343.0 1.4 bitcast_dynamic-update-slice_fusion.2
  344.4 9.6 collective-permute-done.13.refs_2_
  354.0 1.7 collective-permute-done.14.refs_3_
  355.8 65.3 %pick_blocks.6 = bf16[8,2,4,2,64,128]{5,4,3,2,1,0:T(8,128)(2,1)} custom-call(s32[256]{0:T(256)} %reshape.160.refs_0_, bf16[768,512]{1,0:T(8,128)(2,1)} %copy-done.7, bf16[768,512]{1,0:T(8,128)(2,1)} %collective-permute-done.13.refs_2_, bf16[768,512]{1,0:T(8,128)(2,1)} %collective-permute-done.14.refs_3_, bf16[768,512]{1,0:T(8,128)(2,1)} %copy-done.8), custom_call_target="tpu_custom_call" | custom-call | bytes 4194304 | tf_op jit(solution)/shard_map/pick_blocks/pallas_call | solution.py:49
  421.1 4.6 all-to-all-start.3
  425.8 0.6 bitcast_dynamic-update-slice_fusion.1
  426.4 0.6 bitcast_dynamic-update-slice_fusion
  427.0 0.7 copy-done.9
  427.8 2.4 collective-permute-start
  430.2 184.0 %all-reduce.3.cloned.1.call-done.refs_9_ = bf16[2,3,64,512]{3,2,1,0:T(8,128)(2,1)} async-done(((bf16[2,3,64,512]{3,2,1,0:T(8,128)(2,1)}), bf16[2,3,64,512]{3,2,1,0:T(8,128)(2,1)}) %all-reduce.3.cloned.1.call-update) | async-done | bytes 393232 | tf_op jit(solution)/shard_map/psum | solution.py:223
  614.2 0.9 slice.52
  615.6 111.9 %pmax.7 = f32[4,128]{1,0:T(4,128)S(1)} all-reduce(f32[4,128]{1,0:T(4,128)S(1)} %get-tuple-element.20), channel_id=1, replica_groups=mesh['heads'=4,'seq_0'=8,'seq_1'=4,'seq_2'=2] {'seq_0','seq_1','seq_2'}, use_global_device_ids=true, to_apply=%region_3.4 | all-reduce | flops 512 | bytes 4096 | tf_op jit(solution)/shard_map/pmax | solution.py:230
  727.9 1.1 fusion.1
  729.0 0.7 pad_maximum_fusion
  729.8 1.9 collective-permute-start.1
  731.7 5.8 collective-permute-start.2
  737.5 3.8 collective-permute-start.3
  741.2 0.6 pad_add_fusion.refs_1_
  741.8 175.3 %all-reduce.5.cloned.1.call-done = f32[516,128]{1,0:T(8,128)} async-done(((f32[516,128]{1,0:T(8,128)}), f32[516,128]{1,0:T(8,128)}) %all-reduce.5.cloned.1.call-update) | async-done | bytes 264208 | tf_op jit(solution)/shard_map/psum | solution.py:236
  917.1 1.0 slice.53
  918.1 0.7 slice.54
  918.8 0.8 divide_convert_fusion.refs_10_
  920.3 19.9 %attend.1 = bf16[768,512]{1,0:T(8,128)(2,1)} custom-call(s32[144]{0:T(256)} %copy-done.14, s32[4]{0:T(128)} %pad_add_fusion.refs_1_, bf16[768,512]{1,0:T(8,128)(2,1)} %refs_2_.1, bf16[768,512]{1,0:T(8,128)(2,1)} %refs_3_.1, bf16[768,512]{1,0:T(8,128)(2,1)} %refs_4_.3, bf16[64,512]{1,0:T(8,128)(2,1)} %copy-done.10, bf16[64,512]{1,0:T(8,128)(2,1)} %copy-done.11, ...), custom_call_target="tpu_custom_call" | custom-call | flops 805306368 | bytes 12582912 | tf_op jit(solution)/shard_map/attend/pallas_call | solution.py:143
  940.2 6.5 copy.30
  946.7 80.6 %all_to_all.49 = bf16[512,4,1024]{0,2,1:T(8,128)(2,1)} all-to-all(bf16[512,4,1024]{0,2,1:T(8,128)(2,1)} %bitcast.44), channel_id=1, replica_groups=mesh['heads'=4,'seq_0'=8,'seq_1'=4,'seq_2'=2] {'heads'}, dimensions={1} | all-to-all | bytes 8388608 | tf_op jit(solution)/shard_map/all_to_all | solution.py:252
  1027.3 6.3 copy.31
  1033.6 7.7 convolution_convert_fusion
  (69 shorter events, 3.7 us)
Async XLA Ops:
  6.5 20.6 %collective-permute-start.4 = (bf16[768,512]{1,0:T(8,128)(2,1)}, bf16[768,512]{1,0:T(8,128)(2,1)S(1)}, u32[]{:S(2)}, u32[]{:S(2)}) collective-permute-start(bf16[768,512]{1,0:T(8,128)(2,1)} %refs_3_.1), channel_id=1, source_target_pairs={{0,8},{8,16},{16,24},{24,32},{32,40},{40,48},{48,56},{56,0},{1,9},... | collective-permute-start | bytes 2359304 | tf_op jit(solution)/shard_map/ppermute | solution.py:23
  8.5 20.7 %collective-permute-start.5 = (bf16[768,512]{1,0:T(8,128)(2,1)}, bf16[768,512]{1,0:T(8,128)(2,1)S(1)}, u32[]{:S(2)}, u32[]{:S(2)}) collective-permute-start(bf16[768,512]{1,0:T(8,128)(2,1)} %refs_3_.1), channel_id=1, source_target_pairs={{0,56},{8,0},{16,8},{24,16},{32,24},{40,32},{48,40},{56,48},{1,57}... | collective-permute-start | bytes 2359304 | tf_op jit(solution)/shard_map/ppermute | solution.py:23
  8.6 35.5 %collective-permute-start.6 = (bf16[768,512]{1,0:T(8,128)(2,1)}, bf16[768,512]{1,0:T(8,128)(2,1)S(1)}, u32[]{:S(2)}, u32[]{:S(2)}) collective-permute-start(bf16[768,512]{1,0:T(8,128)(2,1)} %refs_4_.3), channel_id=1, source_target_pairs={{0,8},{8,16},{16,24},{24,32},{32,40},{40,48},{48,56},{56,0},{1,9},... | collective-permute-start | bytes 2359304 | tf_op jit(solution)/shard_map/ppermute | solution.py:23
  10.5 35.6 %collective-permute-start.7 = (bf16[768,512]{1,0:T(8,128)(2,1)}, bf16[768,512]{1,0:T(8,128)(2,1)}, u32[]{:S(2)}, u32[]{:S(2)}) collective-permute-start(bf16[768,512]{1,0:T(8,128)(2,1)} %refs_4_.3), channel_id=1, source_target_pairs={{0,56},{8,0},{16,8},{24,16},{32,24},{40,32},{48,40},{56,48},{1,57}... | collective-permute-start | bytes 2359304 | tf_op jit(solution)/shard_map/ppermute | solution.py:23
  27.2 116.7 %copy-start.4 = (bf16[768,512]{1,0:T(8,128)(2,1)}, bf16[768,512]{1,0:T(8,128)(2,1)S(1)}, u32[]{:S(2)}) copy-start(bf16[768,512]{1,0:T(8,128)(2,1)S(1)} %collective-permute-done.4.refs_2_) | copy-start | bytes 2359300
  27.2 34.1 %collective-permute-start.8 = (bf16[768,512]{1,0:T(8,128)(2,1)S(1)}, bf16[768,512]{1,0:T(8,128)(2,1)}, u32[]{:S(2)}, u32[]{:S(2)}) collective-permute-start(bf16[768,512]{1,0:T(8,128)(2,1)S(1)} %collective-permute-done.4.refs_2_), channel_id=1, source_target_pairs={{0,8},{8,16},{16,24},{24,32},{32,40},{40,48},{48,56},{56,0},{1,9},... | collective-permute-start | bytes 2359304 | tf_op jit(solution)/shard_map/ppermute | solution.py:23
  29.1 114.8 %copy-start.5 = (bf16[768,512]{1,0:T(8,128)(2,1)}, bf16[768,512]{1,0:T(8,128)(2,1)S(1)}, u32[]{:S(2)}) copy-start(bf16[768,512]{1,0:T(8,128)(2,1)S(1)} %collective-permute-done.5.refs_3_) | copy-start | bytes 2359300
  29.1 33.8 %collective-permute-start.9 = (bf16[768,512]{1,0:T(8,128)(2,1)S(1)}, bf16[768,512]{1,0:T(8,128)(2,1)}, u32[]{:S(2)}, u32[]{:S(2)}) collective-permute-start(bf16[768,512]{1,0:T(8,128)(2,1)S(1)} %collective-permute-done.5.refs_3_), channel_id=1, source_target_pairs={{0,56},{8,0},{16,8},{24,16},{32,24},{40,32},{48,40},{56,48},{1,57}... | collective-permute-start | bytes 2359304 | tf_op jit(solution)/shard_map/ppermute | solution.py:23
  44.0 99.9 %copy-start.6 = (bf16[768,512]{1,0:T(8,128)(2,1)}, bf16[768,512]{1,0:T(8,128)(2,1)S(1)}, u32[]{:S(2)}) copy-start(bf16[768,512]{1,0:T(8,128)(2,1)S(1)} %collective-permute-done.6.refs_5_) | copy-start | bytes 2359300
  44.0 32.7 %collective-permute-start.10 = (bf16[768,512]{1,0:T(8,128)(2,1)S(1)}, bf16[768,512]{1,0:T(8,128)(2,1)}, u32[]{:S(2)}, u32[]{:S(2)}) collective-permute-start(bf16[768,512]{1,0:T(8,128)(2,1)S(1)} %collective-permute-done.6.refs_5_), channel_id=1, source_target_pairs={{0,8},{8,16},{16,24},{24,32},{32,40},{40,48},{48,56},{56,0},{1,9},... | collective-permute-start | bytes 2359304 | tf_op jit(solution)/shard_map/ppermute | solution.py:23
  46.1 32.5 %collective-permute-start.11 = (bf16[768,512]{1,0:T(8,128)(2,1)}, bf16[768,512]{1,0:T(8,128)(2,1)}, u32[]{:S(2)}, u32[]{:S(2)}) collective-permute-start(bf16[768,512]{1,0:T(8,128)(2,1)} %collective-permute-done.7.refs_6_), channel_id=1, source_target_pairs={{0,56},{8,0},{16,8},{24,16},{32,24},{40,32},{48,40},{56,48},{1,57}... | collective-permute-start | bytes 2359304 | tf_op jit(solution)/shard_map/ppermute | solution.py:23
  49.7 94.2 %copy-start.14 = (s32[144]{0:T(256)}, s32[144]{0:T(256)S(1)}, u32[]{:S(2)}) copy-start(s32[144]{0:T(256)S(1)} %multiply_add_fusion.refs_0_) | copy-start | bytes 1732
  143.9 101.6 %all-to-all-start.2 = ((bf16[8,2,4,2,64,128]{5,4,3,2,1,0:T(8,128)(2,1)}), bf16[8,2,4,2,64,128]{5,4,3,2,1,0:T(8,128)(2,1)S(1)}, u32[]{:S(2)}, u32[]{:S(2)}) async-start(bf16[8,2,4,2,64,128]{5,4,3,2,1,0:T(8,128)(2,1)} %pick_blocks.5), calls=%async_computation.2 | async-start | bytes 4194304 | tf_op jit(solution)/shard_map/all_to_all | solution.py:212
  245.5 1.4 copy-start.3
  246.9 82.8 %all-to-all-start.1 = ((bf16[8,3,4,2,64,128]{5,4,3,2,1,0:T(8,128)(2,1)}), bf16[8,3,4,2,64,128]{5,4,3,2,1,0:T(8,128)(2,1)S(1)}, u32[]{:S(2)}, u32[]{:S(2)}) async-start(bf16[8,3,4,2,64,128]{5,4,3,2,1,0:T(8,128)(2,1)} %pick_blocks.4), calls=%async_computation.1 | async-start | bytes 6291456 | tf_op jit(solution)/shard_map/all_to_all | solution.py:212
  251.7 84.4 %copy-start.15 = (s32[2]{0:T(128)S(1)}, s32[2]{0:T(128)}, u32[]{:S(2)}) copy-start(s32[2]{0:T(128)} %param.10) | copy-start | bytes 28
  251.7 20.9 %collective-permute-start.12 = (bf16[768,512]{1,0:T(8,128)(2,1)}, bf16[768,512]{1,0:T(8,128)(2,1)S(1)}, u32[]{:S(2)}, u32[]{:S(2)}) collective-permute-start(bf16[768,512]{1,0:T(8,128)(2,1)} %collective-permute-done.8.refs_1_), channel_id=1, source_target_pairs={{0,8},{8,16},{16,24},{24,32},{32,40},{40,48},{48,56},{56,0},{1,9},... | collective-permute-start | bytes 2359304 | tf_op jit(solution)/shard_map/ppermute | solution.py:23
  254.9 21.6 %collective-permute-start.15 = (bf16[768,512]{1,0:T(8,128)(2,1)}, bf16[768,512]{1,0:T(8,128)(2,1)S(1)}, u32[]{:S(2)}, u32[]{:S(2)}) collective-permute-start(bf16[768,512]{1,0:T(8,128)(2,1)} %collective-permute-done.11.refs_4_), channel_id=1, source_target_pairs={{0,56},{8,0},{16,8},{24,16},{32,24},{40,32},{48,40},{56,48},{1,57}... | collective-permute-start | bytes 2359304 | tf_op jit(solution)/shard_map/ppermute | solution.py:23
  272.6 1.0 copy-start.7
  273.6 20.3 %collective-permute-start.16 = (bf16[768,512]{1,0:T(8,128)(2,1)S(1)}, bf16[768,512]{1,0:T(8,128)(2,1)}, u32[]{:S(2)}, u32[]{:S(2)}) collective-permute-start(bf16[768,512]{1,0:T(8,128)(2,1)S(1)} %collective-permute-done.12.refs_1_), channel_id=1, source_target_pairs={{0,8},{8,16},{16,24},{24,32},{32,40},{40,48},{48,56},{56,0},{1,9},... | collective-permute-start | bytes 2359304 | tf_op jit(solution)/shard_map/ppermute | solution.py:23
  276.5 17.4 %copy-start.8 = (bf16[768,512]{1,0:T(8,128)(2,1)}, bf16[768,512]{1,0:T(8,128)(2,1)S(1)}, u32[]{:S(2)}) copy-start(bf16[768,512]{1,0:T(8,128)(2,1)S(1)} %collective-permute-done.15.refs_4_) | copy-start | bytes 2359300
  276.5 19.6 %collective-permute-start.17 = (bf16[768,512]{1,0:T(8,128)(2,1)S(1)}, bf16[768,512]{1,0:T(8,128)(2,1)}, u32[]{:S(2)}, u32[]{:S(2)}) collective-permute-start(bf16[768,512]{1,0:T(8,128)(2,1)S(1)} %collective-permute-done.15.refs_4_), channel_id=1, source_target_pairs={{0,56},{8,0},{16,8},{24,16},{32,24},{40,32},{48,40},{56,48},{1,57}... | collective-permute-start | bytes 2359304 | tf_op jit(solution)/shard_map/ppermute | solution.py:23
  329.6 91.5 %copy-start = (bf16[8,3,4,2,64,128]{5,4,3,2,1,0:T(8,128)(2,1)}, bf16[8,3,4,2,64,128]{5,4,3,2,1,0:T(8,128)(2,1)S(1)}, u32[]{:S(2)}) copy-start(bf16[8,3,4,2,64,128]{5,4,3,2,1,0:T(8,128)(2,1)S(1)} %all-to-all-done.1.refs_11_) | copy-start | bytes 9437188
  329.6 91.5 %all-to-all-start.4 = ((bf16[8,1,4,2,64,128]{5,4,3,2,1,0:T(8,128)(2,1)}), bf16[8,1,4,2,64,128]{5,4,3,2,1,0:T(8,128)(2,1)}, u32[]{:S(2)}, u32[]{:S(2)}) async-start(bf16[8,1,4,2,64,128]{5,4,3,2,1,0:T(8,128)(2,1)} %pick_blocks.7), calls=%async_computation.4 | async-start | bytes 2097152 | tf_op jit(solution)/shard_map/all_to_all | solution.py:212
  333.9 20.1 %collective-permute-start.13 = (bf16[768,512]{1,0:T(8,128)(2,1)}, bf16[768,512]{1,0:T(8,128)(2,1)}, u32[]{:S(2)}, u32[]{:S(2)}) collective-permute-start(bf16[768,512]{1,0:T(8,128)(2,1)} %collective-permute-done.9.refs_2_), channel_id=1, source_target_pairs={{0,56},{8,0},{16,8},{24,16},{32,24},{40,32},{48,40},{56,48},{1,57}... | collective-permute-start | bytes 2359304 | tf_op jit(solution)/shard_map/ppermute | solution.py:23
  334.8 21.0 %collective-permute-start.14 = (bf16[768,512]{1,0:T(8,128)(2,1)}, bf16[768,512]{1,0:T(8,128)(2,1)}, u32[]{:S(2)}, u32[]{:S(2)}) collective-permute-start(bf16[768,512]{1,0:T(8,128)(2,1)} %collective-permute-done.10.refs_3_), channel_id=1, source_target_pairs={{0,8},{8,16},{16,24},{24,32},{32,40},{40,48},{48,56},{56,0},{1,9},... | collective-permute-start | bytes 2359304 | tf_op jit(solution)/shard_map/ppermute | solution.py:23
  421.1 4.7 copy-start.1
  421.1 5.3 copy-start.2
  421.1 498.5 %all-to-all-start.3 = ((bf16[8,2,4,2,64,128]{5,4,3,2,1,0:T(8,128)(2,1)}), bf16[8,2,4,2,64,128]{5,4,3,2,1,0:T(8,128)(2,1)}, u32[]{:S(2)}, u32[]{:S(2)}) async-start(bf16[8,2,4,2,64,128]{5,4,3,2,1,0:T(8,128)(2,1)} %pick_blocks.6), calls=%async_computation.3 | async-start | bytes 4194304 | tf_op jit(solution)/shard_map/all_to_all | solution.py:212
  425.7 188.5 %all-reduce.3.cloned.1.call-start = ((), (), s32[]{:S(2)}) async-start(), calls=%async_computation.6 | async-start | bytes 786432 | tf_op jit(solution)/shard_map/psum | solution.py:223
  427.0 0.7 copy-start.9
  427.7 489.4 %all-reduce.5.cloned.1.call-start = ((), (), s32[]{:S(2)}) async-start(), calls=%async_computation.7 | async-start | bytes 532480 | tf_op jit(solution)/shard_map/psum | solution.py:236
  427.8 491.8 %collective-permute-start = (bf16[64,512]{1,0:T(8,128)(2,1)S(1)}, bf16[64,512]{1,0:T(8,128)(2,1)S(1)}, u32[]{:S(2)}, u32[]{:S(2)}) collective-permute-start(bf16[64,512]{1,0:T(8,128)(2,1)S(1)} %get-tuple-element.11), channel_id=1, source_target_pairs={{0,1},{1,2},{2,3},{3,4},{4,5},{5,6},{6,7},{7,8},{8,9},{9,10},{10,1... | collective-permute-start | bytes 196616 | tf_op jit(solution)/shard_map/ppermute | solution.py:189
  729.7 303.9 %all-gather.2.cloned.1.call-start = ((), (), s32[]{:S(2)}) async-start(), calls=%async_computation.8 | async-start | bytes 3932160 | tf_op jit(solution)/shard_map/all_gather | solution.py:253
  729.8 189.8 %collective-permute-start.1 = (bf16[64,512]{1,0:T(8,128)(2,1)S(1)}, bf16[64,512]{1,0:T(8,128)(2,1)S(1)}, u32[]{:S(2)}, u32[]{:S(2)}) collective-permute-start(bf16[64,512]{1,0:T(8,128)(2,1)S(1)} %get-tuple-element.9), channel_id=1, source_target_pairs={{0,1},{1,2},{2,3},{3,4},{4,5},{5,6},{6,7},{7,8},{8,9},{9,10},{10,1... | collective-permute-start | bytes 196616 | tf_op jit(solution)/shard_map/ppermute | solution.py:190
  731.7 187.9 %collective-permute-start.2 = (bf16[64,512]{1,0:T(8,128)(2,1)S(1)}, bf16[64,512]{1,0:T(8,128)(2,1)S(1)}, u32[]{:S(2)}, u32[]{:S(2)}) collective-permute-start(bf16[64,512]{1,0:T(8,128)(2,1)S(1)} %get-tuple-element.10), channel_id=1, source_target_pairs={{1,0},{2,1},{3,2},{4,3},{5,4},{6,5},{7,6},{8,7},{9,8},{10,9},{11,1... | collective-permute-start | bytes 196616 | tf_op jit(solution)/shard_map/ppermute | solution.py:191
  737.5 182.2 %collective-permute-start.3 = (bf16[64,512]{1,0:T(8,128)(2,1)S(1)}, bf16[64,512]{1,0:T(8,128)(2,1)S(1)}, u32[]{:S(2)}, u32[]{:S(2)}) collective-permute-start(bf16[64,512]{1,0:T(8,128)(2,1)S(1)} %get-tuple-element.8), channel_id=1, source_target_pairs={{1,0},{2,1},{3,2},{4,3},{5,4},{6,5},{7,6},{8,7},{9,8},{10,9},{11,1... | collective-permute-start | bytes 196616 | tf_op jit(solution)/shard_map/ppermute | solution.py:192
  919.6 0.6 copy-start.10
  919.6 0.6 copy-start.11
  919.6 0.6 copy-start.12
  919.6 0.6 copy-start.13
Sparse Core Ops, SparseCore 0:
  430.0 184.1 all-reduce.2
  729.8 187.2 all-reduce.4
  940.3 86.2 all-gather.1

commit v2 on v1

--- a/solution.py
+++ b/solution.py
@@ -23,8 +23,13 @@
     return lax.ppermute(shard, "seq_0", [(i, (i + step) % peers) for i in range(peers)])
 
 
+def across(shard, step):
+    peers = lax.axis_size("heads")
+    return lax.ppermute(shard, "heads", [(i, (i + step) % peers) for i in range(peers)])
+
+
 def pick_kernel(n, first, codes, *refs):
-    keys, values, out, sem = refs[:n], refs[n : 2 * n], refs[2 * n], refs[2 * n + 1]
+    keys, values, out = refs[:n], refs[n : 2 * n], refs[2 * n]
 
     def one_peer(peer, carry):
         for run in range(n):
@@ -32,30 +37,104 @@
                 code = codes[(peer * PLANES + first + run) * CAP + rank]
                 rows = pl.ds(pl.multiple_of((code & 15) * BLOCK, BLOCK), BLOCK)
                 cols = pl.ds(pl.multiple_of((code >> 4) * DH, DH), DH)
-                for side, source in enumerate((keys[run], values[run])):
-                    pltpu.make_async_copy(
-                        source.at[rows, cols], out.at[peer, run, rank, side], sem
-                    ).start()
+                out[peer, run, rank, 0] = keys[run][rows, cols]
+                out[peer, run, rank, 1] = values[run][rows, cols]
         return carry
 
     lax.fori_loop(0, INPLANE, one_peer, 0)
-    pltpu.make_async_copy(out, out, sem).wait()
 
 
 def picked(codes, first, keys, values):
     n = len(keys)
     shape = (INPLANE, n, CAP, 2, BLOCK, DH)
-    size = 2 * INPLANE * n * CAP * 2 * BLOCK * DH * 2
+    size = 2 * (sum(k.size for k in keys) * 2 + INPLANE * n * CAP * 2 * BLOCK * DH)
+    vmem = pl.BlockSpec(memory_space=pltpu.VMEM)
     return pl.pallas_call(
         lambda *refs: pick_kernel(n, first, *refs),
         out_shape=jax.ShapeDtypeStruct(shape, jnp.bfloat16),
-        in_specs=[pl.BlockSpec(memory_space=pltpu.SMEM)]
-        + [pl.BlockSpec(memory_space=pl.ANY)] * (2 * n),
-        out_specs=pl.BlockSpec(memory_space=pl.ANY),
-        scratch_shapes=[pltpu.SemaphoreType.DMA],
+        in_specs=[pl.BlockSpec(memory_space=pltpu.SMEM)] + [vmem] * (2 * n),
+        out_specs=vmem,
+        compiler_params=pltpu.CompilerParams(vmem_limit_bytes=32 * 2**20),
         cost_estimate=pl.CostEstimate(flops=0, bytes_accessed=size, transcendentals=0),
         name="pick_blocks",
     )(codes, *keys, *values)
+
+
+def exchanged(asked, first, blocks):
+    n = len(blocks) // 2
+    picks = picked(asked, first, blocks[:n], blocks[n:])
+    return lax.all_to_all(picks, PLANE, split_axis=0, concat_axis=0, tiled=True)
+
+
+def global_kernel(glob, k, v, out):
+    heads = k.shape[1] // DH
+    many = GLOBAL * BLOCK
+    lane = lax.broadcasted_iota(jnp.int32, (many, DH), 1)
+    for h in range(heads):
+        hs = slice(h * DH, (h + 1) * DH)
+        rows = slice(h * many, (h + 1) * many)
+        asking = jnp.concatenate([glob[g, 0, :, hs] for g in range(GLOBAL)], axis=0)
+        scores = lax.dot_general(
+            asking, k[:, hs], (((1,), (1,)), ((), ())), preferred_element_type=jnp.float32
+        ) * (DH ** (-0.5))
+        top = jnp.max(scores, axis=1, keepdims=True).astype(jnp.bfloat16).astype(jnp.float32)
+        weights = jnp.exp(scores - top)
+        total = jnp.sum(weights, axis=1, keepdims=True)
+        upper = weights.astype(jnp.bfloat16)
+        lower = (weights - upper.astype(jnp.float32)).astype(jnp.bfloat16)
+        part = jnp.dot(upper, v[:, hs], preferred_element_type=jnp.float32) + jnp.dot(
+            lower, v[:, hs], preferred_element_type=jnp.float32
+        )
+        out[rows] = packed(part, top, total, lane)
+
+
+def packed(part, top, total, lane):
+    upper = total.astype(jnp.bfloat16).astype(jnp.float32)
+    side = jnp.where(lane == 0, top, jnp.where(lane == 1, upper, total - upper))
+    return jnp.concatenate([part, side], axis=1).astype(jnp.bfloat16)
+
+
+def global_parts(glob, k, v):
+    vmem = pl.BlockSpec(memory_space=pltpu.VMEM)
+    heads = k.shape[1] // DH
+    return pl.pallas_call(
+        global_kernel,
+        out_shape=jax.ShapeDtypeStruct((heads * GLOBAL * BLOCK, 2 * DH), jnp.bfloat16),
+        in_specs=[vmem] * 3,
+        out_specs=vmem,
+        compiler_params=pltpu.CompilerParams(vmem_limit_bytes=32 * 2**20),
+        name="global_parts",
+    )(glob, k, v)
+
+
+def merge_kernel(last, parts, out):
+    rows = parts.shape[1]
+    tops = [parts[p, :, DH : DH + 1].astype(jnp.float32) for p in range(parts.shape[0])]
+    top = tops[0]
+    for other in tops[1:]:
+        top = jnp.maximum(top, other)
+    part = jnp.zeros((rows, DH), jnp.float32)
+    total = jnp.zeros((rows, 1), jnp.float32)
+    for p, own in enumerate(tops):
+        scale = jnp.exp(own - top)
+        part += scale * parts[p, :, :DH].astype(jnp.float32)
+        held = parts[p, :, DH + 1 : DH + 2].astype(jnp.float32)
+        total += scale * (held + parts[p, :, DH + 2 : DH + 3].astype(jnp.float32))
+    if last:
+        out[...] = (part / total).astype(jnp.bfloat16)
+    else:
+        out[...] = packed(part, top, total, lax.broadcasted_iota(jnp.int32, (rows, DH), 1))
+
+
+def merged(parts, last):
+    vmem = pl.BlockSpec(memory_space=pltpu.VMEM)
+    return pl.pallas_call(
+        lambda *refs: merge_kernel(last, *refs),
+        out_shape=jax.ShapeDtypeStruct((parts.shape[1], DH if last else 2 * DH), jnp.bfloat16),
+        in_specs=[vmem],
+        out_specs=vmem,
+        name="merge_parts",
+    )(parts)
 
 
 def attend_kernel(
@@ -132,7 +211,8 @@
         def _():
             at_rows = pl.ds(pl.multiple_of(place[2 + g] * BLOCK, BLOCK), BLOCK)
             for h in range(heads):
-                out[at_rows, h * DH : (h + 1) * DH] = gout[h, g * BLOCK : (g + 1) * BLOCK]
+                first = (h * GLOBAL + g) * BLOCK
+                out[at_rows, h * DH : (h + 1) * DH] = gout[first : first + BLOCK]
 
 
 def attended(slots, place, q, k, v, kb, vb, ka, va, glob, gout, arrived):
@@ -170,6 +250,14 @@
     blocks = rows // BLOCK
     requests = heads * blocks * RANDOM
 
+    me = lax.axis_index("heads")
+    peers = lax.axis_size("heads")
+    width = out_weight.shape[1] // peers
+    weights = []
+    for away in (0, 1, -1, 2):
+        piece = lax.dynamic_slice_in_dim(out_weight, ((me + away) % peers) * width, width, axis=1)
+        weights.append(across(piece, away) if away else piece)
+
     flat = random_blocks.reshape(requests)
     holders = flat // blocks
     number = jnp.arange(requests, dtype=jnp.int32)
@@ -191,14 +279,40 @@
     ka = lax.ppermute(key_vectors[:BLOCK], SEQ, back)
     va = lax.ppermute(value_vectors[:BLOCK], SEQ, back)
 
+    holder = global_blocks // blocks
+    spot = global_blocks % blocks
+    mine = holder == my_index
+    own = []
+    for g in range(GLOBAL):
+        for source in (queries, key_vectors, value_vectors):
+            piece = lax.dynamic_slice_in_dim(source, spot[g] * BLOCK, BLOCK, axis=0)
+            own.append(jnp.where(mine[g], piece, jnp.zeros_like(piece)))
+    own = jnp.concatenate(own).reshape(INPLANE, -1, features)
+    own = lax.all_to_all(own, PLANE, split_axis=0, concat_axis=0, tiled=True).sum(axis=0)
+    own = lax.all_gather(own, "seq_0").sum(axis=0)
+    glob = lax.all_gather(own, PLANE).reshape(GLOBAL, 3, BLOCK, features)
+
+    parts = global_parts(glob, key_vectors, value_vectors).reshape(INPLANE, -1, 2 * DH)
+    parts = lax.all_to_all(parts, PLANE, split_axis=0, concat_axis=0, tiled=True)
+    parts = lax.all_gather(merged(parts, False), "seq_0")
+    gout = lax.all_gather(merged(parts, True), PLANE, tiled=True)
+
     up_k, up_v, down_k, down_v = key_vectors, value_vectors, key_vectors, value_vectors
     keys, values = [key_vectors], [value_vectors]
     arrived = []
     first = 0
+    waiting = None
+    beside = {2: [kb, vb, ka, va, glob], 3: weights, 4: gout}
     for step in range(1, PLANES // 2 + 1):
         last = step == PLANES // 2
         up_k = ring_step(up_k, 1)
         down_v = ring_step(down_v, -1)
+        if waiting is not None:
+            waiting, _, _, arrived, beside[step] = lax.optimization_barrier(
+                (waiting, up_k, down_v, arrived, beside[step])
+            )
+            arrived = arrived + [exchanged(asked, first, waiting)]
+            first += len(waiting) // 2
         if last:
             keys.append(up_k)
             values.append(down_v)
@@ -207,39 +321,13 @@
             down_k = ring_step(down_k, -1)
             keys += [up_k, down_k]
             values += [up_v, down_v]
-        picks = picked(asked, first, keys, values)
-        first += len(keys)
-        arrived.append(lax.all_to_all(picks, PLANE, split_axis=0, concat_axis=0, tiled=True))
+        waiting = keys + values
         keys, values = [], []
-
-    holder = global_blocks // blocks
-    spot = global_blocks % blocks
-    mine = holder == my_index
-    own = []
-    for g in range(GLOBAL):
-        for source in (queries, key_vectors, value_vectors):
-            piece = lax.dynamic_slice_in_dim(source, spot[g] * BLOCK, BLOCK, axis=0)
-            own.append(jnp.where(mine[g], piece, jnp.zeros_like(piece)))
-    glob = lax.psum(jnp.stack(own), SEQ).reshape(GLOBAL, 3, BLOCK, features)
-
-    global_q = glob[:, 0].reshape(GLOBAL * BLOCK, heads, DH)
-    scores = jnp.einsum(
-        "qhd,khd->hqk", global_q, key_vectors.reshape(rows, heads, DH),
-        preferred_element_type=jnp.float32,
-    ) * (DH ** (-0.5))
-    top = lax.pmax(jnp.max(scores, axis=-1), SEQ)
-    weights = jnp.exp(scores - top[..., None])
-    part = jnp.einsum(
-        "hqk,khd->hqd", weights, value_vectors.reshape(rows, heads, DH).astype(jnp.float32),
-        precision=lax.Precision.HIGHEST,
-    )
-    both = lax.psum(
-        jnp.concatenate([part.reshape(-1, DH), jnp.sum(weights, axis=-1).reshape(-1, DH)]), SEQ
-    )
-    many = heads * GLOBAL * BLOCK
-    totals = both[many:].reshape(heads, GLOBAL * BLOCK, 1)
-    gout = (both[:many].reshape(heads, GLOBAL * BLOCK, DH) / totals).astype(jnp.bfloat16)
-
+    waiting, arrived = lax.optimization_barrier((waiting, arrived))
+    arrived = arrived + [exchanged(asked, first, waiting)]
+
+    kb, vb, ka, va, glob = beside[2]
+    weights, gout = beside[3], beside[4]
     place = jnp.concatenate(
         [
             jnp.stack([my_index * blocks, jnp.int32(shards * blocks)]).astype(jnp.int32),
@@ -249,9 +337,21 @@
     attention = attended(
         slots, place, queries, key_vectors, value_vectors, kb, vb, ka, va, glob, gout, arrived
     )
-    weight = lax.all_to_all(out_weight, "heads", split_axis=1, concat_axis=0, tiled=True)
-    whole = lax.all_gather(attention, "heads", axis=1, tiled=True)
-    return jnp.dot(whole, weight, preferred_element_type=jnp.float32).astype(jnp.bfloat16)
+    half = rows // 2
+    own_t, own_b = attention[:half], attention[half:]
+    right_t, left_b = across(own_t, 1), across(own_b, -1)
+    right_b, left_t = across(own_b, 1), across(own_t, -1)
+    far_t, far_b = across(right_t, 1), across(left_b, -1)
+
+    def product(*pieces):
+        total = 0.0
+        for piece, weight in zip(pieces, weights):
+            total = total + jnp.dot(piece, weight, preferred_element_type=jnp.float32)
+        return total.astype(jnp.bfloat16)
+
+    return jnp.concatenate(
+        [product(own_t, right_t, left_t, far_t), product(own_b, right_b, left_b, far_b)]
+    )
 
 
 def solution(mesh):

time: 1050 us -> 384 us (0.37)
  waiting for transfers between devices: 452 us -> 94.8 us
  Pallas kernels: 281 us -> 38 us
  blocking collectives: 202 us -> 142 us
  between operations: 14.8 us -> 1.76 us
  local copies, waits for them, and re-layouts: 22.3 us -> 11.4 us
    psum x2 -> x0, waiting for transfers between devices: 359 us -> none  [the longest x1 184 us: on_device(): glob = lax.psum(jnp.stack(own), SEQ).reshape(GLOBAL, 3, BLOCK, features)]
    pallas_call x4, Pallas kernels: 261 us -> 11.4 us  [picked(): pl.pallas_call(lambda *refs: pick_kernel(n, first, *refs), out_shape=jax....]
    pmax x1 -> x0, blocking collectives: 112 us -> none  [on_device(): top = lax.pmax(jnp.max(scores, axis=-1), SEQ)]
    all_gather x0 -> x4, blocking collectives: none -> 111 us  [the longest x1 54.4 us: on_device(): parts = lax.all_gather(merged(parts, False), 'seq_0')]
    ppermute x14, waiting for transfers between devices: 92.8 us -> 17.4 us  [ring_step(): lax.ppermute(shard, 'seq_0', [(i, (i + step) % peers) for i in range(peer...]
    all_to_all x2 -> x1, blocking collectives: 90.2 us -> 31.1 us  [exchanged(): return lax.all_to_all(picks, PLANE, split_axis=0, concat_axis=0, tiled=True)]
    ppermute x0 -> x9, waiting for transfers between devices: none -> 54.1 us  [across(): lax.ppermute(shard, 'heads', [(i, (i + step) % peers) for i in range(peer...]
    all_to_all x4 -> x6, waiting for transfers between devices: 0.01 us -> 15.2 us  [the longest x3 15.2 us: exchanged(): return lax.all_to_all(picks, PLANE, split_axis=0, concat_axis=0, tiled=True)]
  transfers between devices with their start and end apart: 25 -> 33, of which waited for: 13 -> 10; matrix products, arithmetic and copies ran while one was open for 3% -> 8% of each run, Pallas kernels for 19% -> 3%
where the time goes in v2:
time: 384 us; the launch traced here: 381 us
  blocking collectives  142 us (37%)
  waiting for transfers between devices  94.8 us (25%)
  starting transfers between devices  64.1 us (17%)
  Pallas kernels  38 us (10%)
  other arithmetic  16.9 us (4%)
  matrix products  12 us (3%)
  local copies, waits for them, and re-layouts  11.4 us (3%)
    all_gather x1, blocking collectives, on_device(): parts = lax.all_gather(merged(parts, False), 'seq_0')  54.4 us
    ppermute x9, waiting for transfers between devices, across(): lax.ppermute(shard, 'heads', [(i, (i + step) % peers) for i in range(peer...  54.1 us
    all_to_all x1, blocking collectives, exchanged(): return lax.all_to_all(picks, PLANE, split_axis=0, concat_axis=0, tiled=True)  31.1 us
    all_gather x1, blocking collectives, on_device(): own = lax.all_gather(own, 'seq_0').sum(axis=0)  26.5 us
    pallas_call x1, Pallas kernels, attended(): pl.pallas_call(lambda *refs: attend_kernel(counts, *refs), out_shape=jax....  19.9 us
    ppermute x14, waiting for transfers between devices, ring_step(): lax.ppermute(shard, 'seq_0', [(i, (i + step) % peers) for i in range(peer...  17.4 us
    all_gather x1, blocking collectives, on_device(): glob = lax.all_gather(own, PLANE).reshape(GLOBAL, 3, BLOCK, features)  15.8 us
    ppermute x14, starting transfers between devices, ring_step(): lax.ppermute(shard, 'seq_0', [(i, (i + step) % peers) for i in range(peer...  15.5 us
  transfers between devices with their start and end apart: 33, of which 10 were waited for; matrix products, arithmetic and copies ran while one was open for 8% of the time, Pallas kernels for 3%

profile of v2, /device:TPU:32, one launch (start us, length us, event | category | flops | bytes accessed | tf_op | source)
XLA Modules:
  0.0 381.1 jit_solution(7319030603836156490)
XLA Ops:
  0.0 1.9 collective-permute-start
  2.0 3.9 %collective-permute-start.3 = (bf16[768,512]{1,0:T(8,128)(2,1)}, bf16[768,512]{1,0:T(8,128)(2,1)}, u32[]{:S(2)}, u32[]{:S(2)}) collective-permute-start(bf16[768,512]{1,0:T(8,128)(2,1)} %refs_4_.2), channel_id=1, source_target_pairs={{0,56},{8,0},{16,8},{24,16},{32,24},{40,32},{48,40},{56,48},{1,57}... | collective-permute-start | bytes 2359304 | tf_op jit(solution)/shard_map/ppermute | solution.py:23
  6.7 0.7 sign_compare_fusion
  9.2 4.5 %all-to-all-start.1 = ((s32[8,1,32]{2,1,0:T(1,128)}), s32[8,1,32]{2,1,0:T(1,128)S(1)}, u32[]{:S(2)}, u32[]{:S(2)}) async-start(s32[8,1,32]{2,1,0:T(1,128)} %all_to_all.25), calls=%async_computation.1 | async-start | bytes 8192 | tf_op jit(solution)/shard_map/all_to_all | solution.py:273
  16.8 1.5 select_dynamic-update-slice_fusion.5
  18.3 1.5 select_dynamic-update-slice_fusion.4
  19.9 1.5 select_dynamic-update-slice_fusion.3
  21.4 1.5 select_dynamic-update-slice_fusion.2
  22.9 2.2 select_dynamic-update-slice_fusion.1
  25.2 1.1 collective-permute-start.4
  26.2 12.1 %collective-permute-done.3.refs_6_ = bf16[768,512]{1,0:T(8,128)(2,1)} collective-permute-done((bf16[768,512]{1,0:T(8,128)(2,1)}, bf16[768,512]{1,0:T(8,128)(2,1)}, u32[]{:S(2)}, u32[]{:S(2)}) %collective-permute-start.3) | collective-permute-done | bytes 786464 | tf_op jit(solution)/shard_map/ppermute | solution.py:23
  38.3 1.6 collective-permute-start.5
  39.9 2.2 select_dynamic-update-slice_fusion
  42.2 0.7 copy-done.7
  42.9 4.5 %all-to-all-start = ((bf16[8,48,512]{2,1,0:T(8,128)(2,1)}), bf16[8,48,512]{2,1,0:T(8,128)(2,1)S(1)}, u32[]{:S(2)}, u32[]{:S(2)}) async-start(bf16[8,48,512]{2,1,0:T(8,128)(2,1)} %bitcast.28), calls=%async_computation | async-start | bytes 786432 | tf_op jit(solution)/shard_map/all_to_all | solution.py:291
  47.4 2.4 collective-permute-start.7
  49.8 7.9 %collective-permute-done.7.refs_6_ = bf16[64,512]{1,0:T(8,128)(2,1)} collective-permute-done((bf16[64,512]{1,0:T(8,128)(2,1)}, bf16[64,512]{1,0:T(8,128)(2,1)}, u32[]{:S(2)}, u32[]{:S(2)}) %collective-permute-start.7) | collective-permute-done | bytes 65568 | tf_op jit(solution)/shard_map/ppermute | solution.py:278
  57.7 1.9 collective-permute-start.9
  61.8 2.1 collective-permute-start.6
  63.9 26.5 %all-gather = bf16[384,512]{1,0:T(8,128)(2,1)S(1)} all-gather(bf16[48,512]{1,0:T(8,128)(2,1)} %reduce_sum.43), channel_id=2, replica_groups=mesh['heads'=4,'seq_0'=8,'seq_1'=4,'seq_2'=2] {'seq_0'}, dimensions={0}, use_global_device_ids=true | all-gather | bytes 442368 | tf_op jit(solution)/shard_map/all_gather | solution.py:292
  91.1 1.9 collective-permute-start.8
  93.0 15.8 %all-gather.1 = bf16[384,512]{1,0:T(8,128)(2,1)S(1)} all-gather(bf16[48,512]{1,0:T(8,128)(2,1)} %reduce_sum.44), channel_id=3, replica_groups=mesh['heads'=4,'seq_0'=8,'seq_1'=4,'seq_2'=2] {'seq_1','seq_2'}, dimensions={0}, use_global_device_ids=true | all-gather | bytes 442368 | tf_op jit(solution)/shard_map/all_gather | solution.py:293
  109.5 3.9 %pick_blocks.4 = bf16[8,3,4,2,64,128]{5,4,3,2,1,0:T(8,128)(2,1)} custom-call(s32[256]{0:T(256)S(1)} %reshape.145.refs_0_, bf16[768,512]{1,0:T(8,128)(2,1)S(1)} %copy-done, bf16[768,512]{1,0:T(8,128)(2,1)} %collective-permute-done.refs_2_, bf16[768,512]{1,0:T(8,128)(2,1)S(1)} %collective-permute-done.1.refs_3_, bf16[768,512]{1,0:T(8,128)(2,1)S(1)} %copy-done.1, ...), custom_call_target="tpu_custom_call" | custom-call | bytes 7864320 | tf_op jit(solution)/shard_map/pick_blocks/pallas_call | solution.py:52
  113.4 4.5 %all-to-all-start.2 = ((bf16[8,3,4,2,64,128]{5,4,3,2,1,0:T(8,128)(2,1)}), bf16[8,3,4,2,64,128]{5,4,3,2,1,0:T(8,128)(2,1)}, u32[]{:S(2)}, u32[]{:S(2)}) async-start(bf16[8,3,4,2,64,128]{5,4,3,2,1,0:T(8,128)(2,1)} %pick_blocks.4), calls=%async_computation.2 | async-start | bytes 6291456 | tf_op jit(solution)/shard_map/all_to_all | solution.py:66
  117.9 4.0 %constant_dynamic-slice_fusion = (bf16[512,1024]{1,0:T(8,128)(2,1)}, bf16[512,1024]{1,0:T(8,128)(2,1)S(1)}, bf16[512,1024]{1,0:T(8,128)(2,1)}, bf16[512,1024]{1,0:T(8,128)(2,1)S(1)}) fusion(bf16[512,4096]{1,0:T(8,128)(2,1)} %param.11, s32[]{:T(128)S(6)} %select_n.181, s32[]{:T(128)S(6)} %select_n.177, s32[]{:T(128)S(6)} %select_n.175, s32[]{:T(128)S(6)} %select_n.179), kind=kLoop, calls=%fused_computation.17 | loop fusion | bytes 8388624 | tf_op jit(solution)/shard_map/dynamic_slice | solution.py:258
  121.9 1.5 collective-permute-start.18
  123.4 1.7 collective-permute-start.19
  125.1 1.8 collective-permute-start.20
  126.9 2.0 collective-permute-start.13
  129.0 19.6 %collective-permute-done.18 = bf16[512,1024]{1,0:T(8,128)(2,1)} collective-permute-done((bf16[512,1024]{1,0:T(8,128)(2,1)S(1)}, bf16[512,1024]{1,0:T(8,128)(2,1)}, u32[]{:S(2)}, u32[]{:S(2)}) %collective-permute-start.18) | collective-permute-done | bytes 1048608 | tf_op jit(solution)/shard_map/ppermute | solution.py:28
  148.8 21.4 %collective-permute-done.19 = bf16[512,1024]{1,0:T(8,128)(2,1)} collective-permute-done((bf16[512,1024]{1,0:T(8,128)(2,1)S(1)}, bf16[512,1024]{1,0:T(8,128)(2,1)}, u32[]{:S(2)}, u32[]{:S(2)}) %collective-permute-start.19) | collective-permute-done | bytes 1048608 | tf_op jit(solution)/shard_map/ppermute | solution.py:28
  170.2 2.5 global_parts.1
  172.8 4.5 %all-to-all-start.4 = ((bf16[8,64,256]{2,1,0:T(8,128)(2,1)}), bf16[8,64,256]{2,1,0:T(8,128)(2,1)S(1)}, u32[]{:S(2)}, u32[]{:S(2)}) async-start(bf16[8,64,256]{2,1,0:T(8,128)(2,1)} %bitcast.8), calls=%async_computation.4 | async-start | bytes 524288 | tf_op jit(solution)/shard_map/all_to_all | solution.py:296
  177.3 5.3 %collective-permute-done.15.refs_4_ = bf16[768,512]{1,0:T(8,128)(2,1)} collective-permute-done((bf16[768,512]{1,0:T(8,128)(2,1)}, bf16[768,512]{1,0:T(8,128)(2,1)}, u32[]{:S(2)}, u32[]{:S(2)}) %collective-permute-start.15) | collective-permute-done | bytes 786464 | tf_op jit(solution)/shard_map/ppermute | solution.py:23
  182.5 3.8 pick_blocks.5
  186.3 0.7 copy-done.6
  187.0 4.5 %all-to-all-start.3 = ((bf16[8,2,4,2,64,128]{5,4,3,2,1,0:T(8,128)(2,1)}), bf16[8,2,4,2,64,128]{5,4,3,2,1,0:T(8,128)(2,1)}, u32[]{:S(2)}, u32[]{:S(2)}) async-start(bf16[8,2,4,2,64,128]{5,4,3,2,1,0:T(8,128)(2,1)} %pick_blocks.5), calls=%async_computation.3 | async-start | bytes 4194304 | tf_op jit(solution)/shard_map/all_to_all | solution.py:66
  192.0 1.6 collective-permute-start.14
  193.5 2.5 collective-permute-start.16
  196.0 2.1 merge_parts.2
  198.1 54.4 %all-gather.2 = bf16[512,256]{1,0:T(8,128)(2,1)} all-gather(bf16[64,256]{1,0:T(8,128)(2,1)} %merge_parts.2), channel_id=4, replica_groups=mesh['heads'=4,'seq_0'=8,'seq_1'=4,'seq_2'=2] {'seq_0'}, dimensions={0}, use_global_device_ids=true | all-gather | bytes 294912 | tf_op jit(solution)/shard_map/all_gather | solution.py:297
  252.5 2.0 merge_parts.3
  254.6 14.4 %all_gather.27.refs_10_ = bf16[512,128]{1,0:T(8,128)(2,1)} all-gather(bf16[64,128]{1,0:T(8,128)(2,1)} %merge_parts.3), channel_id=1, replica_groups=mesh['heads'=4,'seq_0'=8,'seq_1'=4,'seq_2'=2] {'seq_1','seq_2'}, dimensions={0}, use_global_device_ids=true | all-gather | bytes 147456 | tf_op jit(solution)/shard_map/all_gather | solution.py:298
  269.0 2.0 pick_blocks.6
  270.9 31.1 %all_to_all.39.refs_13_ = bf16[8,2,4,2,64,128]{5,4,3,2,1,0:T(8,128)(2,1)} all-to-all(bf16[8,2,4,2,64,128]{5,4,3,2,1,0:T(8,128)(2,1)S(1)} %pick_blocks.6), channel_id=1, replica_groups=mesh['heads'=4,'seq_0'=8,'seq_1'=4,'seq_2'=2] {'seq_1','seq_2'}, dimensions={0} | all-to-all | bytes 4194304 | tf_op jit(solution)/shard_map/all_to_all | solution.py:66
  302.0 1.8 pick_blocks.7
  303.8 3.6 all-to-all-start.6
  308.1 15.2 %all-to-all-done.6.refs_14_ = bf16[8,1,4,2,64,128]{5,4,3,2,1,0:T(8,128)(2,1)S(1)} async-done(((bf16[8,1,4,2,64,128]{5,4,3,2,1,0:T(8,128)(2,1)}), bf16[8,1,4,2,64,128]{5,4,3,2,1,0:T(8,128)(2,1)S(1)}, u32[]{:S(2)}, u32[]{:S(2)}) %all-to-all-start.6) | async-done | bytes 1048608 | tf_op jit(solution)/shard_map/all_to_all | solution.py:66
  323.3 1.0 copy-done.5
  324.3 19.9 %attend.1 = bf16[768,512]{1,0:T(8,128)(2,1)} custom-call(s32[144]{0:T(256)} %copy-done.9, s32[4]{0:T(128)} %pad_add_fusion.refs_1_, bf16[768,512]{1,0:T(8,128)(2,1)} %refs_2_.1, bf16[768,512]{1,0:T(8,128)(2,1)} %refs_3_.1, bf16[768,512]{1,0:T(8,128)(2,1)} %refs_4_.2, bf16[64,512]{1,0:T(8,128)(2,1)} %collective-permute-done.6.refs_5_, ...), custom_call_target="tpu_custom_call" | custom-call | flops 805306368 | bytes 12582912 | tf_op jit(solution)/shard_map/attend/pallas_call | solution.py:223
  344.2 1.2 fusion.10
  345.4 3.8 %collective-permute-start.25 = (bf16[384,512]{1,0:T(8,128)(2,1)S(1)}, bf16[384,512]{1,0:T(8,128)(2,1)S(1)}, u32[]{:S(2)}, u32[]{:S(2)}) collective-permute-start(bf16[384,512]{1,0:T(8,128)(2,1)S(1)} %get-tuple-element.77), channel_id=1, source_target_pairs={{0,192},{64,0},{128,64},{192,128},{1,193},{65,1},{129,65},{193,129... | collective-permute-start | bytes 1179656 | tf_op jit(solution)/shard_map/ppermute | solution.py:28
  349.3 1.9 collective-permute-start.22
  351.3 7.9 %collective-permute-done.21 = bf16[384,512]{1,0:T(8,128)(2,1)S(1)} collective-permute-done((bf16[384,512]{1,0:T(8,128)(2,1)S(1)}, bf16[384,512]{1,0:T(8,128)(2,1)S(1)}, u32[]{:S(2)}, u32[]{:S(2)}) %collective-permute-start.21) | collective-permute-done | bytes 393248 | tf_op jit(solution)/shard_map/ppermute | solution.py:28
  359.2 1.8 fusion.13
  361.0 3.3 collective-permute-start.26
  364.3 1.8 fusion.17
  366.1 1.2 collective-permute-done.22
  367.2 1.8 fusion.14
  369.1 1.8 fusion.16
  370.9 4.1 %collective-permute-done.23 = bf16[384,512]{1,0:T(8,128)(2,1)S(1)} collective-permute-done((bf16[384,512]{1,0:T(8,128)(2,1)S(1)}, bf16[384,512]{1,0:T(8,128)(2,1)S(1)}, u32[]{:S(2)}, u32[]{:S(2)}) %collective-permute-start.23) | collective-permute-done | bytes 393248 | tf_op jit(solution)/shard_map/ppermute | solution.py:28
  374.9 1.8 fusion.15
  377.4 1.8 fusion.18
  379.8 1.3 pad_maximum_fusion
  (74 shorter events, 10.8 us)
Async XLA Ops:
  0.0 25.2 %collective-permute-start = (bf16[768,512]{1,0:T(8,128)(2,1)}, bf16[768,512]{1,0:T(8,128)(2,1)}, u32[]{:S(2)}, u32[]{:S(2)}) collective-permute-start(bf16[768,512]{1,0:T(8,128)(2,1)} %refs_3_.1), channel_id=1, source_target_pairs={{0,8},{8,16},{16,24},{24,32},{32,40},{40,48},{48,56},{56,0},{1,9},... | collective-permute-start | bytes 2359304 | tf_op jit(solution)/shard_map/ppermute | solution.py:23
  1.9 106.9 %collective-permute-start.1 = (bf16[768,512]{1,0:T(8,128)(2,1)}, bf16[768,512]{1,0:T(8,128)(2,1)S(1)}, u32[]{:S(2)}, u32[]{:S(2)}) collective-permute-start(bf16[768,512]{1,0:T(8,128)(2,1)} %refs_3_.1), channel_id=1, source_target_pairs={{0,56},{8,0},{16,8},{24,16},{32,24},{40,32},{48,40},{56,48},{1,57}... | collective-permute-start | bytes 2359304 | tf_op jit(solution)/shard_map/ppermute | solution.py:23
  2.0 36.3 %collective-permute-start.3 = (bf16[768,512]{1,0:T(8,128)(2,1)}, bf16[768,512]{1,0:T(8,128)(2,1)}, u32[]{:S(2)}, u32[]{:S(2)}) collective-permute-start(bf16[768,512]{1,0:T(8,128)(2,1)} %refs_4_.2), channel_id=1, source_target_pairs={{0,56},{8,0},{16,8},{24,16},{32,24},{40,32},{48,40},{56,48},{1,57}... | collective-permute-start | bytes 2359304 | tf_op jit(solution)/shard_map/ppermute | solution.py:23
  6.0 102.8 %collective-permute-start.2 = (bf16[768,512]{1,0:T(8,128)(2,1)}, bf16[768,512]{1,0:T(8,128)(2,1)S(1)}, u32[]{:S(2)}, u32[]{:S(2)}) collective-permute-start(bf16[768,512]{1,0:T(8,128)(2,1)} %refs_4_.2), channel_id=1, source_target_pairs={{0,8},{8,16},{16,24},{24,32},{32,40},{40,48},{48,56},{56,0},{1,9},... | collective-permute-start | bytes 2359304 | tf_op jit(solution)/shard_map/ppermute | solution.py:23
  8.4 82.8 %copy-start.9 = (s32[144]{0:T(256)}, s32[144]{0:T(256)S(1)}, u32[]{:S(2)}) copy-start(s32[144]{0:T(256)S(1)} %multiply_add_fusion.refs_0_) | copy-start | bytes 1732
  9.2 33.0 %all-to-all-start.1 = ((s32[8,1,32]{2,1,0:T(1,128)}), s32[8,1,32]{2,1,0:T(1,128)S(1)}, u32[]{:S(2)}, u32[]{:S(2)}) async-start(s32[8,1,32]{2,1,0:T(1,128)} %all_to_all.25), calls=%async_computation.1 | async-start | bytes 8192 | tf_op jit(solution)/shard_map/all_to_all | solution.py:273
  25.2 84.3 %copy-start = (bf16[768,512]{1,0:T(8,128)(2,1)S(1)}, bf16[768,512]{1,0:T(8,128)(2,1)}, u32[]{:S(2)}) copy-start(bf16[768,512]{1,0:T(8,128)(2,1)} %refs_3_.1) | copy-start | bytes 2359300
  25.2 84.3 %copy-start.1 = (bf16[768,512]{1,0:T(8,128)(2,1)S(1)}, bf16[768,512]{1,0:T(8,128)(2,1)}, u32[]{:S(2)}) copy-start(bf16[768,512]{1,0:T(8,128)(2,1)} %refs_4_.2) | copy-start | bytes 2359300
  25.2 84.3 %collective-permute-start.4 = (bf16[768,512]{1,0:T(8,128)(2,1)}, bf16[768,512]{1,0:T(8,128)(2,1)}, u32[]{:S(2)}, u32[]{:S(2)}) collective-permute-start(bf16[768,512]{1,0:T(8,128)(2,1)} %collective-permute-done.refs_2_), channel_id=1, source_target_pairs={{0,8},{8,16},{16,24},{24,32},{32,40},{40,48},{48,56},{56,0},{1,9},... | collective-permute-start | bytes 2359304 | tf_op jit(solution)/shard_map/ppermute | solution.py:23
  38.3 71.2 %collective-permute-start.5 = (bf16[768,512]{1,0:T(8,128)(2,1)}, bf16[768,512]{1,0:T(8,128)(2,1)}, u32[]{:S(2)}, u32[]{:S(2)}) collective-permute-start(bf16[768,512]{1,0:T(8,128)(2,1)} %collective-permute-done.3.refs_6_), channel_id=1, source_target_pairs={{0,56},{8,0},{16,8},{24,16},{32,24},{40,32},{48,40},{56,48},{1,57}... | collective-permute-start | bytes 2359304 | tf_op jit(solution)/shard_map/ppermute | solution.py:23
  42.2 0.7 copy-start.7
  42.9 17.9 %all-to-all-start = ((bf16[8,48,512]{2,1,0:T(8,128)(2,1)}), bf16[8,48,512]{2,1,0:T(8,128)(2,1)S(1)}, u32[]{:S(2)}, u32[]{:S(2)}) async-start(bf16[8,48,512]{2,1,0:T(8,128)(2,1)} %bitcast.28), calls=%async_computation | async-start | bytes 786432 | tf_op jit(solution)/shard_map/all_to_all | solution.py:291
  47.4 10.3 %collective-permute-start.7 = (bf16[64,512]{1,0:T(8,128)(2,1)}, bf16[64,512]{1,0:T(8,128)(2,1)}, u32[]{:S(2)}, u32[]{:S(2)}) collective-permute-start(bf16[64,512]{1,0:T(8,128)(2,1)} %get-tuple-element.80), channel_id=1, source_target_pairs={{0,1},{1,2},{2,3},{3,4},{4,5},{5,6},{6,7},{7,8},{8,9},{9,10},{10,1... | collective-permute-start | bytes 196616 | tf_op jit(solution)/shard_map/ppermute | solution.py:278
  57.7 4.1 %collective-permute-start.9 = (bf16[64,512]{1,0:T(8,128)(2,1)}, bf16[64,512]{1,0:T(8,128)(2,1)}, u32[]{:S(2)}, u32[]{:S(2)}) collective-permute-start(bf16[64,512]{1,0:T(8,128)(2,1)} %get-tuple-element.79), channel_id=1, source_target_pairs={{1,0},{2,1},{3,2},{4,3},{5,4},{6,5},{7,6},{8,7},{9,8},{10,9},{11,1... | collective-permute-start | bytes 196616 | tf_op jit(solution)/shard_map/ppermute | solution.py:280
  61.8 29.3 %collective-permute-start.6 = (bf16[64,512]{1,0:T(8,128)(2,1)}, bf16[64,512]{1,0:T(8,128)(2,1)}, u32[]{:S(2)}, u32[]{:S(2)}) collective-permute-start(bf16[64,512]{1,0:T(8,128)(2,1)} %get-tuple-element.83), channel_id=1, source_target_pairs={{0,1},{1,2},{2,3},{3,4},{4,5},{5,6},{6,7},{7,8},{8,9},{9,10},{10,1... | collective-permute-start | bytes 196616 | tf_op jit(solution)/shard_map/ppermute | solution.py:277
  91.1 17.7 %collective-permute-start.8 = (bf16[64,512]{1,0:T(8,128)(2,1)}, bf16[64,512]{1,0:T(8,128)(2,1)S(1)}, u32[]{:S(2)}, u32[]{:S(2)}) collective-permute-start(bf16[64,512]{1,0:T(8,128)(2,1)} %get-tuple-element.82), channel_id=1, source_target_pairs={{1,0},{2,1},{3,2},{4,3},{5,4},{6,5},{7,6},{8,7},{9,8},{10,9},{11,1... | collective-permute-start | bytes 196616 | tf_op jit(solution)/shard_map/ppermute | solution.py:279
  108.8 61.4 %copy-start.2 = (bf16[384,512]{1,0:T(8,128)(2,1)}, bf16[384,512]{1,0:T(8,128)(2,1)S(1)}, u32[]{:S(2)}) copy-start(bf16[384,512]{1,0:T(8,128)(2,1)S(1)} %all-gather.1) | copy-start | bytes 1179652
  108.8 0.7 copy-start.8
  113.4 59.4 %all-to-all-start.2 = ((bf16[8,3,4,2,64,128]{5,4,3,2,1,0:T(8,128)(2,1)}), bf16[8,3,4,2,64,128]{5,4,3,2,1,0:T(8,128)(2,1)}, u32[]{:S(2)}, u32[]{:S(2)}) async-start(bf16[8,3,4,2,64,128]{5,4,3,2,1,0:T(8,128)(2,1)} %pick_blocks.4), calls=%async_computation.2 | async-start | bytes 6291456 | tf_op jit(solution)/shard_map/all_to_all | solution.py:66
  121.9 26.7 %collective-permute-start.18 = (bf16[512,1024]{1,0:T(8,128)(2,1)S(1)}, bf16[512,1024]{1,0:T(8,128)(2,1)}, u32[]{:S(2)}, u32[]{:S(2)}) collective-permute-start(bf16[512,1024]{1,0:T(8,128)(2,1)S(1)} %get-tuple-element.73), channel_id=1, source_target_pairs={{0,64},{64,128},{128,192},{192,0},{1,65},{65,129},{129,193},{193,1... | collective-permute-start | bytes 3145736 | tf_op jit(solution)/shard_map/ppermute | solution.py:28
  123.4 46.9 %collective-permute-start.19 = (bf16[512,1024]{1,0:T(8,128)(2,1)S(1)}, bf16[512,1024]{1,0:T(8,128)(2,1)}, u32[]{:S(2)}, u32[]{:S(2)}) collective-permute-start(bf16[512,1024]{1,0:T(8,128)(2,1)S(1)} %get-tuple-element.75), channel_id=1, source_target_pairs={{0,192},{64,0},{128,64},{192,128},{1,193},{65,1},{129,65},{193,129... | collective-permute-start | bytes 3145736 | tf_op jit(solution)/shard_map/ppermute | solution.py:28
  125.1 52.1 %collective-permute-start.20 = (bf16[512,1024]{1,0:T(8,128)(2,1)}, bf16[512,1024]{1,0:T(8,128)(2,1)}, u32[]{:S(2)}, u32[]{:S(2)}) collective-permute-start(bf16[512,1024]{1,0:T(8,128)(2,1)} %get-tuple-element.72), channel_id=1, source_target_pairs={{0,128},{64,192},{128,0},{192,64},{1,129},{65,193},{129,1},{193,65... | collective-permute-start | bytes 3145736 | tf_op jit(solution)/shard_map/ppermute | solution.py:28
  126.9 50.3 %collective-permute-start.11 = (bf16[768,512]{1,0:T(8,128)(2,1)S(1)}, bf16[768,512]{1,0:T(8,128)(2,1)}, u32[]{:S(2)}, u32[]{:S(2)}) collective-permute-start(bf16[768,512]{1,0:T(8,128)(2,1)S(1)} %collective-permute-done.1.refs_3_), channel_id=1, source_target_pairs={{0,56},{8,0},{16,8},{24,16},{32,24},{40,32},{48,40},{56,48},{1,57}... | collective-permute-start | bytes 2359304 | tf_op jit(solution)/shard_map/ppermute | solution.py:23
  126.9 50.3 %collective-permute-start.13 = (bf16[768,512]{1,0:T(8,128)(2,1)S(1)}, bf16[768,512]{1,0:T(8,128)(2,1)}, u32[]{:S(2)}, u32[]{:S(2)}) collective-permute-start(bf16[768,512]{1,0:T(8,128)(2,1)S(1)} %collective-permute-done.2.refs_5_), channel_id=1, source_target_pairs={{0,8},{8,16},{16,24},{24,32},{32,40},{40,48},{48,56},{56,0},{1,9},... | collective-permute-start | bytes 2359304 | tf_op jit(solution)/shard_map/ppermute | solution.py:23
  148.6 28.7 %collective-permute-start.10 = (bf16[768,512]{1,0:T(8,128)(2,1)}, bf16[768,512]{1,0:T(8,128)(2,1)}, u32[]{:S(2)}, u32[]{:S(2)}) collective-permute-start(bf16[768,512]{1,0:T(8,128)(2,1)} %collective-permute-done.4.refs_1_), channel_id=1, source_target_pairs={{0,8},{8,16},{16,24},{24,32},{32,40},{40,48},{48,56},{56,0},{1,9},... | collective-permute-start | bytes 2359304 | tf_op jit(solution)/shard_map/ppermute | solution.py:23
  170.2 12.3 %collective-permute-start.15 = (bf16[768,512]{1,0:T(8,128)(2,1)}, bf16[768,512]{1,0:T(8,128)(2,1)}, u32[]{:S(2)}, u32[]{:S(2)}) collective-permute-start(bf16[768,512]{1,0:T(8,128)(2,1)} %collective-permute-done.5.refs_4_), channel_id=1, source_target_pairs={{0,56},{8,0},{16,8},{24,16},{32,24},{40,32},{48,40},{56,48},{1,57}... | collective-permute-start | bytes 2359304 | tf_op jit(solution)/shard_map/ppermute | solution.py:23
  172.8 13.5 %all-to-all-start.4 = ((bf16[8,64,256]{2,1,0:T(8,128)(2,1)}), bf16[8,64,256]{2,1,0:T(8,128)(2,1)S(1)}, u32[]{:S(2)}, u32[]{:S(2)}) async-start(bf16[8,64,256]{2,1,0:T(8,128)(2,1)} %bitcast.8), calls=%async_computation.4 | async-start | bytes 524288 | tf_op jit(solution)/shard_map/all_to_all | solution.py:296
  186.3 0.7 copy-start.6
  187.0 82.0 %all-to-all-start.3 = ((bf16[8,2,4,2,64,128]{5,4,3,2,1,0:T(8,128)(2,1)}), bf16[8,2,4,2,64,128]{5,4,3,2,1,0:T(8,128)(2,1)}, u32[]{:S(2)}, u32[]{:S(2)}) async-start(bf16[8,2,4,2,64,128]{5,4,3,2,1,0:T(8,128)(2,1)} %pick_blocks.5), calls=%async_computation.3 | async-start | bytes 4194304 | tf_op jit(solution)/shard_map/all_to_all | solution.py:66
  191.5 77.5 %collective-permute-start.12 = (bf16[768,512]{1,0:T(8,128)(2,1)}, bf16[768,512]{1,0:T(8,128)(2,1)S(1)}, u32[]{:S(2)}, u32[]{:S(2)}) collective-permute-start(bf16[768,512]{1,0:T(8,128)(2,1)} %collective-permute-done.11.refs_2_), channel_id=1, source_target_pairs={{0,56},{8,0},{16,8},{24,16},{32,24},{40,32},{48,40},{56,48},{1,57}... | collective-permute-start | bytes 2359304 | tf_op jit(solution)/shard_map/ppermute | solution.py:23
  192.0 77.0 %collective-permute-start.14 = (bf16[768,512]{1,0:T(8,128)(2,1)}, bf16[768,512]{1,0:T(8,128)(2,1)S(1)}, u32[]{:S(2)}, u32[]{:S(2)}) collective-permute-start(bf16[768,512]{1,0:T(8,128)(2,1)} %collective-permute-done.13.refs_3_), channel_id=1, source_target_pairs={{0,8},{8,16},{16,24},{24,32},{32,40},{40,48},{48,56},{56,0},{1,9},... | collective-permute-start | bytes 2359304 | tf_op jit(solution)/shard_map/ppermute | solution.py:23
  193.5 75.4 %collective-permute-start.16 = (bf16[768,512]{1,0:T(8,128)(2,1)}, bf16[768,512]{1,0:T(8,128)(2,1)S(1)}, u32[]{:S(2)}, u32[]{:S(2)}) collective-permute-start(bf16[768,512]{1,0:T(8,128)(2,1)} %collective-permute-done.10.refs_1_), channel_id=1, source_target_pairs={{0,8},{8,16},{16,24},{24,32},{32,40},{40,48},{48,56},{56,0},{1,9},... | collective-permute-start | bytes 2359304 | tf_op jit(solution)/shard_map/ppermute | solution.py:23
  196.0 72.9 %collective-permute-start.17 = (bf16[768,512]{1,0:T(8,128)(2,1)}, bf16[768,512]{1,0:T(8,128)(2,1)S(1)}, u32[]{:S(2)}, u32[]{:S(2)}) collective-permute-start(bf16[768,512]{1,0:T(8,128)(2,1)} %collective-permute-done.15.refs_4_), channel_id=1, source_target_pairs={{0,56},{8,0},{16,8},{24,16},{32,24},{40,32},{48,40},{56,48},{1,57}... | collective-permute-start | bytes 2359304 | tf_op jit(solution)/shard_map/ppermute | solution.py:23
  303.8 19.5 %all-to-all-start.6 = ((bf16[8,1,4,2,64,128]{5,4,3,2,1,0:T(8,128)(2,1)}), bf16[8,1,4,2,64,128]{5,4,3,2,1,0:T(8,128)(2,1)S(1)}, u32[]{:S(2)}, u32[]{:S(2)}) async-start(bf16[8,1,4,2,64,128]{5,4,3,2,1,0:T(8,128)(2,1)} %pick_blocks.7), calls=%async_computation.6 | async-start | bytes 2097152 | tf_op jit(solution)/shard_map/all_to_all | solution.py:66
  323.3 1.0 copy-start.5
  345.3 13.8 %collective-permute-start.21 = (bf16[384,512]{1,0:T(8,128)(2,1)S(1)}, bf16[384,512]{1,0:T(8,128)(2,1)S(1)}, u32[]{:S(2)}, u32[]{:S(2)}) collective-permute-start(bf16[384,512]{1,0:T(8,128)(2,1)S(1)} %get-tuple-element.76), channel_id=1, source_target_pairs={{0,64},{64,128},{128,192},{192,0},{1,65},{65,129},{129,193},{193,1... | collective-permute-start | bytes 1179656 | tf_op jit(solution)/shard_map/ppermute | solution.py:28
  345.4 15.5 %collective-permute-start.25 = (bf16[384,512]{1,0:T(8,128)(2,1)S(1)}, bf16[384,512]{1,0:T(8,128)(2,1)S(1)}, u32[]{:S(2)}, u32[]{:S(2)}) collective-permute-start(bf16[384,512]{1,0:T(8,128)(2,1)S(1)} %get-tuple-element.77), channel_id=1, source_target_pairs={{0,192},{64,0},{128,64},{192,128},{1,193},{65,1},{129,65},{193,129... | collective-permute-start | bytes 1179656 | tf_op jit(solution)/shard_map/ppermute | solution.py:28
  349.3 18.0 %collective-permute-start.22 = (bf16[384,512]{1,0:T(8,128)(2,1)S(1)}, bf16[384,512]{1,0:T(8,128)(2,1)S(1)}, u32[]{:S(2)}, u32[]{:S(2)}) collective-permute-start(bf16[384,512]{1,0:T(8,128)(2,1)S(1)} %get-tuple-element.76), channel_id=1, source_target_pairs={{0,192},{64,0},{128,64},{192,128},{1,193},{65,1},{129,65},{193,129... | collective-permute-start | bytes 1179656 | tf_op jit(solution)/shard_map/ppermute | solution.py:28
  351.2 17.8 %collective-permute-start.24 = (bf16[384,512]{1,0:T(8,128)(2,1)S(1)}, bf16[384,512]{1,0:T(8,128)(2,1)S(1)}, u32[]{:S(2)}, u32[]{:S(2)}) collective-permute-start(bf16[384,512]{1,0:T(8,128)(2,1)S(1)} %get-tuple-element.77), channel_id=1, source_target_pairs={{0,64},{64,128},{128,192},{192,0},{1,65},{65,129},{129,193},{193,1... | collective-permute-start | bytes 1179656 | tf_op jit(solution)/shard_map/ppermute | solution.py:28
  359.2 15.8 %collective-permute-start.23 = (bf16[384,512]{1,0:T(8,128)(2,1)S(1)}, bf16[384,512]{1,0:T(8,128)(2,1)S(1)}, u32[]{:S(2)}, u32[]{:S(2)}) collective-permute-start(bf16[384,512]{1,0:T(8,128)(2,1)S(1)} %collective-permute-done.21), channel_id=1, source_target_pairs={{0,64},{64,128},{128,192},{192,0},{1,65},{65,129},{129,193},{193,1... | collective-permute-start | bytes 1179656 | tf_op jit(solution)/shard_map/ppermute | solution.py:28
  361.0 16.4 %collective-permute-start.26 = (bf16[384,512]{1,0:T(8,128)(2,1)S(1)}, bf16[384,512]{1,0:T(8,128)(2,1)S(1)}, u32[]{:S(2)}, u32[]{:S(2)}) collective-permute-start(bf16[384,512]{1,0:T(8,128)(2,1)S(1)} %collective-permute-done.25), channel_id=1, source_target_pairs={{0,192},{64,0},{128,64},{192,128},{1,193},{65,1},{129,65},{193,129... | collective-permute-start | bytes 1179656 | tf_op jit(solution)/shard_map/ppermute | solution.py:28
  370.9 5.9 %copy-start.3 = (bf16[512,1024]{1,0:T(8,128)(2,1)S(1)}, bf16[512,1024]{1,0:T(8,128)(2,1)}, u32[]{:S(2)}) copy-start(bf16[512,1024]{1,0:T(8,128)(2,1)} %get-tuple-element.65) | copy-start | bytes 3145732
  370.9 5.9 %copy-start.4 = (bf16[768,512]{1,0:T(8,128)(2,1)S(1)}, bf16[768,512]{1,0:T(8,128)(2,1)}, u32[]{:S(2)}) copy-start(bf16[768,512]{1,0:T(8,128)(2,1)} %attend.1) | copy-start | bytes 2359300

commit v3 on v1

v3 whole, which is shorter than its diff:
```python
import jax
import jax.numpy as jnp
from jax import lax
from jax.experimental import pallas as pl
from jax.experimental.pallas import tpu as pltpu
from jax.sharding import Mesh
from jax.sharding import PartitionSpec as P

DH = 128
BLOCK = 64
RANDOM = 3
GLOBAL = 2
CAP = 4
PLANES = 8
INPLANE = 8
SEQ = ("seq_0", "seq_1", "seq_2")
PLANE = ("seq_1", "seq_2")
VMEM_LIMIT = 56 * 2**20


def ring_step(shard, step):
    peers = lax.axis_size("seq_0")
    return lax.ppermute(shard, "seq_0", [(i, (i + step) % peers) for i in range(peers)])


def across(shard, step):
    peers = lax.axis_size("heads")
    return lax.ppermute(shard, "heads", [(i, (i + step) % peers) for i in range(peers)])


def pick_kernel(n, first, codes, *refs):
    keys, values = refs[:n], refs[n : 2 * n]
    extra, out = refs[2 * n : -1], refs[-1]

    def one_peer(peer, carry):
        for run in range(n):
            for rank in range(CAP):
                code = codes[(peer * PLANES + first + run) * CAP + rank]
                rows = pl.ds(pl.multiple_of((code & 15) * BLOCK, BLOCK), BLOCK)
                cols = pl.ds(pl.multiple_of((code >> 4) * DH, DH), DH)
                at = (run * CAP + rank) * 2 * BLOCK
                out[peer, at : at + BLOCK] = keys[run][rows, cols]
                out[peer, at + BLOCK : at + 2 * BLOCK] = values[run][rows, cols]
        if extra:
            own = extra[0][pl.ds(pl.multiple_of(peer * BLOCK, BLOCK), BLOCK)].astype(out.dtype)
            at = n * CAP * 2 * BLOCK
            out[peer, at : at + BLOCK] = own[:, :DH]
            out[peer, at + BLOCK : at + 2 * BLOCK] = own[:, DH:]
        return carry

    lax.fori_loop(0, INPLANE, one_peer, 0)


def picked(codes, first, blocks, extra=()):
    n = len(blocks) // 2
    shape = (INPLANE, (n * CAP + len(extra)) * 2 * BLOCK, DH)
    size = 2 * (sum(k.size for k in blocks) + INPLANE * n * CAP * 2 * BLOCK * DH)
    vmem = pl.BlockSpec(memory_space=pltpu.VMEM)
    return pl.pallas_call(
        lambda *refs: pick_kernel(n, first, *refs),
        out_shape=jax.ShapeDtypeStruct(shape, jnp.bfloat16),
        in_specs=[pl.BlockSpec(memory_space=pltpu.SMEM)] + [vmem] * (2 * n + len(extra)),
        out_specs=vmem,
        compiler_params=pltpu.CompilerParams(vmem_limit_bytes=32 * 2**20),
        cost_estimate=pl.CostEstimate(flops=0, bytes_accessed=size, transcendentals=0),
        name="pick_blocks",
    )(codes, *blocks, *extra)


def over_plane(parts):
    return lax.all_to_all(parts, PLANE, split_axis=0, concat_axis=0, tiled=True)


def global_kernel(n, asking, *refs):
    keys, values = refs[:n], refs[n : 2 * n]
    held, out = refs[2 * n : -1], refs[-1]
    heads = asking.shape[1] // DH
    many = GLOBAL * BLOCK
    lane = lax.broadcasted_iota(jnp.int32, (many, DH), 1)
    for h in range(heads):
        hs = slice(h * DH, (h + 1) * DH)
        rows = slice(h * many, (h + 1) * many)
        scores = [
            lax.dot_general(
                asking[:, hs], k[:, hs], (((1,), (1,)), ((), ())),
                preferred_element_type=jnp.float32,
            ) * (DH ** (-0.5))
            for k in keys
        ]
        top = jnp.max(scores[0], axis=1, keepdims=True)
        for other in scores[1:]:
            top = jnp.maximum(top, jnp.max(other, axis=1, keepdims=True))
        top = top.astype(jnp.bfloat16).astype(jnp.float32)
        if held:
            before = held[0][rows, DH : DH + 1]
            top = jnp.maximum(top, before)
            scale = jnp.exp(before - top)
            part = held[0][rows, :DH] * scale
            total = held[0][rows, DH + 1 : DH + 2] * scale
        else:
            part = jnp.zeros((many, DH), jnp.float32)
            total = jnp.zeros((many, 1), jnp.float32)
        for score, v in zip(scores, values):
            weights = jnp.exp(score - top)
            total += jnp.sum(weights, axis=1, keepdims=True)
            part += jnp.dot(
                weights.astype(jnp.bfloat16), v[:, hs], preferred_element_type=jnp.float32
            )
        upper = total.astype(jnp.bfloat16).astype(jnp.float32)
        side = jnp.where(lane == 0, top, jnp.where(lane == 1, total, 0.0))
        side = jnp.where(lane == 2, upper, jnp.where(lane == 3, total - upper, side))
        out[rows] = jnp.concatenate([part, side], axis=1)


def global_parts(asking, blocks, held=()):
    n = len(blocks) // 2
    vmem = pl.BlockSpec(memory_space=pltpu.VMEM)
    rows = asking.shape[0] * asking.shape[1] // DH
    return pl.pallas_call(
        lambda *refs: global_kernel(n, *refs),
        out_shape=jax.ShapeDtypeStruct((rows, 2 * DH), jnp.float32),
        in_specs=[vmem] * (1 + len(blocks) + len(held)),
        out_specs=vmem,
        compiler_params=pltpu.CompilerParams(vmem_limit_bytes=32 * 2**20),
        cost_estimate=pl.CostEstimate(
            flops=4 * rows * DH * 768 * n, bytes_accessed=2**20 * n, transcendentals=rows * 768 * n
        ),
        name="global_parts",
    )(asking, *blocks, *held)


def merge_kernel(parts, out):
    peers = parts.shape[0]
    tops = [parts[p, BLOCK:, 0:1].astype(jnp.float32) for p in range(peers)]
    top = tops[0]
    for other in tops[1:]:
        top = jnp.maximum(top, other)
    part = jnp.zeros((BLOCK, DH), jnp.float32)
    total = jnp.zeros((BLOCK, 1), jnp.float32)
    for p, own in enumerate(tops):
        scale = jnp.exp(own - top)
        part += scale * parts[p, :BLOCK].astype(jnp.float32)
        upper = parts[p, BLOCK:, 2:3].astype(jnp.float32)
        total += scale * (upper + parts[p, BLOCK:, 3:4].astype(jnp.float32))
    whole = (part / total).astype(jnp.bfloat16)
    for p in range(peers):
        out[p] = whole


def merged(parts):
    peers, rows, _ = parts.shape
    return pl.pallas_call(
        merge_kernel,
        out_shape=jax.ShapeDtypeStruct((peers, BLOCK, DH), jnp.bfloat16),
        grid=(1,),
        in_specs=[pl.BlockSpec((peers, 2 * BLOCK, DH), lambda i: (0, rows // (2 * BLOCK) - 1, 0))],
        out_specs=pl.BlockSpec((peers, BLOCK, DH), lambda i: (0, 0, 0)),
        name="merge_parts",
    )(parts)


def patch_kernel(place, gout, attention, *out):
    blocks = attention.shape[0] // BLOCK
    heads = attention.shape[1] // DH
    half = blocks // 2
    for side in range(2):
        out[side][...] = attention[side * half * BLOCK : (side + 1) * half * BLOCK]
        for g in range(GLOBAL):
            spot = place[2 + g] - side * half

            @pl.when((place[2 + g] >= 0) & (spot >= 0) & (spot < half))
            def _():
                at_rows = pl.ds(pl.multiple_of(spot * BLOCK, BLOCK), BLOCK)
                for h in range(heads):
                    out[side][at_rows, h * DH : (h + 1) * DH] = gout[h * GLOBAL + g]


def patched(place, gout, attention):
    rows, features = attention.shape
    vmem = pl.BlockSpec(memory_space=pltpu.VMEM)
    half = jax.ShapeDtypeStruct((rows // 2, features), attention.dtype)
    return pl.pallas_call(
        patch_kernel,
        out_shape=(half, half),
        in_specs=[pl.BlockSpec(memory_space=pltpu.SMEM), vmem, vmem],
        out_specs=(vmem, vmem),
        name="global_rows",
    )(place, gout, attention)


def attend_kernel(
    counts, slots, place, q, k, v, before, after, glob, *refs
):
    n = len(counts)
    arrived, out, held, sems = refs[:n], refs[n], refs[n + 1], refs[n + 2]
    kpad, vpad = refs[n + 3], refs[n + 4]
    copies = []
    at = 0
    for part, count in enumerate(counts):
        copies.append(
            pltpu.make_async_copy(
                arrived[part].at[:, pl.ds(0, count)], held.at[:, pl.ds(at, count)], sems.at[part]
            )
        )
        copies[-1].start()
        at += count
    heads = q.shape[1] // DH
    blocks = q.shape[0] // BLOCK
    rows = q.shape[0]
    for side, (pad, own) in enumerate(((kpad, k), (vpad, v))):
        pad[0:BLOCK] = before[side * BLOCK : (side + 1) * BLOCK]
        pad[BLOCK : BLOCK + rows] = own[...]
        pad[BLOCK + rows :] = after[side * BLOCK : (side + 1) * BLOCK]
    for copy in copies:
        copy.wait()
    scale = DH ** (-0.5)
    col = lax.broadcasted_iota(jnp.int32, (BLOCK, (3 + RANDOM + GLOBAL) * BLOCK), 1)

    def one_block(b, carry):
        at_rows = pl.ds(pl.multiple_of(b * BLOCK, BLOCK), BLOCK)
        win_rows = pl.ds(pl.multiple_of(b * BLOCK, BLOCK), 3 * BLOCK)
        number = place[0] + b
        low = jnp.where(number == 0, BLOCK, 0)
        high = jnp.where(number == place[1] - 1, 2 * BLOCK, 3 * BLOCK)
        valid = (col >= low) & ((col < high) | (col >= 3 * BLOCK))
        for h in range(heads):
            hs = slice(h * DH, (h + 1) * DH)
            picks = []
            for r in range(RANDOM):
                slot = slots[(h * blocks + b) * RANDOM + r]
                at = pl.multiple_of((slot & 31) * 2 * BLOCK, 2 * BLOCK)
                picks.append((slot >> 5, at))
            keys = jnp.concatenate(
                [kpad[win_rows, hs]]
                + [held[p[0], pl.ds(p[1], BLOCK)] for p in picks]
                + [glob[g, 0, :, hs] for g in range(GLOBAL)],
                axis=0,
            )
            values = jnp.concatenate(
                [vpad[win_rows, hs]]
                + [held[p[0], pl.ds(p[1] + BLOCK, BLOCK)] for p in picks]
                + [glob[g, 1, :, hs] for g in range(GLOBAL)],
                axis=0,
            )
            scores = lax.dot_general(
                q[at_rows, hs], keys, (((1,), (1,)), ((), ())),
                preferred_element_type=jnp.float32,
            ) * scale
            scores = jnp.where(valid, scores, -jnp.inf)
            peak = jnp.max(scores, axis=1, keepdims=True)
            weights = jnp.exp(scores - peak)
            total = jnp.sum(weights, axis=1, keepdims=True)
            summed = jnp.dot(
                weights.astype(jnp.bfloat16), values, preferred_element_type=jnp.float32
            )
            out[at_rows, hs] = (summed / total).astype(jnp.bfloat16)
        return carry

    lax.fori_loop(0, blocks, one_block, 0)


def attended(slots, place, q, k, v, before, after, glob, arrived):
    rows, features = q.shape
    unit = CAP * 2 * BLOCK
    counts = tuple(a.shape[1] // unit * unit for a in arrived)
    vmem = pl.BlockSpec(memory_space=pltpu.VMEM)
    smem = pl.BlockSpec(memory_space=pltpu.SMEM)
    return pl.pallas_call(
        lambda *refs: attend_kernel(counts, *refs),
        out_shape=jax.ShapeDtypeStruct((rows, features), jnp.bfloat16),
        in_specs=[smem, smem]
        + [vmem] * 6
        + [pl.BlockSpec(memory_space=pl.ANY)] * len(arrived),
        out_specs=vmem,
        scratch_shapes=[
            pltpu.VMEM((INPLANE, PLANES * unit, DH), jnp.bfloat16),
            pltpu.SemaphoreType.DMA((len(arrived),)),
            pltpu.VMEM((rows + 2 * BLOCK, features), jnp.bfloat16),
            pltpu.VMEM((rows + 2 * BLOCK, features), jnp.bfloat16),
        ],
        compiler_params=pltpu.CompilerParams(vmem_limit_bytes=VMEM_LIMIT),
        cost_estimate=pl.CostEstimate(
            flops=4 * rows * features * 512, bytes_accessed=12 * 2**20, transcendentals=rows * 4 * 512
        ),
        name="attend",
    )(slots, place, q, k, v, before, after, glob, *arrived)


def on_device(queries, key_vectors, value_vectors, random_blocks, global_blocks, out_weight):
    shards = lax.axis_size(SEQ)
    my_index = lax.axis_index(SEQ)
    my_plane = lax.axis_index("seq_0")
    rows, features = queries.shape
    heads = features // DH
    blocks = rows // BLOCK
    requests = heads * blocks * RANDOM

    flat = random_blocks.reshape(requests)
    holders = flat // blocks
    number = jnp.arange(requests, dtype=jnp.int32)
    codes = (number // (blocks * RANDOM)) * 16 + flat % blocks
    earlier = (holders[:, None] == holders[None, :]) & (number[None, :] < number[:, None])
    rank = jnp.sum(earlier.astype(jnp.int32), axis=1)
    apart = (holders // INPLANE - my_plane) % PLANES
    order = jnp.where(apart <= PLANES // 2, jnp.minimum(2 * apart, PLANES - 1), 2 * PLANES - 1 - 2 * apart)
    slots = ((holders % INPLANE) * PLANES + order) * CAP + rank
    every = jnp.arange(INPLANE * PLANES * CAP, dtype=jnp.int32)
    asked = jnp.sum(jnp.where(slots[None, :] == every[:, None], codes[None, :], 0), axis=1)
    asked = asked.astype(jnp.bfloat16).reshape(INPLANE, 1, PLANES * CAP)
    asked = jnp.pad(asked, ((0, 0), (0, 15), (0, features - PLANES * CAP)))

    holder = global_blocks // blocks
    spot = global_blocks % blocks
    mine = holder == my_index

    def cut(source, g):
        piece = lax.dynamic_slice_in_dim(source, spot[g] * BLOCK, BLOCK, axis=0)
        return jnp.where(mine[g], piece, jnp.zeros_like(piece))

    asking = jnp.concatenate([cut(queries, g) for g in range(GLOBAL)])
    shared = jnp.concatenate(
        [cut(source, g) for g in range(GLOBAL) for source in (key_vectors, value_vectors)]
    ).reshape(INPLANE, -1, features)
    asking = jnp.broadcast_to(asking[None], (INPLANE, *asking.shape))
    found = over_plane(jnp.concatenate([asking, shared, asked], axis=1))
    many = GLOBAL * BLOCK
    asking = found[:, :many].sum(axis=0)
    shared = found[:, many:-16].sum(axis=0)
    asked = found[:, -16, : PLANES * CAP].astype(jnp.int32).reshape(-1)

    up_k, up_v, down_k, down_v = key_vectors, value_vectors, key_vectors, value_vectors
    picks = picked(asked, 0, [key_vectors, value_vectors])
    arrived = [over_plane(picks)]
    shared = jnp.broadcast_to(shared[None], (PLANES, *shared.shape))
    shared = lax.all_to_all(shared, "seq_0", split_axis=0, concat_axis=0, tiled=True).sum(axis=0)
    glob = lax.all_gather(shared, PLANE, tiled=True).reshape(GLOBAL, 2, BLOCK, features)
    ahead = [(i, i + 1) for i in range(shards - 1)]
    back = [(j, i) for i, j in ahead]
    me = lax.axis_index("heads")
    peers = lax.axis_size("heads")
    width = out_weight.shape[1] // peers

    def rows_for(away, after):
        piece = lax.dynamic_slice_in_dim(out_weight, ((me + away) % peers) * width, width, axis=1)
        if after is None:
            return piece
        piece, _ = lax.optimization_barrier((piece, after))
        return across(piece, away)

    weights = [rows_for(0, None)]
    first, parts = 1, ()
    for step in range(1, PLANES // 2 + 1):
        up_k = ring_step(up_k, 1)
        down_v = ring_step(down_v, -1)
        if step == 1:
            ends = jnp.concatenate([key_vectors[rows - BLOCK :], value_vectors[rows - BLOCK :]])
            starts = jnp.concatenate([key_vectors[:BLOCK], value_vectors[:BLOCK]])
            ends, starts, _, _ = lax.optimization_barrier((ends, starts, up_k, down_v))
            before = lax.ppermute(ends, SEQ, ahead)
            after = lax.ppermute(starts, SEQ, back)
            beside = (before, after)
        else:
            held, _, _, _, beside, parts = lax.optimization_barrier(
                (held, up_k, down_v, picks, beside, parts)
            )
            if step == 2:
                before, after = beside
            else:
                weights.append(beside)
            beside = rows_for(2 if step == 4 else (1, -1)[step - 2], up_k)
            picks = picked(asked, first, held)
            arrived.append(over_plane(picks))
            first += len(held) // 2
            both = held
            if step == 2:
                both = [*held[:2], key_vectors, *held[2:], value_vectors]
            parts = (global_parts(asking, both, parts),)
        if step < PLANES // 2:
            up_v = ring_step(up_v, 1)
            down_k = ring_step(down_k, -1)
            held = [up_k, down_k, up_v, down_v]
        else:
            held = [up_k, down_v]
    weights.append(beside)
    held, arrived, parts, glob = lax.optimization_barrier((held, arrived, parts, glob))
    parts = (global_parts(asking, held, parts),)
    arrived.append(over_plane(picked(asked, first, held, parts)))
    gout = over_plane(merged(arrived[-1]))

    place = jnp.concatenate(
        [
            jnp.stack([my_index * blocks, jnp.int32(shards * blocks)]).astype(jnp.int32),
            jnp.where(mine, spot, -1).astype(jnp.int32),
        ]
    )
    attention = attended(
        slots, place, queries, key_vectors, value_vectors, before, after, glob, arrived
    )
    own_t, own_b = patched(place, gout, attention)
    right_t, left_b = across(own_t, 1), across(own_b, -1)
    right_b, left_t = across(own_b, 1), across(own_t, -1)
    far_t, far_b = across(right_t, 1), across(left_b, -1)

    def product(*pieces):
        total = 0.0
        for piece, weight in zip(pieces, weights):
            total = total + jnp.dot(piece, weight, preferred_element_type=jnp.float32)
        return total.astype(jnp.bfloat16)

    return jnp.concatenate(
        [product(own_t, right_t, left_t, far_t), product(own_b, right_b, left_b, far_b)]
    )


def solution(mesh):
    torus = Mesh(
        mesh.devices.reshape(mesh.shape["heads"], 8, 4, 2), ("heads", "seq_0", "seq_1", "seq_2")
    )
    in_specs = (
        P(SEQ, "heads"),
        P(SEQ, "heads"),
        P(SEQ, "heads"),
        P("heads", SEQ, None),
        P(),
        P("heads", None),
    )
    out_specs = P(SEQ, "heads")
    return jax.shard_map(
        on_device, mesh=torus, in_specs=in_specs, out_specs=out_specs, check_vma=False
    )
```

time: 1050 us -> 354 us (0.34)
  waiting for transfers between devices: 452 us -> 146 us
  Pallas kernels: 281 us -> 48 us
  blocking collectives: 202 us -> 33.7 us
  starting transfers between devices: 54.1 us -> 69.7 us
  between operations: 14.8 us -> 1.81 us
    psum x2 -> x0, waiting for transfers between devices: 359 us -> none  [the longest x1 184 us: on_device(): glob = lax.psum(jnp.stack(own), SEQ).reshape(GLOBAL, 3, BLOCK, features)]
    pallas_call x4 -> x5, Pallas kernels: 261 us -> 11.7 us  [picked(): pl.pallas_call(lambda *refs: pick_kernel(n, first, *refs), out_shape=jax....]
    pmax x1 -> x0, blocking collectives: 112 us -> none  [on_device(): top = lax.pmax(jnp.max(scores, axis=-1), SEQ)]
    all_to_all x2 -> x0, blocking collectives: 90.2 us -> none  [the longest x1 80.6 us: on_device(): lax.all_to_all(out_weight, 'heads', split_axis=1, concat_axis=0, tiled=True)]
    all_to_all x4 -> x8, waiting for transfers between devices: 0.01 us -> 45.6 us  [the longest x7 36.9 us: over_plane(): return lax.all_to_all(parts, PLANE, split_axis=0, concat_axis=0, tiled=True)]
    all_gather x0 -> x1, blocking collectives: none -> 33.7 us  [on_device(): lax.all_gather(shared, PLANE, tiled=True)]
    ppermute x4 -> x11, waiting for transfers between devices: 0.01 us -> 32.1 us  [the longest x1 20 us: on_device(): before = lax.ppermute(ends, SEQ, ahead)]
    ppermute x14, waiting for transfers between devices: 92.8 us -> 68.1 us  [ring_step(): lax.ppermute(shard, 'seq_0', [(i, (i + step) % peers) for i in range(peer...]
  transfers between devices with their start and end apart: 25 -> 33, of which waited for: 13 -> 15; matrix products, arithmetic and copies ran while one was open for 3% -> 5% of each run, Pallas kernels for 19% -> 12%
where the time goes in v3:
time: 354 us; the launch traced here: 350 us
  waiting for transfers between devices  146 us (41%)
  starting transfers between devices  69.7 us (20%)
  Pallas kernels  48 us (14%)
  blocking collectives  33.7 us (10%)
  local copies, waits for them, and re-layouts  23.6 us (7%)
  other arithmetic  17.4 us (5%)
  matrix products  9.84 us (3%)
    ppermute x14, waiting for transfers between devices, ring_step(): lax.ppermute(shard, 'seq_0', [(i, (i + step) % peers) for i in range(peer...  68.1 us
    all_to_all x7, waiting for transfers between devices, over_plane(): return lax.all_to_all(parts, PLANE, split_axis=0, concat_axis=0, tiled=True)  36.9 us
    all_gather x1, blocking collectives, on_device(): lax.all_gather(shared, PLANE, tiled=True)  33.7 us
    all_to_all x7, starting transfers between devices, over_plane(): return lax.all_to_all(parts, PLANE, split_axis=0, concat_axis=0, tiled=True)  29.4 us
    ppermute x1, waiting for transfers between devices, on_device(): before = lax.ppermute(ends, SEQ, ahead)  20 us
    pallas_call x1, Pallas kernels, attended(): pl.pallas_call(lambda *refs: attend_kernel(counts, *refs), out_shape=jax....  19.8 us
    unnamed x58, local copies, waits for them, and re-layouts  17.1 us
    ppermute x9, starting transfers between devices, across(): lax.ppermute(shard, 'heads', [(i, (i + step) % peers) for i in range(peer...  15.2 us
  transfers between devices with their start and end apart: 33, of which 15 were waited for; matrix products, arithmetic and copies ran while one was open for 5% of the time, Pallas kernels for 12%

profile of v3, /device:TPU:32, one launch (start us, length us, event | category | flops | bytes accessed | tf_op | source)
XLA Modules:
  0.0 349.9 jit_solution(5761214817533031871)
XLA Ops:
  4.7 2.2 fusion.17
  6.9 2.9 fusion.18
  9.8 2.1 dynamic-slice_select_fusion.5
  13.2 1.2 fusion.1
  14.5 4.6 %all-to-all-start = ((bf16[8,176,512]{2,1,0:T(8,128)(2,1)}), bf16[8,176,512]{2,1,0:T(8,128)(2,1)}, u32[]{:S(2)}, u32[]{:S(2)}) async-start(bf16[8,176,512]{2,1,0:T(8,128)(2,1)} %fusion.1), calls=%async_computation | async-start | bytes 2883584 | tf_op jit(solution)/shard_map/all_to_all | solution.py:71
  19.1 2.0 collective-permute-start
  21.2 18.2 %all-to-all-done = bf16[8,176,512]{2,1,0:T(8,128)(2,1)} async-done(((bf16[8,176,512]{2,1,0:T(8,128)(2,1)}), bf16[8,176,512]{2,1,0:T(8,128)(2,1)}, u32[]{:S(2)}, u32[]{:S(2)}) %all-to-all-start) | async-done | bytes 1441824 | tf_op jit(solution)/shard_map/all_to_all | solution.py:71
  41.1 8.6 %all-to-all-start.5 = ((bf16[8,32,512]{2,1,0:T(8,128)(2,1)}), bf16[8,32,512]{2,1,0:T(8,128)(2,1)S(1)}, u32[]{:S(2)}, u32[]{:S(2)}) async-start(bf16[8,32,512]{2,1,0:T(8,128)(2,1)} %broadcast_in_dim.20), calls=%async_computation.5 | async-start | bytes 524288 | tf_op jit(solution)/shard_map/all_to_all | solution.py:335
  50.5 1.8 pick_blocks.5
  52.4 8.7 %all-to-all-done.5 = bf16[8,32,512]{2,1,0:T(8,128)(2,1)S(1)} async-done(((bf16[8,32,512]{2,1,0:T(8,128)(2,1)}), bf16[8,32,512]{2,1,0:T(8,128)(2,1)S(1)}, u32[]{:S(2)}, u32[]{:S(2)}) %all-to-all-start.5) | async-done | bytes 262176 | tf_op jit(solution)/shard_map/all_to_all | solution.py:335
  61.0 4.2 %all-to-all-start.1 = ((bf16[8,512,128]{2,1,0:T(8,128)(2,1)}), bf16[8,512,128]{2,1,0:T(8,128)(2,1)}, u32[]{:S(2)}, u32[]{:S(2)}) async-start(bf16[8,512,128]{2,1,0:T(8,128)(2,1)} %pick_blocks.5), calls=%async_computation.1 | async-start | bytes 2097152 | tf_op jit(solution)/shard_map/all_to_all | solution.py:71
  66.0 1.5 collective-permute-start.5
  68.4 1.9 collective-permute-start.10
  70.3 4.9 %collective-permute-done.8.refs_2_ = bf16[768,512]{1,0:T(8,128)(2,1)} collective-permute-done((bf16[768,512]{1,0:T(8,128)(2,1)S(1)}, bf16[768,512]{1,0:T(8,128)(2,1)}, u32[]{:S(2)}, u32[]{:S(2)}) %collective-permute-start.8) | collective-permute-done | bytes 786464 | tf_op jit(solution)/shard_map/ppermute | solution.py:23
  75.3 1.9 collective-permute-start.11
  77.2 8.6 %collective-permute-done.9.refs_3_.refs_4_ = bf16[768,512]{1,0:T(8,128)(2,1)S(1)} collective-permute-done((bf16[768,512]{1,0:T(8,128)(2,1)S(1)}, bf16[768,512]{1,0:T(8,128)(2,1)S(1)}, u32[]{:S(2)}, u32[]{:S(2)}) %collective-permute-start.9) | collective-permute-done | bytes 786464 | tf_op jit(solution)/shard_map/ppermute | solution.py:23
  85.8 20.0 %collective-permute-done.10.refs_5_ = bf16[128,512]{1,0:T(8,128)(2,1)S(1)} collective-permute-done((bf16[128,512]{1,0:T(8,128)(2,1)S(1)}, bf16[128,512]{1,0:T(8,128)(2,1)S(1)}, u32[]{:S(2)}, u32[]{:S(2)}) %collective-permute-start.10) | collective-permute-done | bytes 131104 | tf_op jit(solution)/shard_map/ppermute | solution.py:359
  106.4 1.9 pick_blocks.6
  108.4 1.4 copy-done.2
  110.6 4.4 %all-to-all-start.2 = ((bf16[8,1024,128]{2,1,0:T(8,128)(2,1)}), bf16[8,1024,128]{2,1,0:T(8,128)(2,1)}, u32[]{:S(2)}, u32[]{:S(2)}) async-start(bf16[8,1024,128]{2,1,0:T(8,128)(2,1)} %copy-done.2), calls=%async_computation.2 | async-start | bytes 4194304 | tf_op jit(solution)/shard_map/all_to_all | solution.py:71
  115.1 3.6 %constant_dynamic-slice_fusion = (bf16[512,1024]{1,0:T(8,128)(2,1)}, bf16[512,1024]{1,0:T(8,128)(2,1)}, bf16[512,1024]{1,0:T(8,128)(2,1)S(1)}) fusion(bf16[512,4096]{1,0:T(8,128)(2,1)} %param.11, s32[]{:T(128)S(6)} %select_n.181, s32[]{:T(128)S(6)} %select_n.177, s32[]{:T(128)S(6)} %select_n.175), kind=kLoop, calls=%fused_computation.32 | loop fusion | bytes 6291468 | tf_op jit(solution)/shard_map/dynamic_slice | solution.py:344
  118.6 1.5 collective-permute-start.14
  120.1 2.0 collective-permute-start.13
  122.4 1.7 collective-permute-start.6
  124.2 1.4 slice_reduce_fusion.refs_0_
  125.6 3.9 %global_parts.4.refs_5_ = f32[512,256]{1,0:T(8,128)S(1)} custom-call(bf16[128,512]{1,0:T(8,128)(2,1)S(1)} %slice_reduce_fusion.refs_0_, bf16[768,512]{1,0:T(8,128)(2,1)S(1)} %collective-permute-done.refs_1_, bf16[768,512]{1,0:T(8,128)(2,1)} %collective-permute-done.8.refs_2_, bf16[768,512]{1,0:T(8,128)(2,1)S(1)} %copy-done.1, ...), custom_call_target="tpu_custom_call" | custom-call | flops 603979776 | bytes 3145728 | tf_op jit(solution)/shard_map/global_parts/pallas_call | solution.py:119
  130.4 10.5 %collective-permute-done.12.refs_2_ = bf16[768,512]{1,0:T(8,128)(2,1)} collective-permute-done((bf16[768,512]{1,0:T(8,128)(2,1)}, bf16[768,512]{1,0:T(8,128)(2,1)}, u32[]{:S(2)}, u32[]{:S(2)}) %collective-permute-start.12) | collective-permute-done | bytes 786464 | tf_op jit(solution)/shard_map/ppermute | solution.py:23
  140.9 15.6 %collective-permute-done.2.refs_1_ = bf16[768,512]{1,0:T(8,128)(2,1)S(1)} collective-permute-done((bf16[768,512]{1,0:T(8,128)(2,1)S(1)}, bf16[768,512]{1,0:T(8,128)(2,1)S(1)}, u32[]{:S(2)}, u32[]{:S(2)}) %collective-permute-start.2) | collective-permute-done | bytes 786464 | tf_op jit(solution)/shard_map/ppermute | solution.py:23
  159.3 3.5 %pick_blocks.7 = bf16[8,1024,128]{2,1,0:T(8,128)(2,1)} custom-call(s32[256]{0:T(256)S(1)} %reshape.152.refs_0_, bf16[768,512]{1,0:T(8,128)(2,1)S(1)} %collective-permute-done.1.refs_1_, bf16[768,512]{1,0:T(8,128)(2,1)} %collective-permute-done.12.refs_2_, bf16[768,512]{1,0:T(8,128)(2,1)} %collective-permute-done.13.refs_3_, ...), custom_call_target="tpu_custom_call" | custom-call | bytes 5242880 | tf_op jit(solution)/shard_map/pick_blocks/pallas_call | solution.py:59
  162.8 4.6 %all-to-all-start.3 = ((bf16[8,1024,128]{2,1,0:T(8,128)(2,1)}), bf16[8,1024,128]{2,1,0:T(8,128)(2,1)}, u32[]{:S(2)}, u32[]{:S(2)}) async-start(bf16[8,1024,128]{2,1,0:T(8,128)(2,1)} %pick_blocks.7), calls=%async_computation.3 | async-start | bytes 4194304 | tf_op jit(solution)/shard_map/all_to_all | solution.py:71
  167.4 1.8 collective-permute-start.17
  169.3 2.2 collective-permute-start.15
  171.5 1.6 collective-permute-start.3
  174.6 4.0 %global_parts.5.refs_5_ = f32[512,256]{1,0:T(8,128)S(1)} custom-call(bf16[128,512]{1,0:T(8,128)(2,1)S(1)} %slice_reduce_fusion.refs_0_, bf16[768,512]{1,0:T(8,128)(2,1)S(1)} %collective-permute-done.1.refs_1_, bf16[768,512]{1,0:T(8,128)(2,1)} %collective-permute-done.12.refs_2_, bf16[768,512]{1,0:T(8,128)(2,1)} %collective-permute-done.13.refs_3_, ...), custom_call_target="tpu_custom_call" | custom-call | flops 402653184 | bytes 2097152 | tf_op jit(solution)/shard_map/global_parts/pallas_call | solution.py:119
  179.4 10.5 %collective-permute-done.15.refs_2_ = bf16[768,512]{1,0:T(8,128)(2,1)S(1)} collective-permute-done((bf16[768,512]{1,0:T(8,128)(2,1)}, bf16[768,512]{1,0:T(8,128)(2,1)S(1)}, u32[]{:S(2)}, u32[]{:S(2)}) %collective-permute-start.15) | collective-permute-done | bytes 786464 | tf_op jit(solution)/shard_map/ppermute | solution.py:23
  189.9 2.2 collective-permute-done.16.refs_3_
  192.1 15.8 %collective-permute-done.3.refs_1_ = bf16[768,512]{1,0:T(8,128)(2,1)S(1)} collective-permute-done((bf16[768,512]{1,0:T(8,128)(2,1)S(1)}, bf16[768,512]{1,0:T(8,128)(2,1)S(1)}, u32[]{:S(2)}, u32[]{:S(2)}) %collective-permute-start.3) | collective-permute-done | bytes 786464 | tf_op jit(solution)/shard_map/ppermute | solution.py:23
  207.9 2.5 pick_blocks.8
  212.2 4.6 %all-to-all-start.4 = ((bf16[8,1024,128]{2,1,0:T(8,128)(2,1)}), bf16[8,1024,128]{2,1,0:T(8,128)(2,1)}, u32[]{:S(2)}, u32[]{:S(2)}) async-start(bf16[8,1024,128]{2,1,0:T(8,128)(2,1)} %pick_blocks.8), calls=%async_computation.4 | async-start | bytes 4194304 | tf_op jit(solution)/shard_map/all_to_all | solution.py:71
  217.4 33.7 %all_gather.3 = bf16[256,512]{1,0:T(8,128)(2,1)} all-gather(bf16[32,512]{1,0:T(8,128)(2,1)} %reduce_sum.58), channel_id=1, replica_groups=mesh['heads'=4,'seq_0'=8,'seq_1'=4,'seq_2'=2] {'seq_1','seq_2'}, dimensions={0}, use_global_device_ids=true | all-gather | bytes 294912 | tf_op jit(solution)/shard_map/all_gather | solution.py:336
  251.1 1.1 copy-done.9
  252.2 1.1 copy-done.13
  254.4 2.4 global_parts.6.refs_3_
  258.6 1.9 global_parts.7.refs_3_
  260.5 1.9 pick_blocks.9
  262.4 3.7 %all-to-all-start.6 = ((bf16[8,640,128]{2,1,0:T(8,128)(2,1)}), bf16[8,640,128]{2,1,0:T(8,128)(2,1)S(1)}, u32[]{:S(2)}, u32[]{:S(2)}) async-start(bf16[8,640,128]{2,1,0:T(8,128)(2,1)} %pick_blocks.9), calls=%async_computation.6 | async-start | bytes 2621440 | tf_op jit(solution)/shard_map/all_to_all | solution.py:71
  266.1 18.7 %all-to-all-done.6.parts.refs_12_ = bf16[8,640,128]{2,1,0:T(8,128)(2,1)S(1)} async-done(((bf16[8,640,128]{2,1,0:T(8,128)(2,1)}), bf16[8,640,128]{2,1,0:T(8,128)(2,1)S(1)}, u32[]{:S(2)}, u32[]{:S(2)}) %all-to-all-start.6) | async-done | bytes 1310752 | tf_op jit(solution)/shard_map/all_to_all | solution.py:71
  285.9 2.1 merge_parts.1
  288.0 3.4 all-to-all-start.7
  291.9 1.8 collective-permute-start.21
  293.8 19.8 %attend.1.attention = bf16[768,512]{1,0:T(8,128)(2,1)} custom-call(s32[144]{0:T(256)} %copy-done.28, s32[4]{0:T(128)} %pad_add_fusion.refs_1_.place, bf16[768,512]{1,0:T(8,128)(2,1)} %refs_2_.3, bf16[768,512]{1,0:T(8,128)(2,1)} %refs_3_.3, bf16[768,512]{1,0:T(8,128)(2,1)} %refs_4_.1, bf16[128,512]{1,0:T(8,128)(2,1)} %copy-done.26, ...), custom_call_target="tpu_custom_call" | custom-call | flops 805306368 | bytes 12582912 | tf_op jit(solution)/shard_map/attend/pallas_call | solution.py:268
  314.2 2.2 global_rows.1
  317.0 2.6 collective-permute-start.19
  319.7 3.2 collective-permute-start.23
  322.9 1.9 fusion.4
  324.9 1.9 fusion.2
  326.8 3.0 collective-permute-done.18
  330.4 6.4 %collective-permute-done.23 = bf16[384,512]{1,0:T(8,128)(2,1)S(1)} collective-permute-done((bf16[384,512]{1,0:T(8,128)(2,1)}, bf16[384,512]{1,0:T(8,128)(2,1)S(1)}, u32[]{:S(2)}, u32[]{:S(2)}) %collective-permute-start.23) | collective-permute-done | bytes 393248 | tf_op jit(solution)/shard_map/ppermute | solution.py:28
  336.8 3.6 %collective-permute-start.24 = (bf16[384,512]{1,0:T(8,128)(2,1)S(1)}, bf16[384,512]{1,0:T(8,128)(2,1)S(1)}, u32[]{:S(2)}, u32[]{:S(2)}) collective-permute-start(bf16[384,512]{1,0:T(8,128)(2,1)S(1)} %collective-permute-done.23), channel_id=1, source_target_pairs={{0,192},{64,0},{128,64},{192,128},{1,193},{65,1},{129,65},{193,129... | collective-permute-start | bytes 1179656 | tf_op jit(solution)/shard_map/ppermute | solution.py:28
  340.4 1.8 fusion.24
  342.2 1.8 fusion.22
  344.7 1.2 collective-permute-done.20
  346.5 1.4 collective-permute-done.24
  348.6 1.3 pad_maximum_fusion
  (115 shorter events, 27.4 us)
Async XLA Ops:
  12.9 1.6 copy-start.28
  14.5 4.6 %copy-start.1 = (bf16[768,512]{1,0:T(8,128)(2,1)S(1)}, bf16[768,512]{1,0:T(8,128)(2,1)}, u32[]{:S(2)}) copy-start(bf16[768,512]{1,0:T(8,128)(2,1)} %refs_3_.3) | copy-start | bytes 2359300
  14.5 6.6 %copy-start = (bf16[768,512]{1,0:T(8,128)(2,1)S(1)}, bf16[768,512]{1,0:T(8,128)(2,1)}, u32[]{:S(2)}) copy-start(bf16[768,512]{1,0:T(8,128)(2,1)} %refs_4_.1) | copy-start | bytes 2359300
  14.5 24.9 %all-to-all-start = ((bf16[8,176,512]{2,1,0:T(8,128)(2,1)}), bf16[8,176,512]{2,1,0:T(8,128)(2,1)}, u32[]{:S(2)}, u32[]{:S(2)}) async-start(bf16[8,176,512]{2,1,0:T(8,128)(2,1)} %fusion.1), calls=%async_computation | async-start | bytes 2883584 | tf_op jit(solution)/shard_map/all_to_all | solution.py:71
  19.1 46.3 %collective-permute-start = (bf16[768,512]{1,0:T(8,128)(2,1)S(1)}, bf16[768,512]{1,0:T(8,128)(2,1)S(1)}, u32[]{:S(2)}, u32[]{:S(2)}) collective-permute-start(bf16[768,512]{1,0:T(8,128)(2,1)S(1)} %copy-done.1), channel_id=1, source_target_pairs={{0,8},{8,16},{16,24},{24,32},{32,40},{40,48},{48,56},{56,0},{1,9},... | collective-permute-start | bytes 2359304 | tf_op jit(solution)/shard_map/ppermute | solution.py:23
  21.1 44.8 %collective-permute-start.4 = (bf16[768,512]{1,0:T(8,128)(2,1)S(1)}, bf16[768,512]{1,0:T(8,128)(2,1)}, u32[]{:S(2)}, u32[]{:S(2)}) collective-permute-start(bf16[768,512]{1,0:T(8,128)(2,1)S(1)} %copy-done), channel_id=1, source_target_pairs={{0,56},{8,0},{16,8},{24,16},{32,24},{40,32},{48,40},{56,48},{1,57}... | collective-permute-start | bytes 2359304 | tf_op jit(solution)/shard_map/ppermute | solution.py:23
  41.1 19.9 %all-to-all-start.5 = ((bf16[8,32,512]{2,1,0:T(8,128)(2,1)}), bf16[8,32,512]{2,1,0:T(8,128)(2,1)S(1)}, u32[]{:S(2)}, u32[]{:S(2)}) async-start(bf16[8,32,512]{2,1,0:T(8,128)(2,1)} %broadcast_in_dim.20), calls=%async_computation.5 | async-start | bytes 524288 | tf_op jit(solution)/shard_map/all_to_all | solution.py:335
  49.7 25.6 %collective-permute-start.8 = (bf16[768,512]{1,0:T(8,128)(2,1)S(1)}, bf16[768,512]{1,0:T(8,128)(2,1)}, u32[]{:S(2)}, u32[]{:S(2)}) collective-permute-start(bf16[768,512]{1,0:T(8,128)(2,1)S(1)} %copy-done.1), channel_id=1, source_target_pairs={{0,56},{8,0},{16,8},{24,16},{32,24},{40,32},{48,40},{56,48},{1,57}... | collective-permute-start | bytes 2359304 | tf_op jit(solution)/shard_map/ppermute | solution.py:23
  61.0 49.6 %all-to-all-start.1 = ((bf16[8,512,128]{2,1,0:T(8,128)(2,1)}), bf16[8,512,128]{2,1,0:T(8,128)(2,1)}, u32[]{:S(2)}, u32[]{:S(2)}) async-start(bf16[8,512,128]{2,1,0:T(8,128)(2,1)} %pick_blocks.5), calls=%async_computation.1 | async-start | bytes 2097152 | tf_op jit(solution)/shard_map/all_to_all | solution.py:71
  65.3 20.5 %collective-permute-start.9 = (bf16[768,512]{1,0:T(8,128)(2,1)S(1)}, bf16[768,512]{1,0:T(8,128)(2,1)S(1)}, u32[]{:S(2)}, u32[]{:S(2)}) collective-permute-start(bf16[768,512]{1,0:T(8,128)(2,1)S(1)} %copy-done), channel_id=1, source_target_pairs={{0,8},{8,16},{16,24},{24,32},{32,40},{40,48},{48,56},{56,0},{1,9},... | collective-permute-start | bytes 2359304 | tf_op jit(solution)/shard_map/ppermute | solution.py:23
  65.4 40.3 %collective-permute-start.1 = (bf16[768,512]{1,0:T(8,128)(2,1)S(1)}, bf16[768,512]{1,0:T(8,128)(2,1)S(1)}, u32[]{:S(2)}, u32[]{:S(2)}) collective-permute-start(bf16[768,512]{1,0:T(8,128)(2,1)S(1)} %collective-permute-done.refs_1_), channel_id=1, source_target_pairs={{0,8},{8,16},{16,24},{24,32},{32,40},{40,48},{48,56},{56,0},{1,9},... | collective-permute-start | bytes 2359304 | tf_op jit(solution)/shard_map/ppermute | solution.py:23
  66.0 40.5 %collective-permute-start.5 = (bf16[768,512]{1,0:T(8,128)(2,1)}, bf16[768,512]{1,0:T(8,128)(2,1)}, u32[]{:S(2)}, u32[]{:S(2)}) collective-permute-start(bf16[768,512]{1,0:T(8,128)(2,1)} %collective-permute-done.4.refs_4_.refs_5_), channel_id=1, source_target_pairs={{0,56},{8,0},{16,8},{24,16},{32,24},{40,32},{48,40},{56,48},{1,57}... | collective-permute-start | bytes 2359304 | tf_op jit(solution)/shard_map/ppermute | solution.py:23
  68.4 37.3 %collective-permute-start.10 = (bf16[128,512]{1,0:T(8,128)(2,1)S(1)}, bf16[128,512]{1,0:T(8,128)(2,1)S(1)}, u32[]{:S(2)}, u32[]{:S(2)}) collective-permute-start(bf16[128,512]{1,0:T(8,128)(2,1)S(1)} %get-tuple-element.38), channel_id=1, source_target_pairs={{0,1},{1,2},{2,3},{3,4},{4,5},{5,6},{6,7},{7,8},{8,9},{9,10},{10,1... | collective-permute-start | bytes 393224 | tf_op jit(solution)/shard_map/ppermute | solution.py:359
  75.3 30.5 %collective-permute-start.11 = (bf16[128,512]{1,0:T(8,128)(2,1)S(1)}, bf16[128,512]{1,0:T(8,128)(2,1)S(1)}, u32[]{:S(2)}, u32[]{:S(2)}) collective-permute-start(bf16[128,512]{1,0:T(8,128)(2,1)S(1)} %get-tuple-element.39), channel_id=1, source_target_pairs={{1,0},{2,1},{3,2},{4,3},{5,4},{6,5},{7,6},{8,7},{9,8},{10,9},{11,1... | collective-permute-start | bytes 393224 | tf_op jit(solution)/shard_map/ppermute | solution.py:360
  105.7 0.6 copy-start.26
  105.7 0.7 copy-start.27
  108.4 1.4 copy-start.2
  109.7 0.9 copy-start.3
  110.6 52.2 %all-to-all-start.2 = ((bf16[8,1024,128]{2,1,0:T(8,128)(2,1)}), bf16[8,1024,128]{2,1,0:T(8,128)(2,1)}, u32[]{:S(2)}, u32[]{:S(2)}) async-start(bf16[8,1024,128]{2,1,0:T(8,128)(2,1)} %copy-done.2), calls=%async_computation.2 | async-start | bytes 4194304 | tf_op jit(solution)/shard_map/all_to_all | solution.py:71
  115.1 5.1 %copy-start.4 = (bf16[768,512]{1,0:T(8,128)(2,1)S(1)}, bf16[768,512]{1,0:T(8,128)(2,1)}, u32[]{:S(2)}) copy-start(bf16[768,512]{1,0:T(8,128)(2,1)} %copy-done.3) | copy-start | bytes 2359300
  118.6 39.7 %collective-permute-start.14 = (bf16[512,1024]{1,0:T(8,128)(2,1)S(1)}, bf16[512,1024]{1,0:T(8,128)(2,1)S(1)}, u32[]{:S(2)}, u32[]{:S(2)}) collective-permute-start(bf16[512,1024]{1,0:T(8,128)(2,1)S(1)} %get-tuple-element.44), channel_id=1, source_target_pairs={{0,64},{64,128},{128,192},{192,0},{1,65},{65,129},{129,193},{193,1... | collective-permute-start | bytes 3145736 | tf_op jit(solution)/shard_map/ppermute | solution.py:28
  120.1 20.7 %collective-permute-start.12 = (bf16[768,512]{1,0:T(8,128)(2,1)}, bf16[768,512]{1,0:T(8,128)(2,1)}, u32[]{:S(2)}, u32[]{:S(2)}) collective-permute-start(bf16[768,512]{1,0:T(8,128)(2,1)} %collective-permute-done.8.refs_2_), channel_id=1, source_target_pairs={{0,56},{8,0},{16,8},{24,16},{32,24},{40,32},{48,40},{56,48},{1,57}... | collective-permute-start | bytes 2359304 | tf_op jit(solution)/shard_map/ppermute | solution.py:23
  120.1 20.7 %collective-permute-start.13 = (bf16[768,512]{1,0:T(8,128)(2,1)S(1)}, bf16[768,512]{1,0:T(8,128)(2,1)}, u32[]{:S(2)}, u32[]{:S(2)}) collective-permute-start(bf16[768,512]{1,0:T(8,128)(2,1)S(1)} %copy-done.4), channel_id=1, source_target_pairs={{0,8},{8,16},{16,24},{24,32},{32,40},{40,48},{48,56},{56,0},{1,9},... | collective-permute-start | bytes 2359304 | tf_op jit(solution)/shard_map/ppermute | solution.py:23
  122.2 34.3 %collective-permute-start.2 = (bf16[768,512]{1,0:T(8,128)(2,1)S(1)}, bf16[768,512]{1,0:T(8,128)(2,1)S(1)}, u32[]{:S(2)}, u32[]{:S(2)}) collective-permute-start(bf16[768,512]{1,0:T(8,128)(2,1)S(1)} %collective-permute-done.1.refs_1_), channel_id=1, source_target_pairs={{0,8},{8,16},{16,24},{24,32},{32,40},{40,48},{48,56},{56,0},{1,9},... | collective-permute-start | bytes 2359304 | tf_op jit(solution)/shard_map/ppermute | solution.py:23
  122.4 35.0 %collective-permute-start.6 = (bf16[768,512]{1,0:T(8,128)(2,1)}, bf16[768,512]{1,0:T(8,128)(2,1)S(1)}, u32[]{:S(2)}, u32[]{:S(2)}) collective-permute-start(bf16[768,512]{1,0:T(8,128)(2,1)} %collective-permute-done.5.refs_4_), channel_id=1, source_target_pairs={{0,56},{8,0},{16,8},{24,16},{32,24},{40,32},{48,40},{56,48},{1,57}... | collective-permute-start | bytes 2359304 | tf_op jit(solution)/shard_map/ppermute | solution.py:23
  129.5 0.9 copy-start.18
  156.5 1.0 copy-start.5
  157.4 0.9 copy-start.7
  158.3 1.0 copy-start.21
  162.8 8.6 %copy-start.6 = (bf16[768,512]{1,0:T(8,128)(2,1)S(1)}, bf16[768,512]{1,0:T(8,128)(2,1)}, u32[]{:S(2)}) copy-start(bf16[768,512]{1,0:T(8,128)(2,1)} %copy-done.5) | copy-start | bytes 2359300
  162.8 49.3 %all-to-all-start.3 = ((bf16[8,1024,128]{2,1,0:T(8,128)(2,1)}), bf16[8,1024,128]{2,1,0:T(8,128)(2,1)}, u32[]{:S(2)}, u32[]{:S(2)}) async-start(bf16[8,1024,128]{2,1,0:T(8,128)(2,1)} %pick_blocks.7), calls=%async_computation.3 | async-start | bytes 4194304 | tf_op jit(solution)/shard_map/all_to_all | solution.py:71
  167.4 40.4 %copy-start.8 = (bf16[768,512]{1,0:T(8,128)(2,1)S(1)}, bf16[768,512]{1,0:T(8,128)(2,1)}, u32[]{:S(2)}) copy-start(bf16[768,512]{1,0:T(8,128)(2,1)} %copy-done.7) | copy-start | bytes 2359300
  167.4 40.4 %collective-permute-start.17 = (bf16[512,1024]{1,0:T(8,128)(2,1)}, bf16[512,1024]{1,0:T(8,128)(2,1)}, u32[]{:S(2)}, u32[]{:S(2)}) collective-permute-start(bf16[512,1024]{1,0:T(8,128)(2,1)} %get-tuple-element.49), channel_id=1, source_target_pairs={{0,192},{64,0},{128,64},{192,128},{1,193},{65,1},{129,65},{193,129... | collective-permute-start | bytes 3145736 | tf_op jit(solution)/shard_map/ppermute | solution.py:28
  169.3 20.6 %collective-permute-start.15 = (bf16[768,512]{1,0:T(8,128)(2,1)}, bf16[768,512]{1,0:T(8,128)(2,1)S(1)}, u32[]{:S(2)}, u32[]{:S(2)}) collective-permute-start(bf16[768,512]{1,0:T(8,128)(2,1)} %collective-permute-done.12.refs_2_), channel_id=1, source_target_pairs={{0,56},{8,0},{16,8},{24,16},{32,24},{40,32},{48,40},{56,48},{1,57}... | collective-permute-start | bytes 2359304 | tf_op jit(solution)/shard_map/ppermute | solution.py:23
  171.5 20.6 %collective-permute-start.16 = (bf16[768,512]{1,0:T(8,128)(2,1)}, bf16[768,512]{1,0:T(8,128)(2,1)S(1)}, u32[]{:S(2)}, u32[]{:S(2)}) collective-permute-start(bf16[768,512]{1,0:T(8,128)(2,1)} %collective-permute-done.13.refs_3_), channel_id=1, source_target_pairs={{0,8},{8,16},{16,24},{24,32},{32,40},{40,48},{48,56},{56,0},{1,9},... | collective-permute-start | bytes 2359304 | tf_op jit(solution)/shard_map/ppermute | solution.py:23
  171.5 36.4 %collective-permute-start.3 = (bf16[768,512]{1,0:T(8,128)(2,1)S(1)}, bf16[768,512]{1,0:T(8,128)(2,1)S(1)}, u32[]{:S(2)}, u32[]{:S(2)}) collective-permute-start(bf16[768,512]{1,0:T(8,128)(2,1)S(1)} %copy-done.6), channel_id=1, source_target_pairs={{0,8},{8,16},{16,24},{24,32},{32,40},{40,48},{48,56},{56,0},{1,9},... | collective-permute-start | bytes 2359304 | tf_op jit(solution)/shard_map/ppermute | solution.py:23
  173.0 34.8 %collective-permute-start.7 = (bf16[768,512]{1,0:T(8,128)(2,1)}, bf16[768,512]{1,0:T(8,128)(2,1)S(1)}, u32[]{:S(2)}, u32[]{:S(2)}) collective-permute-start(bf16[768,512]{1,0:T(8,128)(2,1)} %copy-done.7), channel_id=1, source_target_pairs={{0,56},{8,0},{16,8},{24,16},{32,24},{40,32},{48,40},{56,48},{1,57}... | collective-permute-start | bytes 2359304 | tf_op jit(solution)/shard_map/ppermute | solution.py:23
  173.5 1.0 copy-start.19
  178.6 0.8 copy-start.14
  210.4 0.9 copy-start.10
  211.3 0.9 copy-start.12
  212.2 38.9 %copy-start.11 = (bf16[768,512]{1,0:T(8,128)(2,1)S(1)}, bf16[768,512]{1,0:T(8,128)(2,1)}, u32[]{:S(2)}) copy-start(bf16[768,512]{1,0:T(8,128)(2,1)} %copy-done.10) | copy-start | bytes 2359300
  212.2 45.4 %all-to-all-start.4 = ((bf16[8,1024,128]{2,1,0:T(8,128)(2,1)}), bf16[8,1024,128]{2,1,0:T(8,128)(2,1)}, u32[]{:S(2)}, u32[]{:S(2)}) async-start(bf16[8,1024,128]{2,1,0:T(8,128)(2,1)} %pick_blocks.8), calls=%async_computation.4 | async-start | bytes 4194304 | tf_op jit(solution)/shard_map/all_to_all | solution.py:71
  251.1 1.1 copy-start.9
  252.2 1.1 copy-start.13
  253.4 1.0 copy-start.15
  256.8 0.8 copy-start.16
  257.6 1.0 copy-start.17
  262.4 29.5 %copy-start.23 = (bf16[512,1024]{1,0:T(8,128)(2,1)S(1)}, bf16[512,1024]{1,0:T(8,128)(2,1)}, u32[]{:S(2)}) copy-start(bf16[512,1024]{1,0:T(8,128)(2,1)} %get-tuple-element.69) | copy-start | bytes 3145732
  262.4 22.4 %all-to-all-start.6 = ((bf16[8,640,128]{2,1,0:T(8,128)(2,1)}), bf16[8,640,128]{2,1,0:T(8,128)(2,1)S(1)}, u32[]{:S(2)}, u32[]{:S(2)}) async-start(bf16[8,640,128]{2,1,0:T(8,128)(2,1)} %pick_blocks.9), calls=%async_computation.6 | async-start | bytes 2621440 | tf_op jit(solution)/shard_map/all_to_all | solution.py:71
  284.8 1.1 copy-start.20
  288.0 25.6 %all-to-all-start.7 = ((bf16[8,64,128]{2,1,0:T(8,128)(2,1)}), bf16[8,64,128]{2,1,0:T(8,128)(2,1)S(1)}, u32[]{:S(2)}, u32[]{:S(2)}) async-start(bf16[8,64,128]{2,1,0:T(8,128)(2,1)} %merge_parts.1), calls=%async_computation.7 | async-start | bytes 262144 | tf_op jit(solution)/shard_map/all_to_all | solution.py:71
  291.9 52.7 %collective-permute-start.21 = (bf16[512,1024]{1,0:T(8,128)(2,1)S(1)}, bf16[512,1024]{1,0:T(8,128)(2,1)S(1)}, u32[]{:S(2)}, u32[]{:S(2)}) collective-permute-start(bf16[512,1024]{1,0:T(8,128)(2,1)S(1)} %copy-done.23), channel_id=1, source_target_pairs={{0,128},{64,192},{128,0},{192,64},{1,129},{65,193},{129,1},{193,65... | collective-permute-start | bytes 3145736 | tf_op jit(solution)/shard_map/ppermute | solution.py:28
  313.6 0.6 copy-start.24
  316.4 8.4 %copy-start.25 = (bf16[384,512]{1,0:T(8,128)(2,1)S(1)}, bf16[384,512]{1,0:T(8,128)(2,1)}, u32[]{:S(2)}) copy-start(bf16[384,512]{1,0:T(8,128)(2,1)} %get-tuple-element.70) | copy-start | bytes 1179652
  316.4 13.4 %collective-permute-start.18 = (bf16[384,512]{1,0:T(8,128)(2,1)}, bf16[384,512]{1,0:T(8,128)(2,1)S(1)}, u32[]{:S(2)}, u32[]{:S(2)}) collective-permute-start(bf16[384,512]{1,0:T(8,128)(2,1)} %get-tuple-element.66), channel_id=1, source_target_pairs={{0,64},{64,128},{128,192},{192,0},{1,65},{65,129},{129,193},{193,1... | collective-permute-start | bytes 1179656 | tf_op jit(solution)/shard_map/ppermute | solution.py:28
  317.0 25.2 %collective-permute-start.19 = (bf16[384,512]{1,0:T(8,128)(2,1)}, bf16[384,512]{1,0:T(8,128)(2,1)S(1)}, u32[]{:S(2)}, u32[]{:S(2)}) collective-permute-start(bf16[384,512]{1,0:T(8,128)(2,1)} %get-tuple-element.66), channel_id=1, source_target_pairs={{0,192},{64,0},{128,64},{192,128},{1,193},{65,1},{129,65},{193,129... | collective-permute-start | bytes 1179656 | tf_op jit(solution)/shard_map/ppermute | solution.py:28
  319.7 24.4 %collective-permute-start.22 = (bf16[384,512]{1,0:T(8,128)(2,1)}, bf16[384,512]{1,0:T(8,128)(2,1)S(1)}, u32[]{:S(2)}, u32[]{:S(2)}) collective-permute-start(bf16[384,512]{1,0:T(8,128)(2,1)} %get-tuple-element.70), channel_id=1, source_target_pairs={{0,64},{64,128},{128,192},{192,0},{1,65},{65,129},{129,193},{193,1... | collective-permute-start | bytes 1179656 | tf_op jit(solution)/shard_map/ppermute | solution.py:28
  319.7 17.1 %collective-permute-start.23 = (bf16[384,512]{1,0:T(8,128)(2,1)}, bf16[384,512]{1,0:T(8,128)(2,1)S(1)}, u32[]{:S(2)}, u32[]{:S(2)}) collective-permute-start(bf16[384,512]{1,0:T(8,128)(2,1)} %get-tuple-element.70), channel_id=1, source_target_pairs={{0,192},{64,0},{128,64},{192,128},{1,193},{65,1},{129,65},{193,129... | collective-permute-start | bytes 1179656 | tf_op jit(solution)/shard_map/ppermute | solution.py:28
  324.9 5.0 %copy-start.22 = (bf16[512,1024]{1,0:T(8,128)(2,1)S(1)}, bf16[512,1024]{1,0:T(8,128)(2,1)}, u32[]{:S(2)}) copy-start(bf16[512,1024]{1,0:T(8,128)(2,1)} %copy-done.21) | copy-start | bytes 3145732
  329.8 16.1 %collective-permute-start.20 = (bf16[384,512]{1,0:T(8,128)(2,1)S(1)}, bf16[384,512]{1,0:T(8,128)(2,1)S(1)}, u32[]{:S(2)}, u32[]{:S(2)}) collective-permute-start(bf16[384,512]{1,0:T(8,128)(2,1)S(1)} %collective-permute-done.18), channel_id=1, source_target_pairs={{0,64},{64,128},{128,192},{192,0},{1,65},{65,129},{129,193},{193,1... | collective-permute-start | bytes 1179656 | tf_op jit(solution)/shard_map/ppermute | solution.py:28
  336.8 11.1 %collective-permute-start.24 = (bf16[384,512]{1,0:T(8,128)(2,1)S(1)}, bf16[384,512]{1,0:T(8,128)(2,1)S(1)}, u32[]{:S(2)}, u32[]{:S(2)}) collective-permute-start(bf16[384,512]{1,0:T(8,128)(2,1)S(1)} %collective-permute-done.23), channel_id=1, source_target_pairs={{0,192},{64,0},{128,64},{192,128},{1,193},{65,1},{129,65},{193,129... | collective-permute-start | bytes 1179656 | tf_op jit(solution)/shard_map/ppermute | solution.py:28

commit v4 on v3

--- a/solution.py
+++ b/solution.py
@@ -62,7 +62,7 @@
         in_specs=[pl.BlockSpec(memory_space=pltpu.SMEM)] + [vmem] * (2 * n + len(extra)),
         out_specs=vmem,
         compiler_params=pltpu.CompilerParams(vmem_limit_bytes=32 * 2**20),
-        cost_estimate=pl.CostEstimate(flops=0, bytes_accessed=size, transcendentals=0),
+        cost_estimate=pl.CostEstimate(flops=0, bytes_accessed=24 * 2**20, transcendentals=0),
         name="pick_blocks",
     )(codes, *blocks, *extra)
 
@@ -123,7 +123,7 @@
         out_specs=vmem,
         compiler_params=pltpu.CompilerParams(vmem_limit_bytes=32 * 2**20),
         cost_estimate=pl.CostEstimate(
-            flops=4 * rows * DH * 768 * n, bytes_accessed=2**20 * n, transcendentals=rows * 768 * n
+            flops=4 * rows * DH * 768 * n, bytes_accessed=24 * 2**20, transcendentals=rows * 768 * n
         ),
         name="global_parts",
     )(asking, *blocks, *held)
@@ -322,66 +322,68 @@
         [cut(source, g) for g in range(GLOBAL) for source in (key_vectors, value_vectors)]
     ).reshape(INPLANE, -1, features)
     asking = jnp.broadcast_to(asking[None], (INPLANE, *asking.shape))
-    found = over_plane(jnp.concatenate([asking, shared, asked], axis=1))
+    found = jnp.concatenate([asking, shared, asked], axis=1)
+    up_k, down_v = ring_step(key_vectors, 1), ring_step(value_vectors, -1)
+    up_v, down_k = ring_step(value_vectors, 1), ring_step(key_vectors, -1)
+    me = lax.axis_index("heads")
+    peers = lax.axis_size("heads")
+    width = out_weight.shape[1] // peers
+    weights = [
+        lax.dynamic_slice_in_dim(out_weight, ((me + away) % peers) * width, width, axis=1)
+        for away in (0, 1, -1, 2)
+    ]
+    ends = jnp.concatenate([key_vectors[rows - BLOCK :], value_vectors[rows - BLOCK :]])
+    starts = jnp.concatenate([key_vectors[:BLOCK], value_vectors[:BLOCK]])
+    found, ends, starts, weights, _, _ = lax.optimization_barrier(
+        (found, ends, starts, weights, up_k, down_v)
+    )
+    found = over_plane(found)
     many = GLOBAL * BLOCK
     asking = found[:, :many].sum(axis=0)
     shared = found[:, many:-16].sum(axis=0)
     asked = found[:, -16, : PLANES * CAP].astype(jnp.int32).reshape(-1)
 
-    up_k, up_v, down_k, down_v = key_vectors, value_vectors, key_vectors, value_vectors
+    asked, _, _ = lax.optimization_barrier((asked, up_v, down_k))
     picks = picked(asked, 0, [key_vectors, value_vectors])
     arrived = [over_plane(picks)]
     shared = jnp.broadcast_to(shared[None], (PLANES, *shared.shape))
     shared = lax.all_to_all(shared, "seq_0", split_axis=0, concat_axis=0, tiled=True).sum(axis=0)
-    glob = lax.all_gather(shared, PLANE, tiled=True).reshape(GLOBAL, 2, BLOCK, features)
+    shared = jnp.broadcast_to(shared[None], (INPLANE, *shared.shape))
+    glob = over_plane(shared).reshape(GLOBAL, 2, BLOCK, features)
     ahead = [(i, i + 1) for i in range(shards - 1)]
     back = [(j, i) for i, j in ahead]
-    me = lax.axis_index("heads")
-    peers = lax.axis_size("heads")
-    width = out_weight.shape[1] // peers
-
-    def rows_for(away, after):
-        piece = lax.dynamic_slice_in_dim(out_weight, ((me + away) % peers) * width, width, axis=1)
-        if after is None:
-            return piece
-        piece, _ = lax.optimization_barrier((piece, after))
-        return across(piece, away)
-
-    weights = [rows_for(0, None)]
     first, parts = 1, ()
-    for step in range(1, PLANES // 2 + 1):
+    beside = [lax.ppermute(ends, SEQ, ahead), lax.ppermute(starts, SEQ, back)]
+    held = [up_k, down_k, up_v, down_v]
+    for step in range(2, PLANES // 2 + 1):
+        if step == PLANES // 2:
+            up_k, down_v, _ = lax.optimization_barrier((up_k, down_v, held))
         up_k = ring_step(up_k, 1)
         down_v = ring_step(down_v, -1)
-        if step == 1:
-            ends = jnp.concatenate([key_vectors[rows - BLOCK :], value_vectors[rows - BLOCK :]])
-            starts = jnp.concatenate([key_vectors[:BLOCK], value_vectors[:BLOCK]])
-            ends, starts, _, _ = lax.optimization_barrier((ends, starts, up_k, down_v))
-            before = lax.ppermute(ends, SEQ, ahead)
-            after = lax.ppermute(starts, SEQ, back)
-            beside = (before, after)
+        gate = (up_k, down_v) if step < PLANES // 2 else ()
+        held, _, _, beside, parts = lax.optimization_barrier(
+            (held, gate, picks, beside, parts)
+        )
+        if step == 2:
+            before, after = beside
         else:
-            held, _, _, _, beside, parts = lax.optimization_barrier(
-                (held, up_k, down_v, picks, beside, parts)
-            )
-            if step == 2:
-                before, after = beside
-            else:
-                weights.append(beside)
-            beside = rows_for(2 if step == 4 else (1, -1)[step - 2], up_k)
-            picks = picked(asked, first, held)
-            arrived.append(over_plane(picks))
-            first += len(held) // 2
-            both = held
-            if step == 2:
-                both = [*held[:2], key_vectors, *held[2:], value_vectors]
-            parts = (global_parts(asking, both, parts),)
+            weights[step - 2] = beside
+        beside, _ = lax.optimization_barrier((weights[step - 1], held))
+        beside = across(beside, (1, -1, 2)[step - 2])
+        picks = picked(asked, first, held)
+        arrived.append(over_plane(picks))
+        first += len(held) // 2
+        both = held
+        if step == 2:
+            both = [*held[:2], key_vectors, *held[2:], value_vectors]
+        parts = (global_parts(asking, both, parts),)
         if step < PLANES // 2:
             up_v = ring_step(up_v, 1)
             down_k = ring_step(down_k, -1)
             held = [up_k, down_k, up_v, down_v]
         else:
             held = [up_k, down_v]
-    weights.append(beside)
+    weights[3] = beside
     held, arrived, parts, glob = lax.optimization_barrier((held, arrived, parts, glob))
     parts = (global_parts(asking, held, parts),)
     arrived.append(over_plane(picked(asked, first, held, parts)))

time: 354 us -> 324 us (0.915)
  blocking collectives: 33.7 us -> 18.3 us
  waiting for transfers between devices: 146 us -> 131 us
    all_gather x1 -> x0, blocking collectives: 33.7 us -> none  [on_device(): lax.all_gather(shared, PLANE, tiled=True)]
    all_to_all x0 -> x1, blocking collectives: none -> 18.3 us  [on_device(): lax.all_to_all(shared, 'seq_0', split_axis=0, concat_axis=0, tiled=True)]
    ppermute x14, waiting for transfers between devices: 68.1 us -> 56.1 us  [ring_step(): lax.ppermute(shard, 'seq_0', [(i, (i + step) % peers) for i in range(peer...]
    all_to_all x7 -> x8, waiting for transfers between devices: 36.9 us -> 45.9 us  [over_plane(): return lax.all_to_all(parts, PLANE, split_axis=0, concat_axis=0, tiled=True)]
    all_to_all x1 -> x0, waiting for transfers between devices: 8.68 us -> none  [on_device(): lax.all_to_all(shared, 'seq_0', split_axis=0, concat_axis=0, tiled=True)]
    all_to_all x1 -> x0, starting transfers between devices: 8.57 us -> none  [on_device(): lax.all_to_all(shared, 'seq_0', split_axis=0, concat_axis=0, tiled=True)]
    ppermute x2, waiting for transfers between devices: 20 us -> 13.3 us  [on_device(): beside = [lax.ppermute(ends, SEQ, ahead), lax.ppermute(starts, SEQ, back)]]
    ppermute x2, starting transfers between devices: 3.83 us -> 8.18 us  [on_device(): beside = [lax.ppermute(ends, SEQ, ahead), lax.ppermute(starts, SEQ, back)]]
  transfers between devices with their start and end apart: 33 -> 33, of which waited for: 15 -> 19; matrix products, arithmetic and copies ran while one was open for 5% -> 9% of each run, Pallas kernels for 12% -> 14%
where the time goes in v4:
time: 324 us; the launch traced here: 320 us
  waiting for transfers between devices  131 us (40%)
  starting transfers between devices  72.2 us (22%)
  Pallas kernels  49.8 us (15%)
  local copies, waits for them, and re-layouts  20.9 us (6%)
  blocking collectives  18.3 us (6%)
  other arithmetic  15.2 us (5%)
  matrix products  10.7 us (3%)
    ppermute x14, waiting for transfers between devices, ring_step(): lax.ppermute(shard, 'seq_0', [(i, (i + step) % peers) for i in range(peer...  56.1 us
    all_to_all x8, waiting for transfers between devices, over_plane(): return lax.all_to_all(parts, PLANE, split_axis=0, concat_axis=0, tiled=True)  45.9 us
    all_to_all x8, starting transfers between devices, over_plane(): return lax.all_to_all(parts, PLANE, split_axis=0, concat_axis=0, tiled=True)  32.6 us
    pallas_call x1, Pallas kernels, attended(): pl.pallas_call(lambda *refs: attend_kernel(counts, *refs), out_shape=jax....  20 us
    all_to_all x1, blocking collectives, on_device(): lax.all_to_all(shared, 'seq_0', split_axis=0, concat_axis=0, tiled=True)  18.3 us
    ppermute x9, starting transfers between devices, across(): lax.ppermute(shard, 'heads', [(i, (i + step) % peers) for i in range(peer...  15.9 us
    unnamed x58, local copies, waits for them, and re-layouts  15.8 us
    ppermute x14, starting transfers between devices, ring_step(): lax.ppermute(shard, 'seq_0', [(i, (i + step) % peers) for i in range(peer...  15.5 us
  transfers between devices with their start and end apart: 33, of which 19 were waited for; matrix products, arithmetic and copies ran while one was open for 9% of the time, Pallas kernels for 14%

profile of v4, /device:TPU:32, one launch (start us, length us, event | category | flops | bytes accessed | tf_op | source)
XLA Modules:
  0.0 319.6 jit_solution(18431186871748319894)
XLA Ops:
  0.0 1.9 collective-permute-start
  6.7 2.3 fusion.12
  9.0 2.2 dynamic-slice_select_fusion.5
  12.4 1.3 fusion.11
  14.6 1.2 fusion.1
  16.5 2.1 constant_dynamic-slice_fusion
  19.5 1.8 collective-permute-done.1.refs_4_.refs_5_
  21.3 4.5 %all-to-all-start = ((bf16[8,176,512]{2,1,0:T(8,128)(2,1)}), bf16[8,176,512]{2,1,0:T(8,128)(2,1)}, u32[]{:S(2)}, u32[]{:S(2)}) async-start(bf16[8,176,512]{2,1,0:T(8,128)(2,1)} %fusion.1), calls=%async_computation | async-start | bytes 2883584 | tf_op jit(solution)/shard_map/all_to_all | solution.py:71
  25.8 3.2 %collective-permute-start.2 = (bf16[768,512]{1,0:T(8,128)(2,1)S(1)}, bf16[768,512]{1,0:T(8,128)(2,1)}, u32[]{:S(2)}, u32[]{:S(2)}) collective-permute-start(bf16[768,512]{1,0:T(8,128)(2,1)S(1)} %copy-done), channel_id=1, source_target_pairs={{0,8},{8,16},{16,24},{24,32},{32,40},{40,48},{48,56},{56,0},{1,9},... | collective-permute-start | bytes 2359304 | tf_op jit(solution)/shard_map/ppermute | solution.py:23
  29.0 17.1 %all-to-all-done = bf16[8,176,512]{2,1,0:T(8,128)(2,1)} async-done(((bf16[8,176,512]{2,1,0:T(8,128)(2,1)}), bf16[8,176,512]{2,1,0:T(8,128)(2,1)}, u32[]{:S(2)}, u32[]{:S(2)}) %all-to-all-start) | async-done | bytes 1441824 | tf_op jit(solution)/shard_map/all_to_all | solution.py:71
  47.1 18.3 %all_to_all.45 = bf16[8,32,512]{2,1,0:T(8,128)(2,1)S(1)} all-to-all(bf16[8,32,512]{2,1,0:T(8,128)(2,1)S(1)} %broadcast_in_dim.22), channel_id=1, replica_groups=mesh['heads'=4,'seq_0'=8,'seq_1'=4,'seq_2'=2] {'seq_0'}, dimensions={0} | all-to-all | bytes 524288 | tf_op jit(solution)/shard_map/all_to_all | solution.py:350
  66.1 3.4 %all-to-all-start.6 = ((bf16[8,32,512]{2,1,0:T(8,128)(2,1)}), bf16[8,32,512]{2,1,0:T(8,128)(2,1)S(1)}, u32[]{:S(2)}, u32[]{:S(2)}) async-start(bf16[8,32,512]{2,1,0:T(8,128)(2,1)} %broadcast_in_dim.23), calls=%async_computation.6 | async-start | bytes 524288 | tf_op jit(solution)/shard_map/all_to_all | solution.py:71
  70.4 1.8 pick_blocks.5
  72.2 4.8 %all-to-all-done.6 = bf16[8,32,512]{2,1,0:T(8,128)(2,1)S(1)} async-done(((bf16[8,32,512]{2,1,0:T(8,128)(2,1)}), bf16[8,32,512]{2,1,0:T(8,128)(2,1)S(1)}, u32[]{:S(2)}, u32[]{:S(2)}) %all-to-all-start.6) | async-done | bytes 262176 | tf_op jit(solution)/shard_map/all_to_all | solution.py:71
  77.0 4.2 %all-to-all-start.1 = ((bf16[8,512,128]{2,1,0:T(8,128)(2,1)}), bf16[8,512,128]{2,1,0:T(8,128)(2,1)}, u32[]{:S(2)}, u32[]{:S(2)}) async-start(bf16[8,512,128]{2,1,0:T(8,128)(2,1)} %pick_blocks.5), calls=%async_computation.1 | async-start | bytes 2097152 | tf_op jit(solution)/shard_map/all_to_all | solution.py:71
  81.4 1.9 collective-permute-start.6
  83.4 1.9 collective-permute-start.14
  85.3 6.3 %collective-permute-start.15 = (bf16[128,512]{1,0:T(8,128)(2,1)}, bf16[128,512]{1,0:T(8,128)(2,1)S(1)}, u32[]{:S(2)}, u32[]{:S(2)}) collective-permute-start(bf16[128,512]{1,0:T(8,128)(2,1)} %get-tuple-element.51), channel_id=1, source_target_pairs={{1,0},{2,1},{3,2},{4,3},{5,4},{6,5},{7,6},{8,7},{9,8},{10,9},{11,1... | collective-permute-start | bytes 393224 | tf_op jit(solution)/shard_map/ppermute | solution.py:356
  91.6 13.3 %collective-permute-done.14.refs_5_ = bf16[128,512]{1,0:T(8,128)(2,1)S(1)} collective-permute-done((bf16[128,512]{1,0:T(8,128)(2,1)}, bf16[128,512]{1,0:T(8,128)(2,1)S(1)}, u32[]{:S(2)}, u32[]{:S(2)}) %collective-permute-start.14) | collective-permute-done | bytes 131104 | tf_op jit(solution)/shard_map/ppermute | solution.py:356
  106.4 1.9 pick_blocks.6
  108.4 1.4 copy-done.2
  109.8 4.4 %all-to-all-start.2 = ((bf16[8,1024,128]{2,1,0:T(8,128)(2,1)}), bf16[8,1024,128]{2,1,0:T(8,128)(2,1)}, u32[]{:S(2)}, u32[]{:S(2)}) async-start(bf16[8,1024,128]{2,1,0:T(8,128)(2,1)} %copy-done.2), calls=%async_computation.2 | async-start | bytes 4194304 | tf_op jit(solution)/shard_map/all_to_all | solution.py:71
  114.2 1.6 collective-permute-start.16
  116.0 1.7 collective-permute-start.8
  118.0 1.7 collective-permute-start.7
  119.8 1.4 slice_reduce_fusion.refs_0_
  121.2 4.0 %global_parts.4.refs_5_ = f32[512,256]{1,0:T(8,128)S(1)} custom-call(bf16[128,512]{1,0:T(8,128)(2,1)S(1)} %slice_reduce_fusion.refs_0_, bf16[768,512]{1,0:T(8,128)(2,1)S(1)} %collective-permute-done.refs_1_, bf16[768,512]{1,0:T(8,128)(2,1)} %collective-permute-done.3.refs_2_, bf16[768,512]{1,0:T(8,128)(2,1)S(1)} %copy-done.1, ...), custom_call_target="tpu_custom_call" | custom-call | flops 603979776 | bytes 25165824 | tf_op jit(solution)/shard_map/global_parts/pallas_call | solution.py:119
  125.9 10.5 %collective-permute-done.10.refs_3_ = bf16[768,512]{1,0:T(8,128)(2,1)} collective-permute-done((bf16[768,512]{1,0:T(8,128)(2,1)}, bf16[768,512]{1,0:T(8,128)(2,1)}, u32[]{:S(2)}, u32[]{:S(2)}) %collective-permute-start.10) | collective-permute-done | bytes 786464 | tf_op jit(solution)/shard_map/ppermute | solution.py:23
  136.7 15.7 %collective-permute-done.5.refs_1_ = bf16[768,512]{1,0:T(8,128)(2,1)} collective-permute-done((bf16[768,512]{1,0:T(8,128)(2,1)}, bf16[768,512]{1,0:T(8,128)(2,1)}, u32[]{:S(2)}, u32[]{:S(2)}) %collective-permute-start.5) | collective-permute-done | bytes 786464 | tf_op jit(solution)/shard_map/ppermute | solution.py:23
  153.4 3.3 %pick_blocks.7 = bf16[8,1024,128]{2,1,0:T(8,128)(2,1)} custom-call(s32[256]{0:T(256)S(1)} %reshape.153.refs_0_, bf16[768,512]{1,0:T(8,128)(2,1)S(1)} %copy-done.4, bf16[768,512]{1,0:T(8,128)(2,1)S(1)} %collective-permute-done.8.refs_2_, bf16[768,512]{1,0:T(8,128)(2,1)} %collective-permute-done.10.refs_3_, bf16[768,512]{1,0:T(8,128)(2,1)} %collective-permute-done.6.refs_4_), custom_call_target="tpu_custom_call" | custom-call | bytes 25165824 | tf_op jit(solution)/shard_map/pick_blocks/pallas_call | solution.py:59
  157.6 4.6 %all-to-all-start.3 = ((bf16[8,1024,128]{2,1,0:T(8,128)(2,1)}), bf16[8,1024,128]{2,1,0:T(8,128)(2,1)}, u32[]{:S(2)}, u32[]{:S(2)}) async-start(bf16[8,1024,128]{2,1,0:T(8,128)(2,1)} %pick_blocks.7), calls=%async_computation.3 | async-start | bytes 4194304 | tf_op jit(solution)/shard_map/all_to_all | solution.py:71
  162.2 1.8 collective-permute-start.17
  167.1 3.7 %global_parts.5.refs_5_ = f32[512,256]{1,0:T(8,128)S(1)} custom-call(bf16[128,512]{1,0:T(8,128)(2,1)S(1)} %slice_reduce_fusion.refs_0_, bf16[768,512]{1,0:T(8,128)(2,1)S(1)} %copy-done.5, bf16[768,512]{1,0:T(8,128)(2,1)S(1)} %copy-done.7, bf16[768,512]{1,0:T(8,128)(2,1)} %collective-permute-done.10.refs_3_, bf16[768,512]{1,0:T(8,128)(2,1)} %collective-permute-done.6.refs_4_, ...), custom_call_target="tpu_custom_call" | custom-call | flops 402653184 | bytes 25165824 | tf_op jit(solution)/shard_map/global_parts/pallas_call | solution.py:119
  171.6 12.2 %collective-permute-done.11.refs_3_ = bf16[768,512]{1,0:T(8,128)(2,1)S(1)} collective-permute-done((bf16[768,512]{1,0:T(8,128)(2,1)}, bf16[768,512]{1,0:T(8,128)(2,1)S(1)}, u32[]{:S(2)}, u32[]{:S(2)}) %collective-permute-start.11) | collective-permute-done | bytes 786464 | tf_op jit(solution)/shard_map/ppermute | solution.py:23
  183.9 1.6 collective-permute-done.9.refs_2_
  185.4 2.7 collective-permute-done.17
  188.1 3.3 %pick_blocks.8 = bf16[8,1024,128]{2,1,0:T(8,128)(2,1)} custom-call(s32[256]{0:T(256)S(1)} %reshape.153.refs_0_, bf16[768,512]{1,0:T(8,128)(2,1)} %collective-permute-done.5.refs_1_, bf16[768,512]{1,0:T(8,128)(2,1)S(1)} %collective-permute-done.9.refs_2_, bf16[768,512]{1,0:T(8,128)(2,1)S(1)} %collective-permute-done.11.refs_3_, ...), custom_call_target="tpu_custom_call" | custom-call | bytes 25165824 | tf_op jit(solution)/shard_map/pick_blocks/pallas_call | solution.py:59
  193.2 4.6 %all-to-all-start.4 = ((bf16[8,1024,128]{2,1,0:T(8,128)(2,1)}), bf16[8,1024,128]{2,1,0:T(8,128)(2,1)}, u32[]{:S(2)}, u32[]{:S(2)}) async-start(bf16[8,1024,128]{2,1,0:T(8,128)(2,1)} %pick_blocks.8), calls=%async_computation.4 | async-start | bytes 4194304 | tf_op jit(solution)/shard_map/all_to_all | solution.py:71
  198.7 1.2 collective-permute-start.13
  202.1 3.7 %global_parts.6.refs_3_ = f32[512,256]{1,0:T(8,128)S(1)} custom-call(bf16[128,512]{1,0:T(8,128)(2,1)S(1)} %slice_reduce_fusion.refs_0_, bf16[768,512]{1,0:T(8,128)(2,1)} %collective-permute-done.5.refs_1_, bf16[768,512]{1,0:T(8,128)(2,1)S(1)} %copy-done.11, bf16[768,512]{1,0:T(8,128)(2,1)S(1)} %copy-done.9, bf16[768,512]{1,0:T(8,128)(2,1)} %collective-permute-done.7.refs_4_, ...), custom_call_target="tpu_custom_call" | custom-call | flops 402653184 | bytes 25165824 | tf_op jit(solution)/shard_map/global_parts/pallas_call | solution.py:119
  206.6 11.4 %collective-permute-done.12.refs_1_ = bf16[768,512]{1,0:T(8,128)(2,1)S(1)} collective-permute-done((bf16[768,512]{1,0:T(8,128)(2,1)}, bf16[768,512]{1,0:T(8,128)(2,1)S(1)}, u32[]{:S(2)}, u32[]{:S(2)}) %collective-permute-start.12) | collective-permute-done | bytes 786464 | tf_op jit(solution)/shard_map/ppermute | solution.py:23
  218.0 1.8 collective-permute-done.13.refs_2_
  219.8 5.3 %all-to-all-done.4.refs_11_ = bf16[8,1024,128]{2,1,0:T(8,128)(2,1)} async-done(((bf16[8,1024,128]{2,1,0:T(8,128)(2,1)}), bf16[8,1024,128]{2,1,0:T(8,128)(2,1)}, u32[]{:S(2)}, u32[]{:S(2)}) %all-to-all-start.4) | async-done | bytes 2097184 | tf_op jit(solution)/shard_map/all_to_all | solution.py:71
  226.2 1.9 global_parts.7.refs_3_
  228.0 1.9 pick_blocks.9
  229.9 3.6 %all-to-all-start.7 = ((bf16[8,640,128]{2,1,0:T(8,128)(2,1)}), bf16[8,640,128]{2,1,0:T(8,128)(2,1)S(1)}, u32[]{:S(2)}, u32[]{:S(2)}) async-start(bf16[8,640,128]{2,1,0:T(8,128)(2,1)} %pick_blocks.9), calls=%async_computation.7 | async-start | bytes 2621440 | tf_op jit(solution)/shard_map/all_to_all | solution.py:71
  233.5 18.7 %all-to-all-done.7.parts.refs_12_ = bf16[8,640,128]{2,1,0:T(8,128)(2,1)S(1)} async-done(((bf16[8,640,128]{2,1,0:T(8,128)(2,1)}), bf16[8,640,128]{2,1,0:T(8,128)(2,1)S(1)}, u32[]{:S(2)}, u32[]{:S(2)}) %all-to-all-start.7) | async-done | bytes 1310752 | tf_op jit(solution)/shard_map/all_to_all | solution.py:71
  253.3 2.1 merge_parts.1
  255.3 3.4 %all-to-all-start.8 = ((bf16[8,64,128]{2,1,0:T(8,128)(2,1)}), bf16[8,64,128]{2,1,0:T(8,128)(2,1)S(1)}, u32[]{:S(2)}, u32[]{:S(2)}) async-start(bf16[8,64,128]{2,1,0:T(8,128)(2,1)} %merge_parts.1), calls=%async_computation.8 | async-start | bytes 262144 | tf_op jit(solution)/shard_map/all_to_all | solution.py:71
  259.4 2.7 collective-permute-start.21
  262.1 20.0 %attend.1.attention = bf16[768,512]{1,0:T(8,128)(2,1)} custom-call(s32[144]{0:T(256)} %copy-done.28, s32[4]{0:T(128)} %pad_add_fusion.refs_1_.place, bf16[768,512]{1,0:T(8,128)(2,1)} %refs_2_.3, bf16[768,512]{1,0:T(8,128)(2,1)} %refs_3_.3, bf16[768,512]{1,0:T(8,128)(2,1)} %refs_4_.1, bf16[128,512]{1,0:T(8,128)(2,1)} %copy-done.26, ...), custom_call_target="tpu_custom_call" | custom-call | flops 805306368 | bytes 12582912 | tf_op jit(solution)/shard_map/attend/pallas_call | solution.py:268
  282.8 2.2 global_rows.1
  286.0 2.2 collective-permute-start.19
  288.2 3.2 %collective-permute-start.23 = (bf16[384,512]{1,0:T(8,128)(2,1)}, bf16[384,512]{1,0:T(8,128)(2,1)S(1)}, u32[]{:S(2)}, u32[]{:S(2)}) collective-permute-start(bf16[384,512]{1,0:T(8,128)(2,1)} %get-tuple-element.86), channel_id=1, source_target_pairs={{0,192},{64,0},{128,64},{192,128},{1,193},{65,1},{129,65},{193,129... | collective-permute-start | bytes 1179656 | tf_op jit(solution)/shard_map/ppermute | solution.py:28
  291.4 1.6 fusion.15
  293.6 4.7 %collective-permute-done.18 = bf16[384,512]{1,0:T(8,128)(2,1)S(1)} collective-permute-done((bf16[384,512]{1,0:T(8,128)(2,1)}, bf16[384,512]{1,0:T(8,128)(2,1)S(1)}, u32[]{:S(2)}, u32[]{:S(2)}) %collective-permute-start.18) | collective-permute-done | bytes 393248 | tf_op jit(solution)/shard_map/ppermute | solution.py:28
  298.9 6.6 %collective-permute-done.23 = bf16[384,512]{1,0:T(8,128)(2,1)S(1)} collective-permute-done((bf16[384,512]{1,0:T(8,128)(2,1)}, bf16[384,512]{1,0:T(8,128)(2,1)S(1)}, u32[]{:S(2)}, u32[]{:S(2)}) %collective-permute-start.23) | collective-permute-done | bytes 393248 | tf_op jit(solution)/shard_map/ppermute | solution.py:28
  305.5 3.4 %collective-permute-start.24 = (bf16[384,512]{1,0:T(8,128)(2,1)S(1)}, bf16[384,512]{1,0:T(8,128)(2,1)S(1)}, u32[]{:S(2)}, u32[]{:S(2)}) collective-permute-start(bf16[384,512]{1,0:T(8,128)(2,1)S(1)} %collective-permute-done.23), channel_id=1, source_target_pairs={{0,192},{64,0},{128,64},{192,128},{1,193},{65,1},{129,65},{193,129... | collective-permute-start | bytes 1179656 | tf_op jit(solution)/shard_map/ppermute | solution.py:28
  308.9 1.8 fusion.20
  310.7 1.8 fusion.17
  313.2 1.2 collective-permute-done.20
  314.4 1.8 add_convert_fusion.1
  316.4 1.9 add_convert_fusion
  318.4 1.3 pad_maximum_fusion
  (116 shorter events, 30.9 us)
Async XLA Ops:
  0.0 12.4 %copy-start.1 = (bf16[768,512]{1,0:T(8,128)(2,1)S(1)}, bf16[768,512]{1,0:T(8,128)(2,1)}, u32[]{:S(2)}) copy-start(bf16[768,512]{1,0:T(8,128)(2,1)} %refs_3_.3) | copy-start | bytes 2359300
  0.0 19.5 %collective-permute-start = (bf16[768,512]{1,0:T(8,128)(2,1)}, bf16[768,512]{1,0:T(8,128)(2,1)S(1)}, u32[]{:S(2)}, u32[]{:S(2)}) collective-permute-start(bf16[768,512]{1,0:T(8,128)(2,1)} %refs_3_.3), channel_id=1, source_target_pairs={{0,8},{8,16},{16,24},{24,32},{32,40},{40,48},{48,56},{56,0},{1,9},... | collective-permute-start | bytes 2359304 | tf_op jit(solution)/shard_map/ppermute | solution.py:23
  1.9 19.4 %collective-permute-start.1 = (bf16[768,512]{1,0:T(8,128)(2,1)}, bf16[768,512]{1,0:T(8,128)(2,1)S(1)}, u32[]{:S(2)}, u32[]{:S(2)}) collective-permute-start(bf16[768,512]{1,0:T(8,128)(2,1)} %refs_4_.1), channel_id=1, source_target_pairs={{0,56},{8,0},{16,8},{24,16},{32,24},{40,32},{48,40},{56,48},{1,57}... | collective-permute-start | bytes 2359304 | tf_op jit(solution)/shard_map/ppermute | solution.py:23
  12.2 3.6 %copy-start.28 = (s32[144]{0:T(256)}, s32[144]{0:T(256)S(1)}, u32[]{:S(2)}) copy-start(s32[144]{0:T(256)S(1)} %multiply_add_fusion.refs_0_) | copy-start | bytes 1732
  13.7 2.8 copy-start.22
  18.7 7.1 %copy-start = (bf16[768,512]{1,0:T(8,128)(2,1)S(1)}, bf16[768,512]{1,0:T(8,128)(2,1)}, u32[]{:S(2)}) copy-start(bf16[768,512]{1,0:T(8,128)(2,1)} %refs_4_.1) | copy-start | bytes 2359300
  21.3 24.8 %all-to-all-start = ((bf16[8,176,512]{2,1,0:T(8,128)(2,1)}), bf16[8,176,512]{2,1,0:T(8,128)(2,1)}, u32[]{:S(2)}, u32[]{:S(2)}) async-start(bf16[8,176,512]{2,1,0:T(8,128)(2,1)} %fusion.1), calls=%async_computation | async-start | bytes 2883584 | tf_op jit(solution)/shard_map/all_to_all | solution.py:71
  25.8 44.6 %collective-permute-start.2 = (bf16[768,512]{1,0:T(8,128)(2,1)S(1)}, bf16[768,512]{1,0:T(8,128)(2,1)}, u32[]{:S(2)}, u32[]{:S(2)}) collective-permute-start(bf16[768,512]{1,0:T(8,128)(2,1)S(1)} %copy-done), channel_id=1, source_target_pairs={{0,8},{8,16},{16,24},{24,32},{32,40},{40,48},{48,56},{56,0},{1,9},... | collective-permute-start | bytes 2359304 | tf_op jit(solution)/shard_map/ppermute | solution.py:23
  29.0 41.4 %collective-permute-start.3 = (bf16[768,512]{1,0:T(8,128)(2,1)S(1)}, bf16[768,512]{1,0:T(8,128)(2,1)}, u32[]{:S(2)}, u32[]{:S(2)}) collective-permute-start(bf16[768,512]{1,0:T(8,128)(2,1)S(1)} %copy-done.1), channel_id=1, source_target_pairs={{0,56},{8,0},{16,8},{24,16},{32,24},{40,32},{48,40},{56,48},{1,57}... | collective-permute-start | bytes 2359304 | tf_op jit(solution)/shard_map/ppermute | solution.py:23
  66.1 10.9 %all-to-all-start.6 = ((bf16[8,32,512]{2,1,0:T(8,128)(2,1)}), bf16[8,32,512]{2,1,0:T(8,128)(2,1)S(1)}, u32[]{:S(2)}, u32[]{:S(2)}) async-start(bf16[8,32,512]{2,1,0:T(8,128)(2,1)} %broadcast_in_dim.23), calls=%async_computation.6 | async-start | bytes 524288 | tf_op jit(solution)/shard_map/all_to_all | solution.py:71
  77.0 31.4 %copy-start.23 = (bf16[8,32,512]{2,1,0:T(8,128)(2,1)}, bf16[8,32,512]{2,1,0:T(8,128)(2,1)S(1)}, u32[]{:S(2)}) copy-start(bf16[8,32,512]{2,1,0:T(8,128)(2,1)S(1)} %all-to-all-done.6) | copy-start | bytes 786436
  77.0 32.8 %all-to-all-start.1 = ((bf16[8,512,128]{2,1,0:T(8,128)(2,1)}), bf16[8,512,128]{2,1,0:T(8,128)(2,1)}, u32[]{:S(2)}, u32[]{:S(2)}) async-start(bf16[8,512,128]{2,1,0:T(8,128)(2,1)} %pick_blocks.5), calls=%async_computation.1 | async-start | bytes 2097152 | tf_op jit(solution)/shard_map/all_to_all | solution.py:71
  81.3 23.6 %collective-permute-start.4 = (bf16[768,512]{1,0:T(8,128)(2,1)S(1)}, bf16[768,512]{1,0:T(8,128)(2,1)S(1)}, u32[]{:S(2)}, u32[]{:S(2)}) collective-permute-start(bf16[768,512]{1,0:T(8,128)(2,1)S(1)} %collective-permute-done.refs_1_), channel_id=1, source_target_pairs={{0,8},{8,16},{16,24},{24,32},{32,40},{40,48},{48,56},{56,0},{1,9},... | collective-permute-start | bytes 2359304 | tf_op jit(solution)/shard_map/ppermute | solution.py:23
  81.4 25.0 %collective-permute-start.6 = (bf16[768,512]{1,0:T(8,128)(2,1)S(1)}, bf16[768,512]{1,0:T(8,128)(2,1)}, u32[]{:S(2)}, u32[]{:S(2)}) collective-permute-start(bf16[768,512]{1,0:T(8,128)(2,1)S(1)} %collective-permute-done.1.refs_4_.refs_5_), channel_id=1, source_target_pairs={{0,56},{8,0},{16,8},{24,16},{32,24},{40,32},{48,40},{56,48},{1,57}... | collective-permute-start | bytes 2359304 | tf_op jit(solution)/shard_map/ppermute | solution.py:23
  83.4 21.5 %collective-permute-start.14 = (bf16[128,512]{1,0:T(8,128)(2,1)}, bf16[128,512]{1,0:T(8,128)(2,1)S(1)}, u32[]{:S(2)}, u32[]{:S(2)}) collective-permute-start(bf16[128,512]{1,0:T(8,128)(2,1)} %get-tuple-element.50), channel_id=1, source_target_pairs={{0,1},{1,2},{2,3},{3,4},{4,5},{5,6},{6,7},{7,8},{8,9},{9,10},{10,1... | collective-permute-start | bytes 393224 | tf_op jit(solution)/shard_map/ppermute | solution.py:356
  85.3 19.6 %collective-permute-start.15 = (bf16[128,512]{1,0:T(8,128)(2,1)}, bf16[128,512]{1,0:T(8,128)(2,1)S(1)}, u32[]{:S(2)}, u32[]{:S(2)}) collective-permute-start(bf16[128,512]{1,0:T(8,128)(2,1)} %get-tuple-element.51), channel_id=1, source_target_pairs={{1,0},{2,1},{3,2},{4,3},{5,4},{6,5},{7,6},{8,7},{9,8},{10,9},{11,1... | collective-permute-start | bytes 393224 | tf_op jit(solution)/shard_map/ppermute | solution.py:356
  104.8 5.0 %copy-start.26 = (bf16[128,512]{1,0:T(8,128)(2,1)}, bf16[128,512]{1,0:T(8,128)(2,1)S(1)}, u32[]{:S(2)}) copy-start(bf16[128,512]{1,0:T(8,128)(2,1)S(1)} %collective-permute-done.14.refs_5_) | copy-start | bytes 393220
  104.8 0.7 copy-start.27
  105.5 0.9 copy-start.3
  108.4 1.4 copy-start.2
  109.8 47.8 %all-to-all-start.2 = ((bf16[8,1024,128]{2,1,0:T(8,128)(2,1)}), bf16[8,1024,128]{2,1,0:T(8,128)(2,1)}, u32[]{:S(2)}, u32[]{:S(2)}) async-start(bf16[8,1024,128]{2,1,0:T(8,128)(2,1)} %copy-done.2), calls=%async_computation.2 | async-start | bytes 4194304 | tf_op jit(solution)/shard_map/all_to_all | solution.py:71
  114.2 38.2 %collective-permute-start.16 = (bf16[512,1024]{1,0:T(8,128)(2,1)}, bf16[512,1024]{1,0:T(8,128)(2,1)S(1)}, u32[]{:S(2)}, u32[]{:S(2)}) collective-permute-start(bf16[512,1024]{1,0:T(8,128)(2,1)} %get-tuple-element.57), channel_id=1, source_target_pairs={{0,64},{64,128},{128,192},{192,0},{1,65},{65,129},{129,193},{193,1... | collective-permute-start | bytes 3145736 | tf_op jit(solution)/shard_map/ppermute | solution.py:28
  115.7 20.7 %collective-permute-start.10 = (bf16[768,512]{1,0:T(8,128)(2,1)}, bf16[768,512]{1,0:T(8,128)(2,1)}, u32[]{:S(2)}, u32[]{:S(2)}) collective-permute-start(bf16[768,512]{1,0:T(8,128)(2,1)} %collective-permute-done.2.refs_3_.refs_4_), channel_id=1, source_target_pairs={{0,8},{8,16},{16,24},{24,32},{32,40},{40,48},{48,56},{56,0},{1,9},... | collective-permute-start | bytes 2359304 | tf_op jit(solution)/shard_map/ppermute | solution.py:23
  116.0 20.7 %collective-permute-start.8 = (bf16[768,512]{1,0:T(8,128)(2,1)}, bf16[768,512]{1,0:T(8,128)(2,1)S(1)}, u32[]{:S(2)}, u32[]{:S(2)}) collective-permute-start(bf16[768,512]{1,0:T(8,128)(2,1)} %collective-permute-done.3.refs_2_), channel_id=1, source_target_pairs={{0,56},{8,0},{16,8},{24,16},{32,24},{40,32},{48,40},{56,48},{1,57}... | collective-permute-start | bytes 2359304 | tf_op jit(solution)/shard_map/ppermute | solution.py:23
  117.8 34.6 %collective-permute-start.5 = (bf16[768,512]{1,0:T(8,128)(2,1)}, bf16[768,512]{1,0:T(8,128)(2,1)}, u32[]{:S(2)}, u32[]{:S(2)}) collective-permute-start(bf16[768,512]{1,0:T(8,128)(2,1)} %copy-done.3), channel_id=1, source_target_pairs={{0,8},{8,16},{16,24},{24,32},{32,40},{40,48},{48,56},{56,0},{1,9},... | collective-permute-start | bytes 2359304 | tf_op jit(solution)/shard_map/ppermute | solution.py:23
  118.0 34.3 %collective-permute-start.7 = (bf16[768,512]{1,0:T(8,128)(2,1)}, bf16[768,512]{1,0:T(8,128)(2,1)}, u32[]{:S(2)}, u32[]{:S(2)}) collective-permute-start(bf16[768,512]{1,0:T(8,128)(2,1)} %collective-permute-done.6.refs_4_), channel_id=1, source_target_pairs={{0,56},{8,0},{16,8},{24,16},{32,24},{40,32},{48,40},{56,48},{1,57}... | collective-permute-start | bytes 2359304 | tf_op jit(solution)/shard_map/ppermute | solution.py:23
  121.2 32.3 %copy-start.4 = (bf16[768,512]{1,0:T(8,128)(2,1)S(1)}, bf16[768,512]{1,0:T(8,128)(2,1)}, u32[]{:S(2)}) copy-start(bf16[768,512]{1,0:T(8,128)(2,1)} %copy-done.3) | copy-start | bytes 2359300
  125.1 0.8 copy-start.16
  152.4 1.1 copy-start.20
  156.7 0.9 copy-start.6
  157.6 8.4 %copy-start.5 = (bf16[768,512]{1,0:T(8,128)(2,1)S(1)}, bf16[768,512]{1,0:T(8,128)(2,1)}, u32[]{:S(2)}) copy-start(bf16[768,512]{1,0:T(8,128)(2,1)} %copy-done.3) | copy-start | bytes 2359300
  157.6 7.2 %copy-start.7 = (bf16[768,512]{1,0:T(8,128)(2,1)S(1)}, bf16[768,512]{1,0:T(8,128)(2,1)}, u32[]{:S(2)}) copy-start(bf16[768,512]{1,0:T(8,128)(2,1)} %copy-done.6) | copy-start | bytes 2359300
  157.6 35.6 %all-to-all-start.3 = ((bf16[8,1024,128]{2,1,0:T(8,128)(2,1)}), bf16[8,1024,128]{2,1,0:T(8,128)(2,1)}, u32[]{:S(2)}, u32[]{:S(2)}) async-start(bf16[8,1024,128]{2,1,0:T(8,128)(2,1)} %pick_blocks.7), calls=%async_computation.3 | async-start | bytes 4194304 | tf_op jit(solution)/shard_map/all_to_all | solution.py:71
  162.2 25.9 %collective-permute-start.17 = (bf16[512,1024]{1,0:T(8,128)(2,1)}, bf16[512,1024]{1,0:T(8,128)(2,1)}, u32[]{:S(2)}, u32[]{:S(2)}) collective-permute-start(bf16[512,1024]{1,0:T(8,128)(2,1)} %get-tuple-element.63), channel_id=1, source_target_pairs={{0,192},{64,0},{128,64},{192,128},{1,193},{65,1},{129,65},{193,129... | collective-permute-start | bytes 3145736 | tf_op jit(solution)/shard_map/ppermute | solution.py:28
  164.0 19.9 %collective-permute-start.11 = (bf16[768,512]{1,0:T(8,128)(2,1)}, bf16[768,512]{1,0:T(8,128)(2,1)S(1)}, u32[]{:S(2)}, u32[]{:S(2)}) collective-permute-start(bf16[768,512]{1,0:T(8,128)(2,1)} %collective-permute-done.10.refs_3_), channel_id=1, source_target_pairs={{0,8},{8,16},{16,24},{24,32},{32,40},{40,48},{48,56},{56,0},{1,9},... | collective-permute-start | bytes 2359304 | tf_op jit(solution)/shard_map/ppermute | solution.py:23
  164.9 20.6 %collective-permute-start.9 = (bf16[768,512]{1,0:T(8,128)(2,1)S(1)}, bf16[768,512]{1,0:T(8,128)(2,1)S(1)}, u32[]{:S(2)}, u32[]{:S(2)}) collective-permute-start(bf16[768,512]{1,0:T(8,128)(2,1)S(1)} %copy-done.7), channel_id=1, source_target_pairs={{0,56},{8,0},{16,8},{24,16},{32,24},{40,32},{48,40},{56,48},{1,57}... | collective-permute-start | bytes 2359304 | tf_op jit(solution)/shard_map/ppermute | solution.py:23
  166.0 1.0 copy-start.17
  170.8 0.8 copy-start.12
  191.4 0.9 copy-start.8
  192.3 0.9 copy-start.10
  193.2 6.7 %copy-start.11 = (bf16[768,512]{1,0:T(8,128)(2,1)S(1)}, bf16[768,512]{1,0:T(8,128)(2,1)}, u32[]{:S(2)}) copy-start(bf16[768,512]{1,0:T(8,128)(2,1)} %copy-done.10) | copy-start | bytes 2359300
  193.2 31.9 %all-to-all-start.4 = ((bf16[8,1024,128]{2,1,0:T(8,128)(2,1)}), bf16[8,1024,128]{2,1,0:T(8,128)(2,1)}, u32[]{:S(2)}, u32[]{:S(2)}) async-start(bf16[8,1024,128]{2,1,0:T(8,128)(2,1)} %pick_blocks.8), calls=%async_computation.4 | async-start | bytes 4194304 | tf_op jit(solution)/shard_map/all_to_all | solution.py:71
  197.8 20.2 %collective-permute-start.12 = (bf16[768,512]{1,0:T(8,128)(2,1)}, bf16[768,512]{1,0:T(8,128)(2,1)S(1)}, u32[]{:S(2)}, u32[]{:S(2)}) collective-permute-start(bf16[768,512]{1,0:T(8,128)(2,1)} %collective-permute-done.5.refs_1_), channel_id=1, source_target_pairs={{0,8},{8,16},{16,24},{24,32},{32,40},{40,48},{48,56},{56,0},{1,9},... | collective-permute-start | bytes 2359304 | tf_op jit(solution)/shard_map/ppermute | solution.py:23
  198.7 21.1 %collective-permute-start.13 = (bf16[768,512]{1,0:T(8,128)(2,1)}, bf16[768,512]{1,0:T(8,128)(2,1)S(1)}, u32[]{:S(2)}, u32[]{:S(2)}) collective-permute-start(bf16[768,512]{1,0:T(8,128)(2,1)} %collective-permute-done.7.refs_4_), channel_id=1, source_target_pairs={{0,56},{8,0},{16,8},{24,16},{32,24},{40,32},{48,40},{56,48},{1,57}... | collective-permute-start | bytes 2359304 | tf_op jit(solution)/shard_map/ppermute | solution.py:23
  199.9 1.1 copy-start.9
  201.0 1.0 copy-start.13
  205.8 0.8 copy-start.14
  225.1 1.0 copy-start.15
  229.9 22.3 %all-to-all-start.7 = ((bf16[8,640,128]{2,1,0:T(8,128)(2,1)}), bf16[8,640,128]{2,1,0:T(8,128)(2,1)S(1)}, u32[]{:S(2)}, u32[]{:S(2)}) async-start(bf16[8,640,128]{2,1,0:T(8,128)(2,1)} %pick_blocks.9), calls=%async_computation.7 | async-start | bytes 2621440 | tf_op jit(solution)/shard_map/all_to_all | solution.py:71
  252.2 1.1 copy-start.18
  255.3 26.7 %all-to-all-start.8 = ((bf16[8,64,128]{2,1,0:T(8,128)(2,1)}), bf16[8,64,128]{2,1,0:T(8,128)(2,1)S(1)}, u32[]{:S(2)}, u32[]{:S(2)}) async-start(bf16[8,64,128]{2,1,0:T(8,128)(2,1)} %merge_parts.1), calls=%async_computation.8 | async-start | bytes 262144 | tf_op jit(solution)/shard_map/all_to_all | solution.py:71
  259.4 53.8 %collective-permute-start.21 = (bf16[512,1024]{1,0:T(8,128)(2,1)}, bf16[512,1024]{1,0:T(8,128)(2,1)}, u32[]{:S(2)}, u32[]{:S(2)}) collective-permute-start(bf16[512,1024]{1,0:T(8,128)(2,1)} %get-tuple-element.85), channel_id=1, source_target_pairs={{0,128},{64,192},{128,0},{192,64},{1,129},{65,193},{129,1},{193,65... | collective-permute-start | bytes 3145736 | tf_op jit(solution)/shard_map/ppermute | solution.py:28
  262.1 29.3 %copy-start.19 = (bf16[512,1024]{1,0:T(8,128)(2,1)S(1)}, bf16[512,1024]{1,0:T(8,128)(2,1)}, u32[]{:S(2)}) copy-start(bf16[512,1024]{1,0:T(8,128)(2,1)} %get-tuple-element.81) | copy-start | bytes 3145732
  282.1 0.7 copy-start.24
  284.9 8.1 %copy-start.25 = (bf16[384,512]{1,0:T(8,128)(2,1)S(1)}, bf16[384,512]{1,0:T(8,128)(2,1)}, u32[]{:S(2)}) copy-start(bf16[384,512]{1,0:T(8,128)(2,1)} %get-tuple-element.86) | copy-start | bytes 1179652
  284.9 13.4 %collective-permute-start.18 = (bf16[384,512]{1,0:T(8,128)(2,1)}, bf16[384,512]{1,0:T(8,128)(2,1)S(1)}, u32[]{:S(2)}, u32[]{:S(2)}) collective-permute-start(bf16[384,512]{1,0:T(8,128)(2,1)} %get-tuple-element.80), channel_id=1, source_target_pairs={{0,64},{64,128},{128,192},{192,0},{1,65},{65,129},{129,193},{193,1... | collective-permute-start | bytes 1179656 | tf_op jit(solution)/shard_map/ppermute | solution.py:28
  286.0 24.7 %collective-permute-start.19 = (bf16[384,512]{1,0:T(8,128)(2,1)}, bf16[384,512]{1,0:T(8,128)(2,1)S(1)}, u32[]{:S(2)}, u32[]{:S(2)}) collective-permute-start(bf16[384,512]{1,0:T(8,128)(2,1)} %get-tuple-element.80), channel_id=1, source_target_pairs={{0,192},{64,0},{128,64},{192,128},{1,193},{65,1},{129,65},{193,129... | collective-permute-start | bytes 1179656 | tf_op jit(solution)/shard_map/ppermute | solution.py:28
  288.2 24.4 %collective-permute-start.22 = (bf16[384,512]{1,0:T(8,128)(2,1)}, bf16[384,512]{1,0:T(8,128)(2,1)S(1)}, u32[]{:S(2)}, u32[]{:S(2)}) collective-permute-start(bf16[384,512]{1,0:T(8,128)(2,1)} %get-tuple-element.86), channel_id=1, source_target_pairs={{0,64},{64,128},{128,192},{192,0},{1,65},{65,129},{129,193},{193,1... | collective-permute-start | bytes 1179656 | tf_op jit(solution)/shard_map/ppermute | solution.py:28
  288.2 17.4 %collective-permute-start.23 = (bf16[384,512]{1,0:T(8,128)(2,1)}, bf16[384,512]{1,0:T(8,128)(2,1)S(1)}, u32[]{:S(2)}, u32[]{:S(2)}) collective-permute-start(bf16[384,512]{1,0:T(8,128)(2,1)} %get-tuple-element.86), channel_id=1, source_target_pairs={{0,192},{64,0},{128,64},{192,128},{1,193},{65,1},{129,65},{193,129... | collective-permute-start | bytes 1179656 | tf_op jit(solution)/shard_map/ppermute | solution.py:28
  293.0 5.3 %copy-start.21 = (bf16[512,1024]{1,0:T(8,128)(2,1)S(1)}, bf16[512,1024]{1,0:T(8,128)(2,1)}, u32[]{:S(2)}) copy-start(bf16[512,1024]{1,0:T(8,128)(2,1)} %copy-done.20) | copy-start | bytes 3145732
  298.3 16.1 %collective-permute-start.20 = (bf16[384,512]{1,0:T(8,128)(2,1)S(1)}, bf16[384,512]{1,0:T(8,128)(2,1)S(1)}, u32[]{:S(2)}, u32[]{:S(2)}) collective-permute-start(bf16[384,512]{1,0:T(8,128)(2,1)S(1)} %collective-permute-done.18), channel_id=1, source_target_pairs={{0,64},{64,128},{128,192},{192,0},{1,65},{65,129},{129,193},{193,1... | collective-permute-start | bytes 1179656 | tf_op jit(solution)/shard_map/ppermute | solution.py:28
  305.5 10.9 %collective-permute-start.24 = (bf16[384,512]{1,0:T(8,128)(2,1)S(1)}, bf16[384,512]{1,0:T(8,128)(2,1)S(1)}, u32[]{:S(2)}, u32[]{:S(2)}) collective-permute-start(bf16[384,512]{1,0:T(8,128)(2,1)S(1)} %collective-permute-done.23), channel_id=1, source_target_pairs={{0,192},{64,0},{128,64},{192,128},{1,193},{65,1},{129,65},{193,129... | collective-permute-start | bytes 1179656 | tf_op jit(solution)/shard_map/ppermute | solution.py:28

commit v5 on v4

--- a/solution.py
+++ b/solution.py
@@ -16,6 +16,7 @@
 SEQ = ("seq_0", "seq_1", "seq_2")
 PLANE = ("seq_1", "seq_2")
 VMEM_LIMIT = 56 * 2**20
+COST = 24 * 2**20
 
 
 def ring_step(shard, step):
@@ -129,9 +130,10 @@
     )(asking, *blocks, *held)
 
 
-def merge_kernel(parts, out):
+def merge_rows(parts, first, out):
     peers = parts.shape[0]
-    tops = [parts[p, BLOCK:, 0:1].astype(jnp.float32) for p in range(peers)]
+    sums, side = slice(first, first + BLOCK), slice(first + BLOCK, first + 2 * BLOCK)
+    tops = [parts[p, side, 0:1].astype(jnp.float32) for p in range(peers)]
     top = tops[0]
     for other in tops[1:]:
         top = jnp.maximum(top, other)
@@ -139,74 +141,73 @@
     total = jnp.zeros((BLOCK, 1), jnp.float32)
     for p, own in enumerate(tops):
         scale = jnp.exp(own - top)
-        part += scale * parts[p, :BLOCK].astype(jnp.float32)
-        upper = parts[p, BLOCK:, 2:3].astype(jnp.float32)
-        total += scale * (upper + parts[p, BLOCK:, 3:4].astype(jnp.float32))
+        part += scale * parts[p, sums].astype(jnp.float32)
+        upper = parts[p, side, 2:3].astype(jnp.float32)
+        total += scale * (upper + parts[p, side, 3:4].astype(jnp.float32))
     whole = (part / total).astype(jnp.bfloat16)
     for p in range(peers):
         out[p] = whole
 
 
-def merged(parts):
-    peers, rows, _ = parts.shape
+def joined_kernel(low, gout, out):
+    rows = low.shape[0]
+    out[:rows] = low[...]
+    for h in range(low.shape[1] // DH):
+        for g in range(GLOBAL):
+            at = rows + g * BLOCK
+            out[at : at + BLOCK, h * DH : (h + 1) * DH] = gout[h * GLOBAL + g]
+
+
+def joined(low, gout):
+    vmem = pl.BlockSpec(memory_space=pltpu.VMEM)
     return pl.pallas_call(
-        merge_kernel,
-        out_shape=jax.ShapeDtypeStruct((peers, BLOCK, DH), jnp.bfloat16),
-        grid=(1,),
-        in_specs=[pl.BlockSpec((peers, 2 * BLOCK, DH), lambda i: (0, rows // (2 * BLOCK) - 1, 0))],
-        out_specs=pl.BlockSpec((peers, BLOCK, DH), lambda i: (0, 0, 0)),
-        name="merge_parts",
-    )(parts)
-
-
-def patch_kernel(place, gout, attention, *out):
-    blocks = attention.shape[0] // BLOCK
-    heads = attention.shape[1] // DH
-    half = blocks // 2
-    for side in range(2):
-        out[side][...] = attention[side * half * BLOCK : (side + 1) * half * BLOCK]
-        for g in range(GLOBAL):
-            spot = place[2 + g] - side * half
-
-            @pl.when((place[2 + g] >= 0) & (spot >= 0) & (spot < half))
-            def _():
-                at_rows = pl.ds(pl.multiple_of(spot * BLOCK, BLOCK), BLOCK)
-                for h in range(heads):
-                    out[side][at_rows, h * DH : (h + 1) * DH] = gout[h * GLOBAL + g]
-
-
-def patched(place, gout, attention):
-    rows, features = attention.shape
+        joined_kernel,
+        out_shape=jax.ShapeDtypeStruct((low.shape[0] + GLOBAL * BLOCK, low.shape[1]), low.dtype),
+        in_specs=[vmem, vmem],
+        out_specs=vmem,
+        name="join_global_rows",
+    )(low, gout)
+
+
+def place_kernel(place, top, low, out):
+    half = top.shape[0]
+    out[:half] = top[...]
+    out[half:] = low[:half]
+    for g in range(GLOBAL):
+
+        @pl.when(place[2 + g] >= 0)
+        def _():
+            at_rows = pl.ds(pl.multiple_of(place[2 + g] * BLOCK, BLOCK), BLOCK)
+            out[at_rows] = low[half + g * BLOCK : half + (g + 1) * BLOCK]
+
+
+def placed(place, top, low):
     vmem = pl.BlockSpec(memory_space=pltpu.VMEM)
-    half = jax.ShapeDtypeStruct((rows // 2, features), attention.dtype)
     return pl.pallas_call(
-        patch_kernel,
-        out_shape=(half, half),
+        place_kernel,
+        out_shape=jax.ShapeDtypeStruct((2 * top.shape[0], top.shape[1]), top.dtype),
         in_specs=[pl.BlockSpec(memory_space=pltpu.SMEM), vmem, vmem],
-        out_specs=(vmem, vmem),
-        name="global_rows",
-    )(place, gout, attention)
-
-
-def attend_kernel(
-    counts, slots, place, q, k, v, before, after, glob, *refs
-):
+        out_specs=vmem,
+        compiler_params=pltpu.CompilerParams(vmem_limit_bytes=16 * 2**20),
+        name="place_global_rows",
+    )(place, top, low)
+
+
+def attend_kernel(counts, slots, place, q, k, v, before, after, glob, *refs):
     n = len(counts)
-    arrived, out, held, sems = refs[:n], refs[n], refs[n + 1], refs[n + 2]
-    kpad, vpad = refs[n + 3], refs[n + 4]
+    arrived, acc, stats, held, sems = refs[:n], refs[n], refs[n + 1], refs[n + 2], refs[n + 3]
+    kpad, vpad = refs[n + 4], refs[n + 5]
     copies = []
     at = 0
     for part, count in enumerate(counts):
         copies.append(
-            pltpu.make_async_copy(
-                arrived[part].at[:, pl.ds(0, count)], held.at[:, pl.ds(at, count)], sems.at[part]
-            )
+            pltpu.make_async_copy(arrived[part], held.at[:, pl.ds(at, count)], sems.at[part])
         )
         copies[-1].start()
         at += count
+    rows = q.shape[0]
     heads = q.shape[1] // DH
-    blocks = q.shape[0] // BLOCK
-    rows = q.shape[0]
+    blocks = rows // BLOCK
     for side, (pad, own) in enumerate(((kpad, k), (vpad, v))):
         pad[0:BLOCK] = before[side * BLOCK : (side + 1) * BLOCK]
         pad[BLOCK : BLOCK + rows] = own[...]
@@ -214,22 +215,24 @@
     for copy in copies:
         copy.wait()
     scale = DH ** (-0.5)
-    col = lax.broadcasted_iota(jnp.int32, (BLOCK, (3 + RANDOM + GLOBAL) * BLOCK), 1)
+    col = lax.broadcasted_iota(jnp.int32, (1, (3 + RANDOM + GLOBAL) * BLOCK), 1) // BLOCK
+    lane = lax.broadcasted_iota(jnp.int32, (BLOCK, DH), 1)
 
     def one_block(b, carry):
         at_rows = pl.ds(pl.multiple_of(b * BLOCK, BLOCK), BLOCK)
         win_rows = pl.ds(pl.multiple_of(b * BLOCK, BLOCK), 3 * BLOCK)
         number = place[0] + b
-        low = jnp.where(number == 0, BLOCK, 0)
-        high = jnp.where(number == place[1] - 1, 2 * BLOCK, 3 * BLOCK)
-        valid = (col >= low) & ((col < high) | (col >= 3 * BLOCK))
+        outside = jnp.where(number == 0, 0, -1), jnp.where(number == place[1] - 1, 2, -1)
         for h in range(heads):
             hs = slice(h * DH, (h + 1) * DH)
             picks = []
+            bias = jnp.where((col == outside[0]) | (col == outside[1]), -jnp.inf, 0.0)
             for r in range(RANDOM):
                 slot = slots[(h * blocks + b) * RANDOM + r]
-                at = pl.multiple_of((slot & 31) * 2 * BLOCK, 2 * BLOCK)
-                picks.append((slot >> 5, at))
+                late = ((slot >> 2) & 7) == PLANES - 1
+                bias = jnp.where(col == jnp.where(late, 3 + r, -1), -jnp.inf, bias)
+                slot = jnp.where(late, 0, slot)
+                picks.append((slot >> 5, pl.multiple_of((slot & 31) * 2 * BLOCK, 2 * BLOCK)))
             keys = jnp.concatenate(
                 [kpad[win_rows, hs]]
                 + [held[p[0], pl.ds(p[1], BLOCK)] for p in picks]
@@ -245,15 +248,14 @@
             scores = lax.dot_general(
                 q[at_rows, hs], keys, (((1,), (1,)), ((), ())),
                 preferred_element_type=jnp.float32,
-            ) * scale
-            scores = jnp.where(valid, scores, -jnp.inf)
+            ) * scale + bias
             peak = jnp.max(scores, axis=1, keepdims=True)
             weights = jnp.exp(scores - peak)
             total = jnp.sum(weights, axis=1, keepdims=True)
-            summed = jnp.dot(
+            acc[at_rows, hs] = jnp.dot(
                 weights.astype(jnp.bfloat16), values, preferred_element_type=jnp.float32
             )
-            out[at_rows, hs] = (summed / total).astype(jnp.bfloat16)
+            stats[h, at_rows] = jnp.where(lane < DH // 2, peak, total)
         return carry
 
     lax.fori_loop(0, blocks, one_block, 0)
@@ -261,29 +263,98 @@
 
 def attended(slots, place, q, k, v, before, after, glob, arrived):
     rows, features = q.shape
-    unit = CAP * 2 * BLOCK
-    counts = tuple(a.shape[1] // unit * unit for a in arrived)
+    counts = tuple(a.shape[1] for a in arrived)
     vmem = pl.BlockSpec(memory_space=pltpu.VMEM)
     smem = pl.BlockSpec(memory_space=pltpu.SMEM)
     return pl.pallas_call(
         lambda *refs: attend_kernel(counts, *refs),
-        out_shape=jax.ShapeDtypeStruct((rows, features), jnp.bfloat16),
-        in_specs=[smem, smem]
-        + [vmem] * 6
-        + [pl.BlockSpec(memory_space=pl.ANY)] * len(arrived),
-        out_specs=vmem,
+        out_shape=(
+            jax.ShapeDtypeStruct((rows, features), jnp.float32),
+            jax.ShapeDtypeStruct((features // DH, rows, DH), jnp.float32),
+        ),
+        in_specs=[smem, smem] + [vmem] * 6 + [pl.BlockSpec(memory_space=pl.ANY)] * len(arrived),
+        out_specs=(vmem, vmem),
         scratch_shapes=[
-            pltpu.VMEM((INPLANE, PLANES * unit, DH), jnp.bfloat16),
+            pltpu.VMEM((INPLANE, sum(counts), DH), jnp.bfloat16),
             pltpu.SemaphoreType.DMA((len(arrived),)),
             pltpu.VMEM((rows + 2 * BLOCK, features), jnp.bfloat16),
             pltpu.VMEM((rows + 2 * BLOCK, features), jnp.bfloat16),
         ],
         compiler_params=pltpu.CompilerParams(vmem_limit_bytes=VMEM_LIMIT),
         cost_estimate=pl.CostEstimate(
-            flops=4 * rows * features * 512, bytes_accessed=12 * 2**20, transcendentals=rows * 4 * 512
+            flops=4 * rows * features * 512, bytes_accessed=COST, transcendentals=rows * 4 * 512
         ),
         name="attend",
     )(slots, place, q, k, v, before, after, glob, *arrived)
+
+
+def finish_kernel(late, q, acc, stats, blocks_late, top, low, gout, summed, held):
+    scale = DH ** (-0.5)
+    lane = lax.broadcasted_iota(jnp.int32, (BLOCK, DH), 1)
+    summed[...] = acc[...]
+    held[...] = stats[...]
+
+    def one_late(i, carry):
+        code = late[i]
+
+        @pl.when(code >= 0)
+        def _():
+            h = code >> 4
+            at_rows = pl.ds(pl.multiple_of((code & 15) * BLOCK, BLOCK), BLOCK)
+            cols = pl.ds(pl.multiple_of(h * DH, DH), DH)
+            at = pl.multiple_of((i & (CAP - 1)) * 2 * BLOCK, 2 * BLOCK)
+            peer = i // CAP
+            scores = lax.dot_general(
+                q[at_rows, cols], blocks_late[peer, pl.ds(at, BLOCK)], (((1,), (1,)), ((), ())),
+                preferred_element_type=jnp.float32,
+            ) * scale
+            before = held[h, at_rows, 0:1]
+            peak = jnp.maximum(before, jnp.max(scores, axis=1, keepdims=True))
+            weights = jnp.exp(scores - peak)
+            less = jnp.exp(before - peak)
+            total = held[h, at_rows, DH // 2 : DH // 2 + 1] * less
+            total += jnp.sum(weights, axis=1, keepdims=True)
+            summed[at_rows, cols] = summed[at_rows, cols] * less + jnp.dot(
+                weights.astype(jnp.bfloat16), blocks_late[peer, pl.ds(at + BLOCK, BLOCK)],
+                preferred_element_type=jnp.float32,
+            )
+            held[h, at_rows] = jnp.where(lane < DH // 2, peak, total)
+
+        return carry
+
+    lax.fori_loop(0, INPLANE * CAP, one_late, 0)
+    merge_rows(blocks_late, 2 * CAP * BLOCK, gout)
+    half = top.shape[0]
+    for side, out in enumerate((top, low)):
+
+        def one_block(b, carry):
+            to_rows = pl.ds(pl.multiple_of(b * BLOCK, BLOCK), BLOCK)
+            at_rows = pl.ds(pl.multiple_of(b * BLOCK + side * half, BLOCK), BLOCK)
+            for h in range(held.shape[0]):
+                hs = slice(h * DH, (h + 1) * DH)
+                total = held[h, at_rows, DH // 2 : DH // 2 + 1]
+                out[to_rows, hs] = (summed[at_rows, hs] / total).astype(jnp.bfloat16)
+            return carry
+
+        lax.fori_loop(0, half // BLOCK, one_block, 0)
+
+
+def finished(late, q, acc, stats, blocks_late):
+    vmem = pl.BlockSpec(memory_space=pltpu.VMEM)
+    rows, features = q.shape
+    half = jax.ShapeDtypeStruct((rows // 2, features), jnp.bfloat16)
+    return pl.pallas_call(
+        finish_kernel,
+        out_shape=(half, half, jax.ShapeDtypeStruct((INPLANE, BLOCK, DH), jnp.bfloat16)),
+        in_specs=[pl.BlockSpec(memory_space=pltpu.SMEM)] + [vmem] * 4,
+        out_specs=(vmem, vmem, vmem),
+        scratch_shapes=[
+            pltpu.VMEM(acc.shape, jnp.float32),
+            pltpu.VMEM(stats.shape, jnp.float32),
+        ],
+        compiler_params=pltpu.CompilerParams(vmem_limit_bytes=32 * 2**20),
+        name="late_blocks",
+    )(late, q, acc, stats, blocks_late)
 
 
 def on_device(queries, key_vectors, value_vectors, random_blocks, global_blocks, out_weight):
@@ -306,6 +377,10 @@
     slots = ((holders % INPLANE) * PLANES + order) * CAP + rank
     every = jnp.arange(INPLANE * PLANES * CAP, dtype=jnp.int32)
     asked = jnp.sum(jnp.where(slots[None, :] == every[:, None], codes[None, :], 0), axis=1)
+    asker = number // RANDOM
+    asker = (asker // blocks) * 16 + asker % blocks + 1
+    late = jnp.sum(jnp.where(slots[None, :] == every[:, None], asker[None, :], 0), axis=1) - 1
+    late = late.reshape(INPLANE, PLANES, CAP)[:, PLANES - 1].reshape(-1)
     asked = asked.astype(jnp.bfloat16).reshape(INPLANE, 1, PLANES * CAP)
     asked = jnp.pad(asked, ((0, 0), (0, 15), (0, features - PLANES * CAP)))
 
@@ -346,30 +421,38 @@
     asked, _, _ = lax.optimization_barrier((asked, up_v, down_k))
     picks = picked(asked, 0, [key_vectors, value_vectors])
     arrived = [over_plane(picks)]
-    shared = jnp.broadcast_to(shared[None], (PLANES, *shared.shape))
-    shared = lax.all_to_all(shared, "seq_0", split_axis=0, concat_axis=0, tiled=True).sum(axis=0)
-    shared = jnp.broadcast_to(shared[None], (INPLANE, *shared.shape))
-    glob = over_plane(shared).reshape(GLOBAL, 2, BLOCK, features)
     ahead = [(i, i + 1) for i in range(shards - 1)]
     back = [(j, i) for i, j in ahead]
     first, parts = 1, ()
     beside = [lax.ppermute(ends, SEQ, ahead), lax.ppermute(starts, SEQ, back)]
     held = [up_k, down_k, up_v, down_v]
+    first_pair = (up_v, down_k)
     for step in range(2, PLANES // 2 + 1):
-        if step == PLANES // 2:
-            up_k, down_v, _ = lax.optimization_barrier((up_k, down_v, held))
+        if step > 2:
+            up_k, down_v, _ = lax.optimization_barrier((up_k, down_v, held if step == PLANES // 2 else first_pair))
         up_k = ring_step(up_k, 1)
         down_v = ring_step(down_v, -1)
+        if step > 2:
+            shared, _ = lax.optimization_barrier((shared, arrived[-1]))
+        if step == 3:
+            shared = jnp.broadcast_to(shared[None], (PLANES, *shared.shape))
+            shared = lax.all_to_all(shared, "seq_0", split_axis=0, concat_axis=0, tiled=True)
+            shared = shared.sum(axis=0)
+        elif step == 4:
+            shared = over_plane(jnp.broadcast_to(shared[None], (INPLANE, *shared.shape)))
+            glob = shared.reshape(GLOBAL, 2, BLOCK, features)
+        if step < PLANES // 2:
+            up_v, down_k, _ = lax.optimization_barrier((up_v, down_k, picks))
         gate = (up_k, down_v) if step < PLANES // 2 else ()
-        held, _, _, beside, parts = lax.optimization_barrier(
-            (held, gate, picks, beside, parts)
+        held, _, _, tied, parts = lax.optimization_barrier(
+            (held, gate, arrived[-1], beside if step > 2 else (), parts)
         )
-        if step == 2:
+        if step > 2:
+            weights[step - 2], before, after = tied
+        else:
             before, after = beside
-        else:
-            weights[step - 2] = beside
         beside, _ = lax.optimization_barrier((weights[step - 1], held))
-        beside = across(beside, (1, -1, 2)[step - 2])
+        beside = (across(beside, (1, -1, 2)[step - 2]), before, after)
         picks = picked(asked, first, held)
         arrived.append(over_plane(picks))
         first += len(held) // 2
@@ -383,24 +466,23 @@
             held = [up_k, down_k, up_v, down_v]
         else:
             held = [up_k, down_v]
-    weights[3] = beside
+    weights[3], before, after = beside
     held, arrived, parts, glob = lax.optimization_barrier((held, arrived, parts, glob))
     parts = (global_parts(asking, held, parts),)
     arrived.append(over_plane(picked(asked, first, held, parts)))
-    gout = over_plane(merged(arrived[-1]))
-
     place = jnp.concatenate(
         [
             jnp.stack([my_index * blocks, jnp.int32(shards * blocks)]).astype(jnp.int32),
             jnp.where(mine, spot, -1).astype(jnp.int32),
         ]
     )
-    attention = attended(
-        slots, place, queries, key_vectors, value_vectors, before, after, glob, arrived
-    )
-    own_t, own_b = patched(place, gout, attention)
-    right_t, left_b = across(own_t, 1), across(own_b, -1)
-    right_b, left_t = across(own_b, 1), across(own_t, -1)
+    acc, stats = attended(
+        slots, place, queries, key_vectors, value_vectors, before, after, glob, arrived[:-1]
+    )
+    own_t, own_b, gout = finished(late, queries, acc, stats, arrived[-1])
+    right_t, left_t = across(own_t, 1), across(own_t, -1)
+    own_b = joined(own_b, over_plane(gout))
+    right_b, left_b = across(own_b, 1), across(own_b, -1)
     far_t, far_b = across(right_t, 1), across(left_b, -1)
 
     def product(*pieces):
@@ -409,8 +491,8 @@
             total = total + jnp.dot(piece, weight, preferred_element_type=jnp.float32)
         return total.astype(jnp.bfloat16)
 
-    return jnp.concatenate(
-        [product(own_t, right_t, left_t, far_t), product(own_b, right_b, left_b, far_b)]
+    return placed(
+        place, product(own_t, right_t, left_t, far_t), product(own_b, right_b, left_b, far_b)
     )
 
 

time: 324 us -> 319 us (0.985)
  blocking collectives: 18.3 us -> 0 us
  waiting for transfers between devices: 131 us -> 117 us
  starting transfers between devices: 72.2 us -> 86 us
  Pallas kernels: 49.8 us -> 63.5 us
  matrix products: 10.7 us -> 14.1 us
    all_to_all x8, waiting for transfers between devices: 45.9 us -> 64.3 us  [over_plane(): return lax.all_to_all(parts, PLANE, split_axis=0, concat_axis=0, tiled=True)]
    all_to_all x1 -> x0, blocking collectives: 18.3 us -> none  [on_device(): lax.all_to_all(shared, 'seq_0', split_axis=0, concat_axis=0, tiled=True)]
    ppermute x14, waiting for transfers between devices: 56.1 us -> 40.2 us  [ring_step(): lax.ppermute(shard, 'seq_0', [(i, (i + step) % peers) for i in range(peer...]
    ppermute x2, waiting for transfers between devices: 13.3 us -> 0.01 us  [on_device(): beside = [lax.ppermute(ends, SEQ, ahead), lax.ppermute(starts, SEQ, back)]]
    pallas_call x3 -> x4, Pallas kernels: 24.2 us -> 37 us  [the longest x1 20.5 us: attended(): pl.pallas_call(lambda *refs: attend_kernel(counts, *refs), out_shape=(jax...]
    all_to_all x0 -> x1, starting transfers between devices: none -> 8.44 us  [on_device(): lax.all_to_all(shared, 'seq_0', split_axis=0, concat_axis=0, tiled=True)]
    ppermute x9, waiting for transfers between devices: 15.5 us -> 8.4 us  [across(): lax.ppermute(shard, 'heads', [(i, (i + step) % peers) for i in range(peer...]
    all_to_all x0 -> x1, waiting for transfers between devices: none -> 4.27 us  [on_device(): lax.all_to_all(shared, 'seq_0', split_axis=0, concat_axis=0, tiled=True)]
  transfers between devices with their start and end apart: 33 -> 34, of which waited for: 19 -> 16; matrix products, arithmetic and copies ran while one was open for 9% -> 10% of each run, Pallas kernels for 14% -> 17%
where the time goes in v5:
time: 319 us; the launch traced here: 316 us
  waiting for transfers between devices  117 us (37%)
  starting transfers between devices  86 us (27%)
  Pallas kernels  63.5 us (20%)
  local copies, waits for them, and re-layouts  20.1 us (6%)
  matrix products  14.1 us (4%)
  other arithmetic  13 us (4%)
    all_to_all x8, waiting for transfers between devices, over_plane(): return lax.all_to_all(parts, PLANE, split_axis=0, concat_axis=0, tiled=True)  64.3 us
    ppermute x14, waiting for transfers between devices, ring_step(): lax.ppermute(shard, 'seq_0', [(i, (i + step) % peers) for i in range(peer...  40.2 us
    all_to_all x8, starting transfers between devices, over_plane(): return lax.all_to_all(parts, PLANE, split_axis=0, concat_axis=0, tiled=True)  34.7 us
    pallas_call x1, Pallas kernels, attended(): pl.pallas_call(lambda *refs: attend_kernel(counts, *refs), out_shape=(jax...  20.5 us
    ppermute x14, starting transfers between devices, ring_step(): lax.ppermute(shard, 'seq_0', [(i, (i + step) % peers) for i in range(peer...  17.1 us
    ppermute x9, starting transfers between devices, across(): lax.ppermute(shard, 'heads', [(i, (i + step) % peers) for i in range(peer...  16.9 us
    unnamed x54, local copies, waits for them, and re-layouts  14.1 us
    dot_general x8, matrix products, product(): total = total + jnp.dot(piece, weight, preferred_element_type=jnp.float32)  14.1 us
  transfers between devices with their start and end apart: 34, of which 16 were waited for; matrix products, arithmetic and copies ran while one was open for 10% of the time, Pallas kernels for 17%

profile of v5, /device:TPU:32, one launch (start us, length us, event | category | flops | bytes accessed | tf_op | source)
XLA Modules:
  0.0 315.6 jit_solution(7994935768075078798)
XLA Ops:
  0.0 1.9 collective-permute-start
  7.7 2.2 fusion.14
  9.8 2.1 dynamic-slice_select_fusion.5
  15.9 2.2 constant_dynamic-slice_fusion
  19.5 1.8 collective-permute-done.2.refs_4_.refs_5_
  21.3 4.5 %all-to-all-start = ((bf16[8,176,512]{2,1,0:T(8,128)(2,1)}), bf16[8,176,512]{2,1,0:T(8,128)(2,1)}, u32[]{:S(2)}, u32[]{:S(2)}) async-start(bf16[8,176,512]{2,1,0:T(8,128)(2,1)} %fusion.1), calls=%async_computation | async-start | bytes 2883584 | tf_op jit(solution)/shard_map/all_to_all | solution.py:72
  25.8 2.5 collective-permute-start.5
  29.1 17.0 %all-to-all-done = bf16[8,176,512]{2,1,0:T(8,128)(2,1)} async-done(((bf16[8,176,512]{2,1,0:T(8,128)(2,1)}), bf16[8,176,512]{2,1,0:T(8,128)(2,1)}, u32[]{:S(2)}, u32[]{:S(2)}) %all-to-all-start) | async-done | bytes 1441824 | tf_op jit(solution)/shard_map/all_to_all | solution.py:72
  47.2 2.0 collective-permute-done.4.refs_3_.refs_4_
  49.3 1.8 pick_blocks.5
  51.1 4.4 %all-to-all-start.1 = ((bf16[8,512,128]{2,1,0:T(8,128)(2,1)}), bf16[8,512,128]{2,1,0:T(8,128)(2,1)}, u32[]{:S(2)}, u32[]{:S(2)}) async-start(bf16[8,512,128]{2,1,0:T(8,128)(2,1)} %pick_blocks.5), calls=%async_computation.1 | async-start | bytes 2097152 | tf_op jit(solution)/shard_map/all_to_all | solution.py:72
  56.5 2.1 collective-permute-start.3
  58.6 18.1 %collective-permute-done.1.refs_1_ = bf16[768,512]{1,0:T(8,128)(2,1)S(1)} collective-permute-done((bf16[768,512]{1,0:T(8,128)(2,1)S(1)}, bf16[768,512]{1,0:T(8,128)(2,1)S(1)}, u32[]{:S(2)}, u32[]{:S(2)}) %collective-permute-start.1) | collective-permute-done | bytes 786464 | tf_op jit(solution)/shard_map/ppermute | solution.py:24
  77.6 1.9 pick_blocks.6
  80.9 4.4 %all-to-all-start.2 = ((bf16[8,1024,128]{2,1,0:T(8,128)(2,1)}), bf16[8,1024,128]{2,1,0:T(8,128)(2,1)}, u32[]{:S(2)}, u32[]{:S(2)}) async-start(bf16[8,1024,128]{2,1,0:T(8,128)(2,1)} %copy-done.2), calls=%async_computation.2 | async-start | bytes 4194304 | tf_op jit(solution)/shard_map/all_to_all | solution.py:72
  85.3 1.5 collective-permute-start.12
  86.8 2.1 collective-permute-start.13
  88.9 6.8 %collective-permute-start.14 = (bf16[128,512]{1,0:T(8,128)(2,1)S(1)}, bf16[128,512]{1,0:T(8,128)(2,1)}, u32[]{:S(2)}, u32[]{:S(2)}) collective-permute-start(bf16[128,512]{1,0:T(8,128)(2,1)S(1)} %get-tuple-element.74), channel_id=1, source_target_pairs={{1,0},{2,1},{3,2},{4,3},{5,4},{6,5},{7,6},{8,7},{9,8},{10,9},{11,1... | collective-permute-start | bytes 393224 | tf_op jit(solution)/shard_map/ppermute | solution.py:427
  95.7 1.7 collective-permute-start.6
  97.8 2.6 collective-permute-start.7
  101.4 12.3 %all-to-all-done.2.refs_9_ = bf16[8,1024,128]{2,1,0:T(8,128)(2,1)} async-done(((bf16[8,1024,128]{2,1,0:T(8,128)(2,1)}), bf16[8,1024,128]{2,1,0:T(8,128)(2,1)}, u32[]{:S(2)}, u32[]{:S(2)}) %all-to-all-start.2) | async-done | bytes 2097184 | tf_op jit(solution)/shard_map/all_to_all | solution.py:72
  114.5 8.4 %all-to-all-start.5 = ((bf16[8,32,512]{2,1,0:T(8,128)(2,1)}), bf16[8,32,512]{2,1,0:T(8,128)(2,1)S(1)}, u32[]{:S(2)}, u32[]{:S(2)}) async-start(bf16[8,32,512]{2,1,0:T(8,128)(2,1)} %broadcast_in_dim.29), calls=%async_computation.5 | async-start | bytes 524288 | tf_op jit(solution)/shard_map/all_to_all | solution.py:439
  122.9 1.4 slice_reduce_fusion.refs_0_
  124.3 3.9 %global_parts.4.refs_5_ = f32[512,256]{1,0:T(8,128)S(1)} custom-call(bf16[128,512]{1,0:T(8,128)(2,1)S(1)} %slice_reduce_fusion.refs_0_, bf16[768,512]{1,0:T(8,128)(2,1)S(1)} %collective-permute-done.refs_1_, bf16[768,512]{1,0:T(8,128)(2,1)} %collective-permute-done.5.refs_2_, bf16[768,512]{1,0:T(8,128)(2,1)S(1)} %copy-done, ...), custom_call_target="tpu_custom_call" | custom-call | flops 603979776 | bytes 25165824 | tf_op jit(solution)/shard_map/global_parts/pallas_call | solution.py:120
  129.9 4.2 %collective-permute-done.8.refs_2_ = bf16[768,512]{1,0:T(8,128)(2,1)} collective-permute-done((bf16[768,512]{1,0:T(8,128)(2,1)}, bf16[768,512]{1,0:T(8,128)(2,1)}, u32[]{:S(2)}, u32[]{:S(2)}) %collective-permute-start.8) | collective-permute-done | bytes 786464 | tf_op jit(solution)/shard_map/ppermute | solution.py:24
  134.1 3.5 %pick_blocks.7 = bf16[8,1024,128]{2,1,0:T(8,128)(2,1)} custom-call(s32[256]{0:T(256)S(1)} %reshape.183.refs_0_, bf16[768,512]{1,0:T(8,128)(2,1)S(1)} %copy-done.5, bf16[768,512]{1,0:T(8,128)(2,1)} %collective-permute-done.8.refs_2_, bf16[768,512]{1,0:T(8,128)(2,1)} %collective-permute-done.7.refs_3_, bf16[768,512]{1,0:T(8,128)(2,1)} %collective-permute-done.3.refs_4_), custom_call_target="tpu_custom_call" | custom-call | bytes 25165824 | tf_op jit(solution)/shard_map/pick_blocks/pallas_call | solution.py:60
  137.6 4.3 %all-to-all-done.5 = bf16[8,32,512]{2,1,0:T(8,128)(2,1)S(1)} async-done(((bf16[8,32,512]{2,1,0:T(8,128)(2,1)}), bf16[8,32,512]{2,1,0:T(8,128)(2,1)S(1)}, u32[]{:S(2)}, u32[]{:S(2)}) %all-to-all-start.5) | async-done | bytes 262176 | tf_op jit(solution)/shard_map/all_to_all | solution.py:439
  141.9 5.9 %all-to-all-start.3 = ((bf16[8,1024,128]{2,1,0:T(8,128)(2,1)}), bf16[8,1024,128]{2,1,0:T(8,128)(2,1)}, u32[]{:S(2)}, u32[]{:S(2)}) async-start(bf16[8,1024,128]{2,1,0:T(8,128)(2,1)} %pick_blocks.7), calls=%async_computation.3 | async-start | bytes 4194304 | tf_op jit(solution)/shard_map/all_to_all | solution.py:72
  147.8 2.8 collective-permute-start.15
  150.6 2.0 collective-permute-start.10
  152.7 22.4 %all-to-all-done.3.refs_10_ = bf16[8,1024,128]{2,1,0:T(8,128)(2,1)} async-done(((bf16[8,1024,128]{2,1,0:T(8,128)(2,1)}), bf16[8,1024,128]{2,1,0:T(8,128)(2,1)}, u32[]{:S(2)}, u32[]{:S(2)}) %all-to-all-start.3) | async-done | bytes 2097184 | tf_op jit(solution)/shard_map/all_to_all | solution.py:72
  175.8 3.4 %all-to-all-start.6 = ((bf16[8,32,512]{2,1,0:T(8,128)(2,1)}), bf16[8,32,512]{2,1,0:T(8,128)(2,1)S(1)}, u32[]{:S(2)}, u32[]{:S(2)}) async-start(bf16[8,32,512]{2,1,0:T(8,128)(2,1)} %broadcast_in_dim.30), calls=%async_computation.6 | async-start | bytes 524288 | tf_op jit(solution)/shard_map/all_to_all | solution.py:72
  179.3 4.0 %global_parts.5.refs_5_ = f32[512,256]{1,0:T(8,128)S(1)} custom-call(bf16[128,512]{1,0:T(8,128)(2,1)S(1)} %slice_reduce_fusion.refs_0_, bf16[768,512]{1,0:T(8,128)(2,1)S(1)} %copy-done.6, bf16[768,512]{1,0:T(8,128)(2,1)} %collective-permute-done.8.refs_2_, bf16[768,512]{1,0:T(8,128)(2,1)} %collective-permute-done.7.refs_3_, ...), custom_call_target="tpu_custom_call" | custom-call | flops 402653184 | bytes 25165824 | tf_op jit(solution)/shard_map/global_parts/pallas_call | solution.py:120
  184.1 3.8 %pick_blocks.8 = bf16[8,1024,128]{2,1,0:T(8,128)(2,1)} custom-call(s32[256]{0:T(256)S(1)} %reshape.183.refs_0_, bf16[768,512]{1,0:T(8,128)(2,1)} %collective-permute-done.6.refs_1_, bf16[768,512]{1,0:T(8,128)(2,1)S(1)} %collective-permute-done.9.refs_2_, bf16[768,512]{1,0:T(8,128)(2,1)S(1)} %collective-permute-done.10.refs_3_, ...), custom_call_target="tpu_custom_call" | custom-call | bytes 25165824 | tf_op jit(solution)/shard_map/pick_blocks/pallas_call | solution.py:60
  188.6 4.7 %all-to-all-start.4 = ((bf16[8,1024,128]{2,1,0:T(8,128)(2,1)}), bf16[8,1024,128]{2,1,0:T(8,128)(2,1)}, u32[]{:S(2)}, u32[]{:S(2)}) async-start(bf16[8,1024,128]{2,1,0:T(8,128)(2,1)} %pick_blocks.8), calls=%async_computation.4 | async-start | bytes 4194304 | tf_op jit(solution)/shard_map/all_to_all | solution.py:72
  193.6 1.8 collective-permute-start.17
  197.6 3.7 %global_parts.6.refs_3_ = f32[512,256]{1,0:T(8,128)S(1)} custom-call(bf16[128,512]{1,0:T(8,128)(2,1)S(1)} %slice_reduce_fusion.refs_0_, bf16[768,512]{1,0:T(8,128)(2,1)} %collective-permute-done.6.refs_1_, bf16[768,512]{1,0:T(8,128)(2,1)S(1)} %copy-done.8, bf16[768,512]{1,0:T(8,128)(2,1)S(1)} %copy-done.10, ...), custom_call_target="tpu_custom_call" | custom-call | flops 402653184 | bytes 25165824 | tf_op jit(solution)/shard_map/global_parts/pallas_call | solution.py:120
  202.1 11.4 %collective-permute-done.16.refs_1_ = bf16[768,512]{1,0:T(8,128)(2,1)S(1)} collective-permute-done((bf16[768,512]{1,0:T(8,128)(2,1)}, bf16[768,512]{1,0:T(8,128)(2,1)S(1)}, u32[]{:S(2)}, u32[]{:S(2)}) %collective-permute-start.16) | collective-permute-done | bytes 786464 | tf_op jit(solution)/shard_map/ppermute | solution.py:24
  213.5 7.1 %all-to-all-done.4.refs_11_ = bf16[8,1024,128]{2,1,0:T(8,128)(2,1)} async-done(((bf16[8,1024,128]{2,1,0:T(8,128)(2,1)}), bf16[8,1024,128]{2,1,0:T(8,128)(2,1)}, u32[]{:S(2)}, u32[]{:S(2)}) %all-to-all-start.4) | async-done | bytes 2097184 | tf_op jit(solution)/shard_map/all_to_all | solution.py:72
  221.7 1.9 global_parts.7.refs_3_
  223.6 2.0 pick_blocks.9
  225.5 3.6 %all-to-all-start.7 = ((bf16[8,640,128]{2,1,0:T(8,128)(2,1)}), bf16[8,640,128]{2,1,0:T(8,128)(2,1)S(1)}, u32[]{:S(2)}, u32[]{:S(2)}) async-start(bf16[8,640,128]{2,1,0:T(8,128)(2,1)} %pick_blocks.9), calls=%async_computation.7 | async-start | bytes 2621440 | tf_op jit(solution)/shard_map/all_to_all | solution.py:72
  230.0 3.0 collective-permute-start.21
  233.0 20.5 %attend.1 = (f32[768,512]{1,0:T(8,128)}, f32[4,768,128]{2,1,0:T(8,128)}) custom-call(s32[144]{0:T(256)} %copy-done.26, s32[4]{0:T(128)} %pad_add_fusion.refs_1_.place, bf16[768,512]{1,0:T(8,128)(2,1)} %q.1, bf16[768,512]{1,0:T(8,128)(2,1)} %refs_3_.3, bf16[768,512]{1,0:T(8,128)(2,1)} %refs_4_.1, bf16[128,512]{1,0:T(8,128)(2,1)} %copy-done.25, ...), custom_call_target="tpu_custom_call" | custom-call | flops 805306368 | bytes 25165824 | tf_op jit(solution)/shard_map/attend/pallas_call | solution.py:269
  253.5 1.4 copy-done.17
  254.9 1.4 copy-done.18
  256.3 12.8 %late_blocks.1 = (bf16[384,512]{1,0:T(8,128)(2,1)S(1)}, bf16[384,512]{1,0:T(8,128)(2,1)S(1)}, bf16[8,64,128]{2,1,0:T(8,128)(2,1)}) custom-call(s32[32]{0:T(128)S(1)} %reshape_squeeze.3.late, bf16[768,512]{1,0:T(8,128)(2,1)S(1)} %copy-done.3, f32[768,512]{1,0:T(8,128)S(1)} %copy-done.17, f32[4,768,128]{2,1,0:T(8,128)S(1)} %copy-done.18, ...), custom_call_target="tpu_custom_call" | custom-call | tf_op jit(solution)/shard_map/late_blocks/pallas_call | solution.py:346
  270.2 1.8 collective-permute-start.18
  272.0 3.7 %all-to-all-start.8 = ((bf16[8,64,128]{2,1,0:T(8,128)(2,1)}), bf16[8,64,128]{2,1,0:T(8,128)(2,1)S(1)}, u32[]{:S(2)}, u32[]{:S(2)}) async-start(bf16[8,64,128]{2,1,0:T(8,128)(2,1)} %get-tuple-element.112), calls=%async_computation.8 | async-start | bytes 262144 | tf_op jit(solution)/shard_map/all_to_all | solution.py:72
  276.3 5.5 %all-to-all-done.8.gout = bf16[8,64,128]{2,1,0:T(8,128)(2,1)S(1)} async-done(((bf16[8,64,128]{2,1,0:T(8,128)(2,1)}), bf16[8,64,128]{2,1,0:T(8,128)(2,1)S(1)}, u32[]{:S(2)}, u32[]{:S(2)}) %all-to-all-start.8) | async-done | bytes 131104 | tf_op jit(solution)/shard_map/all_to_all | solution.py:72
  282.5 1.9 join_global_rows.1
  284.4 2.5 collective-permute-start.23
  286.8 1.8 fusion.21
  288.7 1.6 collective-permute-start.20
  290.3 1.9 fusion.19
  292.2 1.9 fusion.20
  294.2 4.2 %collective-permute-done.23 = bf16[512,512]{1,0:T(8,128)(2,1)S(1)} collective-permute-done((bf16[512,512]{1,0:T(8,128)(2,1)}, bf16[512,512]{1,0:T(8,128)(2,1)S(1)}, u32[]{:S(2)}, u32[]{:S(2)}) %collective-permute-start.23) | collective-permute-done | bytes 524320 | tf_op jit(solution)/shard_map/ppermute | solution.py:29
  298.3 3.4 %collective-permute-start.24 = (bf16[512,512]{1,0:T(8,128)(2,1)S(1)}, bf16[512,512]{1,0:T(8,128)(2,1)S(1)}, u32[]{:S(2)}, u32[]{:S(2)}) collective-permute-start(bf16[512,512]{1,0:T(8,128)(2,1)S(1)} %collective-permute-done.23), channel_id=1, source_target_pairs={{0,192},{64,0},{128,64},{192,128},{1,193},{65,1},{129,65},{193,129... | collective-permute-start | bytes 1572872 | tf_op jit(solution)/shard_map/ppermute | solution.py:29
  301.7 1.9 fusion.23
  303.7 2.0 fusion.22
  305.6 4.2 %collective-permute-done.20 = bf16[384,512]{1,0:T(8,128)(2,1)S(1)} collective-permute-done((bf16[384,512]{1,0:T(8,128)(2,1)}, bf16[384,512]{1,0:T(8,128)(2,1)S(1)}, u32[]{:S(2)}, u32[]{:S(2)}) %collective-permute-start.20) | collective-permute-done | bytes 393248 | tf_op jit(solution)/shard_map/ppermute | solution.py:29
  309.9 1.9 add_convert_fusion.1.top
  311.8 2.0 add_convert_fusion.low
  313.8 1.8 place_global_rows.1
  (117 shorter events, 28.4 us)
Async XLA Ops:
  0.0 12.0 %copy-start.1 = (bf16[768,512]{1,0:T(8,128)(2,1)S(1)}, bf16[768,512]{1,0:T(8,128)(2,1)}, u32[]{:S(2)}) copy-start(bf16[768,512]{1,0:T(8,128)(2,1)} %refs_4_.1) | copy-start | bytes 2359300
  0.0 19.5 %collective-permute-start = (bf16[768,512]{1,0:T(8,128)(2,1)}, bf16[768,512]{1,0:T(8,128)(2,1)S(1)}, u32[]{:S(2)}, u32[]{:S(2)}) collective-permute-start(bf16[768,512]{1,0:T(8,128)(2,1)} %refs_3_.3), channel_id=1, source_target_pairs={{0,8},{8,16},{16,24},{24,32},{32,40},{40,48},{48,56},{56,0},{1,9},... | collective-permute-start | bytes 2359304 | tf_op jit(solution)/shard_map/ppermute | solution.py:24
  1.9 19.4 %collective-permute-start.2 = (bf16[768,512]{1,0:T(8,128)(2,1)}, bf16[768,512]{1,0:T(8,128)(2,1)S(1)}, u32[]{:S(2)}, u32[]{:S(2)}) collective-permute-start(bf16[768,512]{1,0:T(8,128)(2,1)} %refs_4_.1), channel_id=1, source_target_pairs={{0,56},{8,0},{16,8},{24,16},{32,24},{40,32},{48,40},{56,48},{1,57}... | collective-permute-start | bytes 2359304 | tf_op jit(solution)/shard_map/ppermute | solution.py:24
  7.4 6.0 %copy-start.26 = (s32[144]{0:T(256)}, s32[144]{0:T(256)S(1)}, u32[]{:S(2)}) copy-start(s32[144]{0:T(256)S(1)} %multiply_add_fusion.refs_0_) | copy-start | bytes 1732
  13.2 2.7 copy-start.22
  18.1 7.6 %copy-start = (bf16[768,512]{1,0:T(8,128)(2,1)S(1)}, bf16[768,512]{1,0:T(8,128)(2,1)}, u32[]{:S(2)}) copy-start(bf16[768,512]{1,0:T(8,128)(2,1)} %refs_3_.3) | copy-start | bytes 2359300
  21.3 24.8 %all-to-all-start = ((bf16[8,176,512]{2,1,0:T(8,128)(2,1)}), bf16[8,176,512]{2,1,0:T(8,128)(2,1)}, u32[]{:S(2)}, u32[]{:S(2)}) async-start(bf16[8,176,512]{2,1,0:T(8,128)(2,1)} %fusion.1), calls=%async_computation | async-start | bytes 2883584 | tf_op jit(solution)/shard_map/all_to_all | solution.py:72
  25.8 21.4 %collective-permute-start.5 = (bf16[768,512]{1,0:T(8,128)(2,1)S(1)}, bf16[768,512]{1,0:T(8,128)(2,1)}, u32[]{:S(2)}, u32[]{:S(2)}) collective-permute-start(bf16[768,512]{1,0:T(8,128)(2,1)S(1)} %copy-done), channel_id=1, source_target_pairs={{0,56},{8,0},{16,8},{24,16},{32,24},{40,32},{48,40},{56,48},{1,57}... | collective-permute-start | bytes 2359304 | tf_op jit(solution)/shard_map/ppermute | solution.py:24
  28.3 21.0 %collective-permute-start.4 = (bf16[768,512]{1,0:T(8,128)(2,1)S(1)}, bf16[768,512]{1,0:T(8,128)(2,1)}, u32[]{:S(2)}, u32[]{:S(2)}) collective-permute-start(bf16[768,512]{1,0:T(8,128)(2,1)S(1)} %copy-done.1), channel_id=1, source_target_pairs={{0,8},{8,16},{16,24},{24,32},{32,40},{40,48},{48,56},{56,0},{1,9},... | collective-permute-start | bytes 2359304 | tf_op jit(solution)/shard_map/ppermute | solution.py:24
  51.1 26.5 %all-to-all-start.1 = ((bf16[8,512,128]{2,1,0:T(8,128)(2,1)}), bf16[8,512,128]{2,1,0:T(8,128)(2,1)}, u32[]{:S(2)}, u32[]{:S(2)}) async-start(bf16[8,512,128]{2,1,0:T(8,128)(2,1)} %pick_blocks.5), calls=%async_computation.1 | async-start | bytes 2097152 | tf_op jit(solution)/shard_map/all_to_all | solution.py:72
  55.5 21.2 %collective-permute-start.1 = (bf16[768,512]{1,0:T(8,128)(2,1)S(1)}, bf16[768,512]{1,0:T(8,128)(2,1)S(1)}, u32[]{:S(2)}, u32[]{:S(2)}) collective-permute-start(bf16[768,512]{1,0:T(8,128)(2,1)S(1)} %collective-permute-done.refs_1_), channel_id=1, source_target_pairs={{0,8},{8,16},{16,24},{24,32},{32,40},{40,48},{48,56},{56,0},{1,9},... | collective-permute-start | bytes 2359304 | tf_op jit(solution)/shard_map/ppermute | solution.py:24
  56.5 21.1 %collective-permute-start.3 = (bf16[768,512]{1,0:T(8,128)(2,1)S(1)}, bf16[768,512]{1,0:T(8,128)(2,1)}, u32[]{:S(2)}, u32[]{:S(2)}) collective-permute-start(bf16[768,512]{1,0:T(8,128)(2,1)S(1)} %collective-permute-done.2.refs_4_.refs_5_), channel_id=1, source_target_pairs={{0,56},{8,0},{16,8},{24,16},{32,24},{40,32},{48,40},{56,48},{1,57}... | collective-permute-start | bytes 2359304 | tf_op jit(solution)/shard_map/ppermute | solution.py:24
  76.7 0.9 copy-start.4
  79.5 1.3 copy-start.2
  80.9 32.9 %all-to-all-start.2 = ((bf16[8,1024,128]{2,1,0:T(8,128)(2,1)}), bf16[8,1024,128]{2,1,0:T(8,128)(2,1)}, u32[]{:S(2)}, u32[]{:S(2)}) async-start(bf16[8,1024,128]{2,1,0:T(8,128)(2,1)} %copy-done.2), calls=%async_computation.2 | async-start | bytes 4194304 | tf_op jit(solution)/shard_map/all_to_all | solution.py:72
  85.3 48.8 %collective-permute-start.12 = (bf16[512,1024]{1,0:T(8,128)(2,1)}, bf16[512,1024]{1,0:T(8,128)(2,1)}, u32[]{:S(2)}, u32[]{:S(2)}) collective-permute-start(bf16[512,1024]{1,0:T(8,128)(2,1)} %get-tuple-element.72), channel_id=1, source_target_pairs={{0,64},{64,128},{128,192},{192,0},{1,65},{65,129},{129,193},{193,1... | collective-permute-start | bytes 3145736 | tf_op jit(solution)/shard_map/ppermute | solution.py:29
  86.8 11.0 %collective-permute-start.13 = (bf16[128,512]{1,0:T(8,128)(2,1)S(1)}, bf16[128,512]{1,0:T(8,128)(2,1)S(1)}, u32[]{:S(2)}, u32[]{:S(2)}) collective-permute-start(bf16[128,512]{1,0:T(8,128)(2,1)S(1)} %get-tuple-element.73), channel_id=1, source_target_pairs={{0,1},{1,2},{2,3},{3,4},{4,5},{5,6},{6,7},{7,8},{8,9},{9,10},{10,1... | collective-permute-start | bytes 393224 | tf_op jit(solution)/shard_map/ppermute | solution.py:427
  88.9 11.5 %collective-permute-start.14 = (bf16[128,512]{1,0:T(8,128)(2,1)S(1)}, bf16[128,512]{1,0:T(8,128)(2,1)}, u32[]{:S(2)}, u32[]{:S(2)}) collective-permute-start(bf16[128,512]{1,0:T(8,128)(2,1)S(1)} %get-tuple-element.74), channel_id=1, source_target_pairs={{1,0},{2,1},{3,2},{4,3},{5,4},{6,5},{7,6},{8,7},{9,8},{10,9},{11,1... | collective-permute-start | bytes 393224 | tf_op jit(solution)/shard_map/ppermute | solution.py:427
  95.7 33.3 %collective-permute-start.6 = (bf16[768,512]{1,0:T(8,128)(2,1)}, bf16[768,512]{1,0:T(8,128)(2,1)}, u32[]{:S(2)}, u32[]{:S(2)}) collective-permute-start(bf16[768,512]{1,0:T(8,128)(2,1)} %copy-done.4), channel_id=1, source_target_pairs={{0,8},{8,16},{16,24},{24,32},{32,40},{40,48},{48,56},{56,0},{1,9},... | collective-permute-start | bytes 2359304 | tf_op jit(solution)/shard_map/ppermute | solution.py:24
  97.4 31.6 %collective-permute-start.11 = (bf16[768,512]{1,0:T(8,128)(2,1)}, bf16[768,512]{1,0:T(8,128)(2,1)}, u32[]{:S(2)}, u32[]{:S(2)}) collective-permute-start(bf16[768,512]{1,0:T(8,128)(2,1)} %collective-permute-done.3.refs_4_), channel_id=1, source_target_pairs={{0,56},{8,0},{16,8},{24,16},{32,24},{40,32},{48,40},{56,48},{1,57}... | collective-permute-start | bytes 2359304 | tf_op jit(solution)/shard_map/ppermute | solution.py:24
  97.8 16.6 %copy-start.25 = (bf16[128,512]{1,0:T(8,128)(2,1)}, bf16[128,512]{1,0:T(8,128)(2,1)S(1)}, u32[]{:S(2)}) copy-start(bf16[128,512]{1,0:T(8,128)(2,1)S(1)} %collective-permute-done.13.refs_5_) | copy-start | bytes 393220
  97.8 32.0 %collective-permute-start.7 = (bf16[768,512]{1,0:T(8,128)(2,1)}, bf16[768,512]{1,0:T(8,128)(2,1)}, u32[]{:S(2)}, u32[]{:S(2)}) collective-permute-start(bf16[768,512]{1,0:T(8,128)(2,1)} %collective-permute-done.4.refs_3_.refs_4_), channel_id=1, source_target_pairs={{0,8},{8,16},{16,24},{24,32},{32,40},{40,48},{48,56},{56,0},{1,9},... | collective-permute-start | bytes 2359304 | tf_op jit(solution)/shard_map/ppermute | solution.py:24
  100.5 33.6 %collective-permute-start.8 = (bf16[768,512]{1,0:T(8,128)(2,1)}, bf16[768,512]{1,0:T(8,128)(2,1)}, u32[]{:S(2)}, u32[]{:S(2)}) collective-permute-start(bf16[768,512]{1,0:T(8,128)(2,1)} %collective-permute-done.5.refs_2_), channel_id=1, source_target_pairs={{0,56},{8,0},{16,8},{24,16},{32,24},{40,32},{48,40},{56,48},{1,57}... | collective-permute-start | bytes 2359304 | tf_op jit(solution)/shard_map/ppermute | solution.py:24
  114.5 27.4 %all-to-all-start.5 = ((bf16[8,32,512]{2,1,0:T(8,128)(2,1)}), bf16[8,32,512]{2,1,0:T(8,128)(2,1)S(1)}, u32[]{:S(2)}, u32[]{:S(2)}) async-start(bf16[8,32,512]{2,1,0:T(8,128)(2,1)} %broadcast_in_dim.29), calls=%async_computation.5 | async-start | bytes 524288 | tf_op jit(solution)/shard_map/all_to_all | solution.py:439
  124.3 9.8 %copy-start.5 = (bf16[768,512]{1,0:T(8,128)(2,1)S(1)}, bf16[768,512]{1,0:T(8,128)(2,1)}, u32[]{:S(2)}) copy-start(bf16[768,512]{1,0:T(8,128)(2,1)} %copy-done.4) | copy-start | bytes 2359300
  128.2 0.8 copy-start.15
  137.6 41.7 %copy-start.16 = (f32[512,256]{1,0:T(8,128)S(1)}, f32[512,256]{1,0:T(8,128)}, u32[]{:S(2)}) copy-start(f32[512,256]{1,0:T(8,128)} %copy-done.15) | copy-start | bytes 1572868
  141.9 33.2 %all-to-all-start.3 = ((bf16[8,1024,128]{2,1,0:T(8,128)(2,1)}), bf16[8,1024,128]{2,1,0:T(8,128)(2,1)}, u32[]{:S(2)}, u32[]{:S(2)}) async-start(bf16[8,1024,128]{2,1,0:T(8,128)(2,1)} %pick_blocks.7), calls=%async_computation.3 | async-start | bytes 4194304 | tf_op jit(solution)/shard_map/all_to_all | solution.py:72
  147.8 31.5 %copy-start.6 = (bf16[768,512]{1,0:T(8,128)(2,1)S(1)}, bf16[768,512]{1,0:T(8,128)(2,1)}, u32[]{:S(2)}) copy-start(bf16[768,512]{1,0:T(8,128)(2,1)} %copy-done.4) | copy-start | bytes 2359300
  147.8 36.3 %collective-permute-start.15 = (bf16[512,1024]{1,0:T(8,128)(2,1)}, bf16[512,1024]{1,0:T(8,128)(2,1)}, u32[]{:S(2)}, u32[]{:S(2)}) collective-permute-start(bf16[512,1024]{1,0:T(8,128)(2,1)} %get-tuple-element.80), channel_id=1, source_target_pairs={{0,192},{64,0},{128,64},{192,128},{1,193},{65,1},{129,65},{193,129... | collective-permute-start | bytes 3145736 | tf_op jit(solution)/shard_map/ppermute | solution.py:29
  150.6 33.4 %collective-permute-start.9 = (bf16[768,512]{1,0:T(8,128)(2,1)}, bf16[768,512]{1,0:T(8,128)(2,1)S(1)}, u32[]{:S(2)}, u32[]{:S(2)}) collective-permute-start(bf16[768,512]{1,0:T(8,128)(2,1)} %collective-permute-done.8.refs_2_), channel_id=1, source_target_pairs={{0,56},{8,0},{16,8},{24,16},{32,24},{40,32},{48,40},{56,48},{1,57}... | collective-permute-start | bytes 2359304 | tf_op jit(solution)/shard_map/ppermute | solution.py:24
  150.6 33.4 %collective-permute-start.10 = (bf16[768,512]{1,0:T(8,128)(2,1)}, bf16[768,512]{1,0:T(8,128)(2,1)S(1)}, u32[]{:S(2)}, u32[]{:S(2)}) collective-permute-start(bf16[768,512]{1,0:T(8,128)(2,1)} %collective-permute-done.7.refs_3_), channel_id=1, source_target_pairs={{0,8},{8,16},{16,24},{24,32},{32,40},{40,48},{48,56},{56,0},{1,9},... | collective-permute-start | bytes 2359304 | tf_op jit(solution)/shard_map/ppermute | solution.py:24
  175.8 12.1 %all-to-all-start.6 = ((bf16[8,32,512]{2,1,0:T(8,128)(2,1)}), bf16[8,32,512]{2,1,0:T(8,128)(2,1)S(1)}, u32[]{:S(2)}, u32[]{:S(2)}) async-start(bf16[8,32,512]{2,1,0:T(8,128)(2,1)} %broadcast_in_dim.30), calls=%async_computation.6 | async-start | bytes 524288 | tf_op jit(solution)/shard_map/all_to_all | solution.py:72
  183.2 0.8 copy-start.11
  184.0 3.9 %copy-start.7 = (bf16[768,512]{1,0:T(8,128)(2,1)}, bf16[768,512]{1,0:T(8,128)(2,1)S(1)}, u32[]{:S(2)}) copy-start(bf16[768,512]{1,0:T(8,128)(2,1)S(1)} %collective-permute-done.9.refs_2_) | copy-start | bytes 2359300
  184.0 3.9 %copy-start.9 = (bf16[768,512]{1,0:T(8,128)(2,1)}, bf16[768,512]{1,0:T(8,128)(2,1)S(1)}, u32[]{:S(2)}) copy-start(bf16[768,512]{1,0:T(8,128)(2,1)S(1)} %collective-permute-done.10.refs_3_) | copy-start | bytes 2359300
  187.9 0.7 copy-start.23
  187.9 7.4 %copy-start.8 = (bf16[768,512]{1,0:T(8,128)(2,1)S(1)}, bf16[768,512]{1,0:T(8,128)(2,1)}, u32[]{:S(2)}) copy-start(bf16[768,512]{1,0:T(8,128)(2,1)} %copy-done.7) | copy-start | bytes 2359300
  188.6 32.0 %all-to-all-start.4 = ((bf16[8,1024,128]{2,1,0:T(8,128)(2,1)}), bf16[8,1024,128]{2,1,0:T(8,128)(2,1)}, u32[]{:S(2)}, u32[]{:S(2)}) async-start(bf16[8,1024,128]{2,1,0:T(8,128)(2,1)} %pick_blocks.8), calls=%async_computation.4 | async-start | bytes 4194304 | tf_op jit(solution)/shard_map/all_to_all | solution.py:72
  193.3 20.2 %collective-permute-start.16 = (bf16[768,512]{1,0:T(8,128)(2,1)}, bf16[768,512]{1,0:T(8,128)(2,1)S(1)}, u32[]{:S(2)}, u32[]{:S(2)}) collective-permute-start(bf16[768,512]{1,0:T(8,128)(2,1)} %collective-permute-done.6.refs_1_), channel_id=1, source_target_pairs={{0,8},{8,16},{16,24},{24,32},{32,40},{40,48},{48,56},{56,0},{1,9},... | collective-permute-start | bytes 2359304 | tf_op jit(solution)/shard_map/ppermute | solution.py:24
  193.6 20.0 %collective-permute-start.17 = (bf16[768,512]{1,0:T(8,128)(2,1)}, bf16[768,512]{1,0:T(8,128)(2,1)S(1)}, u32[]{:S(2)}, u32[]{:S(2)}) collective-permute-start(bf16[768,512]{1,0:T(8,128)(2,1)} %collective-permute-done.11.refs_4_), channel_id=1, source_target_pairs={{0,56},{8,0},{16,8},{24,16},{32,24},{40,32},{48,40},{56,48},{1,57}... | collective-permute-start | bytes 2359304 | tf_op jit(solution)/shard_map/ppermute | solution.py:24
  195.4 1.1 copy-start.10
  196.5 1.0 copy-start.12
  201.3 0.8 copy-start.13
  220.7 1.0 copy-start.14
  225.5 28.0 %all-to-all-start.7 = ((bf16[8,640,128]{2,1,0:T(8,128)(2,1)}), bf16[8,640,128]{2,1,0:T(8,128)(2,1)S(1)}, u32[]{:S(2)}, u32[]{:S(2)}) async-start(bf16[8,640,128]{2,1,0:T(8,128)(2,1)} %pick_blocks.9), calls=%async_computation.7 | async-start | bytes 2621440 | tf_op jit(solution)/shard_map/all_to_all | solution.py:72
  230.0 23.5 %copy-start.3 = (bf16[768,512]{1,0:T(8,128)(2,1)S(1)}, bf16[768,512]{1,0:T(8,128)(2,1)}, u32[]{:S(2)}) copy-start(bf16[768,512]{1,0:T(8,128)(2,1)} %q.1) | copy-start | bytes 2359300
  230.0 75.7 %collective-permute-start.21 = (bf16[512,1024]{1,0:T(8,128)(2,1)}, bf16[512,1024]{1,0:T(8,128)(2,1)}, u32[]{:S(2)}, u32[]{:S(2)}) collective-permute-start(bf16[512,1024]{1,0:T(8,128)(2,1)} %get-tuple-element.110), channel_id=1, source_target_pairs={{0,128},{64,192},{128,0},{192,64},{1,129},{65,193},{129,1},{193,65... | collective-permute-start | bytes 3145736 | tf_op jit(solution)/shard_map/ppermute | solution.py:29
  253.5 1.4 copy-start.17
  254.9 1.4 copy-start.18
  256.3 19.3 %copy-start.21 = (bf16[512,1024]{1,0:T(8,128)(2,1)S(1)}, bf16[512,1024]{1,0:T(8,128)(2,1)}, u32[]{:S(2)}) copy-start(bf16[512,1024]{1,0:T(8,128)(2,1)} %get-tuple-element.106) | copy-start | bytes 3145732
  269.2 0.8 copy-start.19
  269.9 22.3 %collective-permute-start.19 = (bf16[384,512]{1,0:T(8,128)(2,1)S(1)}, bf16[384,512]{1,0:T(8,128)(2,1)}, u32[]{:S(2)}, u32[]{:S(2)}) collective-permute-start(bf16[384,512]{1,0:T(8,128)(2,1)S(1)} %get-tuple-element.105), channel_id=1, source_target_pairs={{0,192},{64,0},{128,64},{192,128},{1,193},{65,1},{129,65},{193,129... | collective-permute-start | bytes 1179656 | tf_op jit(solution)/shard_map/ppermute | solution.py:29
  270.2 18.5 %collective-permute-start.18 = (bf16[384,512]{1,0:T(8,128)(2,1)S(1)}, bf16[384,512]{1,0:T(8,128)(2,1)}, u32[]{:S(2)}, u32[]{:S(2)}) collective-permute-start(bf16[384,512]{1,0:T(8,128)(2,1)S(1)} %get-tuple-element.105), channel_id=1, source_target_pairs={{0,64},{64,128},{128,192},{192,0},{1,65},{65,129},{129,193},{193,1... | collective-permute-start | bytes 1179656 | tf_op jit(solution)/shard_map/ppermute | solution.py:29
  272.0 9.9 %all-to-all-start.8 = ((bf16[8,64,128]{2,1,0:T(8,128)(2,1)}), bf16[8,64,128]{2,1,0:T(8,128)(2,1)S(1)}, u32[]{:S(2)}, u32[]{:S(2)}) async-start(bf16[8,64,128]{2,1,0:T(8,128)(2,1)} %get-tuple-element.112), calls=%async_computation.8 | async-start | bytes 262144 | tf_op jit(solution)/shard_map/all_to_all | solution.py:72
  281.8 0.7 copy-start.24
  284.4 14.0 %collective-permute-start.23 = (bf16[512,512]{1,0:T(8,128)(2,1)}, bf16[512,512]{1,0:T(8,128)(2,1)S(1)}, u32[]{:S(2)}, u32[]{:S(2)}) collective-permute-start(bf16[512,512]{1,0:T(8,128)(2,1)} %join_global_rows.1), channel_id=1, source_target_pairs={{0,192},{64,0},{128,64},{192,128},{1,193},{65,1},{129,65},{193,129... | collective-permute-start | bytes 1572872 | tf_op jit(solution)/shard_map/ppermute | solution.py:29
  286.8 16.8 %collective-permute-start.22 = (bf16[512,512]{1,0:T(8,128)(2,1)}, bf16[512,512]{1,0:T(8,128)(2,1)S(1)}, u32[]{:S(2)}, u32[]{:S(2)}) collective-permute-start(bf16[512,512]{1,0:T(8,128)(2,1)} %join_global_rows.1), channel_id=1, source_target_pairs={{0,64},{64,128},{128,192},{192,0},{1,65},{65,129},{129,193},{193,1... | collective-permute-start | bytes 1572872 | tf_op jit(solution)/shard_map/ppermute | solution.py:29
  288.7 21.2 %collective-permute-start.20 = (bf16[384,512]{1,0:T(8,128)(2,1)}, bf16[384,512]{1,0:T(8,128)(2,1)S(1)}, u32[]{:S(2)}, u32[]{:S(2)}) collective-permute-start(bf16[384,512]{1,0:T(8,128)(2,1)} %collective-permute-done.18), channel_id=1, source_target_pairs={{0,64},{64,128},{128,192},{192,0},{1,65},{65,129},{129,193},{193,1... | collective-permute-start | bytes 1179656 | tf_op jit(solution)/shard_map/ppermute | solution.py:29
  298.3 13.5 %collective-permute-start.24 = (bf16[512,512]{1,0:T(8,128)(2,1)S(1)}, bf16[512,512]{1,0:T(8,128)(2,1)S(1)}, u32[]{:S(2)}, u32[]{:S(2)}) collective-permute-start(bf16[512,512]{1,0:T(8,128)(2,1)S(1)} %collective-permute-done.23), channel_id=1, source_target_pairs={{0,192},{64,0},{128,64},{192,128},{1,193},{65,1},{129,65},{193,129... | collective-permute-start | bytes 1572872 | tf_op jit(solution)/shard_map/ppermute | solution.py:29
  311.8 2.0 copy-start.20

commit v6 on v5

--- a/solution.py
+++ b/solution.py
@@ -42,9 +42,13 @@
                 at = (run * CAP + rank) * 2 * BLOCK
                 out[peer, at : at + BLOCK] = keys[run][rows, cols]
                 out[peer, at + BLOCK : at + 2 * BLOCK] = values[run][rows, cols]
-        if extra:
+        at = n * CAP * 2 * BLOCK
+        if extra and extra[0].shape[0] < BLOCK:
+            few = extra[0].shape[0]
+            for h in range(extra[0].shape[1] // DH):
+                out[peer, at + h * few : at + (h + 1) * few] = extra[0][:, h * DH : (h + 1) * DH]
+        elif extra:
             own = extra[0][pl.ds(pl.multiple_of(peer * BLOCK, BLOCK), BLOCK)].astype(out.dtype)
-            at = n * CAP * 2 * BLOCK
             out[peer, at : at + BLOCK] = own[:, :DH]
             out[peer, at + BLOCK : at + 2 * BLOCK] = own[:, DH:]
         return carry
@@ -54,7 +58,8 @@
 
 def picked(codes, first, blocks, extra=()):
     n = len(blocks) // 2
-    shape = (INPLANE, (n * CAP + len(extra)) * 2 * BLOCK, DH)
+    tail = sum(e.size if e.shape[0] < BLOCK else e.size // INPLANE for e in extra) // DH
+    shape = (INPLANE, n * CAP * 2 * BLOCK + tail, DH)
     size = 2 * (sum(k.size for k in blocks) + INPLANE * n * CAP * 2 * BLOCK * DH)
     vmem = pl.BlockSpec(memory_space=pltpu.VMEM)
     return pl.pallas_call(
@@ -149,51 +154,57 @@
         out[p] = whole
 
 
-def joined_kernel(low, gout, out):
-    rows = low.shape[0]
-    out[:rows] = low[...]
-    for h in range(low.shape[1] // DH):
-        for g in range(GLOBAL):
-            at = rows + g * BLOCK
-            out[at : at + BLOCK, h * DH : (h + 1) * DH] = gout[h * GLOBAL + g]
-
-
-def joined(low, gout):
-    vmem = pl.BlockSpec(memory_space=pltpu.VMEM)
-    return pl.pallas_call(
-        joined_kernel,
-        out_shape=jax.ShapeDtypeStruct((low.shape[0] + GLOBAL * BLOCK, low.shape[1]), low.dtype),
-        in_specs=[vmem, vmem],
-        out_specs=vmem,
-        name="join_global_rows",
-    )(low, gout)
-
-
-def place_kernel(place, top, low, out):
+def times(pieces, weights):
+    total = jnp.dot(pieces[0][...], weights[0][...], preferred_element_type=jnp.float32)
+    for piece, weight in zip(pieces[1:], weights[1:]):
+        total += jnp.dot(piece[...], weight[...], preferred_element_type=jnp.float32)
+    return total.astype(jnp.bfloat16)
+
+
+def upper_kernel(*refs):
+    refs[8][...] = times(refs[:4], refs[4:8])
+
+
+def lower_kernel(place, top, *refs):
+    low, rows, weights, out = refs[:4], refs[4:8], refs[8:12], refs[12]
     half = top.shape[0]
     out[:half] = top[...]
-    out[half:] = low[:half]
+    out[half:] = times(low, weights)
+    replaced = times(rows, weights)
     for g in range(GLOBAL):
 
         @pl.when(place[2 + g] >= 0)
         def _():
             at_rows = pl.ds(pl.multiple_of(place[2 + g] * BLOCK, BLOCK), BLOCK)
-            out[at_rows] = low[half + g * BLOCK : half + (g + 1) * BLOCK]
-
-
-def placed(place, top, low):
-    vmem = pl.BlockSpec(memory_space=pltpu.VMEM)
+            out[at_rows] = replaced[g * BLOCK : (g + 1) * BLOCK]
+
+
+def product(pieces, weights, place=None, top=None, rows=()):
+    features, width = weights[0].shape
+    step = width // 4
+    whole = [pl.BlockSpec(p.shape, lambda i: (0, 0)) for p in (*pieces, *rows)]
+    sliced = [pl.BlockSpec((features, step), lambda i: (0, i))] * 4
+    head = [] if top is None else [place, top]
+    half = pieces[0].shape[0]
+    tall = half if top is None else 2 * half
+    specs = [] if top is None else [
+        pl.BlockSpec(memory_space=pltpu.SMEM), pl.BlockSpec((half, step), lambda i: (0, i))
+    ]
     return pl.pallas_call(
-        place_kernel,
-        out_shape=jax.ShapeDtypeStruct((2 * top.shape[0], top.shape[1]), top.dtype),
-        in_specs=[pl.BlockSpec(memory_space=pltpu.SMEM), vmem, vmem],
-        out_specs=vmem,
-        compiler_params=pltpu.CompilerParams(vmem_limit_bytes=16 * 2**20),
-        name="place_global_rows",
-    )(place, top, low)
-
-
-def attend_kernel(counts, slots, place, q, k, v, before, after, glob, *refs):
+        upper_kernel if top is None else lower_kernel,
+        out_shape=jax.ShapeDtypeStruct((tall, width), jnp.bfloat16),
+        grid=(4,),
+        in_specs=specs + whole + sliced,
+        out_specs=pl.BlockSpec((tall, step), lambda i: (0, i)),
+        compiler_params=pltpu.CompilerParams(vmem_limit_bytes=32 * 2**20),
+        cost_estimate=pl.CostEstimate(
+            flops=8 * half * features * width, bytes_accessed=8 * 2**20, transcendentals=0
+        ),
+        name="upper_product" if top is None else "lower_product",
+    )(*head, *pieces, *rows, *weights)
+
+
+def attend_kernel(counts, slots, place, q, k, v, before, after, *refs):
     n = len(counts)
     arrived, acc, stats, held, sems = refs[:n], refs[n], refs[n + 1], refs[n + 2], refs[n + 3]
     kpad, vpad = refs[n + 4], refs[n + 5]
@@ -217,51 +228,65 @@
     scale = DH ** (-0.5)
     col = lax.broadcasted_iota(jnp.int32, (1, (3 + RANDOM + GLOBAL) * BLOCK), 1) // BLOCK
     lane = lax.broadcasted_iota(jnp.int32, (BLOCK, DH), 1)
+    few = GLOBAL * 2 * BLOCK // INPLANE
 
     def one_block(b, carry):
         at_rows = pl.ds(pl.multiple_of(b * BLOCK, BLOCK), BLOCK)
         win_rows = pl.ds(pl.multiple_of(b * BLOCK, BLOCK), 3 * BLOCK)
         number = place[0] + b
         outside = jnp.where(number == 0, 0, -1), jnp.where(number == place[1] - 1, 2, -1)
-        for h in range(heads):
-            hs = slice(h * DH, (h + 1) * DH)
-            picks = []
-            bias = jnp.where((col == outside[0]) | (col == outside[1]), -jnp.inf, 0.0)
-            for r in range(RANDOM):
-                slot = slots[(h * blocks + b) * RANDOM + r]
-                late = ((slot >> 2) & 7) == PLANES - 1
-                bias = jnp.where(col == jnp.where(late, 3 + r, -1), -jnp.inf, bias)
-                slot = jnp.where(late, 0, slot)
-                picks.append((slot >> 5, pl.multiple_of((slot & 31) * 2 * BLOCK, 2 * BLOCK)))
-            keys = jnp.concatenate(
-                [kpad[win_rows, hs]]
-                + [held[p[0], pl.ds(p[1], BLOCK)] for p in picks]
-                + [glob[g, 0, :, hs] for g in range(GLOBAL)],
-                axis=0,
-            )
-            values = jnp.concatenate(
-                [vpad[win_rows, hs]]
-                + [held[p[0], pl.ds(p[1] + BLOCK, BLOCK)] for p in picks]
-                + [glob[g, 1, :, hs] for g in range(GLOBAL)],
-                axis=0,
-            )
-            scores = lax.dot_general(
-                q[at_rows, hs], keys, (((1,), (1,)), ((), ())),
-                preferred_element_type=jnp.float32,
-            ) * scale + bias
-            peak = jnp.max(scores, axis=1, keepdims=True)
-            weights = jnp.exp(scores - peak)
-            total = jnp.sum(weights, axis=1, keepdims=True)
-            acc[at_rows, hs] = jnp.dot(
-                weights.astype(jnp.bfloat16), values, preferred_element_type=jnp.float32
-            )
-            stats[h, at_rows] = jnp.where(lane < DH // 2, peak, total)
+        for pair in range(0, heads, 2):
+            both = range(pair, pair + 2)
+            found, scores = [], []
+            for h in both:
+                hs = slice(h * DH, (h + 1) * DH)
+                picks = []
+                bias = jnp.where((col == outside[0]) | (col == outside[1]), -jnp.inf, 0.0)
+                for r in range(RANDOM):
+                    slot = slots[(h * blocks + b) * RANDOM + r]
+                    late = ((slot >> 2) & 7) == PLANES - 1
+                    bias = jnp.where(col == jnp.where(late, 3 + r, -1), -jnp.inf, bias)
+                    slot = jnp.where(late, 0, slot)
+                    picks.append((slot >> 5, pl.multiple_of((slot & 31) * 2 * BLOCK, 2 * BLOCK)))
+                found.append(picks)
+                at = sum(counts) + (h - heads) * few
+                keys = jnp.concatenate(
+                    [kpad[win_rows, hs]]
+                    + [held[p[0], pl.ds(p[1], BLOCK)] for p in picks]
+                    + [held[4 * g + i, at : at + few] for g in range(GLOBAL) for i in range(2)],
+                    axis=0,
+                )
+                scores.append(
+                    lax.dot_general(
+                        q[at_rows, hs], keys, (((1,), (1,)), ((), ())),
+                        preferred_element_type=jnp.float32,
+                    ) * scale + bias
+                )
+            peaks = [jnp.max(own, axis=1, keepdims=True) for own in scores]
+            weights = [jnp.exp(own - peak) for own, peak in zip(scores, peaks)]
+            totals = [jnp.sum(own, axis=1, keepdims=True) for own in weights]
+            sums = []
+            for h, picks, own in zip(both, found, weights):
+                hs = slice(h * DH, (h + 1) * DH)
+                at = sum(counts) + (h - heads) * few
+                values = jnp.concatenate(
+                    [vpad[win_rows, hs]]
+                    + [held[p[0], pl.ds(p[1] + BLOCK, BLOCK)] for p in picks]
+                    + [held[4 * g + 2 + i, at : at + few] for g in range(GLOBAL) for i in range(2)],
+                    axis=0,
+                )
+                sums.append(
+                    jnp.dot(own.astype(jnp.bfloat16), values, preferred_element_type=jnp.float32)
+                )
+            for h, own, peak, total in zip(both, sums, peaks, totals):
+                acc[at_rows, h * DH : (h + 1) * DH] = own
+                stats[h, at_rows] = jnp.where(lane < DH // 2, peak, total)
         return carry
 
     lax.fori_loop(0, blocks, one_block, 0)
 
 
-def attended(slots, place, q, k, v, before, after, glob, arrived):
+def attended(slots, place, q, k, v, before, after, arrived):
     rows, features = q.shape
     counts = tuple(a.shape[1] for a in arrived)
     vmem = pl.BlockSpec(memory_space=pltpu.VMEM)
@@ -272,7 +297,7 @@
             jax.ShapeDtypeStruct((rows, features), jnp.float32),
             jax.ShapeDtypeStruct((features // DH, rows, DH), jnp.float32),
         ),
-        in_specs=[smem, smem] + [vmem] * 6 + [pl.BlockSpec(memory_space=pl.ANY)] * len(arrived),
+        in_specs=[smem, smem] + [vmem] * 5 + [pl.BlockSpec(memory_space=pl.ANY)] * len(arrived),
         out_specs=(vmem, vmem),
         scratch_shapes=[
             pltpu.VMEM((INPLANE, sum(counts), DH), jnp.bfloat16),
@@ -285,7 +310,7 @@
             flops=4 * rows * features * 512, bytes_accessed=COST, transcendentals=rows * 4 * 512
         ),
         name="attend",
-    )(slots, place, q, k, v, before, after, glob, *arrived)
+    )(slots, place, q, k, v, before, after, *arrived)
 
 
 def finish_kernel(late, q, acc, stats, blocks_late, top, low, gout, summed, held):
@@ -294,35 +319,43 @@
     summed[...] = acc[...]
     held[...] = stats[...]
 
-    def one_late(i, carry):
-        code = late[i]
-
-        @pl.when(code >= 0)
-        def _():
-            h = code >> 4
-            at_rows = pl.ds(pl.multiple_of((code & 15) * BLOCK, BLOCK), BLOCK)
-            cols = pl.ds(pl.multiple_of(h * DH, DH), DH)
-            at = pl.multiple_of((i & (CAP - 1)) * 2 * BLOCK, 2 * BLOCK)
-            peer = i // CAP
+    def one_peer(peer, carry):
+        found = []
+        for rank in range(CAP):
+            code = late[peer * CAP + rank]
+            near = jnp.maximum(code, 0)
+            at_rows = pl.ds(pl.multiple_of((near & 15) * BLOCK, BLOCK), BLOCK)
+            cols = pl.ds(pl.multiple_of((near >> 4) * DH, DH), DH)
             scores = lax.dot_general(
-                q[at_rows, cols], blocks_late[peer, pl.ds(at, BLOCK)], (((1,), (1,)), ((), ())),
-                preferred_element_type=jnp.float32,
+                q[at_rows, cols], blocks_late[peer, 2 * rank * BLOCK : (2 * rank + 1) * BLOCK],
+                (((1,), (1,)), ((), ())), preferred_element_type=jnp.float32,
             ) * scale
-            before = held[h, at_rows, 0:1]
-            peak = jnp.maximum(before, jnp.max(scores, axis=1, keepdims=True))
-            weights = jnp.exp(scores - peak)
-            less = jnp.exp(before - peak)
-            total = held[h, at_rows, DH // 2 : DH // 2 + 1] * less
-            total += jnp.sum(weights, axis=1, keepdims=True)
-            summed[at_rows, cols] = summed[at_rows, cols] * less + jnp.dot(
-                weights.astype(jnp.bfloat16), blocks_late[peer, pl.ds(at + BLOCK, BLOCK)],
+            found.append((code, near >> 4, at_rows, cols, scores))
+        peaks = [jnp.max(own[-1], axis=1, keepdims=True) for own in found]
+        weights = [jnp.exp(own[-1] - peak) for own, peak in zip(found, peaks)]
+        totals = [jnp.sum(own, axis=1, keepdims=True) for own in weights]
+        sums = [
+            jnp.dot(
+                own.astype(jnp.bfloat16),
+                blocks_late[peer, (2 * rank + 1) * BLOCK : (2 * rank + 2) * BLOCK],
                 preferred_element_type=jnp.float32,
             )
-            held[h, at_rows] = jnp.where(lane < DH // 2, peak, total)
+            for rank, own in enumerate(weights)
+        ]
+        for (code, h, at_rows, cols, _), peak, total, own in zip(found, peaks, totals, sums):
+
+            @pl.when(code >= 0)
+            def _():
+                before = held[h, at_rows, 0:1]
+                top = jnp.maximum(before, peak)
+                less, more = jnp.exp(before - top), jnp.exp(peak - top)
+                summed[at_rows, cols] = summed[at_rows, cols] * less + own * more
+                both = held[h, at_rows, DH // 2 : DH // 2 + 1] * less + total * more
+                held[h, at_rows] = jnp.where(lane < DH // 2, top, both)
 
         return carry
 
-    lax.fori_loop(0, INPLANE * CAP, one_late, 0)
+    lax.fori_loop(0, INPLANE, one_peer, 0)
     merge_rows(blocks_late, 2 * CAP * BLOCK, gout)
     half = top.shape[0]
     for side, out in enumerate((top, low)):
@@ -423,6 +456,9 @@
     arrived = [over_plane(picks)]
     ahead = [(i, i + 1) for i in range(shards - 1)]
     back = [(j, i) for i, j in ahead]
+    for apart in (1, 2, 4):
+        pairs = [(i, i ^ apart) for i in range(PLANES)]
+        shared = shared + lax.ppermute(shared, "seq_0", pairs)
     first, parts = 1, ()
     beside = [lax.ppermute(ends, SEQ, ahead), lax.ppermute(starts, SEQ, back)]
     held = [up_k, down_k, up_v, down_v]
@@ -432,28 +468,20 @@
             up_k, down_v, _ = lax.optimization_barrier((up_k, down_v, held if step == PLANES // 2 else first_pair))
         up_k = ring_step(up_k, 1)
         down_v = ring_step(down_v, -1)
-        if step > 2:
-            shared, _ = lax.optimization_barrier((shared, arrived[-1]))
-        if step == 3:
-            shared = jnp.broadcast_to(shared[None], (PLANES, *shared.shape))
-            shared = lax.all_to_all(shared, "seq_0", split_axis=0, concat_axis=0, tiled=True)
-            shared = shared.sum(axis=0)
-        elif step == 4:
-            shared = over_plane(jnp.broadcast_to(shared[None], (INPLANE, *shared.shape)))
-            glob = shared.reshape(GLOBAL, 2, BLOCK, features)
         if step < PLANES // 2:
             up_v, down_k, _ = lax.optimization_barrier((up_v, down_k, picks))
         gate = (up_k, down_v) if step < PLANES // 2 else ()
-        held, _, _, tied, parts = lax.optimization_barrier(
-            (held, gate, arrived[-1], beside if step > 2 else (), parts)
+        held, _, _, tied, parts, shared = lax.optimization_barrier(
+            (held, gate, arrived[-1], beside if step > 2 else (), parts, shared)
         )
         if step > 2:
-            weights[step - 2], before, after = tied
+            weights[turn], before, after = tied
         else:
             before, after = beside
-        beside, _ = lax.optimization_barrier((weights[step - 1], held))
-        beside = (across(beside, (1, -1, 2)[step - 2]), before, after)
-        picks = picked(asked, first, held)
+        turn, away = ((3, 2), (1, 1), (2, -1))[step - 2]
+        beside, _ = lax.optimization_barrier((weights[turn], held))
+        beside = (across(beside, away), before, after)
+        picks = picked(asked, first, held, (shared,) if step == PLANES // 2 else ())
         arrived.append(over_plane(picks))
         first += len(held) // 2
         both = held
@@ -466,8 +494,8 @@
             held = [up_k, down_k, up_v, down_v]
         else:
             held = [up_k, down_v]
-    weights[3], before, after = beside
-    held, arrived, parts, glob = lax.optimization_barrier((held, arrived, parts, glob))
+    held, arrived, parts, beside = lax.optimization_barrier((held, arrived, parts, beside))
+    weights[turn], before, after = beside
     parts = (global_parts(asking, held, parts),)
     arrived.append(over_plane(picked(asked, first, held, parts)))
     place = jnp.concatenate(
@@ -477,23 +505,17 @@
         ]
     )
     acc, stats = attended(
-        slots, place, queries, key_vectors, value_vectors, before, after, glob, arrived[:-1]
+        slots, place, queries, key_vectors, value_vectors, before, after, arrived[:-1]
     )
     own_t, own_b, gout = finished(late, queries, acc, stats, arrived[-1])
     right_t, left_t = across(own_t, 1), across(own_t, -1)
-    own_b = joined(own_b, over_plane(gout))
     right_b, left_b = across(own_b, 1), across(own_b, -1)
     far_t, far_b = across(right_t, 1), across(left_b, -1)
-
-    def product(*pieces):
-        total = 0.0
-        for piece, weight in zip(pieces, weights):
-            total = total + jnp.dot(piece, weight, preferred_element_type=jnp.float32)
-        return total.astype(jnp.bfloat16)
-
-    return placed(
-        place, product(own_t, right_t, left_t, far_t), product(own_b, right_b, left_b, far_b)
-    )
+    gout = over_plane(gout).reshape(heads, GLOBAL * BLOCK, DH)
+    gout = gout.transpose(1, 0, 2).reshape(GLOBAL * BLOCK, features)
+    rows_g = (gout, across(gout, 1), across(gout, -1), across(gout, 2))
+    top = product((own_t, right_t, left_t, far_t), weights)
+    return product((own_b, right_b, left_b, far_b), weights, place, top, rows_g)
 
 
 def solution(mesh):

time: 319 us -> 315 us (0.987)
  local copies, waits for them, and re-layouts: 20.1 us -> 38.7 us
  starting transfers between devices: 86 us -> 70.6 us
  matrix products: 14.1 us -> 0 us
  Pallas kernels: 63.5 us -> 52.9 us
  waiting for transfers between devices: 117 us -> 126 us
  blocking collectives: 0 us -> 8.81 us
    all_to_all x8 -> x6, waiting for transfers between devices: 64.3 us -> 22.9 us  [over_plane(): return lax.all_to_all(parts, PLANE, split_axis=0, concat_axis=0, tiled=True)]
    ppermute x0 -> x3, waiting for transfers between devices: none -> 24.7 us  [on_device(): shared = shared + lax.ppermute(shared, 'seq_0', pairs)]
    unnamed x54 -> x97, local copies, waits for them, and re-layouts: 14.1 us -> 34.3 us
    ppermute x9 -> x12, waiting for transfers between devices: 8.4 us -> 25.4 us  [across(): lax.ppermute(shard, 'heads', [(i, (i + step) % peers) for i in range(peer...]
    dot_general x8 -> x0, matrix products: 14.1 us -> none  [product(): total = total + jnp.dot(piece, weight, preferred_element_type=jnp.float32)]
    ppermute x14, waiting for transfers between devices: 40.2 us -> 53.2 us  [ring_step(): lax.ppermute(shard, 'seq_0', [(i, (i + step) % peers) for i in range(peer...]
    all_to_all x8 -> x6, starting transfers between devices: 34.7 us -> 25.6 us  [over_plane(): return lax.all_to_all(parts, PLANE, split_axis=0, concat_axis=0, tiled=True)]
    all_to_all x0 -> x1, blocking collectives: none -> 8.81 us  [over_plane(): return lax.all_to_all(parts, PLANE, split_axis=0, concat_axis=0, tiled=True)]
  transfers between devices with their start and end apart: 34 -> 37, of which waited for: 16 -> 21; matrix products, arithmetic and copies ran while one was open for 10% -> 6% of each run, Pallas kernels for 17% -> 9%
where the time goes in v6:
time: 315 us; the launch traced here: 313 us
  waiting for transfers between devices  126 us (40%)
  starting transfers between devices  70.6 us (22%)
  Pallas kernels  52.9 us (17%)
  local copies, waits for them, and re-layouts  38.7 us (12%)
  other arithmetic  14.2 us (5%)
  blocking collectives  8.81 us (3%)
    ppermute x14, waiting for transfers between devices, ring_step(): lax.ppermute(shard, 'seq_0', [(i, (i + step) % peers) for i in range(peer...  53.2 us
    unnamed x97, local copies, waits for them, and re-layouts  34.3 us
    all_to_all x6, starting transfers between devices, over_plane(): return lax.all_to_all(parts, PLANE, split_axis=0, concat_axis=0, tiled=True)  25.6 us
    ppermute x12, waiting for transfers between devices, across(): lax.ppermute(shard, 'heads', [(i, (i + step) % peers) for i in range(peer...  25.4 us
    ppermute x3, waiting for transfers between devices, on_device(): shared = shared + lax.ppermute(shared, 'seq_0', pairs)  24.7 us
    all_to_all x6, waiting for transfers between devices, over_plane(): return lax.all_to_all(parts, PLANE, split_axis=0, concat_axis=0, tiled=True)  22.9 us
    ppermute x14, starting transfers between devices, ring_step(): lax.ppermute(shard, 'seq_0', [(i, (i + step) % peers) for i in range(peer...  16.7 us
    pallas_call x1, Pallas kernels, attended(): pl.pallas_call(lambda *refs: attend_kernel(counts, *refs), out_shape=(jax...  15.5 us
  transfers between devices with their start and end apart: 37, of which 21 were waited for; matrix products, arithmetic and copies ran while one was open for 6% of the time, Pallas kernels for 9%

profile of v6, /device:TPU:32, one launch (start us, length us, event | category | flops | bytes accessed | tf_op | source)
XLA Modules:
  0.0 313.2 jit_solution(15552225136394013496)
XLA Ops:
  0.0 1.9 collective-permute-start
  6.6 2.1 fusion.14
  8.8 2.1 dynamic-slice_select_fusion.5
  12.1 1.2 fusion.15
  14.2 1.2 fusion.1
  16.2 1.9 constant_dynamic-slice_fusion
  18.1 1.4 collective-permute-done.refs_1_
  19.5 1.9 collective-permute-done.2.refs_4_.refs_5_
  21.4 4.5 %all-to-all-start = ((bf16[8,176,512]{2,1,0:T(8,128)(2,1)}), bf16[8,176,512]{2,1,0:T(8,128)(2,1)}, u32[]{:S(2)}, u32[]{:S(2)}) async-start(bf16[8,176,512]{2,1,0:T(8,128)(2,1)} %fusion.1), calls=%async_computation | async-start | bytes 2883584 | tf_op jit(solution)/shard_map/all_to_all | solution.py:77
  25.9 3.1 collective-permute-start.4
  29.0 17.2 %all-to-all-done = bf16[8,176,512]{2,1,0:T(8,128)(2,1)} async-done(((bf16[8,176,512]{2,1,0:T(8,128)(2,1)}), bf16[8,176,512]{2,1,0:T(8,128)(2,1)}, u32[]{:S(2)}, u32[]{:S(2)}) %all-to-all-start) | async-done | bytes 1441824 | tf_op jit(solution)/shard_map/all_to_all | solution.py:77
  47.0 3.0 collective-permute-done.5.refs_2_
  51.8 4.4 %all-to-all-start.1 = ((bf16[8,512,128]{2,1,0:T(8,128)(2,1)}), bf16[8,512,128]{2,1,0:T(8,128)(2,1)}, u32[]{:S(2)}, u32[]{:S(2)}) async-start(bf16[8,512,128]{2,1,0:T(8,128)(2,1)} %copy-done.10), calls=%async_computation.1 | async-start | bytes 2097152 | tf_op jit(solution)/shard_map/all_to_all | solution.py:77
  56.3 1.7 collective-permute-start.1
  60.2 16.7 %collective-permute-done.10 = bf16[32,512]{1,0:T(8,128)(2,1)S(1)} collective-permute-done((bf16[32,512]{1,0:T(8,128)(2,1)S(1)}, bf16[32,512]{1,0:T(8,128)(2,1)S(1)}, u32[]{:S(2)}, u32[]{:S(2)}) %collective-permute-start.10) | collective-permute-done | bytes 32800 | tf_op jit(solution)/shard_map/ppermute | solution.py:461
  77.0 2.8 collective-permute-start.11
  79.8 2.1 collective-permute-done.11
  81.9 2.2 collective-permute-start.12
  84.1 6.0 %collective-permute-done.12 = bf16[32,512]{1,0:T(8,128)(2,1)S(1)} collective-permute-done((bf16[32,512]{1,0:T(8,128)(2,1)S(1)}, bf16[32,512]{1,0:T(8,128)(2,1)S(1)}, u32[]{:S(2)}, u32[]{:S(2)}) %collective-permute-start.12) | collective-permute-done | bytes 32800 | tf_op jit(solution)/shard_map/ppermute | solution.py:461
  91.6 2.2 pick_blocks.6
  93.8 1.3 copy-done.2
  95.1 4.3 %all-to-all-start.2 = ((bf16[8,1024,128]{2,1,0:T(8,128)(2,1)}), bf16[8,1024,128]{2,1,0:T(8,128)(2,1)}, u32[]{:S(2)}, u32[]{:S(2)}) async-start(bf16[8,1024,128]{2,1,0:T(8,128)(2,1)} %copy-done.2), calls=%async_computation.2 | async-start | bytes 4194304 | tf_op jit(solution)/shard_map/all_to_all | solution.py:77
  99.4 3.1 collective-permute-start.17
  102.5 1.9 collective-permute-start.18
  104.4 5.8 %collective-permute-start.19 = (bf16[128,512]{1,0:T(8,128)(2,1)}, bf16[128,512]{1,0:T(8,128)(2,1)S(1)}, u32[]{:S(2)}, u32[]{:S(2)}) collective-permute-start(bf16[128,512]{1,0:T(8,128)(2,1)} %get-tuple-element.79), channel_id=1, source_target_pairs={{1,0},{2,1},{3,2},{4,3},{5,4},{6,5},{7,6},{8,7},{9,8},{10,9},{11,1... | collective-permute-start | bytes 393224 | tf_op jit(solution)/shard_map/ppermute | solution.py:463
  110.2 3.2 %collective-permute-start.6 = (bf16[768,512]{1,0:T(8,128)(2,1)}, bf16[768,512]{1,0:T(8,128)(2,1)S(1)}, u32[]{:S(2)}, u32[]{:S(2)}) collective-permute-start(bf16[768,512]{1,0:T(8,128)(2,1)} %copy-done.25), channel_id=1, source_target_pairs={{0,8},{8,16},{16,24},{24,32},{32,40},{40,48},{48,56},{56,0},{1,9},... | collective-permute-start | bytes 2359304 | tf_op jit(solution)/shard_map/ppermute | solution.py:24
  113.4 2.0 collective-permute-start.8
  116.1 1.4 slice_reduce_fusion.refs_0_
  117.5 4.1 %global_parts.4.refs_5_ = f32[512,256]{1,0:T(8,128)S(1)} custom-call(bf16[128,512]{1,0:T(8,128)(2,1)S(1)} %slice_reduce_fusion.refs_0_, bf16[768,512]{1,0:T(8,128)(2,1)S(1)} %copy-done.24, bf16[768,512]{1,0:T(8,128)(2,1)} %collective-permute-done.5.refs_2_, bf16[768,512]{1,0:T(8,128)(2,1)S(1)} %copy-done, ...), custom_call_target="tpu_custom_call" | custom-call | flops 603979776 | bytes 25165824 | tf_op jit(solution)/shard_map/global_parts/pallas_call | solution.py:125
  122.4 7.1 %collective-permute-done.6.refs_1_ = bf16[768,512]{1,0:T(8,128)(2,1)S(1)} collective-permute-done((bf16[768,512]{1,0:T(8,128)(2,1)}, bf16[768,512]{1,0:T(8,128)(2,1)S(1)}, u32[]{:S(2)}, u32[]{:S(2)}) %collective-permute-start.6) | collective-permute-done | bytes 786464 | tf_op jit(solution)/shard_map/ppermute | solution.py:24
  129.5 4.3 %collective-permute-done.7.refs_4_ = bf16[768,512]{1,0:T(8,128)(2,1)S(1)} collective-permute-done((bf16[768,512]{1,0:T(8,128)(2,1)}, bf16[768,512]{1,0:T(8,128)(2,1)S(1)}, u32[]{:S(2)}, u32[]{:S(2)}) %collective-permute-start.7) | collective-permute-done | bytes 786464 | tf_op jit(solution)/shard_map/ppermute | solution.py:24
  134.7 11.0 %collective-permute-done.8.refs_3_ = bf16[768,512]{1,0:T(8,128)(2,1)S(1)} collective-permute-done((bf16[768,512]{1,0:T(8,128)(2,1)}, bf16[768,512]{1,0:T(8,128)(2,1)S(1)}, u32[]{:S(2)}, u32[]{:S(2)}) %collective-permute-start.8) | collective-permute-done | bytes 786464 | tf_op jit(solution)/shard_map/ppermute | solution.py:24
  146.6 2.6 collective-permute-done.9.refs_2_
  154.5 1.7 pick_blocks.7
  156.2 1.3 copy-done.3
  157.5 4.3 %all-to-all-start.3 = ((bf16[8,1024,128]{2,1,0:T(8,128)(2,1)}), bf16[8,1024,128]{2,1,0:T(8,128)(2,1)}, u32[]{:S(2)}, u32[]{:S(2)}) async-start(bf16[8,1024,128]{2,1,0:T(8,128)(2,1)} %copy-done.3), calls=%async_computation.3 | async-start | bytes 4194304 | tf_op jit(solution)/shard_map/all_to_all | solution.py:77
  162.6 2.0 collective-permute-start.14
  169.0 3.5 %global_parts.5.refs_5_ = f32[512,256]{1,0:T(8,128)S(1)} custom-call(bf16[128,512]{1,0:T(8,128)(2,1)S(1)} %slice_reduce_fusion.refs_0_, bf16[768,512]{1,0:T(8,128)(2,1)S(1)} %copy-done.27, bf16[768,512]{1,0:T(8,128)(2,1)S(1)} %copy-done.33, bf16[768,512]{1,0:T(8,128)(2,1)S(1)} %copy-done.30, bf16[768,512]{1,0:T(8,128)(2,1)} %collective-permute-done.3.refs_4_, ...), custom_call_target="tpu_custom_call" | custom-call | flops 402653184 | bytes 25165824 | tf_op jit(solution)/shard_map/global_parts/pallas_call | solution.py:125
  173.3 8.9 %collective-permute-done.13.refs_2_ = bf16[768,512]{1,0:T(8,128)(2,1)S(1)} collective-permute-done((bf16[768,512]{1,0:T(8,128)(2,1)}, bf16[768,512]{1,0:T(8,128)(2,1)S(1)}, u32[]{:S(2)}, u32[]{:S(2)}) %collective-permute-start.13) | collective-permute-done | bytes 786464 | tf_op jit(solution)/shard_map/ppermute | solution.py:24
  183.5 5.2 %collective-permute-done.20.refs_5_.refs_9_ = bf16[512,1024]{1,0:T(8,128)(2,1)S(1)} collective-permute-done((bf16[512,1024]{1,0:T(8,128)(2,1)}, bf16[512,1024]{1,0:T(8,128)(2,1)S(1)}, u32[]{:S(2)}, u32[]{:S(2)}) %collective-permute-start.20) | collective-permute-done | bytes 1048608 | tf_op jit(solution)/shard_map/ppermute | solution.py:29
  189.7 1.1 copy-done.15
  191.6 2.6 pick_blocks.8
  194.2 4.5 %all-to-all-start.4 = ((bf16[8,1152,128]{2,1,0:T(8,128)(2,1)}), bf16[8,1152,128]{2,1,0:T(8,128)(2,1)}, u32[]{:S(2)}, u32[]{:S(2)}) async-start(bf16[8,1152,128]{2,1,0:T(8,128)(2,1)} %pick_blocks.8), calls=%async_computation.4 | async-start | bytes 4718592 | tf_op jit(solution)/shard_map/all_to_all | solution.py:77
  199.2 1.5 collective-permute-start.15
  203.4 2.3 global_parts.6.refs_3_
  206.5 12.1 %collective-permute-done.15.refs_1_ = bf16[768,512]{1,0:T(8,128)(2,1)S(1)} collective-permute-done((bf16[768,512]{1,0:T(8,128)(2,1)S(1)}, bf16[768,512]{1,0:T(8,128)(2,1)S(1)}, u32[]{:S(2)}, u32[]{:S(2)}) %collective-permute-start.15) | collective-permute-done | bytes 786464 | tf_op jit(solution)/shard_map/ppermute | solution.py:24
  220.8 3.7 %collective-permute-done.21.refs_6_.refs_10_ = bf16[512,1024]{1,0:T(8,128)(2,1)S(1)} collective-permute-done((bf16[512,1024]{1,0:T(8,128)(2,1)}, bf16[512,1024]{1,0:T(8,128)(2,1)S(1)}, u32[]{:S(2)}, u32[]{:S(2)}) %collective-permute-start.21) | collective-permute-done | bytes 1048608 | tf_op jit(solution)/shard_map/ppermute | solution.py:29
  225.4 3.4 %all-to-all-done.4.refs_10_ = bf16[8,1152,128]{2,1,0:T(8,128)(2,1)} async-done(((bf16[8,1152,128]{2,1,0:T(8,128)(2,1)}), bf16[8,1152,128]{2,1,0:T(8,128)(2,1)}, u32[]{:S(2)}, u32[]{:S(2)}) %all-to-all-start.4) | async-done | bytes 2359328 | tf_op jit(solution)/shard_map/all_to_all | solution.py:77
  232.1 1.9 global_parts.7.refs_3_
  234.0 2.0 pick_blocks.9
  236.0 3.6 %all-to-all-start.5 = ((bf16[8,640,128]{2,1,0:T(8,128)(2,1)}), bf16[8,640,128]{2,1,0:T(8,128)(2,1)S(1)}, u32[]{:S(2)}, u32[]{:S(2)}) async-start(bf16[8,640,128]{2,1,0:T(8,128)(2,1)} %pick_blocks.9), calls=%async_computation.5 | async-start | bytes 2621440 | tf_op jit(solution)/shard_map/all_to_all | solution.py:77
  240.4 15.5 %attend.1 = (f32[768,512]{1,0:T(8,128)}, f32[4,768,128]{2,1,0:T(8,128)}) custom-call(s32[144]{0:T(256)} %copy-done.47, s32[4]{0:T(128)} %pad_add_fusion.refs_1_.place, bf16[768,512]{1,0:T(8,128)(2,1)} %q.1, bf16[768,512]{1,0:T(8,128)(2,1)} %refs_3_.3, bf16[768,512]{1,0:T(8,128)(2,1)} %refs_4_.1, bf16[128,512]{1,0:T(8,128)(2,1)} %copy-done.45, ...), custom_call_target="tpu_custom_call" | custom-call | flops 805306368 | bytes 25165824 | tf_op jit(solution)/shard_map/attend/pallas_call | solution.py:294
  255.9 2.4 all-to-all-done.5.blocks_late
  258.2 1.4 copy-done.40
  259.7 1.4 copy-done.41
  261.1 8.4 %late_blocks.1 = (bf16[384,512]{1,0:T(8,128)(2,1)S(1)}, bf16[384,512]{1,0:T(8,128)(2,1)S(1)}, bf16[8,64,128]{2,1,0:T(8,128)(2,1)S(1)}) custom-call(s32[32]{0:T(128)S(1)} %reshape_squeeze.3.late, bf16[768,512]{1,0:T(8,128)(2,1)S(1)} %copy-done.11, f32[768,512]{1,0:T(8,128)S(1)} %copy-done.40, f32[4,768,128]{2,1,0:T(8,128)S(1)} %copy-done.41, ...), custom_call_target="tpu_custom_call" | custom-call | tf_op jit(solution)/shard_map/late_blocks/pallas_call | solution.py:379
  270.1 2.6 collective-permute-start.26
  272.8 9.5 %collective-permute-done.22.refs_1_ = bf16[384,512]{1,0:T(8,128)(2,1)S(1)} collective-permute-done((bf16[384,512]{1,0:T(8,128)(2,1)S(1)}, bf16[384,512]{1,0:T(8,128)(2,1)S(1)}, u32[]{:S(2)}, u32[]{:S(2)}) %collective-permute-start.22) | collective-permute-done | bytes 393248 | tf_op jit(solution)/shard_map/ppermute | solution.py:29
  282.2 3.7 %collective-permute-start.27 = (bf16[384,512]{1,0:T(8,128)(2,1)S(1)}, bf16[384,512]{1,0:T(8,128)(2,1)S(1)}, u32[]{:S(2)}, u32[]{:S(2)}) collective-permute-start(bf16[384,512]{1,0:T(8,128)(2,1)S(1)} %collective-permute-done.26.refs_2_), channel_id=1, source_target_pairs={{0,192},{64,0},{128,64},{192,128},{1,193},{65,1},{129,65},{193,129... | collective-permute-start | bytes 1179656 | tf_op jit(solution)/shard_map/ppermute | solution.py:29
  285.9 8.8 %all_to_all.35 = bf16[8,64,128]{2,1,0:T(8,128)(2,1)S(1)} all-to-all(bf16[8,64,128]{2,1,0:T(8,128)(2,1)S(1)} %get-tuple-element.118), channel_id=1, replica_groups=mesh['heads'=4,'seq_0'=8,'seq_1'=4,'seq_2'=2] {'seq_1','seq_2'}, dimensions={0} | all-to-all | bytes 262144 | tf_op jit(solution)/shard_map/all_to_all | solution.py:77
  295.0 3.2 %collective-permute-start.29 = (bf16[128,512]{1,0:T(8,128)(2,1)S(1)}, bf16[128,512]{1,0:T(8,128)(2,1)S(1)}, u32[]{:S(2)}, u32[]{:S(2)}) collective-permute-start(bf16[128,512]{1,0:T(8,128)(2,1)S(1)} %bitcast.13), channel_id=1, source_target_pairs={{0,192},{64,0},{128,64},{192,128},{1,193},{65,1},{129,65},{193,129... | collective-permute-start | bytes 393224 | tf_op jit(solution)/shard_map/ppermute | solution.py:29
  298.2 3.0 upper_product.1.top
  301.2 7.0 %collective-permute-done.28.refs_5_ = bf16[128,512]{1,0:T(8,128)(2,1)S(1)} collective-permute-done((bf16[128,512]{1,0:T(8,128)(2,1)S(1)}, bf16[128,512]{1,0:T(8,128)(2,1)S(1)}, u32[]{:S(2)}, u32[]{:S(2)}) %collective-permute-start.28) | collective-permute-done | bytes 131104 | tf_op jit(solution)/shard_map/ppermute | solution.py:29
  308.3 4.9 %lower_product.1 = bf16[768,1024]{1,0:T(8,128)(2,1)} custom-call(s32[4]{0:T(128)S(1)} %copy-done.43, bf16[384,1024]{1,0:T(8,128)(2,1)S(1)} %upper_product.1.top, bf16[384,512]{1,0:T(8,128)(2,1)S(1)} %get-tuple-element.117.refs_0_, bf16[384,512]{1,0:T(8,128)(2,1)S(1)} %collective-permute-done.25.refs_1_, ...), custom_call_target="tpu_custom_call" | custom-call | flops 1610612736 | bytes 8388608 | tf_op jit(solution)/shard_map/lower_product/pallas_call | solution.py:193
  (160 shorter events, 42.3 us)
Async XLA Ops:
  0.0 12.1 %copy-start.1 = (bf16[768,512]{1,0:T(8,128)(2,1)S(1)}, bf16[768,512]{1,0:T(8,128)(2,1)}, u32[]{:S(2)}) copy-start(bf16[768,512]{1,0:T(8,128)(2,1)} %refs_4_.1) | copy-start | bytes 2359300
  0.0 19.5 %collective-permute-start = (bf16[768,512]{1,0:T(8,128)(2,1)}, bf16[768,512]{1,0:T(8,128)(2,1)S(1)}, u32[]{:S(2)}, u32[]{:S(2)}) collective-permute-start(bf16[768,512]{1,0:T(8,128)(2,1)} %refs_3_.3), channel_id=1, source_target_pairs={{0,8},{8,16},{16,24},{24,32},{32,40},{40,48},{48,56},{56,0},{1,9},... | collective-permute-start | bytes 2359304 | tf_op jit(solution)/shard_map/ppermute | solution.py:24
  1.9 19.5 %collective-permute-start.2 = (bf16[768,512]{1,0:T(8,128)(2,1)}, bf16[768,512]{1,0:T(8,128)(2,1)}, u32[]{:S(2)}, u32[]{:S(2)}) collective-permute-start(bf16[768,512]{1,0:T(8,128)(2,1)} %refs_4_.1), channel_id=1, source_target_pairs={{0,56},{8,0},{16,8},{24,16},{32,24},{40,32},{48,40},{56,48},{1,57}... | collective-permute-start | bytes 2359304 | tf_op jit(solution)/shard_map/ppermute | solution.py:24
  11.8 3.6 %copy-start.47 = (s32[144]{0:T(256)}, s32[144]{0:T(256)S(1)}, u32[]{:S(2)}) copy-start(s32[144]{0:T(256)S(1)} %multiply_add_fusion.refs_0_) | copy-start | bytes 1732
  13.4 2.8 copy-start.44
  18.1 11.0 %copy-start = (bf16[768,512]{1,0:T(8,128)(2,1)S(1)}, bf16[768,512]{1,0:T(8,128)(2,1)}, u32[]{:S(2)}) copy-start(bf16[768,512]{1,0:T(8,128)(2,1)} %refs_3_.3) | copy-start | bytes 2359300
  19.5 72.1 %copy-start.23 = (bf16[768,512]{1,0:T(8,128)(2,1)}, bf16[768,512]{1,0:T(8,128)(2,1)S(1)}, u32[]{:S(2)}) copy-start(bf16[768,512]{1,0:T(8,128)(2,1)S(1)} %collective-permute-done.refs_1_) | copy-start | bytes 2359300
  21.4 24.8 %all-to-all-start = ((bf16[8,176,512]{2,1,0:T(8,128)(2,1)}), bf16[8,176,512]{2,1,0:T(8,128)(2,1)}, u32[]{:S(2)}, u32[]{:S(2)}) async-start(bf16[8,176,512]{2,1,0:T(8,128)(2,1)} %fusion.1), calls=%async_computation | async-start | bytes 2883584 | tf_op jit(solution)/shard_map/all_to_all | solution.py:77
  25.9 21.1 %collective-permute-start.4 = (bf16[768,512]{1,0:T(8,128)(2,1)S(1)}, bf16[768,512]{1,0:T(8,128)(2,1)}, u32[]{:S(2)}, u32[]{:S(2)}) collective-permute-start(bf16[768,512]{1,0:T(8,128)(2,1)S(1)} %copy-done.1), channel_id=1, source_target_pairs={{0,8},{8,16},{16,24},{24,32},{32,40},{40,48},{48,56},{56,0},{1,9},... | collective-permute-start | bytes 2359304 | tf_op jit(solution)/shard_map/ppermute | solution.py:24
  29.0 21.0 %collective-permute-start.5 = (bf16[768,512]{1,0:T(8,128)(2,1)S(1)}, bf16[768,512]{1,0:T(8,128)(2,1)}, u32[]{:S(2)}, u32[]{:S(2)}) collective-permute-start(bf16[768,512]{1,0:T(8,128)(2,1)S(1)} %copy-done), channel_id=1, source_target_pairs={{0,56},{8,0},{16,8},{24,16},{32,24},{40,32},{48,40},{56,48},{1,57}... | collective-permute-start | bytes 2359304 | tf_op jit(solution)/shard_map/ppermute | solution.py:24
  51.8 39.7 %all-to-all-start.1 = ((bf16[8,512,128]{2,1,0:T(8,128)(2,1)}), bf16[8,512,128]{2,1,0:T(8,128)(2,1)}, u32[]{:S(2)}, u32[]{:S(2)}) async-start(bf16[8,512,128]{2,1,0:T(8,128)(2,1)} %copy-done.10), calls=%async_computation.1 | async-start | bytes 2097152 | tf_op jit(solution)/shard_map/all_to_all | solution.py:77
  56.3 34.4 %collective-permute-start.1 = (bf16[768,512]{1,0:T(8,128)(2,1)S(1)}, bf16[768,512]{1,0:T(8,128)(2,1)S(1)}, u32[]{:S(2)}, u32[]{:S(2)}) collective-permute-start(bf16[768,512]{1,0:T(8,128)(2,1)S(1)} %collective-permute-done.refs_1_), channel_id=1, source_target_pairs={{0,8},{8,16},{16,24},{24,32},{32,40},{40,48},{48,56},{56,0},{1,9},... | collective-permute-start | bytes 2359304 | tf_op jit(solution)/shard_map/ppermute | solution.py:24
  58.0 33.5 %collective-permute-start.3 = (bf16[768,512]{1,0:T(8,128)(2,1)}, bf16[768,512]{1,0:T(8,128)(2,1)}, u32[]{:S(2)}, u32[]{:S(2)}) collective-permute-start(bf16[768,512]{1,0:T(8,128)(2,1)} %collective-permute-done.2.refs_4_.refs_5_), channel_id=1, source_target_pairs={{0,56},{8,0},{16,8},{24,16},{32,24},{40,32},{48,40},{56,48},{1,57}... | collective-permute-start | bytes 2359304 | tf_op jit(solution)/shard_map/ppermute | solution.py:24
  59.3 17.6 %collective-permute-start.10 = (bf16[32,512]{1,0:T(8,128)(2,1)S(1)}, bf16[32,512]{1,0:T(8,128)(2,1)S(1)}, u32[]{:S(2)}, u32[]{:S(2)}) collective-permute-start(bf16[32,512]{1,0:T(8,128)(2,1)S(1)} %slice_reduce_fusion.1), channel_id=1, source_target_pairs={{0,8},{8,0},{16,24},{24,16},{32,40},{40,32},{48,56},{56,48},{1,9},... | collective-permute-start | bytes 98312 | tf_op jit(solution)/shard_map/ppermute | solution.py:461
  77.0 4.9 %collective-permute-start.11 = (bf16[32,512]{1,0:T(8,128)(2,1)S(1)}, bf16[32,512]{1,0:T(8,128)(2,1)S(1)}, u32[]{:S(2)}, u32[]{:S(2)}) collective-permute-start(bf16[32,512]{1,0:T(8,128)(2,1)S(1)} %add.194), channel_id=1, source_target_pairs={{0,16},{8,24},{16,0},{24,8},{32,48},{40,56},{48,32},{56,40},{1,17}... | collective-permute-start | bytes 98312 | tf_op jit(solution)/shard_map/ppermute | solution.py:461
  81.9 8.2 %collective-permute-start.12 = (bf16[32,512]{1,0:T(8,128)(2,1)S(1)}, bf16[32,512]{1,0:T(8,128)(2,1)S(1)}, u32[]{:S(2)}, u32[]{:S(2)}) collective-permute-start(bf16[32,512]{1,0:T(8,128)(2,1)S(1)} %add.195), channel_id=1, source_target_pairs={{0,32},{8,40},{16,48},{24,56},{32,0},{40,8},{48,16},{56,24},{1,33}... | collective-permute-start | bytes 98312 | tf_op jit(solution)/shard_map/ppermute | solution.py:461
  93.8 1.3 copy-start.2
  95.1 56.0 %all-to-all-start.2 = ((bf16[8,1024,128]{2,1,0:T(8,128)(2,1)}), bf16[8,1024,128]{2,1,0:T(8,128)(2,1)}, u32[]{:S(2)}, u32[]{:S(2)}) async-start(bf16[8,1024,128]{2,1,0:T(8,128)(2,1)} %copy-done.2), calls=%async_computation.2 | async-start | bytes 4194304 | tf_op jit(solution)/shard_map/all_to_all | solution.py:77
  99.4 18.0 %copy-start.24 = (bf16[768,512]{1,0:T(8,128)(2,1)S(1)}, bf16[768,512]{1,0:T(8,128)(2,1)}, u32[]{:S(2)}) copy-start(bf16[768,512]{1,0:T(8,128)(2,1)} %copy-done.23) | copy-start | bytes 2359300
  99.4 50.7 %collective-permute-start.17 = (bf16[512,1024]{1,0:T(8,128)(2,1)}, bf16[512,1024]{1,0:T(8,128)(2,1)S(1)}, u32[]{:S(2)}, u32[]{:S(2)}) collective-permute-start(bf16[512,1024]{1,0:T(8,128)(2,1)} %get-tuple-element.77), channel_id=1, source_target_pairs={{0,128},{64,192},{128,0},{192,64},{1,129},{65,193},{129,1},{193,65... | collective-permute-start | bytes 3145736 | tf_op jit(solution)/shard_map/ppermute | solution.py:29
  102.5 10.8 %collective-permute-start.18 = (bf16[128,512]{1,0:T(8,128)(2,1)}, bf16[128,512]{1,0:T(8,128)(2,1)S(1)}, u32[]{:S(2)}, u32[]{:S(2)}) collective-permute-start(bf16[128,512]{1,0:T(8,128)(2,1)} %get-tuple-element.78), channel_id=1, source_target_pairs={{0,1},{1,2},{2,3},{3,4},{4,5},{5,6},{6,7},{7,8},{8,9},{9,10},{10,1... | collective-permute-start | bytes 393224 | tf_op jit(solution)/shard_map/ppermute | solution.py:463
  104.4 11.0 %collective-permute-start.19 = (bf16[128,512]{1,0:T(8,128)(2,1)}, bf16[128,512]{1,0:T(8,128)(2,1)S(1)}, u32[]{:S(2)}, u32[]{:S(2)}) collective-permute-start(bf16[128,512]{1,0:T(8,128)(2,1)} %get-tuple-element.79), channel_id=1, source_target_pairs={{1,0},{2,1},{3,2},{4,3},{5,4},{6,5},{7,6},{8,7},{9,8},{10,9},{11,1... | collective-permute-start | bytes 393224 | tf_op jit(solution)/shard_map/ppermute | solution.py:463
  110.2 19.2 %collective-permute-start.6 = (bf16[768,512]{1,0:T(8,128)(2,1)}, bf16[768,512]{1,0:T(8,128)(2,1)S(1)}, u32[]{:S(2)}, u32[]{:S(2)}) collective-permute-start(bf16[768,512]{1,0:T(8,128)(2,1)} %copy-done.25), channel_id=1, source_target_pairs={{0,8},{8,16},{16,24},{24,32},{32,40},{40,48},{48,56},{56,0},{1,9},... | collective-permute-start | bytes 2359304 | tf_op jit(solution)/shard_map/ppermute | solution.py:24
  113.4 20.4 %collective-permute-start.7 = (bf16[768,512]{1,0:T(8,128)(2,1)}, bf16[768,512]{1,0:T(8,128)(2,1)S(1)}, u32[]{:S(2)}, u32[]{:S(2)}) collective-permute-start(bf16[768,512]{1,0:T(8,128)(2,1)} %collective-permute-done.3.refs_4_), channel_id=1, source_target_pairs={{0,56},{8,0},{16,8},{24,16},{32,24},{40,32},{48,40},{56,48},{1,57}... | collective-permute-start | bytes 2359304 | tf_op jit(solution)/shard_map/ppermute | solution.py:24
  113.4 2.0 copy-start.45
  113.4 32.3 %collective-permute-start.8 = (bf16[768,512]{1,0:T(8,128)(2,1)}, bf16[768,512]{1,0:T(8,128)(2,1)S(1)}, u32[]{:S(2)}, u32[]{:S(2)}) collective-permute-start(bf16[768,512]{1,0:T(8,128)(2,1)} %collective-permute-done.4.refs_3_.refs_4_), channel_id=1, source_target_pairs={{0,8},{8,16},{16,24},{24,32},{32,40},{40,48},{48,56},{56,0},{1,9},... | collective-permute-start | bytes 2359304 | tf_op jit(solution)/shard_map/ppermute | solution.py:24
  115.4 33.8 %collective-permute-start.9 = (bf16[768,512]{1,0:T(8,128)(2,1)}, bf16[768,512]{1,0:T(8,128)(2,1)S(1)}, u32[]{:S(2)}, u32[]{:S(2)}) collective-permute-start(bf16[768,512]{1,0:T(8,128)(2,1)} %collective-permute-done.5.refs_2_), channel_id=1, source_target_pairs={{0,56},{8,0},{16,8},{24,16},{32,24},{40,32},{48,40},{56,48},{1,57}... | collective-permute-start | bytes 2359304 | tf_op jit(solution)/shard_map/ppermute | solution.py:24
  151.1 1.1 copy-start.26
  152.2 1.1 copy-start.29
  153.4 1.1 copy-start.32
  156.2 1.3 copy-start.3
  157.5 32.2 %all-to-all-start.3 = ((bf16[8,1024,128]{2,1,0:T(8,128)(2,1)}), bf16[8,1024,128]{2,1,0:T(8,128)(2,1)}, u32[]{:S(2)}, u32[]{:S(2)}) async-start(bf16[8,1024,128]{2,1,0:T(8,128)(2,1)} %copy-done.3), calls=%async_computation.3 | async-start | bytes 4194304 | tf_op jit(solution)/shard_map/all_to_all | solution.py:77
  161.9 27.8 %copy-start.13 = (bf16[768,512]{1,0:T(8,128)(2,1)S(1)}, bf16[768,512]{1,0:T(8,128)(2,1)}, u32[]{:S(2)}) copy-start(bf16[768,512]{1,0:T(8,128)(2,1)} %copy-done.12) | copy-start | bytes 2359300
  161.9 26.9 %collective-permute-start.20 = (bf16[512,1024]{1,0:T(8,128)(2,1)}, bf16[512,1024]{1,0:T(8,128)(2,1)S(1)}, u32[]{:S(2)}, u32[]{:S(2)}) collective-permute-start(bf16[512,1024]{1,0:T(8,128)(2,1)} %get-tuple-element.86), channel_id=1, source_target_pairs={{0,64},{64,128},{128,192},{192,0},{1,65},{65,129},{129,193},{193,1... | collective-permute-start | bytes 3145736 | tf_op jit(solution)/shard_map/ppermute | solution.py:29
  162.6 19.7 %collective-permute-start.13 = (bf16[768,512]{1,0:T(8,128)(2,1)}, bf16[768,512]{1,0:T(8,128)(2,1)S(1)}, u32[]{:S(2)}, u32[]{:S(2)}) collective-permute-start(bf16[768,512]{1,0:T(8,128)(2,1)} %copy-done.31), channel_id=1, source_target_pairs={{0,56},{8,0},{16,8},{24,16},{32,24},{40,32},{48,40},{56,48},{1,57}... | collective-permute-start | bytes 2359304 | tf_op jit(solution)/shard_map/ppermute | solution.py:24
  162.6 20.1 %collective-permute-start.14 = (bf16[768,512]{1,0:T(8,128)(2,1)}, bf16[768,512]{1,0:T(8,128)(2,1)S(1)}, u32[]{:S(2)}, u32[]{:S(2)}) collective-permute-start(bf16[768,512]{1,0:T(8,128)(2,1)} %copy-done.28), channel_id=1, source_target_pairs={{0,8},{8,16},{16,24},{24,32},{32,40},{40,48},{48,56},{56,0},{1,9},... | collective-permute-start | bytes 2359304 | tf_op jit(solution)/shard_map/ppermute | solution.py:24
  164.6 1.1 copy-start.27
  165.7 1.1 copy-start.30
  166.9 1.1 copy-start.33
  189.7 1.1 copy-start.15
  194.2 34.6 %all-to-all-start.4 = ((bf16[8,1152,128]{2,1,0:T(8,128)(2,1)}), bf16[8,1152,128]{2,1,0:T(8,128)(2,1)}, u32[]{:S(2)}, u32[]{:S(2)}) async-start(bf16[8,1152,128]{2,1,0:T(8,128)(2,1)} %pick_blocks.8), calls=%async_computation.4 | async-start | bytes 4718592 | tf_op jit(solution)/shard_map/all_to_all | solution.py:77
  198.7 25.8 %collective-permute-start.21 = (bf16[512,1024]{1,0:T(8,128)(2,1)}, bf16[512,1024]{1,0:T(8,128)(2,1)S(1)}, u32[]{:S(2)}, u32[]{:S(2)}) collective-permute-start(bf16[512,1024]{1,0:T(8,128)(2,1)} %get-tuple-element.98), channel_id=1, source_target_pairs={{0,192},{64,0},{128,64},{192,128},{1,193},{65,1},{129,65},{193,129... | collective-permute-start | bytes 3145736 | tf_op jit(solution)/shard_map/ppermute | solution.py:29
  199.2 19.5 %collective-permute-start.15 = (bf16[768,512]{1,0:T(8,128)(2,1)S(1)}, bf16[768,512]{1,0:T(8,128)(2,1)S(1)}, u32[]{:S(2)}, u32[]{:S(2)}) collective-permute-start(bf16[768,512]{1,0:T(8,128)(2,1)S(1)} %collective-permute-done.6.refs_1_), channel_id=1, source_target_pairs={{0,8},{8,16},{16,24},{24,32},{32,40},{40,48},{48,56},{56,0},{1,9},... | collective-permute-start | bytes 2359304 | tf_op jit(solution)/shard_map/ppermute | solution.py:24
  200.7 19.2 %collective-permute-start.16 = (bf16[768,512]{1,0:T(8,128)(2,1)S(1)}, bf16[768,512]{1,0:T(8,128)(2,1)S(1)}, u32[]{:S(2)}, u32[]{:S(2)}) collective-permute-start(bf16[768,512]{1,0:T(8,128)(2,1)S(1)} %copy-done.13), channel_id=1, source_target_pairs={{0,56},{8,0},{16,8},{24,16},{32,24},{40,32},{48,40},{56,48},{1,57}... | collective-permute-start | bytes 2359304 | tf_op jit(solution)/shard_map/ppermute | solution.py:24
  228.8 1.1 copy-start.18
  232.1 1.9 copy-start.19
  232.1 1.9 copy-start.22
  236.0 22.3 %all-to-all-start.5 = ((bf16[8,640,128]{2,1,0:T(8,128)(2,1)}), bf16[8,640,128]{2,1,0:T(8,128)(2,1)S(1)}, u32[]{:S(2)}, u32[]{:S(2)}) async-start(bf16[8,640,128]{2,1,0:T(8,128)(2,1)} %pick_blocks.9), calls=%async_computation.5 | async-start | bytes 2621440 | tf_op jit(solution)/shard_map/all_to_all | solution.py:77
  240.4 17.9 %copy-start.11 = (bf16[768,512]{1,0:T(8,128)(2,1)S(1)}, bf16[768,512]{1,0:T(8,128)(2,1)}, u32[]{:S(2)}) copy-start(bf16[768,512]{1,0:T(8,128)(2,1)} %q.1) | copy-start | bytes 2359300
  258.2 1.4 copy-start.40
  259.7 1.4 copy-start.41
  261.1 37.1 %copy-start.5 = (bf16[512,1024]{1,0:T(8,128)(2,1)S(1)}, bf16[512,1024]{1,0:T(8,128)(2,1)}, u32[]{:S(2)}) copy-start(bf16[512,1024]{1,0:T(8,128)(2,1)} %copy-done.4) | copy-start | bytes 3145732
  261.1 37.1 %copy-start.7 = (bf16[512,1024]{1,0:T(8,128)(2,1)S(1)}, bf16[512,1024]{1,0:T(8,128)(2,1)}, u32[]{:S(2)}) copy-start(bf16[512,1024]{1,0:T(8,128)(2,1)} %copy-done.6) | copy-start | bytes 3145732
  261.1 37.1 %copy-start.9 = (bf16[512,1024]{1,0:T(8,128)(2,1)S(1)}, bf16[512,1024]{1,0:T(8,128)(2,1)}, u32[]{:S(2)}) copy-start(bf16[512,1024]{1,0:T(8,128)(2,1)} %copy-done.8) | copy-start | bytes 3145732
  269.4 12.8 %collective-permute-start.22 = (bf16[384,512]{1,0:T(8,128)(2,1)S(1)}, bf16[384,512]{1,0:T(8,128)(2,1)S(1)}, u32[]{:S(2)}, u32[]{:S(2)}) collective-permute-start(bf16[384,512]{1,0:T(8,128)(2,1)S(1)} %get-tuple-element.112.refs_0_), channel_id=1, source_target_pairs={{0,64},{64,128},{128,192},{192,0},{1,65},{65,129},{129,193},{193,1... | collective-permute-start | bytes 1179656 | tf_op jit(solution)/shard_map/ppermute | solution.py:29
  270.1 12.1 %collective-permute-start.26 = (bf16[384,512]{1,0:T(8,128)(2,1)S(1)}, bf16[384,512]{1,0:T(8,128)(2,1)S(1)}, u32[]{:S(2)}, u32[]{:S(2)}) collective-permute-start(bf16[384,512]{1,0:T(8,128)(2,1)S(1)} %get-tuple-element.117.refs_0_), channel_id=1, source_target_pairs={{0,192},{64,0},{128,64},{192,128},{1,193},{65,1},{129,65},{193,129... | collective-permute-start | bytes 1179656 | tf_op jit(solution)/shard_map/ppermute | solution.py:29
  272.7 22.2 %collective-permute-start.23 = (bf16[384,512]{1,0:T(8,128)(2,1)S(1)}, bf16[384,512]{1,0:T(8,128)(2,1)S(1)}, u32[]{:S(2)}, u32[]{:S(2)}) collective-permute-start(bf16[384,512]{1,0:T(8,128)(2,1)S(1)} %get-tuple-element.112.refs_0_), channel_id=1, source_target_pairs={{0,192},{64,0},{128,64},{192,128},{1,193},{65,1},{129,65},{193,129... | collective-permute-start | bytes 1179656 | tf_op jit(solution)/shard_map/ppermute | solution.py:29
  282.2 15.9 %collective-permute-start.24 = (bf16[384,512]{1,0:T(8,128)(2,1)S(1)}, bf16[384,512]{1,0:T(8,128)(2,1)S(1)}, u32[]{:S(2)}, u32[]{:S(2)}) collective-permute-start(bf16[384,512]{1,0:T(8,128)(2,1)S(1)} %collective-permute-done.22.refs_1_), channel_id=1, source_target_pairs={{0,64},{64,128},{128,192},{192,0},{1,65},{65,129},{129,193},{193,1... | collective-permute-start | bytes 1179656 | tf_op jit(solution)/shard_map/ppermute | solution.py:29
  282.2 26.0 %collective-permute-start.25 = (bf16[384,512]{1,0:T(8,128)(2,1)S(1)}, bf16[384,512]{1,0:T(8,128)(2,1)S(1)}, u32[]{:S(2)}, u32[]{:S(2)}) collective-permute-start(bf16[384,512]{1,0:T(8,128)(2,1)S(1)} %get-tuple-element.117.refs_0_), channel_id=1, source_target_pairs={{0,64},{64,128},{128,192},{192,0},{1,65},{65,129},{129,193},{193,1... | collective-permute-start | bytes 1179656 | tf_op jit(solution)/shard_map/ppermute | solution.py:29
  282.2 26.0 %collective-permute-start.27 = (bf16[384,512]{1,0:T(8,128)(2,1)S(1)}, bf16[384,512]{1,0:T(8,128)(2,1)S(1)}, u32[]{:S(2)}, u32[]{:S(2)}) collective-permute-start(bf16[384,512]{1,0:T(8,128)(2,1)S(1)} %collective-permute-done.26.refs_2_), channel_id=1, source_target_pairs={{0,192},{64,0},{128,64},{192,128},{1,193},{65,1},{129,65},{193,129... | collective-permute-start | bytes 1179656 | tf_op jit(solution)/shard_map/ppermute | solution.py:29
  294.8 13.4 %copy-start.43 = (s32[4]{0:T(128)S(1)}, s32[4]{0:T(128)}, u32[]{:S(2)}) copy-start(s32[4]{0:T(128)} %pad_add_fusion.refs_1_.place) | copy-start | bytes 52
  294.9 13.4 %collective-permute-start.28 = (bf16[128,512]{1,0:T(8,128)(2,1)S(1)}, bf16[128,512]{1,0:T(8,128)(2,1)S(1)}, u32[]{:S(2)}, u32[]{:S(2)}) collective-permute-start(bf16[128,512]{1,0:T(8,128)(2,1)S(1)} %bitcast.12), channel_id=1, source_target_pairs={{0,64},{64,128},{128,192},{192,0},{1,65},{65,129},{129,193},{193,1... | collective-permute-start | bytes 393224 | tf_op jit(solution)/shard_map/ppermute | solution.py:29
  295.0 13.3 %collective-permute-start.29 = (bf16[128,512]{1,0:T(8,128)(2,1)S(1)}, bf16[128,512]{1,0:T(8,128)(2,1)S(1)}, u32[]{:S(2)}, u32[]{:S(2)}) collective-permute-start(bf16[128,512]{1,0:T(8,128)(2,1)S(1)} %bitcast.13), channel_id=1, source_target_pairs={{0,192},{64,0},{128,64},{192,128},{1,193},{65,1},{129,65},{193,129... | collective-permute-start | bytes 393224 | tf_op jit(solution)/shard_map/ppermute | solution.py:29
  298.2 10.1 %collective-permute-start.30 = (bf16[128,512]{1,0:T(8,128)(2,1)S(1)}, bf16[128,512]{1,0:T(8,128)(2,1)S(1)}, u32[]{:S(2)}, u32[]{:S(2)}) collective-permute-start(bf16[128,512]{1,0:T(8,128)(2,1)S(1)} %bitcast.14), channel_id=1, source_target_pairs={{0,128},{64,192},{128,0},{192,64},{1,129},{65,193},{129,1},{193,65... | collective-permute-start | bytes 393224 | tf_op jit(solution)/shard_map/ppermute | solution.py:29
  (21 other events, 19.4 us)

commit v7 on v6

--- a/solution.py
+++ b/solution.py
@@ -135,9 +135,9 @@
     )(asking, *blocks, *held)
 
 
-def merge_rows(parts, first, out):
+def merge_kernel(parts, out):
     peers = parts.shape[0]
-    sums, side = slice(first, first + BLOCK), slice(first + BLOCK, first + 2 * BLOCK)
+    sums, side = slice(0, BLOCK), slice(BLOCK, 2 * BLOCK)
     tops = [parts[p, side, 0:1].astype(jnp.float32) for p in range(peers)]
     top = tops[0]
     for other in tops[1:]:
@@ -152,6 +152,18 @@
     whole = (part / total).astype(jnp.bfloat16)
     for p in range(peers):
         out[p] = whole
+
+
+def merged(parts):
+    peers, rows, _ = parts.shape
+    return pl.pallas_call(
+        merge_kernel,
+        out_shape=jax.ShapeDtypeStruct((peers, BLOCK, DH), jnp.bfloat16),
+        grid=(1,),
+        in_specs=[pl.BlockSpec((peers, 2 * BLOCK, DH), lambda i: (0, rows // (2 * BLOCK) - 1, 0))],
+        out_specs=pl.BlockSpec((peers, BLOCK, DH), lambda i: (0, 0, 0)),
+        name="merge_parts",
+    )(parts)
 
 
 def times(pieces, weights):
@@ -313,7 +325,7 @@
     )(slots, place, q, k, v, before, after, *arrived)
 
 
-def finish_kernel(late, q, acc, stats, blocks_late, top, low, gout, summed, held):
+def finish_kernel(late, q, acc, stats, blocks_late, top, low, summed, held):
     scale = DH ** (-0.5)
     lane = lax.broadcasted_iota(jnp.int32, (BLOCK, DH), 1)
     summed[...] = acc[...]
@@ -356,7 +368,6 @@
         return carry
 
     lax.fori_loop(0, INPLANE, one_peer, 0)
-    merge_rows(blocks_late, 2 * CAP * BLOCK, gout)
     half = top.shape[0]
     for side, out in enumerate((top, low)):
 
@@ -378,14 +389,15 @@
     half = jax.ShapeDtypeStruct((rows // 2, features), jnp.bfloat16)
     return pl.pallas_call(
         finish_kernel,
-        out_shape=(half, half, jax.ShapeDtypeStruct((INPLANE, BLOCK, DH), jnp.bfloat16)),
+        out_shape=(half, half),
         in_specs=[pl.BlockSpec(memory_space=pltpu.SMEM)] + [vmem] * 4,
-        out_specs=(vmem, vmem, vmem),
+        out_specs=(vmem, vmem),
         scratch_shapes=[
             pltpu.VMEM(acc.shape, jnp.float32),
             pltpu.VMEM(stats.shape, jnp.float32),
         ],
         compiler_params=pltpu.CompilerParams(vmem_limit_bytes=32 * 2**20),
+        cost_estimate=pl.CostEstimate(flops=0, bytes_accessed=COST, transcendentals=0),
         name="late_blocks",
     )(late, q, acc, stats, blocks_late)
 
@@ -451,53 +463,59 @@
     shared = found[:, many:-16].sum(axis=0)
     asked = found[:, -16, : PLANES * CAP].astype(jnp.int32).reshape(-1)
 
-    asked, _, _ = lax.optimization_barrier((asked, up_v, down_k))
+    firsts, seconds = [(up_k, down_v)], [(up_v, down_k)]
+    for step in range(2, PLANES // 2 + 1):
+        up, down = firsts[-1]
+        if step == 3:
+            up, down, _ = lax.optimization_barrier((up, down, seconds[0]))
+        firsts.append((ring_step(up, 1), ring_step(down, -1)))
+        if step < PLANES // 2:
+            up, down = seconds[-1]
+            seconds.append((ring_step(up, 1), ring_step(down, -1)))
+    ahead = [(i, i + 1) for i in range(shards - 1)]
+    back = [(j, i) for i, j in ahead]
+    before, after = lax.ppermute(ends, SEQ, ahead), lax.ppermute(starts, SEQ, back)
+
+    def doubled(own, apart, when):
+        own, _ = lax.optimization_barrier((own, when))
+        return own + lax.ppermute(own, "seq_0", [(i, i ^ apart) for i in range(PLANES)])
+
+    def spread(turn, away, when):
+        piece, _ = lax.optimization_barrier((weights[turn], when))
+        return across(piece, away)
+
+    asked, before, after, _ = lax.optimization_barrier((asked, before, after, firsts[1]))
     picks = picked(asked, 0, [key_vectors, value_vectors])
     arrived = [over_plane(picks)]
-    ahead = [(i, i + 1) for i in range(shards - 1)]
-    back = [(j, i) for i, j in ahead]
-    for apart in (1, 2, 4):
-        pairs = [(i, i ^ apart) for i in range(PLANES)]
-        shared = shared + lax.ppermute(shared, "seq_0", pairs)
+    shared = doubled(shared, 1, seconds[0])
+    weights[3] = spread(3, 2, seconds[0])
     first, parts = 1, ()
-    beside = [lax.ppermute(ends, SEQ, ahead), lax.ppermute(starts, SEQ, back)]
-    held = [up_k, down_k, up_v, down_v]
-    first_pair = (up_v, down_k)
-    for step in range(2, PLANES // 2 + 1):
-        if step > 2:
-            up_k, down_v, _ = lax.optimization_barrier((up_k, down_v, held if step == PLANES // 2 else first_pair))
-        up_k = ring_step(up_k, 1)
-        down_v = ring_step(down_v, -1)
-        if step < PLANES // 2:
-            up_v, down_k, _ = lax.optimization_barrier((up_v, down_k, picks))
-        gate = (up_k, down_v) if step < PLANES // 2 else ()
-        held, _, _, tied, parts, shared = lax.optimization_barrier(
-            (held, gate, arrived[-1], beside if step > 2 else (), parts, shared)
+    for step in range(1, PLANES // 2):
+        (up_k, down_v), (up_v, down_k) = firsts[step - 1], seconds[step - 1]
+        held = [up_k, down_k, up_v, down_v]
+        held, _, _, parts, shared = lax.optimization_barrier(
+            (held, firsts[min(step + 1, PLANES // 2 - 1)], picks, parts, shared)
         )
-        if step > 2:
-            weights[turn], before, after = tied
-        else:
-            before, after = beside
-        turn, away = ((3, 2), (1, 1), (2, -1))[step - 2]
-        beside, _ = lax.optimization_barrier((weights[turn], held))
-        beside = (across(beside, away), before, after)
-        picks = picked(asked, first, held, (shared,) if step == PLANES // 2 else ())
+        if step == 2:
+            weights[3], held = lax.optimization_barrier((weights[3], held))
+            weights[1] = spread(1, 1, firsts[2])
+        elif step == 3:
+            weights[1], held = lax.optimization_barrier((weights[1], held))
+            weights[2] = spread(2, -1, seconds[1])
+        picks = picked(asked, first, held, (shared,) if step == 3 else ())
         arrived.append(over_plane(picks))
         first += len(held) // 2
-        both = held
-        if step == 2:
-            both = [*held[:2], key_vectors, *held[2:], value_vectors]
-        parts = (global_parts(asking, both, parts),)
-        if step < PLANES // 2:
-            up_v = ring_step(up_v, 1)
-            down_k = ring_step(down_k, -1)
-            held = [up_k, down_k, up_v, down_v]
-        else:
-            held = [up_k, down_v]
-    held, arrived, parts, beside = lax.optimization_barrier((held, arrived, parts, beside))
-    weights[turn], before, after = beside
+        if step == 1:
+            held = [*held[:2], key_vectors, *held[2:], value_vectors]
+        parts = (global_parts(asking, held, parts),)
+        if step < 3:
+            shared = doubled(shared, 2 * step, firsts[step])
+    held, arrived, parts, weights[2] = lax.optimization_barrier(
+        (list(firsts[-1]), arrived, parts, weights[2])
+    )
     parts = (global_parts(asking, held, parts),)
     arrived.append(over_plane(picked(asked, first, held, parts)))
+
     place = jnp.concatenate(
         [
             jnp.stack([my_index * blocks, jnp.int32(shards * blocks)]).astype(jnp.int32),
@@ -507,12 +525,16 @@
     acc, stats = attended(
         slots, place, queries, key_vectors, value_vectors, before, after, arrived[:-1]
     )
-    own_t, own_b, gout = finished(late, queries, acc, stats, arrived[-1])
+    arrived[-1], acc = lax.optimization_barrier((arrived[-1], acc))
+    rows_here = merged(arrived[-1])
+    gout = over_plane(rows_here)
+    arrived[-1], _ = lax.optimization_barrier((arrived[-1], rows_here))
+    own_t, own_b = finished(late, queries, acc, stats, arrived[-1])
+    own_t, own_b, gout = lax.optimization_barrier((own_t, own_b, gout))
     right_t, left_t = across(own_t, 1), across(own_t, -1)
     right_b, left_b = across(own_b, 1), across(own_b, -1)
     far_t, far_b = across(right_t, 1), across(left_b, -1)
-    gout = over_plane(gout).reshape(heads, GLOBAL * BLOCK, DH)
-    gout = gout.transpose(1, 0, 2).reshape(GLOBAL * BLOCK, features)
+    gout = gout.reshape(heads, -1, DH).transpose(1, 0, 2).reshape(-1, features)
     rows_g = (gout, across(gout, 1), across(gout, -1), across(gout, 2))
     top = product((own_t, right_t, left_t, far_t), weights)
     return product((own_b, right_b, left_b, far_b), weights, place, top, rows_g)

time: 315 us -> 329 us (1.044)
  waiting for transfers between devices: 126 us -> 138 us
  blocking collectives: 8.81 us -> 0 us
  starting transfers between devices: 70.6 us -> 76.3 us
  Pallas kernels: 52.9 us -> 56.5 us
    ppermute x5, waiting for transfers between devices: 24.7 us -> 63.6 us  [the longest x1 33.2 us: on_device(): lax.ppermute(ends, SEQ, ahead)]
    ppermute x14, waiting for transfers between devices: 53.2 us -> 27.9 us  [ring_step(): lax.ppermute(shard, 'seq_0', [(i, (i + step) % peers) for i in range(peer...]
    all_to_all x6 -> x7, waiting for transfers between devices: 22.9 us -> 5.83 us  [over_plane(): return lax.all_to_all(parts, PLANE, split_axis=0, concat_axis=0, tiled=True)]
    ppermute x12, waiting for transfers between devices: 25.4 us -> 41.2 us  [across(): lax.ppermute(shard, 'heads', [(i, (i + step) % peers) for i in range(peer...]
    all_to_all x1 -> x0, blocking collectives: 8.81 us -> none  [over_plane(): return lax.all_to_all(parts, PLANE, split_axis=0, concat_axis=0, tiled=True)]
    all_to_all x6 -> x7, starting transfers between devices: 25.6 us -> 31.1 us  [over_plane(): return lax.all_to_all(parts, PLANE, split_axis=0, concat_axis=0, tiled=True)]
    unnamed x97 -> x87, local copies, waits for them, and re-layouts: 34.3 us -> 31.5 us
    pallas_call x1 -> x2, Pallas kernels: 8.35 us -> 10.1 us  [the longest x1 7.99 us: finished(): pl.pallas_call(finish_kernel, out_shape=(half, half), in_specs=[pl.BlockS...]
  transfers between devices with their start and end apart: 37 -> 38, of which waited for: 21 -> 17; matrix products, arithmetic and copies ran while one was open for 6% -> 6% of each run, Pallas kernels for 9% -> 14%
where the time goes in v7:
time: 329 us; the launch traced here: 325 us
  waiting for transfers between devices  138 us (42%)
  starting transfers between devices  76.3 us (23%)
  Pallas kernels  56.5 us (17%)
  local copies, waits for them, and re-layouts  35.9 us (11%)
  other arithmetic  15.9 us (5%)
    ppermute x12, waiting for transfers between devices, across(): lax.ppermute(shard, 'heads', [(i, (i + step) % peers) for i in range(peer...  41.2 us
    ppermute x1, waiting for transfers between devices, on_device(): lax.ppermute(ends, SEQ, ahead)  33.2 us
    unnamed x87, local copies, waits for them, and re-layouts  31.5 us
    all_to_all x7, starting transfers between devices, over_plane(): return lax.all_to_all(parts, PLANE, split_axis=0, concat_axis=0, tiled=True)  31.1 us
    ppermute x3, waiting for transfers between devices, doubled(): lax.ppermute(own, 'seq_0', [(i, i ^ apart) for i in range(PLANES)])  28.4 us
    ppermute x14, waiting for transfers between devices, ring_step(): lax.ppermute(shard, 'seq_0', [(i, (i + step) % peers) for i in range(peer...  27.9 us
    ppermute x14, starting transfers between devices, ring_step(): lax.ppermute(shard, 'seq_0', [(i, (i + step) % peers) for i in range(peer...  18 us
    ppermute x12, starting transfers between devices, across(): lax.ppermute(shard, 'heads', [(i, (i + step) % peers) for i in range(peer...  15.8 us
  transfers between devices with their start and end apart: 38, of which 17 were waited for; matrix products, arithmetic and copies ran while one was open for 6% of the time, Pallas kernels for 14%

profile of v7, /device:TPU:32, one launch (start us, length us, event | category | flops | bytes accessed | tf_op | source)
XLA Modules:
  0.0 324.9 jit_solution(16927553971290764912)
XLA Ops:
  0.0 1.9 collective-permute-start
  2.0 1.2 broadcast_select_fusion
  7.2 2.3 fusion.14
  9.5 2.2 dynamic-slice_select_fusion.5
  13.0 1.3 fusion.15
  15.1 1.2 fusion.1
  17.1 1.9 constant_dynamic-slice_fusion
  19.5 1.9 collective-permute-done.1.refs_4_.refs_5_
  21.4 4.5 %all-to-all-start = ((bf16[8,176,512]{2,1,0:T(8,128)(2,1)}), bf16[8,176,512]{2,1,0:T(8,128)(2,1)}, u32[]{:S(2)}, u32[]{:S(2)}) async-start(bf16[8,176,512]{2,1,0:T(8,128)(2,1)} %fusion.1), calls=%async_computation | async-start | bytes 2883584 | tf_op jit(solution)/shard_map/all_to_all | solution.py:77
  25.9 3.1 collective-permute-start.4
  29.0 3.0 collective-permute-start.6
  32.0 1.9 collective-permute-start.2
  33.9 33.2 %collective-permute-done.2.refs_5_ = bf16[128,512]{1,0:T(8,128)(2,1)} collective-permute-done((bf16[128,512]{1,0:T(8,128)(2,1)S(1)}, bf16[128,512]{1,0:T(8,128)(2,1)}, u32[]{:S(2)}, u32[]{:S(2)}) %collective-permute-start.2) | collective-permute-done | bytes 131104 | tf_op jit(solution)/shard_map/ppermute | solution.py:477
  67.1 1.9 collective-permute-start.3
  69.8 2.0 collective-permute-done.3.refs_6_
  73.7 6.3 %all-to-all-start.1 = ((bf16[8,512,128]{2,1,0:T(8,128)(2,1)}), bf16[8,512,128]{2,1,0:T(8,128)(2,1)}, u32[]{:S(2)}, u32[]{:S(2)}) async-start(bf16[8,512,128]{2,1,0:T(8,128)(2,1)} %copy-done.13), calls=%async_computation.1 | async-start | bytes 2097152 | tf_op jit(solution)/shard_map/all_to_all | solution.py:77
  80.0 3.0 collective-permute-start.8
  84.2 17.4 %collective-permute-done.12 = bf16[32,512]{1,0:T(8,128)(2,1)S(1)} collective-permute-done((bf16[32,512]{1,0:T(8,128)(2,1)S(1)}, bf16[32,512]{1,0:T(8,128)(2,1)S(1)}, u32[]{:S(2)}, u32[]{:S(2)}) %collective-permute-start.12) | collective-permute-done | bytes 32800 | tf_op jit(solution)/shard_map/ppermute | solution.py:481
  102.8 2.2 pick_blocks.6
  105.0 1.3 copy-done.4
  106.3 4.5 %all-to-all-start.2 = ((bf16[8,1024,128]{2,1,0:T(8,128)(2,1)}), bf16[8,1024,128]{2,1,0:T(8,128)(2,1)}, u32[]{:S(2)}, u32[]{:S(2)}) async-start(bf16[8,1024,128]{2,1,0:T(8,128)(2,1)} %copy-done.4), calls=%async_computation.2 | async-start | bytes 4194304 | tf_op jit(solution)/shard_map/all_to_all | solution.py:77
  110.8 3.1 collective-permute-start.13
  113.9 3.6 %collective-permute-start.16 = (bf16[32,512]{1,0:T(8,128)(2,1)S(1)}, bf16[32,512]{1,0:T(8,128)(2,1)S(1)}, u32[]{:S(2)}, u32[]{:S(2)}) collective-permute-start(bf16[32,512]{1,0:T(8,128)(2,1)S(1)} %add.194), channel_id=1, source_target_pairs={{0,16},{8,24},{16,0},{24,8},{32,48},{40,56},{48,32},{56,40},{1,17}... | collective-permute-start | bytes 98312 | tf_op jit(solution)/shard_map/ppermute | solution.py:481
  117.6 2.0 collective-permute-start.15
  120.3 1.3 collective-permute-start.9
  121.5 1.4 slice_reduce_fusion.refs_0_
  122.9 4.1 %global_parts.4.refs_5_ = f32[512,256]{1,0:T(8,128)S(1)} custom-call(bf16[128,512]{1,0:T(8,128)(2,1)S(1)} %slice_reduce_fusion.refs_0_, bf16[768,512]{1,0:T(8,128)(2,1)S(1)} %copy-done.25, bf16[768,512]{1,0:T(8,128)(2,1)} %collective-permute-done.7.refs_2_, bf16[768,512]{1,0:T(8,128)(2,1)S(1)} %copy-done.2, ...), custom_call_target="tpu_custom_call" | custom-call | flops 603979776 | bytes 25165824 | tf_op jit(solution)/shard_map/global_parts/pallas_call | solution.py:125
  128.5 9.7 %collective-permute-done.14.refs_2_ = bf16[768,512]{1,0:T(8,128)(2,1)} collective-permute-done((bf16[768,512]{1,0:T(8,128)(2,1)}, bf16[768,512]{1,0:T(8,128)(2,1)}, u32[]{:S(2)}, u32[]{:S(2)}) %collective-permute-start.14) | collective-permute-done | bytes 786464 | tf_op jit(solution)/shard_map/ppermute | solution.py:24
  139.0 14.9 %collective-permute-done.11.refs_2_ = bf16[768,512]{1,0:T(8,128)(2,1)S(1)} collective-permute-done((bf16[768,512]{1,0:T(8,128)(2,1)S(1)}, bf16[768,512]{1,0:T(8,128)(2,1)S(1)}, u32[]{:S(2)}, u32[]{:S(2)}) %collective-permute-start.11) | collective-permute-done | bytes 786464 | tf_op jit(solution)/shard_map/ppermute | solution.py:24
  156.7 2.4 pick_blocks.7
  159.1 1.3 copy-done.5
  160.4 4.4 %all-to-all-start.3 = ((bf16[8,1024,128]{2,1,0:T(8,128)(2,1)}), bf16[8,1024,128]{2,1,0:T(8,128)(2,1)}, u32[]{:S(2)}, u32[]{:S(2)}) async-start(bf16[8,1024,128]{2,1,0:T(8,128)(2,1)} %copy-done.5), calls=%async_computation.3 | async-start | bytes 4194304 | tf_op jit(solution)/shard_map/all_to_all | solution.py:77
  165.5 2.8 collective-permute-start.18
  168.2 3.8 %collective-permute-start.20 = (bf16[32,512]{1,0:T(8,128)(2,1)}, bf16[32,512]{1,0:T(8,128)(2,1)S(1)}, u32[]{:S(2)}, u32[]{:S(2)}) collective-permute-start(bf16[32,512]{1,0:T(8,128)(2,1)} %add.195), channel_id=1, source_target_pairs={{0,32},{8,40},{16,48},{24,56},{32,0},{40,8},{48,16},{56,24},{1,33}... | collective-permute-start | bytes 98312 | tf_op jit(solution)/shard_map/ppermute | solution.py:481
  173.1 4.2 %global_parts.5.refs_5_ = f32[512,256]{1,0:T(8,128)S(1)} custom-call(bf16[128,512]{1,0:T(8,128)(2,1)S(1)} %slice_reduce_fusion.refs_0_, bf16[768,512]{1,0:T(8,128)(2,1)} %collective-permute-done.4.refs_1_, bf16[768,512]{1,0:T(8,128)(2,1)} %collective-permute-done.14.refs_2_, bf16[768,512]{1,0:T(8,128)(2,1)} %collective-permute-done.15.refs_3_, ...), custom_call_target="tpu_custom_call" | custom-call | flops 402653184 | bytes 25165824 | tf_op jit(solution)/shard_map/global_parts/pallas_call | solution.py:125
  178.1 11.0 %collective-permute-done.20 = bf16[32,512]{1,0:T(8,128)(2,1)S(1)} collective-permute-done((bf16[32,512]{1,0:T(8,128)(2,1)}, bf16[32,512]{1,0:T(8,128)(2,1)S(1)}, u32[]{:S(2)}, u32[]{:S(2)}) %collective-permute-start.20) | collective-permute-done | bytes 32800 | tf_op jit(solution)/shard_map/ppermute | solution.py:481
  189.8 2.0 collective-permute-done.17.refs_5_.refs_9_
  192.8 3.1 pick_blocks.8
  197.8 4.4 %all-to-all-start.4 = ((bf16[8,1152,128]{2,1,0:T(8,128)(2,1)}), bf16[8,1152,128]{2,1,0:T(8,128)(2,1)}, u32[]{:S(2)}, u32[]{:S(2)}) async-start(bf16[8,1152,128]{2,1,0:T(8,128)(2,1)} %pick_blocks.8), calls=%async_computation.4 | async-start | bytes 4718592 | tf_op jit(solution)/shard_map/all_to_all | solution.py:77
  202.3 1.2 collective-permute-start.21
  206.8 3.5 %global_parts.6.refs_3_ = f32[512,256]{1,0:T(8,128)S(1)} custom-call(bf16[128,512]{1,0:T(8,128)(2,1)S(1)} %slice_reduce_fusion.refs_0_, bf16[768,512]{1,0:T(8,128)(2,1)} %collective-permute-done.8.refs_1_, bf16[768,512]{1,0:T(8,128)(2,1)S(1)} %copy-done.20, bf16[768,512]{1,0:T(8,128)(2,1)S(1)} %copy-done.22, ...), custom_call_target="tpu_custom_call" | custom-call | flops 402653184 | bytes 25165824 | tf_op jit(solution)/shard_map/global_parts/pallas_call | solution.py:125
  211.1 17.0 %collective-permute-done.21.refs_6_.refs_10_ = bf16[512,1024]{1,0:T(8,128)(2,1)S(1)} collective-permute-done((bf16[512,1024]{1,0:T(8,128)(2,1)}, bf16[512,1024]{1,0:T(8,128)(2,1)S(1)}, u32[]{:S(2)}, u32[]{:S(2)}) %collective-permute-start.21) | collective-permute-done | bytes 1048608 | tf_op jit(solution)/shard_map/ppermute | solution.py:29
  229.0 3.4 %all-to-all-done.4.refs_10_ = bf16[8,1152,128]{2,1,0:T(8,128)(2,1)} async-done(((bf16[8,1152,128]{2,1,0:T(8,128)(2,1)}), bf16[8,1152,128]{2,1,0:T(8,128)(2,1)}, u32[]{:S(2)}, u32[]{:S(2)}) %all-to-all-start.4) | async-done | bytes 2359328 | tf_op jit(solution)/shard_map/all_to_all | solution.py:77
  234.6 1.9 global_parts.7.refs_3_
  238.3 3.7 %all-to-all-start.5 = ((bf16[8,640,128]{2,1,0:T(8,128)(2,1)}), bf16[8,640,128]{2,1,0:T(8,128)(2,1)S(1)}, u32[]{:S(2)}, u32[]{:S(2)}) async-start(bf16[8,640,128]{2,1,0:T(8,128)(2,1)} %copy-done.6), calls=%async_computation.5 | async-start | bytes 2621440 | tf_op jit(solution)/shard_map/all_to_all | solution.py:77
  242.8 15.4 %attend.1 = (f32[768,512]{1,0:T(8,128)}, f32[4,768,128]{2,1,0:T(8,128)}) custom-call(s32[144]{0:T(256)} %copy-done.41, s32[4]{0:T(128)} %pad_add_fusion.refs_1_.place, bf16[768,512]{1,0:T(8,128)(2,1)} %q.1, bf16[768,512]{1,0:T(8,128)(2,1)} %refs_3_.3, bf16[768,512]{1,0:T(8,128)(2,1)} %refs_4_.1, bf16[128,512]{1,0:T(8,128)(2,1)} %collective-permute-done.2.refs_5_, ...), custom_call_target="tpu_custom_call" | custom-call | flops 805306368 | bytes 25165824 | tf_op jit(solution)/shard_map/attend/pallas_call | solution.py:306
  258.3 2.4 all-to-all-done.5.parts.blocks_late
  261.8 2.1 merge_parts.1
  263.9 3.4 %all-to-all-start.6 = ((bf16[8,64,128]{2,1,0:T(8,128)(2,1)}), bf16[8,64,128]{2,1,0:T(8,128)(2,1)S(1)}, u32[]{:S(2)}, u32[]{:S(2)}) async-start(bf16[8,64,128]{2,1,0:T(8,128)(2,1)} %merge_parts.1), calls=%async_computation.6 | async-start | bytes 262144 | tf_op jit(solution)/shard_map/all_to_all | solution.py:77
  267.4 1.3 copy-done.1
  268.7 1.4 copy-done.32
  270.1 1.4 copy-done.33
  271.5 8.0 %late_blocks.1 = (bf16[384,512]{1,0:T(8,128)(2,1)S(1)}, bf16[384,512]{1,0:T(8,128)(2,1)S(1)}) custom-call(s32[32]{0:T(128)S(1)} %reshape_squeeze.3.late, bf16[768,512]{1,0:T(8,128)(2,1)S(1)} %copy-done.14, f32[768,512]{1,0:T(8,128)S(1)} %copy-done.32, f32[4,768,128]{2,1,0:T(8,128)S(1)} %copy-done.33, bf16[8,640,128]{2,1,0:T(8,128)(2,1)S(1)} %copy-done.1), custom_call_target="tpu_custom_call" | custom-call | bytes 25165824 | tf_op jit(solution)/shard_map/late_blocks/pallas_call | solution.py:390
  280.3 3.2 collective-permute-start.26
  284.3 9.4 %collective-permute-done.22.refs_1_ = bf16[384,512]{1,0:T(8,128)(2,1)S(1)} collective-permute-done((bf16[384,512]{1,0:T(8,128)(2,1)}, bf16[384,512]{1,0:T(8,128)(2,1)S(1)}, u32[]{:S(2)}, u32[]{:S(2)}) %collective-permute-start.22) | collective-permute-done | bytes 393248 | tf_op jit(solution)/shard_map/ppermute | solution.py:29
  293.7 3.3 %collective-permute-start.27 = (bf16[384,512]{1,0:T(8,128)(2,1)S(1)}, bf16[384,512]{1,0:T(8,128)(2,1)S(1)}, u32[]{:S(2)}, u32[]{:S(2)}) collective-permute-start(bf16[384,512]{1,0:T(8,128)(2,1)S(1)} %collective-permute-done.26.refs_2_), channel_id=1, source_target_pairs={{0,192},{64,0},{128,64},{192,128},{1,193},{65,1},{129,65},{193,129... | collective-permute-start | bytes 1179656 | tf_op jit(solution)/shard_map/ppermute | solution.py:29
  297.2 4.4 %collective-permute-done.23.refs_2_ = bf16[384,512]{1,0:T(8,128)(2,1)S(1)} collective-permute-done((bf16[384,512]{1,0:T(8,128)(2,1)}, bf16[384,512]{1,0:T(8,128)(2,1)S(1)}, u32[]{:S(2)}, u32[]{:S(2)}) %collective-permute-start.23) | collective-permute-done | bytes 393248 | tf_op jit(solution)/shard_map/ppermute | solution.py:29
  301.6 3.6 %collective-permute-start.29 = (bf16[128,512]{1,0:T(8,128)(2,1)S(1)}, bf16[128,512]{1,0:T(8,128)(2,1)S(1)}, u32[]{:S(2)}, u32[]{:S(2)}) collective-permute-start(bf16[128,512]{1,0:T(8,128)(2,1)S(1)} %bitcast.13), channel_id=1, source_target_pairs={{0,192},{64,0},{128,64},{192,128},{1,193},{65,1},{129,65},{193,129... | collective-permute-start | bytes 393224 | tf_op jit(solution)/shard_map/ppermute | solution.py:29
  305.2 1.7 collective-permute-done.24.refs_3_
  306.8 1.2 copy-done.10
  308.1 1.2 copy-done.12
  310.3 3.0 upper_product.1.top
  313.3 6.7 %collective-permute-done.28.refs_5_ = bf16[128,512]{1,0:T(8,128)(2,1)S(1)} collective-permute-done((bf16[128,512]{1,0:T(8,128)(2,1)S(1)}, bf16[128,512]{1,0:T(8,128)(2,1)S(1)}, u32[]{:S(2)}, u32[]{:S(2)}) %collective-permute-start.28) | collective-permute-done | bytes 131104 | tf_op jit(solution)/shard_map/ppermute | solution.py:29
  320.0 4.9 %lower_product.1 = bf16[768,1024]{1,0:T(8,128)(2,1)} custom-call(s32[4]{0:T(128)S(1)} %copy-done.36, bf16[384,1024]{1,0:T(8,128)(2,1)S(1)} %upper_product.1.top, bf16[384,512]{1,0:T(8,128)(2,1)S(1)} %get-tuple-element.129.refs_0_, bf16[384,512]{1,0:T(8,128)(2,1)S(1)} %collective-permute-done.25.refs_1_, ...), custom_call_target="tpu_custom_call" | custom-call | flops 1610612736 | bytes 8388608 | tf_op jit(solution)/shard_map/lower_product/pallas_call | solution.py:205
  (152 shorter events, 36.8 us)
Async XLA Ops:
  0.0 13.0 %copy-start.3 = (bf16[768,512]{1,0:T(8,128)(2,1)S(1)}, bf16[768,512]{1,0:T(8,128)(2,1)}, u32[]{:S(2)}) copy-start(bf16[768,512]{1,0:T(8,128)(2,1)} %refs_4_.1) | copy-start | bytes 2359300
  0.0 19.5 %collective-permute-start = (bf16[768,512]{1,0:T(8,128)(2,1)}, bf16[768,512]{1,0:T(8,128)(2,1)S(1)}, u32[]{:S(2)}, u32[]{:S(2)}) collective-permute-start(bf16[768,512]{1,0:T(8,128)(2,1)} %refs_3_.3), channel_id=1, source_target_pairs={{0,8},{8,16},{16,24},{24,32},{32,40},{40,48},{48,56},{56,0},{1,9},... | collective-permute-start | bytes 2359304 | tf_op jit(solution)/shard_map/ppermute | solution.py:24
  1.9 19.5 %collective-permute-start.1 = (bf16[768,512]{1,0:T(8,128)(2,1)}, bf16[768,512]{1,0:T(8,128)(2,1)}, u32[]{:S(2)}, u32[]{:S(2)}) collective-permute-start(bf16[768,512]{1,0:T(8,128)(2,1)} %refs_4_.1), channel_id=1, source_target_pairs={{0,56},{8,0},{16,8},{24,16},{32,24},{40,32},{48,40},{56,48},{1,57}... | collective-permute-start | bytes 2359304 | tf_op jit(solution)/shard_map/ppermute | solution.py:24
  12.7 3.7 %copy-start.41 = (s32[144]{0:T(256)}, s32[144]{0:T(256)S(1)}, u32[]{:S(2)}) copy-start(s32[144]{0:T(256)S(1)} %multiply_add_fusion.refs_0_) | copy-start | bytes 1732
  14.3 2.8 copy-start.37
  19.0 13.0 %copy-start.2 = (bf16[768,512]{1,0:T(8,128)(2,1)S(1)}, bf16[768,512]{1,0:T(8,128)(2,1)}, u32[]{:S(2)}) copy-start(bf16[768,512]{1,0:T(8,128)(2,1)} %refs_3_.3) | copy-start | bytes 2359300
  19.5 53.2 %copy-start.23 = (bf16[768,512]{1,0:T(8,128)(2,1)}, bf16[768,512]{1,0:T(8,128)(2,1)S(1)}, u32[]{:S(2)}) copy-start(bf16[768,512]{1,0:T(8,128)(2,1)S(1)} %collective-permute-done.refs_1_) | copy-start | bytes 2359300
  21.4 47.6 %all-to-all-start = ((bf16[8,176,512]{2,1,0:T(8,128)(2,1)}), bf16[8,176,512]{2,1,0:T(8,128)(2,1)}, u32[]{:S(2)}, u32[]{:S(2)}) async-start(bf16[8,176,512]{2,1,0:T(8,128)(2,1)} %fusion.1), calls=%async_computation | async-start | bytes 2883584 | tf_op jit(solution)/shard_map/all_to_all | solution.py:77
  25.9 45.9 %collective-permute-start.4 = (bf16[768,512]{1,0:T(8,128)(2,1)S(1)}, bf16[768,512]{1,0:T(8,128)(2,1)}, u32[]{:S(2)}, u32[]{:S(2)}) collective-permute-start(bf16[768,512]{1,0:T(8,128)(2,1)S(1)} %collective-permute-done.refs_1_), channel_id=1, source_target_pairs={{0,8},{8,16},{16,24},{24,32},{32,40},{40,48},{48,56},{56,0},{1,9},... | collective-permute-start | bytes 2359304 | tf_op jit(solution)/shard_map/ppermute | solution.py:24
  29.0 42.8 %collective-permute-start.5 = (bf16[768,512]{1,0:T(8,128)(2,1)}, bf16[768,512]{1,0:T(8,128)(2,1)}, u32[]{:S(2)}, u32[]{:S(2)}) collective-permute-start(bf16[768,512]{1,0:T(8,128)(2,1)} %collective-permute-done.1.refs_4_.refs_5_), channel_id=1, source_target_pairs={{0,56},{8,0},{16,8},{24,16},{32,24},{40,32},{48,40},{56,48},{1,57}... | collective-permute-start | bytes 2359304 | tf_op jit(solution)/shard_map/ppermute | solution.py:24
  29.0 50.9 %collective-permute-start.6 = (bf16[768,512]{1,0:T(8,128)(2,1)S(1)}, bf16[768,512]{1,0:T(8,128)(2,1)}, u32[]{:S(2)}, u32[]{:S(2)}) collective-permute-start(bf16[768,512]{1,0:T(8,128)(2,1)S(1)} %copy-done.3), channel_id=1, source_target_pairs={{0,8},{8,16},{16,24},{24,32},{32,40},{40,48},{48,56},{56,0},{1,9},... | collective-permute-start | bytes 2359304 | tf_op jit(solution)/shard_map/ppermute | solution.py:24
  32.0 48.0 %collective-permute-start.7 = (bf16[768,512]{1,0:T(8,128)(2,1)S(1)}, bf16[768,512]{1,0:T(8,128)(2,1)}, u32[]{:S(2)}, u32[]{:S(2)}) collective-permute-start(bf16[768,512]{1,0:T(8,128)(2,1)S(1)} %copy-done.2), channel_id=1, source_target_pairs={{0,56},{8,0},{16,8},{24,16},{32,24},{40,32},{48,40},{56,48},{1,57}... | collective-permute-start | bytes 2359304 | tf_op jit(solution)/shard_map/ppermute | solution.py:24
  32.0 35.1 %collective-permute-start.2 = (bf16[128,512]{1,0:T(8,128)(2,1)S(1)}, bf16[128,512]{1,0:T(8,128)(2,1)}, u32[]{:S(2)}, u32[]{:S(2)}) collective-permute-start(bf16[128,512]{1,0:T(8,128)(2,1)S(1)} %get-tuple-element.69), channel_id=1, source_target_pairs={{0,1},{1,2},{2,3},{3,4},{4,5},{5,6},{6,7},{7,8},{8,9},{9,10},{10,1... | collective-permute-start | bytes 393224 | tf_op jit(solution)/shard_map/ppermute | solution.py:477
  67.1 4.7 %collective-permute-start.3 = (bf16[128,512]{1,0:T(8,128)(2,1)}, bf16[128,512]{1,0:T(8,128)(2,1)S(1)}, u32[]{:S(2)}, u32[]{:S(2)}) collective-permute-start(bf16[128,512]{1,0:T(8,128)(2,1)} %get-tuple-element.70), channel_id=1, source_target_pairs={{1,0},{2,1},{3,2},{4,3},{5,4},{6,5},{7,6},{8,7},{9,8},{10,9},{11,1... | collective-permute-start | bytes 393224 | tf_op jit(solution)/shard_map/ppermute | solution.py:477
  71.8 1.9 copy-start.38
  73.7 32.6 %all-to-all-start.1 = ((bf16[8,512,128]{2,1,0:T(8,128)(2,1)}), bf16[8,512,128]{2,1,0:T(8,128)(2,1)}, u32[]{:S(2)}, u32[]{:S(2)}) async-start(bf16[8,512,128]{2,1,0:T(8,128)(2,1)} %copy-done.13), calls=%async_computation.1 | async-start | bytes 2097152 | tf_op jit(solution)/shard_map/all_to_all | solution.py:77
  79.9 21.7 %collective-permute-start.10 = (bf16[768,512]{1,0:T(8,128)(2,1)}, bf16[768,512]{1,0:T(8,128)(2,1)S(1)}, u32[]{:S(2)}, u32[]{:S(2)}) collective-permute-start(bf16[768,512]{1,0:T(8,128)(2,1)} %collective-permute-done.5.refs_4_), channel_id=1, source_target_pairs={{0,56},{8,0},{16,8},{24,16},{32,24},{40,32},{48,40},{56,48},{1,57}... | collective-permute-start | bytes 2359304 | tf_op jit(solution)/shard_map/ppermute | solution.py:24
  80.0 21.6 %collective-permute-start.8 = (bf16[768,512]{1,0:T(8,128)(2,1)}, bf16[768,512]{1,0:T(8,128)(2,1)}, u32[]{:S(2)}, u32[]{:S(2)}) collective-permute-start(bf16[768,512]{1,0:T(8,128)(2,1)} %collective-permute-done.4.refs_1_), channel_id=1, source_target_pairs={{0,8},{8,16},{16,24},{24,32},{32,40},{40,48},{48,56},{56,0},{1,9},... | collective-permute-start | bytes 2359304 | tf_op jit(solution)/shard_map/ppermute | solution.py:24
  84.1 17.5 %collective-permute-start.12 = (bf16[32,512]{1,0:T(8,128)(2,1)S(1)}, bf16[32,512]{1,0:T(8,128)(2,1)S(1)}, u32[]{:S(2)}, u32[]{:S(2)}) collective-permute-start(bf16[32,512]{1,0:T(8,128)(2,1)S(1)} %slice_reduce_fusion.1), channel_id=1, source_target_pairs={{0,8},{8,0},{16,24},{24,16},{32,40},{40,32},{48,56},{56,48},{1,9},... | collective-permute-start | bytes 98312 | tf_op jit(solution)/shard_map/ppermute | solution.py:481
  101.6 12.3 %copy-start.39 = (bf16[32,512]{1,0:T(8,128)(2,1)}, bf16[32,512]{1,0:T(8,128)(2,1)S(1)}, u32[]{:S(2)}) copy-start(bf16[32,512]{1,0:T(8,128)(2,1)S(1)} %add.194) | copy-start | bytes 98308
  101.6 1.1 copy-start.24
  105.0 1.3 copy-start.4
  106.3 54.1 %all-to-all-start.2 = ((bf16[8,1024,128]{2,1,0:T(8,128)(2,1)}), bf16[8,1024,128]{2,1,0:T(8,128)(2,1)}, u32[]{:S(2)}, u32[]{:S(2)}) async-start(bf16[8,1024,128]{2,1,0:T(8,128)(2,1)} %copy-done.4), calls=%async_computation.2 | async-start | bytes 4194304 | tf_op jit(solution)/shard_map/all_to_all | solution.py:77
  110.7 12.2 %copy-start.25 = (bf16[768,512]{1,0:T(8,128)(2,1)S(1)}, bf16[768,512]{1,0:T(8,128)(2,1)}, u32[]{:S(2)}) copy-start(bf16[768,512]{1,0:T(8,128)(2,1)} %copy-done.23) | copy-start | bytes 2359300
  110.8 44.9 %collective-permute-start.13 = (bf16[512,1024]{1,0:T(8,128)(2,1)}, bf16[512,1024]{1,0:T(8,128)(2,1)S(1)}, u32[]{:S(2)}, u32[]{:S(2)}) collective-permute-start(bf16[512,1024]{1,0:T(8,128)(2,1)} %get-tuple-element.80), channel_id=1, source_target_pairs={{0,128},{64,192},{128,0},{192,64},{1,129},{65,193},{129,1},{193,65... | collective-permute-start | bytes 3145736 | tf_op jit(solution)/shard_map/ppermute | solution.py:29
  113.9 6.4 %collective-permute-start.16 = (bf16[32,512]{1,0:T(8,128)(2,1)S(1)}, bf16[32,512]{1,0:T(8,128)(2,1)S(1)}, u32[]{:S(2)}, u32[]{:S(2)}) collective-permute-start(bf16[32,512]{1,0:T(8,128)(2,1)S(1)} %add.194), channel_id=1, source_target_pairs={{0,16},{8,24},{16,0},{24,8},{32,48},{40,56},{48,32},{56,40},{1,17}... | collective-permute-start | bytes 98312 | tf_op jit(solution)/shard_map/ppermute | solution.py:481
  117.5 20.7 %collective-permute-start.14 = (bf16[768,512]{1,0:T(8,128)(2,1)}, bf16[768,512]{1,0:T(8,128)(2,1)}, u32[]{:S(2)}, u32[]{:S(2)}) collective-permute-start(bf16[768,512]{1,0:T(8,128)(2,1)} %collective-permute-done.7.refs_2_), channel_id=1, source_target_pairs={{0,56},{8,0},{16,8},{24,16},{32,24},{40,32},{48,40},{56,48},{1,57}... | collective-permute-start | bytes 2359304 | tf_op jit(solution)/shard_map/ppermute | solution.py:24
  117.6 21.4 %collective-permute-start.15 = (bf16[768,512]{1,0:T(8,128)(2,1)}, bf16[768,512]{1,0:T(8,128)(2,1)}, u32[]{:S(2)}, u32[]{:S(2)}) collective-permute-start(bf16[768,512]{1,0:T(8,128)(2,1)} %collective-permute-done.6.refs_3_.refs_4_), channel_id=1, source_target_pairs={{0,8},{8,16},{16,24},{24,32},{32,40},{40,48},{48,56},{56,0},{1,9},... | collective-permute-start | bytes 2359304 | tf_op jit(solution)/shard_map/ppermute | solution.py:24
  119.5 34.4 %collective-permute-start.11 = (bf16[768,512]{1,0:T(8,128)(2,1)S(1)}, bf16[768,512]{1,0:T(8,128)(2,1)S(1)}, u32[]{:S(2)}, u32[]{:S(2)}) collective-permute-start(bf16[768,512]{1,0:T(8,128)(2,1)S(1)} %collective-permute-done.10.refs_4_), channel_id=1, source_target_pairs={{0,56},{8,0},{16,8},{24,16},{32,24},{40,32},{48,40},{56,48},{1,57}... | collective-permute-start | bytes 2359304 | tf_op jit(solution)/shard_map/ppermute | solution.py:24
  120.3 34.5 %collective-permute-start.9 = (bf16[768,512]{1,0:T(8,128)(2,1)}, bf16[768,512]{1,0:T(8,128)(2,1)S(1)}, u32[]{:S(2)}, u32[]{:S(2)}) collective-permute-start(bf16[768,512]{1,0:T(8,128)(2,1)} %collective-permute-done.8.refs_1_), channel_id=1, source_target_pairs={{0,8},{8,16},{16,24},{24,32},{32,40},{40,48},{48,56},{56,0},{1,9},... | collective-permute-start | bytes 2359304 | tf_op jit(solution)/shard_map/ppermute | solution.py:24
  122.9 4.9 %copy-start.40 = (bf16[32,512]{1,0:T(8,128)(2,1)S(1)}, bf16[32,512]{1,0:T(8,128)(2,1)}, u32[]{:S(2)}) copy-start(bf16[32,512]{1,0:T(8,128)(2,1)} %copy-done.39) | copy-start | bytes 98308
  159.1 1.3 copy-start.5
  160.4 37.4 %all-to-all-start.3 = ((bf16[8,1024,128]{2,1,0:T(8,128)(2,1)}), bf16[8,1024,128]{2,1,0:T(8,128)(2,1)}, u32[]{:S(2)}, u32[]{:S(2)}) async-start(bf16[8,1024,128]{2,1,0:T(8,128)(2,1)} %copy-done.5), calls=%async_computation.3 | async-start | bytes 4194304 | tf_op jit(solution)/shard_map/all_to_all | solution.py:77
  164.8 27.0 %collective-permute-start.17 = (bf16[512,1024]{1,0:T(8,128)(2,1)}, bf16[512,1024]{1,0:T(8,128)(2,1)S(1)}, u32[]{:S(2)}, u32[]{:S(2)}) collective-permute-start(bf16[512,1024]{1,0:T(8,128)(2,1)} %get-tuple-element.92), channel_id=1, source_target_pairs={{0,64},{64,128},{128,192},{192,0},{1,65},{65,129},{129,193},{193,1... | collective-permute-start | bytes 3145736 | tf_op jit(solution)/shard_map/ppermute | solution.py:29
  165.5 24.3 %collective-permute-start.18 = (bf16[768,512]{1,0:T(8,128)(2,1)}, bf16[768,512]{1,0:T(8,128)(2,1)S(1)}, u32[]{:S(2)}, u32[]{:S(2)}) collective-permute-start(bf16[768,512]{1,0:T(8,128)(2,1)} %collective-permute-done.14.refs_2_), channel_id=1, source_target_pairs={{0,56},{8,0},{16,8},{24,16},{32,24},{40,32},{48,40},{56,48},{1,57}... | collective-permute-start | bytes 2359304 | tf_op jit(solution)/shard_map/ppermute | solution.py:24
  168.2 21.6 %collective-permute-start.19 = (bf16[768,512]{1,0:T(8,128)(2,1)}, bf16[768,512]{1,0:T(8,128)(2,1)S(1)}, u32[]{:S(2)}, u32[]{:S(2)}) collective-permute-start(bf16[768,512]{1,0:T(8,128)(2,1)} %collective-permute-done.15.refs_3_), channel_id=1, source_target_pairs={{0,8},{8,16},{16,24},{24,32},{32,40},{40,48},{48,56},{56,0},{1,9},... | collective-permute-start | bytes 2359304 | tf_op jit(solution)/shard_map/ppermute | solution.py:24
  168.2 20.8 %collective-permute-start.20 = (bf16[32,512]{1,0:T(8,128)(2,1)}, bf16[32,512]{1,0:T(8,128)(2,1)S(1)}, u32[]{:S(2)}, u32[]{:S(2)}) collective-permute-start(bf16[32,512]{1,0:T(8,128)(2,1)} %add.195), channel_id=1, source_target_pairs={{0,32},{8,40},{16,48},{24,56},{32,0},{40,8},{48,16},{56,24},{1,33}... | collective-permute-start | bytes 98312 | tf_op jit(solution)/shard_map/ppermute | solution.py:481
  197.8 34.6 %all-to-all-start.4 = ((bf16[8,1152,128]{2,1,0:T(8,128)(2,1)}), bf16[8,1152,128]{2,1,0:T(8,128)(2,1)}, u32[]{:S(2)}, u32[]{:S(2)}) async-start(bf16[8,1152,128]{2,1,0:T(8,128)(2,1)} %pick_blocks.8), calls=%async_computation.4 | async-start | bytes 4718592 | tf_op jit(solution)/shard_map/all_to_all | solution.py:77
  202.3 30.1 %copy-start.16 = (bf16[768,512]{1,0:T(8,128)(2,1)S(1)}, bf16[768,512]{1,0:T(8,128)(2,1)}, u32[]{:S(2)}) copy-start(bf16[768,512]{1,0:T(8,128)(2,1)} %copy-done.15) | copy-start | bytes 2359300
  202.3 25.8 %collective-permute-start.21 = (bf16[512,1024]{1,0:T(8,128)(2,1)}, bf16[512,1024]{1,0:T(8,128)(2,1)S(1)}, u32[]{:S(2)}, u32[]{:S(2)}) collective-permute-start(bf16[512,1024]{1,0:T(8,128)(2,1)} %get-tuple-element.107), channel_id=1, source_target_pairs={{0,192},{64,0},{128,64},{192,128},{1,193},{65,1},{129,65},{193,129... | collective-permute-start | bytes 3145736 | tf_op jit(solution)/shard_map/ppermute | solution.py:29
  203.5 1.1 copy-start.20
  204.6 1.1 copy-start.22
  232.4 1.1 copy-start.18
  238.3 3.8 %copy-start.42 = (s32[2]{0:T(128)S(1)}, s32[2]{0:T(128)}, u32[]{:S(2)}) copy-start(s32[2]{0:T(128)} %get-tuple-element.133) | copy-start | bytes 28
  238.3 22.4 %all-to-all-start.5 = ((bf16[8,640,128]{2,1,0:T(8,128)(2,1)}), bf16[8,640,128]{2,1,0:T(8,128)(2,1)S(1)}, u32[]{:S(2)}, u32[]{:S(2)}) async-start(bf16[8,640,128]{2,1,0:T(8,128)(2,1)} %copy-done.6), calls=%async_computation.5 | async-start | bytes 2621440 | tf_op jit(solution)/shard_map/all_to_all | solution.py:77
  258.3 9.1 %copy-start.14 = (bf16[768,512]{1,0:T(8,128)(2,1)S(1)}, bf16[768,512]{1,0:T(8,128)(2,1)}, u32[]{:S(2)}) copy-start(bf16[768,512]{1,0:T(8,128)(2,1)} %q.1) | copy-start | bytes 2359300
  260.8 1.1 copy-start
  263.9 16.4 %all-to-all-start.6 = ((bf16[8,64,128]{2,1,0:T(8,128)(2,1)}), bf16[8,64,128]{2,1,0:T(8,128)(2,1)S(1)}, u32[]{:S(2)}, u32[]{:S(2)}) async-start(bf16[8,64,128]{2,1,0:T(8,128)(2,1)} %merge_parts.1), calls=%async_computation.6 | async-start | bytes 262144 | tf_op jit(solution)/shard_map/all_to_all | solution.py:77
  267.4 1.3 copy-start.1
  268.7 1.4 copy-start.32
  270.1 1.4 copy-start.33
  271.5 35.3 %copy-start.8 = (bf16[512,1024]{1,0:T(8,128)(2,1)S(1)}, bf16[512,1024]{1,0:T(8,128)(2,1)}, u32[]{:S(2)}) copy-start(bf16[512,1024]{1,0:T(8,128)(2,1)} %copy-done.7) | copy-start | bytes 3145732
  280.3 13.4 %collective-permute-start.22 = (bf16[384,512]{1,0:T(8,128)(2,1)}, bf16[384,512]{1,0:T(8,128)(2,1)S(1)}, u32[]{:S(2)}, u32[]{:S(2)}) collective-permute-start(bf16[384,512]{1,0:T(8,128)(2,1)} %copy-done.34), channel_id=1, source_target_pairs={{0,64},{64,128},{128,192},{192,0},{1,65},{65,129},{129,193},{193,1... | collective-permute-start | bytes 1179656 | tf_op jit(solution)/shard_map/ppermute | solution.py:29
  280.3 13.4 %collective-permute-start.26 = (bf16[384,512]{1,0:T(8,128)(2,1)S(1)}, bf16[384,512]{1,0:T(8,128)(2,1)S(1)}, u32[]{:S(2)}, u32[]{:S(2)}) collective-permute-start(bf16[384,512]{1,0:T(8,128)(2,1)S(1)} %get-tuple-element.129.refs_0_), channel_id=1, source_target_pairs={{0,192},{64,0},{128,64},{192,128},{1,193},{65,1},{129,65},{193,129... | collective-permute-start | bytes 1179656 | tf_op jit(solution)/shard_map/ppermute | solution.py:29
  283.5 18.0 %collective-permute-start.23 = (bf16[384,512]{1,0:T(8,128)(2,1)}, bf16[384,512]{1,0:T(8,128)(2,1)S(1)}, u32[]{:S(2)}, u32[]{:S(2)}) collective-permute-start(bf16[384,512]{1,0:T(8,128)(2,1)} %copy-done.34), channel_id=1, source_target_pairs={{0,192},{64,0},{128,64},{192,128},{1,193},{65,1},{129,65},{193,129... | collective-permute-start | bytes 1179656 | tf_op jit(solution)/shard_map/ppermute | solution.py:29
  293.7 13.2 %collective-permute-start.24 = (bf16[384,512]{1,0:T(8,128)(2,1)S(1)}, bf16[384,512]{1,0:T(8,128)(2,1)S(1)}, u32[]{:S(2)}, u32[]{:S(2)}) collective-permute-start(bf16[384,512]{1,0:T(8,128)(2,1)S(1)} %collective-permute-done.22.refs_1_), channel_id=1, source_target_pairs={{0,64},{64,128},{128,192},{192,0},{1,65},{65,129},{129,193},{193,1... | collective-permute-start | bytes 1179656 | tf_op jit(solution)/shard_map/ppermute | solution.py:29
  293.7 26.3 %collective-permute-start.25 = (bf16[384,512]{1,0:T(8,128)(2,1)S(1)}, bf16[384,512]{1,0:T(8,128)(2,1)S(1)}, u32[]{:S(2)}, u32[]{:S(2)}) collective-permute-start(bf16[384,512]{1,0:T(8,128)(2,1)S(1)} %get-tuple-element.129.refs_0_), channel_id=1, source_target_pairs={{0,64},{64,128},{128,192},{192,0},{1,65},{65,129},{129,193},{193,1... | collective-permute-start | bytes 1179656 | tf_op jit(solution)/shard_map/ppermute | solution.py:29
  293.7 26.3 %collective-permute-start.27 = (bf16[384,512]{1,0:T(8,128)(2,1)S(1)}, bf16[384,512]{1,0:T(8,128)(2,1)S(1)}, u32[]{:S(2)}, u32[]{:S(2)}) collective-permute-start(bf16[384,512]{1,0:T(8,128)(2,1)S(1)} %collective-permute-done.26.refs_2_), channel_id=1, source_target_pairs={{0,192},{64,0},{128,64},{192,128},{1,193},{65,1},{129,65},{193,129... | collective-permute-start | bytes 1179656 | tf_op jit(solution)/shard_map/ppermute | solution.py:29
  297.1 23.0 %copy-start.36 = (s32[4]{0:T(128)S(1)}, s32[4]{0:T(128)}, u32[]{:S(2)}) copy-start(s32[4]{0:T(128)} %pad_add_fusion.refs_1_.place) | copy-start | bytes 52
  297.1 22.9 %collective-permute-start.28 = (bf16[128,512]{1,0:T(8,128)(2,1)S(1)}, bf16[128,512]{1,0:T(8,128)(2,1)S(1)}, u32[]{:S(2)}, u32[]{:S(2)}) collective-permute-start(bf16[128,512]{1,0:T(8,128)(2,1)S(1)} %bitcast.12), channel_id=1, source_target_pairs={{0,64},{64,128},{128,192},{192,0},{1,65},{65,129},{129,193},{193,1... | collective-permute-start | bytes 393224 | tf_op jit(solution)/shard_map/ppermute | solution.py:29
  301.6 18.4 %collective-permute-start.29 = (bf16[128,512]{1,0:T(8,128)(2,1)S(1)}, bf16[128,512]{1,0:T(8,128)(2,1)S(1)}, u32[]{:S(2)}, u32[]{:S(2)}) collective-permute-start(bf16[128,512]{1,0:T(8,128)(2,1)S(1)} %bitcast.13), channel_id=1, source_target_pairs={{0,192},{64,0},{128,64},{192,128},{1,193},{65,1},{129,65},{193,129... | collective-permute-start | bytes 393224 | tf_op jit(solution)/shard_map/ppermute | solution.py:29
  306.8 13.2 %collective-permute-start.30 = (bf16[128,512]{1,0:T(8,128)(2,1)S(1)}, bf16[128,512]{1,0:T(8,128)(2,1)S(1)}, u32[]{:S(2)}, u32[]{:S(2)}) collective-permute-start(bf16[128,512]{1,0:T(8,128)(2,1)S(1)} %bitcast.14), channel_id=1, source_target_pairs={{0,128},{64,192},{128,0},{192,64},{1,129},{65,193},{129,1},{193,65... | collective-permute-start | bytes 393224 | tf_op jit(solution)/shard_map/ppermute | solution.py:29
  306.8 1.2 copy-start.10
  308.1 1.2 copy-start.12
  (17 other events, 15.9 us)

commit v8 on v6

--- a/solution.py
+++ b/solution.py
@@ -456,9 +456,11 @@
     arrived = [over_plane(picks)]
     ahead = [(i, i + 1) for i in range(shards - 1)]
     back = [(j, i) for i, j in ahead]
-    for apart in (1, 2, 4):
-        pairs = [(i, i ^ apart) for i in range(PLANES)]
-        shared = shared + lax.ppermute(shared, "seq_0", pairs)
+
+    def doubled(own, apart):
+        return own + lax.ppermute(own, "seq_0", [(i, i ^ apart) for i in range(PLANES)])
+
+    shared = doubled(shared, 1)
     first, parts = 1, ()
     beside = [lax.ppermute(ends, SEQ, ahead), lax.ppermute(starts, SEQ, back)]
     held = [up_k, down_k, up_v, down_v]
@@ -481,6 +483,8 @@
         turn, away = ((3, 2), (1, 1), (2, -1))[step - 2]
         beside, _ = lax.optimization_barrier((weights[turn], held))
         beside = (across(beside, away), before, after)
+        if step < PLANES // 2:
+            shared = doubled(shared, 2 * (step - 1))
         picks = picked(asked, first, held, (shared,) if step == PLANES // 2 else ())
         arrived.append(over_plane(picks))
         first += len(held) // 2
@@ -494,7 +498,7 @@
             held = [up_k, down_k, up_v, down_v]
         else:
             held = [up_k, down_v]
-    held, arrived, parts, beside = lax.optimization_barrier((held, arrived, parts, beside))
+    held, _, parts, beside = lax.optimization_barrier((held, picks, parts, beside))
     weights[turn], before, after = beside
     parts = (global_parts(asking, held, parts),)
     arrived.append(over_plane(picked(asked, first, held, parts)))

time: 315 us -> 311 us (0.987)
  waiting for transfers between devices: 126 us -> 105 us
  starting transfers between devices: 70.6 us -> 89.1 us
  local copies, waits for them, and re-layouts: 38.7 us -> 32.6 us
    all_to_all x6, starting transfers between devices: 25.6 us -> 40.1 us  [over_plane(): return lax.all_to_all(parts, PLANE, split_axis=0, concat_axis=0, tiled=True)]
    ppermute x14, waiting for transfers between devices: 53.2 us -> 41.4 us  [ring_step(): lax.ppermute(shard, 'seq_0', [(i, (i + step) % peers) for i in range(peer...]
    ppermute x12, waiting for transfers between devices: 25.4 us -> 18.4 us  [across(): lax.ppermute(shard, 'heads', [(i, (i + step) % peers) for i in range(peer...]
    unnamed x97 -> x81, local copies, waits for them, and re-layouts: 34.3 us -> 28.1 us
    ppermute x12, starting transfers between devices: 14.6 us -> 18.9 us  [across(): lax.ppermute(shard, 'heads', [(i, (i + step) % peers) for i in range(peer...]
    all_to_all x6, waiting for transfers between devices: 22.9 us -> 19.6 us  [over_plane(): return lax.all_to_all(parts, PLANE, split_axis=0, concat_axis=0, tiled=True)]
  transfers between devices with their start and end apart: 37 -> 37, of which waited for: 21 -> 16; matrix products, arithmetic and copies ran while one was open for 6% -> 7% of each run, Pallas kernels for 9% -> 10%
where the time goes in v8:
time: 311 us; the launch traced here: 308 us
  waiting for transfers between devices  105 us (34%)
  starting transfers between devices  89.1 us (29%)
  Pallas kernels  53.1 us (17%)
  local copies, waits for them, and re-layouts  32.6 us (10%)
  other arithmetic  17.2 us (6%)
  blocking collectives  8.89 us (3%)
    ppermute x14, waiting for transfers between devices, ring_step(): lax.ppermute(shard, 'seq_0', [(i, (i + step) % peers) for i in range(peer...  41.4 us
    all_to_all x6, starting transfers between devices, over_plane(): return lax.all_to_all(parts, PLANE, split_axis=0, concat_axis=0, tiled=True)  40.1 us
    unnamed x81, local copies, waits for them, and re-layouts  28.1 us
    ppermute x3, waiting for transfers between devices, doubled(): lax.ppermute(own, 'seq_0', [(i, i ^ apart) for i in range(PLANES)])  26 us
    all_to_all x6, waiting for transfers between devices, over_plane(): return lax.all_to_all(parts, PLANE, split_axis=0, concat_axis=0, tiled=True)  19.6 us
    ppermute x12, starting transfers between devices, across(): lax.ppermute(shard, 'heads', [(i, (i + step) % peers) for i in range(peer...  18.9 us
    ppermute x12, waiting for transfers between devices, across(): lax.ppermute(shard, 'heads', [(i, (i + step) % peers) for i in range(peer...  18.4 us
    ppermute x14, starting transfers between devices, ring_step(): lax.ppermute(shard, 'seq_0', [(i, (i + step) % peers) for i in range(peer...  16.8 us
  transfers between devices with their start and end apart: 37, of which 16 were waited for; matrix products, arithmetic and copies ran while one was open for 7% of the time, Pallas kernels for 10%

profile of v8, /device:TPU:32, one launch (start us, length us, event | category | flops | bytes accessed | tf_op | source)
XLA Modules:
  0.0 308.0 jit_solution(3702656814882669517)
XLA Ops:
  0.0 1.9 collective-permute-start
  6.8 2.2 fusion.14
  9.0 2.2 dynamic-slice_select_fusion.5
  12.4 1.3 fusion.15
  14.6 1.2 fusion.1
  16.6 1.9 constant_dynamic-slice_fusion
  19.5 1.9 collective-permute-done.2.refs_4_.refs_5_
  21.4 4.5 %all-to-all-start = ((bf16[8,176,512]{2,1,0:T(8,128)(2,1)}), bf16[8,176,512]{2,1,0:T(8,128)(2,1)}, u32[]{:S(2)}, u32[]{:S(2)}) async-start(bf16[8,176,512]{2,1,0:T(8,128)(2,1)} %fusion.1), calls=%async_computation | async-start | bytes 2883584 | tf_op jit(solution)/shard_map/all_to_all | solution.py:77
  25.9 3.1 %collective-permute-start.4 = (bf16[768,512]{1,0:T(8,128)(2,1)S(1)}, bf16[768,512]{1,0:T(8,128)(2,1)}, u32[]{:S(2)}, u32[]{:S(2)}) collective-permute-start(bf16[768,512]{1,0:T(8,128)(2,1)S(1)} %copy-done.1), channel_id=1, source_target_pairs={{0,8},{8,16},{16,24},{24,32},{32,40},{40,48},{48,56},{56,0},{1,9},... | collective-permute-start | bytes 2359304 | tf_op jit(solution)/shard_map/ppermute | solution.py:24
  29.0 17.2 %all-to-all-done = bf16[8,176,512]{2,1,0:T(8,128)(2,1)} async-done(((bf16[8,176,512]{2,1,0:T(8,128)(2,1)}), bf16[8,176,512]{2,1,0:T(8,128)(2,1)}, u32[]{:S(2)}, u32[]{:S(2)}) %all-to-all-start) | async-done | bytes 1441824 | tf_op jit(solution)/shard_map/all_to_all | solution.py:77
  47.0 3.0 collective-permute-done.5.refs_2_
  51.8 4.4 %all-to-all-start.1 = ((bf16[8,512,128]{2,1,0:T(8,128)(2,1)}), bf16[8,512,128]{2,1,0:T(8,128)(2,1)}, u32[]{:S(2)}, u32[]{:S(2)}) async-start(bf16[8,512,128]{2,1,0:T(8,128)(2,1)} %copy-done.10), calls=%async_computation.1 | async-start | bytes 2097152 | tf_op jit(solution)/shard_map/all_to_all | solution.py:77
  56.3 1.7 collective-permute-start.1
  60.2 16.7 %collective-permute-done.10 = bf16[32,512]{1,0:T(8,128)(2,1)S(1)} collective-permute-done((bf16[32,512]{1,0:T(8,128)(2,1)S(1)}, bf16[32,512]{1,0:T(8,128)(2,1)S(1)}, u32[]{:S(2)}, u32[]{:S(2)}) %collective-permute-start.10) | collective-permute-done | bytes 32800 | tf_op jit(solution)/shard_map/ppermute | solution.py:461
  78.5 2.2 pick_blocks.6
  80.7 1.3 copy-done.2
  82.0 4.4 %all-to-all-start.2 = ((bf16[8,1024,128]{2,1,0:T(8,128)(2,1)}), bf16[8,1024,128]{2,1,0:T(8,128)(2,1)}, u32[]{:S(2)}, u32[]{:S(2)}) async-start(bf16[8,1024,128]{2,1,0:T(8,128)(2,1)} %copy-done.2), calls=%async_computation.2 | async-start | bytes 4194304 | tf_op jit(solution)/shard_map/all_to_all | solution.py:77
  86.4 3.1 %collective-permute-start.15 = (bf16[512,1024]{1,0:T(8,128)(2,1)}, bf16[512,1024]{1,0:T(8,128)(2,1)S(1)}, u32[]{:S(2)}, u32[]{:S(2)}) collective-permute-start(bf16[512,1024]{1,0:T(8,128)(2,1)} %get-tuple-element.73), channel_id=1, source_target_pairs={{0,128},{64,192},{128,0},{192,64},{1,129},{65,193},{129,1},{193,65... | collective-permute-start | bytes 3145736 | tf_op jit(solution)/shard_map/ppermute | solution.py:29
  89.5 2.0 collective-permute-start.16
  91.6 5.8 %collective-permute-start.17 = (bf16[128,512]{1,0:T(8,128)(2,1)}, bf16[128,512]{1,0:T(8,128)(2,1)S(1)}, u32[]{:S(2)}, u32[]{:S(2)}) collective-permute-start(bf16[128,512]{1,0:T(8,128)(2,1)} %get-tuple-element.75), channel_id=1, source_target_pairs={{1,0},{2,1},{3,2},{4,3},{5,4},{6,5},{7,6},{8,7},{9,8},{10,9},{11,1... | collective-permute-start | bytes 393224 | tf_op jit(solution)/shard_map/ppermute | solution.py:465
  97.4 2.8 collective-permute-start.18
  100.6 1.6 collective-permute-start.7
  102.3 1.5 collective-permute-start.8
  103.8 2.1 collective-permute-start.9
  105.8 1.4 slice_reduce_fusion.refs_0_
  107.2 4.1 %global_parts.4.refs_5_ = f32[512,256]{1,0:T(8,128)S(1)} custom-call(bf16[128,512]{1,0:T(8,128)(2,1)S(1)} %slice_reduce_fusion.refs_0_, bf16[768,512]{1,0:T(8,128)(2,1)S(1)} %copy-done.18, bf16[768,512]{1,0:T(8,128)(2,1)} %collective-permute-done.5.refs_2_, bf16[768,512]{1,0:T(8,128)(2,1)S(1)} %copy-done, ...), custom_call_target="tpu_custom_call" | custom-call | flops 603979776 | bytes 25165824 | tf_op jit(solution)/shard_map/global_parts/pallas_call | solution.py:125
  112.1 1.4 add.195
  113.5 6.7 %collective-permute-done.6.refs_1_ = bf16[768,512]{1,0:T(8,128)(2,1)S(1)} collective-permute-done((bf16[768,512]{1,0:T(8,128)(2,1)}, bf16[768,512]{1,0:T(8,128)(2,1)S(1)}, u32[]{:S(2)}, u32[]{:S(2)}) %collective-permute-start.6) | collective-permute-done | bytes 786464 | tf_op jit(solution)/shard_map/ppermute | solution.py:24
  121.2 14.2 %collective-permute-done.8.refs_3_ = bf16[768,512]{1,0:T(8,128)(2,1)S(1)} collective-permute-done((bf16[768,512]{1,0:T(8,128)(2,1)}, bf16[768,512]{1,0:T(8,128)(2,1)S(1)}, u32[]{:S(2)}, u32[]{:S(2)}) %collective-permute-start.8) | collective-permute-done | bytes 786464 | tf_op jit(solution)/shard_map/ppermute | solution.py:24
  141.6 1.7 pick_blocks.7
  143.3 1.3 copy-done.3
  144.6 17.8 %all-to-all-start.3 = ((bf16[8,1024,128]{2,1,0:T(8,128)(2,1)}), bf16[8,1024,128]{2,1,0:T(8,128)(2,1)}, u32[]{:S(2)}, u32[]{:S(2)}) async-start(bf16[8,1024,128]{2,1,0:T(8,128)(2,1)} %copy-done.3), calls=%async_computation.3 | async-start | bytes 4194304 | tf_op jit(solution)/shard_map/all_to_all | solution.py:77
  162.5 1.6 collective-permute-start.19
  164.5 1.6 collective-permute-start.12
  166.1 1.7 collective-permute-start.20
  172.2 3.5 %global_parts.5.refs_5_ = f32[512,256]{1,0:T(8,128)S(1)} custom-call(bf16[128,512]{1,0:T(8,128)(2,1)S(1)} %slice_reduce_fusion.refs_0_, bf16[768,512]{1,0:T(8,128)(2,1)S(1)} %copy-done.21, bf16[768,512]{1,0:T(8,128)(2,1)S(1)} %copy-done.27, bf16[768,512]{1,0:T(8,128)(2,1)S(1)} %copy-done.24, bf16[768,512]{1,0:T(8,128)(2,1)} %collective-permute-done.3.refs_4_, ...), custom_call_target="tpu_custom_call" | custom-call | flops 402653184 | bytes 25165824 | tf_op jit(solution)/shard_map/global_parts/pallas_call | solution.py:125
  176.5 9.3 %collective-permute-done.20 = bf16[32,512]{1,0:T(8,128)(2,1)S(1)} collective-permute-done((bf16[32,512]{1,0:T(8,128)(2,1)}, bf16[32,512]{1,0:T(8,128)(2,1)S(1)}, u32[]{:S(2)}, u32[]{:S(2)}) %collective-permute-start.20) | collective-permute-done | bytes 32800 | tf_op jit(solution)/shard_map/ppermute | solution.py:461
  185.8 1.4 add.196.refs_5_
  188.1 1.4 collective-permute-done.19.refs_5_.refs_9_
  192.4 2.5 pick_blocks.8
  194.9 4.4 %all-to-all-start.4 = ((bf16[8,1152,128]{2,1,0:T(8,128)(2,1)}), bf16[8,1152,128]{2,1,0:T(8,128)(2,1)}, u32[]{:S(2)}, u32[]{:S(2)}) async-start(bf16[8,1152,128]{2,1,0:T(8,128)(2,1)} %pick_blocks.8), calls=%async_computation.4 | async-start | bytes 4718592 | tf_op jit(solution)/shard_map/all_to_all | solution.py:77
  199.4 2.1 collective-permute-start.21
  201.5 1.7 collective-permute-start.13
  205.7 2.3 global_parts.6.refs_3_
  208.0 13.3 %collective-permute-done.13.refs_1_ = bf16[768,512]{1,0:T(8,128)(2,1)S(1)} collective-permute-done((bf16[768,512]{1,0:T(8,128)(2,1)S(1)}, bf16[768,512]{1,0:T(8,128)(2,1)S(1)}, u32[]{:S(2)}, u32[]{:S(2)}) %collective-permute-start.13) | collective-permute-done | bytes 786464 | tf_op jit(solution)/shard_map/ppermute | solution.py:24
  222.4 2.7 collective-permute-done.21.refs_6_.refs_10_
  226.1 1.8 global_parts.7.refs_3_
  228.0 1.9 pick_blocks.9
  229.9 4.4 %all-to-all-start.5 = ((bf16[8,640,128]{2,1,0:T(8,128)(2,1)}), bf16[8,640,128]{2,1,0:T(8,128)(2,1)S(1)}, u32[]{:S(2)}, u32[]{:S(2)}) async-start(bf16[8,640,128]{2,1,0:T(8,128)(2,1)} %pick_blocks.9), calls=%async_computation.5 | async-start | bytes 2621440 | tf_op jit(solution)/shard_map/all_to_all | solution.py:77
  235.2 15.5 %attend.1 = (f32[768,512]{1,0:T(8,128)}, f32[4,768,128]{2,1,0:T(8,128)}) custom-call(s32[144]{0:T(256)} %copy-done.39, s32[4]{0:T(128)} %pad_add_fusion.refs_1_.place, bf16[768,512]{1,0:T(8,128)(2,1)} %q.1, bf16[768,512]{1,0:T(8,128)(2,1)} %refs_3_.3, bf16[768,512]{1,0:T(8,128)(2,1)} %refs_4_.1, bf16[128,512]{1,0:T(8,128)(2,1)} %copy-done.37, ...), custom_call_target="tpu_custom_call" | custom-call | flops 805306368 | bytes 25165824 | tf_op jit(solution)/shard_map/attend/pallas_call | solution.py:294
  250.7 2.4 all-to-all-done.5.blocks_late
  253.1 1.4 copy-done.32
  254.5 1.4 copy-done.33
  255.9 8.7 %late_blocks.1 = (bf16[384,512]{1,0:T(8,128)(2,1)S(1)}, bf16[384,512]{1,0:T(8,128)(2,1)S(1)}, bf16[8,64,128]{2,1,0:T(8,128)(2,1)S(1)}) custom-call(s32[32]{0:T(128)S(1)} %reshape_squeeze.3.late, bf16[768,512]{1,0:T(8,128)(2,1)S(1)} %copy-done.11, f32[768,512]{1,0:T(8,128)S(1)} %copy-done.32, f32[4,768,128]{2,1,0:T(8,128)S(1)} %copy-done.33, ...), custom_call_target="tpu_custom_call" | custom-call | tf_op jit(solution)/shard_map/late_blocks/pallas_call | solution.py:379
  264.7 3.2 %collective-permute-start.26 = (bf16[384,512]{1,0:T(8,128)(2,1)S(1)}, bf16[384,512]{1,0:T(8,128)(2,1)S(1)}, u32[]{:S(2)}, u32[]{:S(2)}) collective-permute-start(bf16[384,512]{1,0:T(8,128)(2,1)S(1)} %get-tuple-element.109.refs_0_), channel_id=1, source_target_pairs={{0,192},{64,0},{128,64},{192,128},{1,193},{65,1},{129,65},{193,129... | collective-permute-start | bytes 1179656 | tf_op jit(solution)/shard_map/ppermute | solution.py:29
  268.0 1.4 collective-permute-start.23
  269.4 7.7 %collective-permute-done.22.refs_1_ = bf16[384,512]{1,0:T(8,128)(2,1)S(1)} collective-permute-done((bf16[384,512]{1,0:T(8,128)(2,1)S(1)}, bf16[384,512]{1,0:T(8,128)(2,1)S(1)}, u32[]{:S(2)}, u32[]{:S(2)}) %collective-permute-start.22) | collective-permute-done | bytes 393248 | tf_op jit(solution)/shard_map/ppermute | solution.py:29
  277.8 3.3 %collective-permute-start.27 = (bf16[384,512]{1,0:T(8,128)(2,1)S(1)}, bf16[384,512]{1,0:T(8,128)(2,1)S(1)}, u32[]{:S(2)}, u32[]{:S(2)}) collective-permute-start(bf16[384,512]{1,0:T(8,128)(2,1)S(1)} %collective-permute-done.26.refs_2_), channel_id=1, source_target_pairs={{0,192},{64,0},{128,64},{192,128},{1,193},{65,1},{129,65},{193,129... | collective-permute-start | bytes 1179656 | tf_op jit(solution)/shard_map/ppermute | solution.py:29
  281.2 8.9 %all_to_all.35 = bf16[8,64,128]{2,1,0:T(8,128)(2,1)S(1)} all-to-all(bf16[8,64,128]{2,1,0:T(8,128)(2,1)S(1)} %get-tuple-element.110), channel_id=1, replica_groups=mesh['heads'=4,'seq_0'=8,'seq_1'=4,'seq_2'=2] {'seq_1','seq_2'}, dimensions={0} | all-to-all | bytes 262144 | tf_op jit(solution)/shard_map/all_to_all | solution.py:77
  290.3 3.2 %collective-permute-start.29 = (bf16[128,512]{1,0:T(8,128)(2,1)S(1)}, bf16[128,512]{1,0:T(8,128)(2,1)S(1)}, u32[]{:S(2)}, u32[]{:S(2)}) collective-permute-start(bf16[128,512]{1,0:T(8,128)(2,1)S(1)} %bitcast.13), channel_id=1, source_target_pairs={{0,192},{64,0},{128,64},{192,128},{1,193},{65,1},{129,65},{193,129... | collective-permute-start | bytes 393224 | tf_op jit(solution)/shard_map/ppermute | solution.py:29
  293.5 3.0 upper_product.1.top
  296.5 4.4 %collective-permute-done.28.refs_5_ = bf16[128,512]{1,0:T(8,128)(2,1)S(1)} collective-permute-done((bf16[128,512]{1,0:T(8,128)(2,1)S(1)}, bf16[128,512]{1,0:T(8,128)(2,1)S(1)}, u32[]{:S(2)}, u32[]{:S(2)}) %collective-permute-start.28) | collective-permute-done | bytes 131104 | tf_op jit(solution)/shard_map/ppermute | solution.py:29
  301.0 2.1 collective-permute-done.30.refs_7_
  303.1 4.9 %lower_product.1 = bf16[768,1024]{1,0:T(8,128)(2,1)} custom-call(s32[4]{0:T(128)S(1)} %copy-done.35, bf16[384,1024]{1,0:T(8,128)(2,1)S(1)} %upper_product.1.top, bf16[384,512]{1,0:T(8,128)(2,1)S(1)} %get-tuple-element.109.refs_0_, bf16[384,512]{1,0:T(8,128)(2,1)S(1)} %collective-permute-done.25.refs_1_, ...), custom_call_target="tpu_custom_call" | custom-call | flops 1610612736 | bytes 8388608 | tf_op jit(solution)/shard_map/lower_product/pallas_call | solution.py:193
  (144 shorter events, 37.8 us)
Async XLA Ops:
  0.0 12.4 %copy-start.1 = (bf16[768,512]{1,0:T(8,128)(2,1)S(1)}, bf16[768,512]{1,0:T(8,128)(2,1)}, u32[]{:S(2)}) copy-start(bf16[768,512]{1,0:T(8,128)(2,1)} %refs_4_.1) | copy-start | bytes 2359300
  0.0 19.5 %collective-permute-start = (bf16[768,512]{1,0:T(8,128)(2,1)}, bf16[768,512]{1,0:T(8,128)(2,1)S(1)}, u32[]{:S(2)}, u32[]{:S(2)}) collective-permute-start(bf16[768,512]{1,0:T(8,128)(2,1)} %refs_3_.3), channel_id=1, source_target_pairs={{0,8},{8,16},{16,24},{24,32},{32,40},{40,48},{48,56},{56,0},{1,9},... | collective-permute-start | bytes 2359304 | tf_op jit(solution)/shard_map/ppermute | solution.py:24
  1.9 19.5 %collective-permute-start.2 = (bf16[768,512]{1,0:T(8,128)(2,1)}, bf16[768,512]{1,0:T(8,128)(2,1)}, u32[]{:S(2)}, u32[]{:S(2)}) collective-permute-start(bf16[768,512]{1,0:T(8,128)(2,1)} %refs_4_.1), channel_id=1, source_target_pairs={{0,56},{8,0},{16,8},{24,16},{32,24},{40,32},{48,40},{56,48},{1,57}... | collective-permute-start | bytes 2359304 | tf_op jit(solution)/shard_map/ppermute | solution.py:24
  12.2 3.7 %copy-start.39 = (s32[144]{0:T(256)}, s32[144]{0:T(256)S(1)}, u32[]{:S(2)}) copy-start(s32[144]{0:T(256)S(1)} %multiply_add_fusion.refs_0_) | copy-start | bytes 1732
  13.7 2.8 copy-start.36
  18.4 10.6 %copy-start = (bf16[768,512]{1,0:T(8,128)(2,1)S(1)}, bf16[768,512]{1,0:T(8,128)(2,1)}, u32[]{:S(2)}) copy-start(bf16[768,512]{1,0:T(8,128)(2,1)} %refs_3_.3) | copy-start | bytes 2359300
  19.5 59.0 %copy-start.17 = (bf16[768,512]{1,0:T(8,128)(2,1)}, bf16[768,512]{1,0:T(8,128)(2,1)S(1)}, u32[]{:S(2)}) copy-start(bf16[768,512]{1,0:T(8,128)(2,1)S(1)} %collective-permute-done.refs_1_) | copy-start | bytes 2359300
  21.4 24.8 %all-to-all-start = ((bf16[8,176,512]{2,1,0:T(8,128)(2,1)}), bf16[8,176,512]{2,1,0:T(8,128)(2,1)}, u32[]{:S(2)}, u32[]{:S(2)}) async-start(bf16[8,176,512]{2,1,0:T(8,128)(2,1)} %fusion.1), calls=%async_computation | async-start | bytes 2883584 | tf_op jit(solution)/shard_map/all_to_all | solution.py:77
  25.9 21.1 %collective-permute-start.4 = (bf16[768,512]{1,0:T(8,128)(2,1)S(1)}, bf16[768,512]{1,0:T(8,128)(2,1)}, u32[]{:S(2)}, u32[]{:S(2)}) collective-permute-start(bf16[768,512]{1,0:T(8,128)(2,1)S(1)} %copy-done.1), channel_id=1, source_target_pairs={{0,8},{8,16},{16,24},{24,32},{32,40},{40,48},{48,56},{56,0},{1,9},... | collective-permute-start | bytes 2359304 | tf_op jit(solution)/shard_map/ppermute | solution.py:24
  29.0 21.0 %collective-permute-start.5 = (bf16[768,512]{1,0:T(8,128)(2,1)S(1)}, bf16[768,512]{1,0:T(8,128)(2,1)}, u32[]{:S(2)}, u32[]{:S(2)}) collective-permute-start(bf16[768,512]{1,0:T(8,128)(2,1)S(1)} %copy-done), channel_id=1, source_target_pairs={{0,56},{8,0},{16,8},{24,16},{32,24},{40,32},{48,40},{56,48},{1,57}... | collective-permute-start | bytes 2359304 | tf_op jit(solution)/shard_map/ppermute | solution.py:24
  51.8 26.6 %all-to-all-start.1 = ((bf16[8,512,128]{2,1,0:T(8,128)(2,1)}), bf16[8,512,128]{2,1,0:T(8,128)(2,1)}, u32[]{:S(2)}, u32[]{:S(2)}) async-start(bf16[8,512,128]{2,1,0:T(8,128)(2,1)} %copy-done.10), calls=%async_computation.1 | async-start | bytes 2097152 | tf_op jit(solution)/shard_map/all_to_all | solution.py:77
  56.3 21.3 %collective-permute-start.1 = (bf16[768,512]{1,0:T(8,128)(2,1)S(1)}, bf16[768,512]{1,0:T(8,128)(2,1)S(1)}, u32[]{:S(2)}, u32[]{:S(2)}) collective-permute-start(bf16[768,512]{1,0:T(8,128)(2,1)S(1)} %collective-permute-done.refs_1_), channel_id=1, source_target_pairs={{0,8},{8,16},{16,24},{24,32},{32,40},{40,48},{48,56},{56,0},{1,9},... | collective-permute-start | bytes 2359304 | tf_op jit(solution)/shard_map/ppermute | solution.py:24
  58.0 20.4 %collective-permute-start.3 = (bf16[768,512]{1,0:T(8,128)(2,1)}, bf16[768,512]{1,0:T(8,128)(2,1)}, u32[]{:S(2)}, u32[]{:S(2)}) collective-permute-start(bf16[768,512]{1,0:T(8,128)(2,1)} %collective-permute-done.2.refs_4_.refs_5_), channel_id=1, source_target_pairs={{0,56},{8,0},{16,8},{24,16},{32,24},{40,32},{48,40},{56,48},{1,57}... | collective-permute-start | bytes 2359304 | tf_op jit(solution)/shard_map/ppermute | solution.py:24
  59.3 17.6 %collective-permute-start.10 = (bf16[32,512]{1,0:T(8,128)(2,1)S(1)}, bf16[32,512]{1,0:T(8,128)(2,1)S(1)}, u32[]{:S(2)}, u32[]{:S(2)}) collective-permute-start(bf16[32,512]{1,0:T(8,128)(2,1)S(1)} %slice_reduce_fusion.1), channel_id=1, source_target_pairs={{0,8},{8,0},{16,24},{24,16},{32,40},{40,32},{48,56},{56,48},{1,9},... | collective-permute-start | bytes 98312 | tf_op jit(solution)/shard_map/ppermute | solution.py:461
  80.7 1.3 copy-start.2
  82.0 56.2 %all-to-all-start.2 = ((bf16[8,1024,128]{2,1,0:T(8,128)(2,1)}), bf16[8,1024,128]{2,1,0:T(8,128)(2,1)}, u32[]{:S(2)}, u32[]{:S(2)}) async-start(bf16[8,1024,128]{2,1,0:T(8,128)(2,1)} %copy-done.2), calls=%async_computation.2 | async-start | bytes 4194304 | tf_op jit(solution)/shard_map/all_to_all | solution.py:77
  86.4 20.8 %copy-start.18 = (bf16[768,512]{1,0:T(8,128)(2,1)S(1)}, bf16[768,512]{1,0:T(8,128)(2,1)}, u32[]{:S(2)}) copy-start(bf16[768,512]{1,0:T(8,128)(2,1)} %copy-done.17) | copy-start | bytes 2359300
  86.4 50.7 %collective-permute-start.15 = (bf16[512,1024]{1,0:T(8,128)(2,1)}, bf16[512,1024]{1,0:T(8,128)(2,1)S(1)}, u32[]{:S(2)}, u32[]{:S(2)}) collective-permute-start(bf16[512,1024]{1,0:T(8,128)(2,1)} %get-tuple-element.73), channel_id=1, source_target_pairs={{0,128},{64,192},{128,0},{192,64},{1,129},{65,193},{129,1},{193,65... | collective-permute-start | bytes 3145736 | tf_op jit(solution)/shard_map/ppermute | solution.py:29
  89.5 11.1 %collective-permute-start.16 = (bf16[128,512]{1,0:T(8,128)(2,1)}, bf16[128,512]{1,0:T(8,128)(2,1)S(1)}, u32[]{:S(2)}, u32[]{:S(2)}) collective-permute-start(bf16[128,512]{1,0:T(8,128)(2,1)} %get-tuple-element.74), channel_id=1, source_target_pairs={{0,1},{1,2},{2,3},{3,4},{4,5},{5,6},{6,7},{7,8},{8,9},{9,10},{10,1... | collective-permute-start | bytes 393224 | tf_op jit(solution)/shard_map/ppermute | solution.py:465
  91.6 10.7 %collective-permute-start.17 = (bf16[128,512]{1,0:T(8,128)(2,1)}, bf16[128,512]{1,0:T(8,128)(2,1)S(1)}, u32[]{:S(2)}, u32[]{:S(2)}) collective-permute-start(bf16[128,512]{1,0:T(8,128)(2,1)} %get-tuple-element.75), channel_id=1, source_target_pairs={{1,0},{2,1},{3,2},{4,3},{5,4},{6,5},{7,6},{8,7},{9,8},{10,9},{11,1... | collective-permute-start | bytes 393224 | tf_op jit(solution)/shard_map/ppermute | solution.py:465
  97.4 6.4 %collective-permute-start.18 = (bf16[32,512]{1,0:T(8,128)(2,1)}, bf16[32,512]{1,0:T(8,128)(2,1)S(1)}, u32[]{:S(2)}, u32[]{:S(2)}) collective-permute-start(bf16[32,512]{1,0:T(8,128)(2,1)} %add.194), channel_id=1, source_target_pairs={{0,16},{8,24},{16,0},{24,8},{32,48},{40,56},{48,32},{56,40},{1,17}... | collective-permute-start | bytes 98312 | tf_op jit(solution)/shard_map/ppermute | solution.py:461
  100.2 20.0 %collective-permute-start.6 = (bf16[768,512]{1,0:T(8,128)(2,1)}, bf16[768,512]{1,0:T(8,128)(2,1)S(1)}, u32[]{:S(2)}, u32[]{:S(2)}) collective-permute-start(bf16[768,512]{1,0:T(8,128)(2,1)} %copy-done.19), channel_id=1, source_target_pairs={{0,8},{8,16},{16,24},{24,32},{32,40},{40,48},{48,56},{56,0},{1,9},... | collective-permute-start | bytes 2359304 | tf_op jit(solution)/shard_map/ppermute | solution.py:24
  100.6 3.1 %copy-start.37 = (bf16[128,512]{1,0:T(8,128)(2,1)}, bf16[128,512]{1,0:T(8,128)(2,1)S(1)}, u32[]{:S(2)}) copy-start(bf16[128,512]{1,0:T(8,128)(2,1)S(1)} %collective-permute-done.16.refs_5_) | copy-start | bytes 393220
  100.6 19.6 %collective-permute-start.7 = (bf16[768,512]{1,0:T(8,128)(2,1)}, bf16[768,512]{1,0:T(8,128)(2,1)S(1)}, u32[]{:S(2)}, u32[]{:S(2)}) collective-permute-start(bf16[768,512]{1,0:T(8,128)(2,1)} %collective-permute-done.3.refs_4_), channel_id=1, source_target_pairs={{0,56},{8,0},{16,8},{24,16},{32,24},{40,32},{48,40},{56,48},{1,57}... | collective-permute-start | bytes 2359304 | tf_op jit(solution)/shard_map/ppermute | solution.py:24
  102.3 3.6 %copy-start.38 = (bf16[128,512]{1,0:T(8,128)(2,1)}, bf16[128,512]{1,0:T(8,128)(2,1)S(1)}, u32[]{:S(2)}) copy-start(bf16[128,512]{1,0:T(8,128)(2,1)S(1)} %collective-permute-done.17.refs_6_) | copy-start | bytes 393220
  102.3 33.1 %collective-permute-start.8 = (bf16[768,512]{1,0:T(8,128)(2,1)}, bf16[768,512]{1,0:T(8,128)(2,1)S(1)}, u32[]{:S(2)}, u32[]{:S(2)}) collective-permute-start(bf16[768,512]{1,0:T(8,128)(2,1)} %collective-permute-done.4.refs_3_.refs_4_), channel_id=1, source_target_pairs={{0,8},{8,16},{16,24},{24,32},{32,40},{40,48},{48,56},{56,0},{1,9},... | collective-permute-start | bytes 2359304 | tf_op jit(solution)/shard_map/ppermute | solution.py:24
  103.8 32.5 %collective-permute-start.9 = (bf16[768,512]{1,0:T(8,128)(2,1)}, bf16[768,512]{1,0:T(8,128)(2,1)S(1)}, u32[]{:S(2)}, u32[]{:S(2)}) collective-permute-start(bf16[768,512]{1,0:T(8,128)(2,1)} %collective-permute-done.5.refs_2_), channel_id=1, source_target_pairs={{0,56},{8,0},{16,8},{24,16},{32,24},{40,32},{48,40},{56,48},{1,57}... | collective-permute-start | bytes 2359304 | tf_op jit(solution)/shard_map/ppermute | solution.py:24
  138.2 1.1 copy-start.20
  139.3 1.1 copy-start.23
  140.5 1.1 copy-start.26
  143.3 1.3 copy-start.3
  144.6 45.8 %all-to-all-start.3 = ((bf16[8,1024,128]{2,1,0:T(8,128)(2,1)}), bf16[8,1024,128]{2,1,0:T(8,128)(2,1)}, u32[]{:S(2)}, u32[]{:S(2)}) async-start(bf16[8,1024,128]{2,1,0:T(8,128)(2,1)} %copy-done.3), calls=%async_computation.3 | async-start | bytes 4194304 | tf_op jit(solution)/shard_map/all_to_all | solution.py:77
  162.5 28.0 %copy-start.13 = (bf16[768,512]{1,0:T(8,128)(2,1)S(1)}, bf16[768,512]{1,0:T(8,128)(2,1)}, u32[]{:S(2)}) copy-start(bf16[768,512]{1,0:T(8,128)(2,1)} %copy-done.12) | copy-start | bytes 2359300
  162.5 27.0 %collective-permute-start.19 = (bf16[512,1024]{1,0:T(8,128)(2,1)}, bf16[512,1024]{1,0:T(8,128)(2,1)S(1)}, u32[]{:S(2)}, u32[]{:S(2)}) collective-permute-start(bf16[512,1024]{1,0:T(8,128)(2,1)} %get-tuple-element.82), channel_id=1, source_target_pairs={{0,64},{64,128},{128,192},{192,0},{1,65},{65,129},{129,193},{193,1... | collective-permute-start | bytes 3145736 | tf_op jit(solution)/shard_map/ppermute | solution.py:29
  164.1 23.1 %collective-permute-start.11 = (bf16[768,512]{1,0:T(8,128)(2,1)}, bf16[768,512]{1,0:T(8,128)(2,1)S(1)}, u32[]{:S(2)}, u32[]{:S(2)}) collective-permute-start(bf16[768,512]{1,0:T(8,128)(2,1)} %copy-done.25), channel_id=1, source_target_pairs={{0,56},{8,0},{16,8},{24,16},{32,24},{40,32},{48,40},{56,48},{1,57}... | collective-permute-start | bytes 2359304 | tf_op jit(solution)/shard_map/ppermute | solution.py:24
  164.5 22.7 %collective-permute-start.12 = (bf16[768,512]{1,0:T(8,128)(2,1)}, bf16[768,512]{1,0:T(8,128)(2,1)S(1)}, u32[]{:S(2)}, u32[]{:S(2)}) collective-permute-start(bf16[768,512]{1,0:T(8,128)(2,1)} %copy-done.22), channel_id=1, source_target_pairs={{0,8},{8,16},{16,24},{24,32},{32,40},{40,48},{48,56},{56,0},{1,9},... | collective-permute-start | bytes 2359304 | tf_op jit(solution)/shard_map/ppermute | solution.py:24
  166.1 19.7 %collective-permute-start.20 = (bf16[32,512]{1,0:T(8,128)(2,1)}, bf16[32,512]{1,0:T(8,128)(2,1)S(1)}, u32[]{:S(2)}, u32[]{:S(2)}) collective-permute-start(bf16[32,512]{1,0:T(8,128)(2,1)} %add.195), channel_id=1, source_target_pairs={{0,32},{8,40},{16,48},{24,56},{32,0},{40,8},{48,16},{56,24},{1,33}... | collective-permute-start | bytes 98312 | tf_op jit(solution)/shard_map/ppermute | solution.py:461
  167.8 1.1 copy-start.21
  168.9 1.1 copy-start.24
  170.1 1.1 copy-start.27
  171.2 1.0 copy-start.31
  190.5 1.1 copy-start.15
  194.9 35.0 %all-to-all-start.4 = ((bf16[8,1152,128]{2,1,0:T(8,128)(2,1)}), bf16[8,1152,128]{2,1,0:T(8,128)(2,1)}, u32[]{:S(2)}, u32[]{:S(2)}) async-start(bf16[8,1152,128]{2,1,0:T(8,128)(2,1)} %pick_blocks.8), calls=%async_computation.4 | async-start | bytes 4718592 | tf_op jit(solution)/shard_map/all_to_all | solution.py:77
  199.4 25.8 %collective-permute-start.21 = (bf16[512,1024]{1,0:T(8,128)(2,1)}, bf16[512,1024]{1,0:T(8,128)(2,1)S(1)}, u32[]{:S(2)}, u32[]{:S(2)}) collective-permute-start(bf16[512,1024]{1,0:T(8,128)(2,1)} %get-tuple-element.94), channel_id=1, source_target_pairs={{0,192},{64,0},{128,64},{192,128},{1,193},{65,1},{129,65},{193,129... | collective-permute-start | bytes 3145736 | tf_op jit(solution)/shard_map/ppermute | solution.py:29
  201.5 19.8 %collective-permute-start.13 = (bf16[768,512]{1,0:T(8,128)(2,1)S(1)}, bf16[768,512]{1,0:T(8,128)(2,1)S(1)}, u32[]{:S(2)}, u32[]{:S(2)}) collective-permute-start(bf16[768,512]{1,0:T(8,128)(2,1)S(1)} %collective-permute-done.6.refs_1_), channel_id=1, source_target_pairs={{0,8},{8,16},{16,24},{24,32},{32,40},{40,48},{48,56},{56,0},{1,9},... | collective-permute-start | bytes 2359304 | tf_op jit(solution)/shard_map/ppermute | solution.py:24
  203.2 19.2 %collective-permute-start.14 = (bf16[768,512]{1,0:T(8,128)(2,1)S(1)}, bf16[768,512]{1,0:T(8,128)(2,1)S(1)}, u32[]{:S(2)}, u32[]{:S(2)}) collective-permute-start(bf16[768,512]{1,0:T(8,128)(2,1)S(1)} %copy-done.13), channel_id=1, source_target_pairs={{0,56},{8,0},{16,8},{24,16},{32,24},{40,32},{48,40},{56,48},{1,57}... | collective-permute-start | bytes 2359304 | tf_op jit(solution)/shard_map/ppermute | solution.py:24
  203.5 1.1 copy-start.16
  229.9 23.2 %all-to-all-start.5 = ((bf16[8,640,128]{2,1,0:T(8,128)(2,1)}), bf16[8,640,128]{2,1,0:T(8,128)(2,1)S(1)}, u32[]{:S(2)}, u32[]{:S(2)}) async-start(bf16[8,640,128]{2,1,0:T(8,128)(2,1)} %pick_blocks.9), calls=%async_computation.5 | async-start | bytes 2621440 | tf_op jit(solution)/shard_map/all_to_all | solution.py:77
  235.2 17.9 %copy-start.11 = (bf16[768,512]{1,0:T(8,128)(2,1)S(1)}, bf16[768,512]{1,0:T(8,128)(2,1)}, u32[]{:S(2)}) copy-start(bf16[768,512]{1,0:T(8,128)(2,1)} %q.1) | copy-start | bytes 2359300
  253.1 1.4 copy-start.32
  254.5 1.4 copy-start.33
  255.9 37.6 %copy-start.5 = (bf16[512,1024]{1,0:T(8,128)(2,1)S(1)}, bf16[512,1024]{1,0:T(8,128)(2,1)}, u32[]{:S(2)}) copy-start(bf16[512,1024]{1,0:T(8,128)(2,1)} %copy-done.4) | copy-start | bytes 3145732
  255.9 37.6 %copy-start.7 = (bf16[512,1024]{1,0:T(8,128)(2,1)S(1)}, bf16[512,1024]{1,0:T(8,128)(2,1)}, u32[]{:S(2)}) copy-start(bf16[512,1024]{1,0:T(8,128)(2,1)} %copy-done.6) | copy-start | bytes 3145732
  255.9 37.6 %copy-start.9 = (bf16[512,1024]{1,0:T(8,128)(2,1)S(1)}, bf16[512,1024]{1,0:T(8,128)(2,1)}, u32[]{:S(2)}) copy-start(bf16[512,1024]{1,0:T(8,128)(2,1)} %copy-done.8) | copy-start | bytes 3145732
  264.6 12.5 %collective-permute-start.22 = (bf16[384,512]{1,0:T(8,128)(2,1)S(1)}, bf16[384,512]{1,0:T(8,128)(2,1)S(1)}, u32[]{:S(2)}, u32[]{:S(2)}) collective-permute-start(bf16[384,512]{1,0:T(8,128)(2,1)S(1)} %get-tuple-element.104.refs_0_), channel_id=1, source_target_pairs={{0,64},{64,128},{128,192},{192,0},{1,65},{65,129},{129,193},{193,1... | collective-permute-start | bytes 1179656 | tf_op jit(solution)/shard_map/ppermute | solution.py:29
  264.7 13.1 %collective-permute-start.26 = (bf16[384,512]{1,0:T(8,128)(2,1)S(1)}, bf16[384,512]{1,0:T(8,128)(2,1)S(1)}, u32[]{:S(2)}, u32[]{:S(2)}) collective-permute-start(bf16[384,512]{1,0:T(8,128)(2,1)S(1)} %get-tuple-element.109.refs_0_), channel_id=1, source_target_pairs={{0,192},{64,0},{128,64},{192,128},{1,193},{65,1},{129,65},{193,129... | collective-permute-start | bytes 1179656 | tf_op jit(solution)/shard_map/ppermute | solution.py:29
  268.0 22.3 %collective-permute-start.23 = (bf16[384,512]{1,0:T(8,128)(2,1)S(1)}, bf16[384,512]{1,0:T(8,128)(2,1)S(1)}, u32[]{:S(2)}, u32[]{:S(2)}) collective-permute-start(bf16[384,512]{1,0:T(8,128)(2,1)S(1)} %get-tuple-element.104.refs_0_), channel_id=1, source_target_pairs={{0,192},{64,0},{128,64},{192,128},{1,193},{65,1},{129,65},{193,129... | collective-permute-start | bytes 1179656 | tf_op jit(solution)/shard_map/ppermute | solution.py:29
  277.1 16.4 %collective-permute-start.24 = (bf16[384,512]{1,0:T(8,128)(2,1)S(1)}, bf16[384,512]{1,0:T(8,128)(2,1)S(1)}, u32[]{:S(2)}, u32[]{:S(2)}) collective-permute-start(bf16[384,512]{1,0:T(8,128)(2,1)S(1)} %collective-permute-done.22.refs_1_), channel_id=1, source_target_pairs={{0,64},{64,128},{128,192},{192,0},{1,65},{65,129},{129,193},{193,1... | collective-permute-start | bytes 1179656 | tf_op jit(solution)/shard_map/ppermute | solution.py:29
  277.1 25.9 %collective-permute-start.25 = (bf16[384,512]{1,0:T(8,128)(2,1)S(1)}, bf16[384,512]{1,0:T(8,128)(2,1)S(1)}, u32[]{:S(2)}, u32[]{:S(2)}) collective-permute-start(bf16[384,512]{1,0:T(8,128)(2,1)S(1)} %get-tuple-element.109.refs_0_), channel_id=1, source_target_pairs={{0,64},{64,128},{128,192},{192,0},{1,65},{65,129},{129,193},{193,1... | collective-permute-start | bytes 1179656 | tf_op jit(solution)/shard_map/ppermute | solution.py:29
  277.8 25.3 %collective-permute-start.27 = (bf16[384,512]{1,0:T(8,128)(2,1)S(1)}, bf16[384,512]{1,0:T(8,128)(2,1)S(1)}, u32[]{:S(2)}, u32[]{:S(2)}) collective-permute-start(bf16[384,512]{1,0:T(8,128)(2,1)S(1)} %collective-permute-done.26.refs_2_), channel_id=1, source_target_pairs={{0,192},{64,0},{128,64},{192,128},{1,193},{65,1},{129,65},{193,129... | collective-permute-start | bytes 1179656 | tf_op jit(solution)/shard_map/ppermute | solution.py:29
  290.2 12.9 %copy-start.35 = (s32[4]{0:T(128)S(1)}, s32[4]{0:T(128)}, u32[]{:S(2)}) copy-start(s32[4]{0:T(128)} %pad_add_fusion.refs_1_.place) | copy-start | bytes 52
  290.2 10.8 %collective-permute-start.28 = (bf16[128,512]{1,0:T(8,128)(2,1)S(1)}, bf16[128,512]{1,0:T(8,128)(2,1)S(1)}, u32[]{:S(2)}, u32[]{:S(2)}) collective-permute-start(bf16[128,512]{1,0:T(8,128)(2,1)S(1)} %bitcast.12), channel_id=1, source_target_pairs={{0,64},{64,128},{128,192},{192,0},{1,65},{65,129},{129,193},{193,1... | collective-permute-start | bytes 393224 | tf_op jit(solution)/shard_map/ppermute | solution.py:29
  290.3 10.7 %collective-permute-start.29 = (bf16[128,512]{1,0:T(8,128)(2,1)S(1)}, bf16[128,512]{1,0:T(8,128)(2,1)S(1)}, u32[]{:S(2)}, u32[]{:S(2)}) collective-permute-start(bf16[128,512]{1,0:T(8,128)(2,1)S(1)} %bitcast.13), channel_id=1, source_target_pairs={{0,192},{64,0},{128,64},{192,128},{1,193},{65,1},{129,65},{193,129... | collective-permute-start | bytes 393224 | tf_op jit(solution)/shard_map/ppermute | solution.py:29
  293.5 9.5 %collective-permute-start.30 = (bf16[128,512]{1,0:T(8,128)(2,1)S(1)}, bf16[128,512]{1,0:T(8,128)(2,1)S(1)}, u32[]{:S(2)}, u32[]{:S(2)}) collective-permute-start(bf16[128,512]{1,0:T(8,128)(2,1)S(1)} %bitcast.14), channel_id=1, source_target_pairs={{0,128},{64,192},{128,0},{192,64},{1,129},{65,193},{129,1},{193,65... | collective-permute-start | bytes 393224 | tf_op jit(solution)/shard_map/ppermute | solution.py:29
  (13 other events, 11.8 us)

commit v9 on v8

--- a/solution.py
+++ b/solution.py
@@ -451,9 +451,7 @@
     shared = found[:, many:-16].sum(axis=0)
     asked = found[:, -16, : PLANES * CAP].astype(jnp.int32).reshape(-1)
 
-    asked, _, _ = lax.optimization_barrier((asked, up_v, down_k))
-    picks = picked(asked, 0, [key_vectors, value_vectors])
-    arrived = [over_plane(picks)]
+    picks, arrived = (), []
     ahead = [(i, i + 1) for i in range(shards - 1)]
     back = [(j, i) for i, j in ahead]
 
@@ -461,9 +459,9 @@
         return own + lax.ppermute(own, "seq_0", [(i, i ^ apart) for i in range(PLANES)])
 
     shared = doubled(shared, 1)
-    first, parts = 1, ()
-    beside = [lax.ppermute(ends, SEQ, ahead), lax.ppermute(starts, SEQ, back)]
-    held = [up_k, down_k, up_v, down_v]
+    first, parts = 0, ()
+    beside = ()
+    held = [key_vectors, up_k, down_k, value_vectors, up_v, down_v]
     first_pair = (up_v, down_k)
     for step in range(2, PLANES // 2 + 1):
         if step > 2:
@@ -474,24 +472,25 @@
             up_v, down_k, _ = lax.optimization_barrier((up_v, down_k, picks))
         gate = (up_k, down_v) if step < PLANES // 2 else ()
         held, _, _, tied, parts, shared = lax.optimization_barrier(
-            (held, gate, arrived[-1], beside if step > 2 else (), parts, shared)
+            (held, gate, arrived[-1:], beside if step > 2 else (), parts, shared)
         )
         if step > 2:
-            weights[turn], before, after = tied
-        else:
-            before, after = beside
+            weights[turn] = tied[0]
+        if step > 3:
+            before, after = tied[1:]
         turn, away = ((3, 2), (1, 1), (2, -1))[step - 2]
         beside, _ = lax.optimization_barrier((weights[turn], held))
-        beside = (across(beside, away), before, after)
-        if step < PLANES // 2:
-            shared = doubled(shared, 2 * (step - 1))
+        beside = (across(beside, away),)
+        if step == 3:
+            ends, starts, _ = lax.optimization_barrier((ends, starts, held))
+            beside += (lax.ppermute(ends, SEQ, ahead), lax.ppermute(starts, SEQ, back))
+        if step == 3:
+            shared, _ = lax.optimization_barrier((shared, held))
+            shared = doubled(doubled(shared, 2), 4)
         picks = picked(asked, first, held, (shared,) if step == PLANES // 2 else ())
         arrived.append(over_plane(picks))
         first += len(held) // 2
-        both = held
-        if step == 2:
-            both = [*held[:2], key_vectors, *held[2:], value_vectors]
-        parts = (global_parts(asking, both, parts),)
+        parts = (global_parts(asking, held, parts),)
         if step < PLANES // 2:
             up_v = ring_step(up_v, 1)
             down_k = ring_step(down_k, -1)
@@ -499,7 +498,7 @@
         else:
             held = [up_k, down_v]
     held, _, parts, beside = lax.optimization_barrier((held, picks, parts, beside))
-    weights[turn], before, after = beside
+    weights[turn] = beside[0]
     parts = (global_parts(asking, held, parts),)
     arrived.append(over_plane(picked(asked, first, held, parts)))
     place = jnp.concatenate(

time: 311 us -> 291 us (0.936)
  starting transfers between devices: 89.1 us -> 71.5 us
  local copies, waits for them, and re-layouts: 32.6 us -> 25.6 us
  Pallas kernels: 53.1 us -> 57.4 us
  waiting for transfers between devices: 105 us -> 109 us
    all_to_all x6 -> x5, starting transfers between devices: 40.1 us -> 22 us  [over_plane(): return lax.all_to_all(parts, PLANE, split_axis=0, concat_axis=0, tiled=True)]
    ppermute x3, waiting for transfers between devices: 26 us -> 33.4 us  [doubled(): lax.ppermute(own, 'seq_0', [(i, i ^ apart) for i in range(PLANES)])]
    unnamed x81 -> x63, local copies, waits for them, and re-layouts: 28.1 us -> 21.3 us
    ppermute x12, waiting for transfers between devices: 18.4 us -> 14.1 us  [across(): lax.ppermute(shard, 'heads', [(i, (i + step) % peers) for i in range(peer...]
    pallas_call x5 -> x4, Pallas kernels: 9.24 us -> 12.4 us  [picked(): pl.pallas_call(lambda *refs: pick_kernel(n, first, *refs), out_shape=jax....]
    all_to_all x6 -> x5, waiting for transfers between devices: 19.6 us -> 17.1 us  [over_plane(): return lax.all_to_all(parts, PLANE, split_axis=0, concat_axis=0, tiled=True)]
  transfers between devices with their start and end apart: 37 -> 36, of which waited for: 16 -> 19; matrix products, arithmetic and copies ran while one was open for 7% -> 6% of each run, Pallas kernels for 10% -> 11%
where the time goes in v9:
time: 291 us; the launch traced here: 288 us
  waiting for transfers between devices  109 us (37%)
  starting transfers between devices  71.5 us (25%)
  Pallas kernels  57.4 us (20%)
  local copies, waits for them, and re-layouts  25.6 us (9%)
  other arithmetic  14.2 us (5%)
  blocking collectives  8.51 us (3%)
    ppermute x14, waiting for transfers between devices, ring_step(): lax.ppermute(shard, 'seq_0', [(i, (i + step) % peers) for i in range(peer...  44.4 us
    ppermute x3, waiting for transfers between devices, doubled(): lax.ppermute(own, 'seq_0', [(i, i ^ apart) for i in range(PLANES)])  33.4 us
    all_to_all x5, starting transfers between devices, over_plane(): return lax.all_to_all(parts, PLANE, split_axis=0, concat_axis=0, tiled=True)  22 us
    unnamed x63, local copies, waits for them, and re-layouts  21.3 us
    ppermute x12, starting transfers between devices, across(): lax.ppermute(shard, 'heads', [(i, (i + step) % peers) for i in range(peer...  19.6 us
    ppermute x14, starting transfers between devices, ring_step(): lax.ppermute(shard, 'seq_0', [(i, (i + step) % peers) for i in range(peer...  17.2 us
    all_to_all x5, waiting for transfers between devices, over_plane(): return lax.all_to_all(parts, PLANE, split_axis=0, concat_axis=0, tiled=True)  17.1 us
    pallas_call x1, Pallas kernels, attended(): pl.pallas_call(lambda *refs: attend_kernel(counts, *refs), out_shape=(jax...  15.4 us
  transfers between devices with their start and end apart: 36, of which 19 were waited for; matrix products, arithmetic and copies ran while one was open for 6% of the time, Pallas kernels for 11%

profile of v9, /device:TPU:32, one launch (start us, length us, event | category | flops | bytes accessed | tf_op | source)
XLA Modules:
  0.0 287.7 jit_solution(14072823027425530911)
XLA Ops:
  0.0 1.9 collective-permute-start
  6.5 2.2 fusion.14
  8.7 2.1 dynamic-slice_select_fusion.5
  12.0 1.2 fusion.15
  14.1 1.2 fusion.1
  16.1 1.9 constant_dynamic-slice_fusion
  18.0 1.5 collective-permute-done.refs_2_
  19.5 1.9 collective-permute-done.2.refs_6_
  21.4 4.5 %all-to-all-start = ((bf16[8,176,512]{2,1,0:T(8,128)(2,1)}), bf16[8,176,512]{2,1,0:T(8,128)(2,1)}, u32[]{:S(2)}, u32[]{:S(2)}) async-start(bf16[8,176,512]{2,1,0:T(8,128)(2,1)} %fusion.1), calls=%async_computation | async-start | bytes 2883584 | tf_op jit(solution)/shard_map/all_to_all | solution.py:77
  25.9 3.1 %collective-permute-start.4 = (bf16[768,512]{1,0:T(8,128)(2,1)S(1)}, bf16[768,512]{1,0:T(8,128)(2,1)}, u32[]{:S(2)}, u32[]{:S(2)}) collective-permute-start(bf16[768,512]{1,0:T(8,128)(2,1)S(1)} %copy-done.1), channel_id=1, source_target_pairs={{0,8},{8,16},{16,24},{24,32},{32,40},{40,48},{48,56},{56,0},{1,9},... | collective-permute-start | bytes 2359304 | tf_op jit(solution)/shard_map/ppermute | solution.py:24
  29.0 3.0 %collective-permute-start.1 = (bf16[768,512]{1,0:T(8,128)(2,1)S(1)}, bf16[768,512]{1,0:T(8,128)(2,1)}, u32[]{:S(2)}, u32[]{:S(2)}) collective-permute-start(bf16[768,512]{1,0:T(8,128)(2,1)S(1)} %collective-permute-done.refs_2_), channel_id=1, source_target_pairs={{0,8},{8,16},{16,24},{24,32},{32,40},{40,48},{48,56},{56,0},{1,9},... | collective-permute-start | bytes 2359304 | tf_op jit(solution)/shard_map/ppermute | solution.py:24
  32.0 14.2 %all-to-all-done = bf16[8,176,512]{2,1,0:T(8,128)(2,1)} async-done(((bf16[8,176,512]{2,1,0:T(8,128)(2,1)}), bf16[8,176,512]{2,1,0:T(8,128)(2,1)}, u32[]{:S(2)}, u32[]{:S(2)}) %all-to-all-start) | async-done | bytes 1441824 | tf_op jit(solution)/shard_map/all_to_all | solution.py:77
  47.2 2.4 collective-permute-start.9
  50.4 13.7 %collective-permute-done.9 = bf16[32,512]{1,0:T(8,128)(2,1)S(1)} collective-permute-done((bf16[32,512]{1,0:T(8,128)(2,1)S(1)}, bf16[32,512]{1,0:T(8,128)(2,1)S(1)}, u32[]{:S(2)}, u32[]{:S(2)}) %collective-permute-start.9) | collective-permute-done | bytes 32800 | tf_op jit(solution)/shard_map/ppermute | solution.py:459
  64.7 2.2 collective-permute-done.3.refs_4_
  66.9 4.1 %pick_blocks.4 = bf16[8,1536,128]{2,1,0:T(8,128)(2,1)} custom-call(s32[256]{0:T(256)S(1)} %reshape.185.refs_0_, bf16[768,512]{1,0:T(8,128)(2,1)S(1)} %copy-done, bf16[768,512]{1,0:T(8,128)(2,1)S(1)} %collective-permute-done.refs_2_, bf16[768,512]{1,0:T(8,128)(2,1)} %collective-permute-done.5.refs_3_, bf16[768,512]{1,0:T(8,128)(2,1)S(1)} %copy-done.1, ...), custom_call_target="tpu_custom_call" | custom-call | bytes 25165824 | tf_op jit(solution)/shard_map/pick_blocks/pallas_call | solution.py:65
  71.0 4.5 %all-to-all-start.1 = ((bf16[8,1536,128]{2,1,0:T(8,128)(2,1)}), bf16[8,1536,128]{2,1,0:T(8,128)(2,1)}, u32[]{:S(2)}, u32[]{:S(2)}) async-start(bf16[8,1536,128]{2,1,0:T(8,128)(2,1)} %pick_blocks.4), calls=%async_computation.1 | async-start | bytes 6291456 | tf_op jit(solution)/shard_map/all_to_all | solution.py:77
  75.4 3.1 %collective-permute-start.13 = (bf16[512,1024]{1,0:T(8,128)(2,1)}, bf16[512,1024]{1,0:T(8,128)(2,1)S(1)}, u32[]{:S(2)}, u32[]{:S(2)}) collective-permute-start(bf16[512,1024]{1,0:T(8,128)(2,1)} %get-tuple-element.72), channel_id=1, source_target_pairs={{0,128},{64,192},{128,0},{192,64},{1,129},{65,193},{129,1},{193,65... | collective-permute-start | bytes 3145736 | tf_op jit(solution)/shard_map/ppermute | solution.py:29
  78.5 3.0 %collective-permute-start.7 = (bf16[768,512]{1,0:T(8,128)(2,1)}, bf16[768,512]{1,0:T(8,128)(2,1)}, u32[]{:S(2)}, u32[]{:S(2)}) collective-permute-start(bf16[768,512]{1,0:T(8,128)(2,1)} %collective-permute-done.4.refs_5_), channel_id=1, source_target_pairs={{0,8},{8,16},{16,24},{24,32},{32,40},{40,48},{48,56},{56,0},{1,9},... | collective-permute-start | bytes 2359304 | tf_op jit(solution)/shard_map/ppermute | solution.py:24
  82.1 1.5 collective-permute-start.6
  83.6 1.4 slice_reduce_fusion.refs_0_
  85.0 4.1 %global_parts.4.refs_5_ = f32[512,256]{1,0:T(8,128)S(1)} custom-call(bf16[128,512]{1,0:T(8,128)(2,1)S(1)} %slice_reduce_fusion.refs_0_, bf16[768,512]{1,0:T(8,128)(2,1)S(1)} %copy-done, bf16[768,512]{1,0:T(8,128)(2,1)S(1)} %collective-permute-done.refs_2_, bf16[768,512]{1,0:T(8,128)(2,1)} %collective-permute-done.5.refs_3_, bf16[768,512]{1,0:T(8,128)(2,1)S(1)} %copy-done.1, ...), custom_call_target="tpu_custom_call" | custom-call | flops 603979776 | bytes 25165824 | tf_op jit(solution)/shard_map/global_parts/pallas_call | solution.py:125
  89.9 9.9 %collective-permute-done.7.refs_3_ = bf16[768,512]{1,0:T(8,128)(2,1)} collective-permute-done((bf16[768,512]{1,0:T(8,128)(2,1)}, bf16[768,512]{1,0:T(8,128)(2,1)}, u32[]{:S(2)}, u32[]{:S(2)}) %collective-permute-start.7) | collective-permute-done | bytes 786464 | tf_op jit(solution)/shard_map/ppermute | solution.py:24
  99.8 2.5 collective-permute-done.8.refs_2_
  102.3 15.6 %collective-permute-done.12.refs_4_ = bf16[768,512]{1,0:T(8,128)(2,1)S(1)} collective-permute-done((bf16[768,512]{1,0:T(8,128)(2,1)}, bf16[768,512]{1,0:T(8,128)(2,1)S(1)}, u32[]{:S(2)}, u32[]{:S(2)}) %collective-permute-start.12) | collective-permute-done | bytes 786464 | tf_op jit(solution)/shard_map/ppermute | solution.py:24
  120.8 3.7 %pick_blocks.5 = bf16[8,1024,128]{2,1,0:T(8,128)(2,1)} custom-call(s32[256]{0:T(256)S(1)} %reshape.185.refs_0_, bf16[768,512]{1,0:T(8,128)(2,1)} %collective-permute-done.1.refs_1_, bf16[768,512]{1,0:T(8,128)(2,1)} %collective-permute-done.8.refs_2_, bf16[768,512]{1,0:T(8,128)(2,1)} %collective-permute-done.7.refs_3_, ...), custom_call_target="tpu_custom_call" | custom-call | bytes 25165824 | tf_op jit(solution)/shard_map/pick_blocks/pallas_call | solution.py:65
  124.5 4.5 %all-to-all-start.2 = ((bf16[8,1024,128]{2,1,0:T(8,128)(2,1)}), bf16[8,1024,128]{2,1,0:T(8,128)(2,1)}, u32[]{:S(2)}, u32[]{:S(2)}) async-start(bf16[8,1024,128]{2,1,0:T(8,128)(2,1)} %pick_blocks.5), calls=%async_computation.2 | async-start | bytes 4194304 | tf_op jit(solution)/shard_map/all_to_all | solution.py:77
  130.0 1.7 collective-permute-start.11
  131.7 2.7 collective-permute-start.17
  134.4 15.8 %collective-permute-done.17 = bf16[32,512]{1,0:T(8,128)(2,1)S(1)} collective-permute-done((bf16[32,512]{1,0:T(8,128)(2,1)S(1)}, bf16[32,512]{1,0:T(8,128)(2,1)S(1)}, u32[]{:S(2)}, u32[]{:S(2)}) %collective-permute-start.17) | collective-permute-done | bytes 32800 | tf_op jit(solution)/shard_map/ppermute | solution.py:459
  150.2 2.1 collective-permute-start.18
  152.3 1.9 collective-permute-start.15
  154.2 3.9 %collective-permute-done.18 = bf16[32,512]{1,0:T(8,128)(2,1)S(1)} collective-permute-done((bf16[32,512]{1,0:T(8,128)(2,1)S(1)}, bf16[32,512]{1,0:T(8,128)(2,1)S(1)}, u32[]{:S(2)}, u32[]{:S(2)}) %collective-permute-start.18) | collective-permute-done | bytes 32800 | tf_op jit(solution)/shard_map/ppermute | solution.py:459
  158.1 3.6 %collective-permute-start.16 = (bf16[128,512]{1,0:T(8,128)(2,1)}, bf16[128,512]{1,0:T(8,128)(2,1)S(1)}, u32[]{:S(2)}, u32[]{:S(2)}) collective-permute-start(bf16[128,512]{1,0:T(8,128)(2,1)} %get-tuple-element.83), channel_id=1, source_target_pairs={{1,0},{2,1},{3,2},{4,3},{5,4},{6,5},{7,6},{8,7},{9,8},{10,9},{11,1... | collective-permute-start | bytes 393224 | tf_op jit(solution)/shard_map/ppermute | solution.py:486
  161.8 4.2 %global_parts.5.refs_5_ = f32[512,256]{1,0:T(8,128)S(1)} custom-call(bf16[128,512]{1,0:T(8,128)(2,1)S(1)} %slice_reduce_fusion.refs_0_, bf16[768,512]{1,0:T(8,128)(2,1)} %collective-permute-done.1.refs_1_, bf16[768,512]{1,0:T(8,128)(2,1)} %collective-permute-done.8.refs_2_, bf16[768,512]{1,0:T(8,128)(2,1)} %collective-permute-done.7.refs_3_, ...), custom_call_target="tpu_custom_call" | custom-call | flops 402653184 | bytes 25165824 | tf_op jit(solution)/shard_map/global_parts/pallas_call | solution.py:125
  173.3 2.6 pick_blocks.6
  175.9 4.4 %all-to-all-start.3 = ((bf16[8,1152,128]{2,1,0:T(8,128)(2,1)}), bf16[8,1152,128]{2,1,0:T(8,128)(2,1)}, u32[]{:S(2)}, u32[]{:S(2)}) async-start(bf16[8,1152,128]{2,1,0:T(8,128)(2,1)} %pick_blocks.6), calls=%async_computation.3 | async-start | bytes 4718592 | tf_op jit(solution)/shard_map/all_to_all | solution.py:77
  180.3 2.7 collective-permute-start.21
  183.0 1.3 collective-permute-start.19
  185.1 1.2 copy-done.9
  187.4 1.1 copy-done.15
  190.7 2.3 global_parts.6.refs_3_
  193.0 9.7 %collective-permute-done.19.refs_1_ = bf16[768,512]{1,0:T(8,128)(2,1)S(1)} collective-permute-done((bf16[768,512]{1,0:T(8,128)(2,1)}, bf16[768,512]{1,0:T(8,128)(2,1)S(1)}, u32[]{:S(2)}, u32[]{:S(2)}) %collective-permute-start.19) | collective-permute-done | bytes 786464 | tf_op jit(solution)/shard_map/ppermute | solution.py:24
  203.8 2.5 collective-permute-done.21.refs_6_.refs_10_
  206.2 1.8 global_parts.7.refs_3_
  208.1 1.9 pick_blocks.7
  210.3 4.2 %all-to-all-start.4 = ((bf16[8,640,128]{2,1,0:T(8,128)(2,1)}), bf16[8,640,128]{2,1,0:T(8,128)(2,1)S(1)}, u32[]{:S(2)}, u32[]{:S(2)}) async-start(bf16[8,640,128]{2,1,0:T(8,128)(2,1)} %pick_blocks.7), calls=%async_computation.4 | async-start | bytes 2621440 | tf_op jit(solution)/shard_map/all_to_all | solution.py:77
  215.3 15.4 %attend.1 = (f32[768,512]{1,0:T(8,128)}, f32[4,768,128]{2,1,0:T(8,128)}) custom-call(s32[144]{0:T(256)} %copy-done.30, s32[4]{0:T(128)} %pad_add_fusion.refs_1_.place, bf16[768,512]{1,0:T(8,128)(2,1)} %q.1, bf16[768,512]{1,0:T(8,128)(2,1)} %refs_3_.1, bf16[768,512]{1,0:T(8,128)(2,1)} %refs_4_.3, bf16[128,512]{1,0:T(8,128)(2,1)} %copy-done.27, ...), custom_call_target="tpu_custom_call" | custom-call | flops 805306368 | bytes 25165824 | tf_op jit(solution)/shard_map/attend/pallas_call | solution.py:294
  230.7 2.6 all-to-all-done.4.blocks_late
  233.3 1.1 copy-done.6
  234.4 1.4 copy-done.23
  235.8 1.4 copy-done.24
  237.2 9.2 %late_blocks.1 = (bf16[384,512]{1,0:T(8,128)(2,1)S(1)}, bf16[384,512]{1,0:T(8,128)(2,1)S(1)}, bf16[8,64,128]{2,1,0:T(8,128)(2,1)S(1)}) custom-call(s32[32]{0:T(128)S(1)} %reshape_squeeze.3.late, bf16[768,512]{1,0:T(8,128)(2,1)S(1)} %copy-done.6, f32[768,512]{1,0:T(8,128)S(1)} %copy-done.23, f32[4,768,128]{2,1,0:T(8,128)S(1)} %copy-done.24, ...), custom_call_target="tpu_custom_call" | custom-call | tf_op jit(solution)/shard_map/late_blocks/pallas_call | solution.py:379
  246.5 3.2 %collective-permute-start.26 = (bf16[384,512]{1,0:T(8,128)(2,1)S(1)}, bf16[384,512]{1,0:T(8,128)(2,1)S(1)}, u32[]{:S(2)}, u32[]{:S(2)}) collective-permute-start(bf16[384,512]{1,0:T(8,128)(2,1)S(1)} %get-tuple-element.109.refs_0_), channel_id=1, source_target_pairs={{0,192},{64,0},{128,64},{192,128},{1,193},{65,1},{129,65},{193,129... | collective-permute-start | bytes 1179656 | tf_op jit(solution)/shard_map/ppermute | solution.py:29
  249.8 1.5 collective-permute-start.23
  251.3 6.7 %collective-permute-done.22.refs_1_ = bf16[384,512]{1,0:T(8,128)(2,1)S(1)} collective-permute-done((bf16[384,512]{1,0:T(8,128)(2,1)S(1)}, bf16[384,512]{1,0:T(8,128)(2,1)S(1)}, u32[]{:S(2)}, u32[]{:S(2)}) %collective-permute-start.22) | collective-permute-done | bytes 393248 | tf_op jit(solution)/shard_map/ppermute | solution.py:29
  258.0 1.2 collective-permute-start.25
  259.3 3.7 %collective-permute-start.27 = (bf16[384,512]{1,0:T(8,128)(2,1)S(1)}, bf16[384,512]{1,0:T(8,128)(2,1)S(1)}, u32[]{:S(2)}, u32[]{:S(2)}) collective-permute-start(bf16[384,512]{1,0:T(8,128)(2,1)S(1)} %collective-permute-done.26.refs_2_), channel_id=1, source_target_pairs={{0,192},{64,0},{128,64},{192,128},{1,193},{65,1},{129,65},{193,129... | collective-permute-start | bytes 1179656 | tf_op jit(solution)/shard_map/ppermute | solution.py:29
  263.0 8.5 %all_to_all.30 = bf16[8,64,128]{2,1,0:T(8,128)(2,1)S(1)} all-to-all(bf16[8,64,128]{2,1,0:T(8,128)(2,1)S(1)} %get-tuple-element.110), channel_id=1, replica_groups=mesh['heads'=4,'seq_0'=8,'seq_1'=4,'seq_2'=2] {'seq_1','seq_2'}, dimensions={0} | all-to-all | bytes 262144 | tf_op jit(solution)/shard_map/all_to_all | solution.py:77
  271.8 3.2 %collective-permute-start.29 = (bf16[128,512]{1,0:T(8,128)(2,1)S(1)}, bf16[128,512]{1,0:T(8,128)(2,1)S(1)}, u32[]{:S(2)}, u32[]{:S(2)}) collective-permute-start(bf16[128,512]{1,0:T(8,128)(2,1)S(1)} %bitcast.13), channel_id=1, source_target_pairs={{0,192},{64,0},{128,64},{192,128},{1,193},{65,1},{129,65},{193,129... | collective-permute-start | bytes 393224 | tf_op jit(solution)/shard_map/ppermute | solution.py:29
  275.0 3.0 %upper_product.1.top = bf16[384,1024]{1,0:T(8,128)(2,1)S(1)} custom-call(bf16[384,512]{1,0:T(8,128)(2,1)S(1)} %get-tuple-element.104.refs_0_, bf16[384,512]{1,0:T(8,128)(2,1)S(1)} %collective-permute-done.22.refs_1_, bf16[384,512]{1,0:T(8,128)(2,1)S(1)} %collective-permute-done.23.refs_2_, bf16[384,512]{1,0:T(8,128)(2,1)S(1)} %collective-permute-done.24.refs_3_, ...), custom_call_target="tpu_custom_call" | custom-call | flops 1610612736 | bytes 8388608 | tf_op jit(solution)/shard_map/upper_product/pallas_call | solution.py:193
  278.0 3.2 %collective-permute-done.28.refs_5_ = bf16[128,512]{1,0:T(8,128)(2,1)S(1)} collective-permute-done((bf16[128,512]{1,0:T(8,128)(2,1)S(1)}, bf16[128,512]{1,0:T(8,128)(2,1)S(1)}, u32[]{:S(2)}, u32[]{:S(2)}) %collective-permute-start.28) | collective-permute-done | bytes 131104 | tf_op jit(solution)/shard_map/ppermute | solution.py:29
  281.2 1.6 collective-permute-done.30.refs_7_
  282.8 4.9 %lower_product.1 = bf16[768,1024]{1,0:T(8,128)(2,1)} custom-call(s32[4]{0:T(128)S(1)} %copy-done.25, bf16[384,1024]{1,0:T(8,128)(2,1)S(1)} %upper_product.1.top, bf16[384,512]{1,0:T(8,128)(2,1)S(1)} %get-tuple-element.109.refs_0_, bf16[384,512]{1,0:T(8,128)(2,1)S(1)} %collective-permute-done.25.refs_1_, ...), custom_call_target="tpu_custom_call" | custom-call | flops 1610612736 | bytes 8388608 | tf_op jit(solution)/shard_map/lower_product/pallas_call | solution.py:193
  (123 shorter events, 27.6 us)
Async XLA Ops:
  0.0 12.0 %copy-start.1 = (bf16[768,512]{1,0:T(8,128)(2,1)S(1)}, bf16[768,512]{1,0:T(8,128)(2,1)}, u32[]{:S(2)}) copy-start(bf16[768,512]{1,0:T(8,128)(2,1)} %refs_4_.3) | copy-start | bytes 2359300
  0.0 19.5 %collective-permute-start = (bf16[768,512]{1,0:T(8,128)(2,1)}, bf16[768,512]{1,0:T(8,128)(2,1)S(1)}, u32[]{:S(2)}, u32[]{:S(2)}) collective-permute-start(bf16[768,512]{1,0:T(8,128)(2,1)} %refs_3_.1), channel_id=1, source_target_pairs={{0,8},{8,16},{16,24},{24,32},{32,40},{40,48},{48,56},{56,0},{1,9},... | collective-permute-start | bytes 2359304 | tf_op jit(solution)/shard_map/ppermute | solution.py:24
  1.9 19.5 %collective-permute-start.2 = (bf16[768,512]{1,0:T(8,128)(2,1)}, bf16[768,512]{1,0:T(8,128)(2,1)}, u32[]{:S(2)}, u32[]{:S(2)}) collective-permute-start(bf16[768,512]{1,0:T(8,128)(2,1)} %refs_4_.3), channel_id=1, source_target_pairs={{0,56},{8,0},{16,8},{24,16},{32,24},{40,32},{48,40},{56,48},{1,57}... | collective-permute-start | bytes 2359304 | tf_op jit(solution)/shard_map/ppermute | solution.py:24
  11.8 3.6 %copy-start.30 = (s32[144]{0:T(256)}, s32[144]{0:T(256)S(1)}, u32[]{:S(2)}) copy-start(s32[144]{0:T(256)S(1)} %multiply_add_fusion.refs_0_) | copy-start | bytes 1732
  13.3 2.8 copy-start.26
  18.0 11.0 %copy-start = (bf16[768,512]{1,0:T(8,128)(2,1)S(1)}, bf16[768,512]{1,0:T(8,128)(2,1)}, u32[]{:S(2)}) copy-start(bf16[768,512]{1,0:T(8,128)(2,1)} %refs_3_.1) | copy-start | bytes 2359300
  21.4 24.8 %all-to-all-start = ((bf16[8,176,512]{2,1,0:T(8,128)(2,1)}), bf16[8,176,512]{2,1,0:T(8,128)(2,1)}, u32[]{:S(2)}, u32[]{:S(2)}) async-start(bf16[8,176,512]{2,1,0:T(8,128)(2,1)} %fusion.1), calls=%async_computation | async-start | bytes 2883584 | tf_op jit(solution)/shard_map/all_to_all | solution.py:77
  25.9 38.8 %collective-permute-start.4 = (bf16[768,512]{1,0:T(8,128)(2,1)S(1)}, bf16[768,512]{1,0:T(8,128)(2,1)}, u32[]{:S(2)}, u32[]{:S(2)}) collective-permute-start(bf16[768,512]{1,0:T(8,128)(2,1)S(1)} %copy-done.1), channel_id=1, source_target_pairs={{0,8},{8,16},{16,24},{24,32},{32,40},{40,48},{48,56},{56,0},{1,9},... | collective-permute-start | bytes 2359304 | tf_op jit(solution)/shard_map/ppermute | solution.py:24
  29.0 35.7 %collective-permute-start.5 = (bf16[768,512]{1,0:T(8,128)(2,1)S(1)}, bf16[768,512]{1,0:T(8,128)(2,1)}, u32[]{:S(2)}, u32[]{:S(2)}) collective-permute-start(bf16[768,512]{1,0:T(8,128)(2,1)S(1)} %copy-done), channel_id=1, source_target_pairs={{0,56},{8,0},{16,8},{24,16},{32,24},{40,32},{48,40},{56,48},{1,57}... | collective-permute-start | bytes 2359304 | tf_op jit(solution)/shard_map/ppermute | solution.py:24
  29.0 35.7 %collective-permute-start.1 = (bf16[768,512]{1,0:T(8,128)(2,1)S(1)}, bf16[768,512]{1,0:T(8,128)(2,1)}, u32[]{:S(2)}, u32[]{:S(2)}) collective-permute-start(bf16[768,512]{1,0:T(8,128)(2,1)S(1)} %collective-permute-done.refs_2_), channel_id=1, source_target_pairs={{0,8},{8,16},{16,24},{24,32},{32,40},{40,48},{48,56},{56,0},{1,9},... | collective-permute-start | bytes 2359304 | tf_op jit(solution)/shard_map/ppermute | solution.py:24
  32.0 34.9 %collective-permute-start.3 = (bf16[768,512]{1,0:T(8,128)(2,1)}, bf16[768,512]{1,0:T(8,128)(2,1)}, u32[]{:S(2)}, u32[]{:S(2)}) collective-permute-start(bf16[768,512]{1,0:T(8,128)(2,1)} %collective-permute-done.2.refs_6_), channel_id=1, source_target_pairs={{0,56},{8,0},{16,8},{24,16},{32,24},{40,32},{48,40},{56,48},{1,57}... | collective-permute-start | bytes 2359304 | tf_op jit(solution)/shard_map/ppermute | solution.py:24
  47.2 16.9 %collective-permute-start.9 = (bf16[32,512]{1,0:T(8,128)(2,1)S(1)}, bf16[32,512]{1,0:T(8,128)(2,1)S(1)}, u32[]{:S(2)}, u32[]{:S(2)}) collective-permute-start(bf16[32,512]{1,0:T(8,128)(2,1)S(1)} %slice_reduce_fusion.1), channel_id=1, source_target_pairs={{0,8},{8,0},{16,24},{24,16},{32,40},{40,32},{48,56},{56,48},{1,9},... | collective-permute-start | bytes 98312 | tf_op jit(solution)/shard_map/ppermute | solution.py:459
  71.0 49.8 %all-to-all-start.1 = ((bf16[8,1536,128]{2,1,0:T(8,128)(2,1)}), bf16[8,1536,128]{2,1,0:T(8,128)(2,1)}, u32[]{:S(2)}, u32[]{:S(2)}) async-start(bf16[8,1536,128]{2,1,0:T(8,128)(2,1)} %pick_blocks.4), calls=%async_computation.1 | async-start | bytes 6291456 | tf_op jit(solution)/shard_map/all_to_all | solution.py:77
  75.4 44.3 %collective-permute-start.13 = (bf16[512,1024]{1,0:T(8,128)(2,1)}, bf16[512,1024]{1,0:T(8,128)(2,1)S(1)}, u32[]{:S(2)}, u32[]{:S(2)}) collective-permute-start(bf16[512,1024]{1,0:T(8,128)(2,1)} %get-tuple-element.72), channel_id=1, source_target_pairs={{0,128},{64,192},{128,0},{192,64},{1,129},{65,193},{129,1},{193,65... | collective-permute-start | bytes 3145736 | tf_op jit(solution)/shard_map/ppermute | solution.py:29
  78.5 21.2 %collective-permute-start.7 = (bf16[768,512]{1,0:T(8,128)(2,1)}, bf16[768,512]{1,0:T(8,128)(2,1)}, u32[]{:S(2)}, u32[]{:S(2)}) collective-permute-start(bf16[768,512]{1,0:T(8,128)(2,1)} %collective-permute-done.4.refs_5_), channel_id=1, source_target_pairs={{0,8},{8,16},{16,24},{24,32},{32,40},{40,48},{48,56},{56,0},{1,9},... | collective-permute-start | bytes 2359304 | tf_op jit(solution)/shard_map/ppermute | solution.py:24
  81.5 20.7 %collective-permute-start.8 = (bf16[768,512]{1,0:T(8,128)(2,1)}, bf16[768,512]{1,0:T(8,128)(2,1)}, u32[]{:S(2)}, u32[]{:S(2)}) collective-permute-start(bf16[768,512]{1,0:T(8,128)(2,1)} %collective-permute-done.5.refs_3_), channel_id=1, source_target_pairs={{0,56},{8,0},{16,8},{24,16},{32,24},{40,32},{48,40},{56,48},{1,57}... | collective-permute-start | bytes 2359304 | tf_op jit(solution)/shard_map/ppermute | solution.py:24
  81.5 36.4 %collective-permute-start.12 = (bf16[768,512]{1,0:T(8,128)(2,1)}, bf16[768,512]{1,0:T(8,128)(2,1)S(1)}, u32[]{:S(2)}, u32[]{:S(2)}) collective-permute-start(bf16[768,512]{1,0:T(8,128)(2,1)} %collective-permute-done.3.refs_4_), channel_id=1, source_target_pairs={{0,56},{8,0},{16,8},{24,16},{32,24},{40,32},{48,40},{56,48},{1,57}... | collective-permute-start | bytes 2359304 | tf_op jit(solution)/shard_map/ppermute | solution.py:24
  82.1 36.7 %collective-permute-start.6 = (bf16[768,512]{1,0:T(8,128)(2,1)}, bf16[768,512]{1,0:T(8,128)(2,1)S(1)}, u32[]{:S(2)}, u32[]{:S(2)}) collective-permute-start(bf16[768,512]{1,0:T(8,128)(2,1)} %collective-permute-done.1.refs_1_), channel_id=1, source_target_pairs={{0,8},{8,16},{16,24},{24,32},{32,40},{40,48},{48,56},{56,0},{1,9},... | collective-permute-start | bytes 2359304 | tf_op jit(solution)/shard_map/ppermute | solution.py:24
  117.9 0.9 copy-start.7
  118.8 0.9 copy-start.10
  119.7 1.0 copy-start.2
  124.5 7.2 %copy-start.29 = (bf16[32,512]{1,0:T(8,128)(2,1)S(1)}, bf16[32,512]{1,0:T(8,128)(2,1)}, u32[]{:S(2)}) copy-start(bf16[32,512]{1,0:T(8,128)(2,1)} %add.194) | copy-start | bytes 98308
  124.5 37.3 %copy-start.22 = (f32[512,256]{1,0:T(8,128)S(1)}, f32[512,256]{1,0:T(8,128)}, u32[]{:S(2)}) copy-start(f32[512,256]{1,0:T(8,128)} %copy-done.21) | copy-start | bytes 1572868
  124.5 45.4 %all-to-all-start.2 = ((bf16[8,1024,128]{2,1,0:T(8,128)(2,1)}), bf16[8,1024,128]{2,1,0:T(8,128)(2,1)}, u32[]{:S(2)}, u32[]{:S(2)}) async-start(bf16[8,1024,128]{2,1,0:T(8,128)(2,1)} %pick_blocks.5), calls=%async_computation.2 | async-start | bytes 4194304 | tf_op jit(solution)/shard_map/all_to_all | solution.py:77
  129.1 40.9 %collective-permute-start.14 = (bf16[512,1024]{1,0:T(8,128)(2,1)}, bf16[512,1024]{1,0:T(8,128)(2,1)S(1)}, u32[]{:S(2)}, u32[]{:S(2)}) collective-permute-start(bf16[512,1024]{1,0:T(8,128)(2,1)} %get-tuple-element.79), channel_id=1, source_target_pairs={{0,64},{64,128},{128,192},{192,0},{1,65},{65,129},{129,193},{193,1... | collective-permute-start | bytes 3145736 | tf_op jit(solution)/shard_map/ppermute | solution.py:29
  129.7 37.1 %collective-permute-start.10 = (bf16[768,512]{1,0:T(8,128)(2,1)}, bf16[768,512]{1,0:T(8,128)(2,1)S(1)}, u32[]{:S(2)}, u32[]{:S(2)}) collective-permute-start(bf16[768,512]{1,0:T(8,128)(2,1)} %collective-permute-done.8.refs_2_), channel_id=1, source_target_pairs={{0,56},{8,0},{16,8},{24,16},{32,24},{40,32},{48,40},{56,48},{1,57}... | collective-permute-start | bytes 2359304 | tf_op jit(solution)/shard_map/ppermute | solution.py:24
  130.0 37.7 %collective-permute-start.11 = (bf16[768,512]{1,0:T(8,128)(2,1)}, bf16[768,512]{1,0:T(8,128)(2,1)S(1)}, u32[]{:S(2)}, u32[]{:S(2)}) collective-permute-start(bf16[768,512]{1,0:T(8,128)(2,1)} %collective-permute-done.7.refs_3_), channel_id=1, source_target_pairs={{0,8},{8,16},{16,24},{24,32},{32,40},{40,48},{48,56},{56,0},{1,9},... | collective-permute-start | bytes 2359304 | tf_op jit(solution)/shard_map/ppermute | solution.py:24
  131.7 18.5 %collective-permute-start.17 = (bf16[32,512]{1,0:T(8,128)(2,1)S(1)}, bf16[32,512]{1,0:T(8,128)(2,1)S(1)}, u32[]{:S(2)}, u32[]{:S(2)}) collective-permute-start(bf16[32,512]{1,0:T(8,128)(2,1)S(1)} %copy-done.29), channel_id=1, source_target_pairs={{0,16},{8,24},{16,0},{24,8},{32,48},{40,56},{48,32},{56,40},{1,17}... | collective-permute-start | bytes 98312 | tf_op jit(solution)/shard_map/ppermute | solution.py:459
  150.2 19.7 %copy-start.8 = (bf16[768,512]{1,0:T(8,128)(2,1)S(1)}, bf16[768,512]{1,0:T(8,128)(2,1)}, u32[]{:S(2)}) copy-start(bf16[768,512]{1,0:T(8,128)(2,1)} %copy-done.7) | copy-start | bytes 2359300
  150.2 7.9 %collective-permute-start.18 = (bf16[32,512]{1,0:T(8,128)(2,1)S(1)}, bf16[32,512]{1,0:T(8,128)(2,1)S(1)}, u32[]{:S(2)}, u32[]{:S(2)}) collective-permute-start(bf16[32,512]{1,0:T(8,128)(2,1)S(1)} %add.195), channel_id=1, source_target_pairs={{0,32},{8,40},{16,48},{24,56},{32,0},{40,8},{48,16},{56,24},{1,33}... | collective-permute-start | bytes 98312 | tf_op jit(solution)/shard_map/ppermute | solution.py:459
  152.3 16.3 %collective-permute-start.15 = (bf16[128,512]{1,0:T(8,128)(2,1)}, bf16[128,512]{1,0:T(8,128)(2,1)S(1)}, u32[]{:S(2)}, u32[]{:S(2)}) collective-permute-start(bf16[128,512]{1,0:T(8,128)(2,1)} %get-tuple-element.82), channel_id=1, source_target_pairs={{0,1},{1,2},{2,3},{3,4},{4,5},{5,6},{6,7},{7,8},{8,9},{9,10},{10,1... | collective-permute-start | bytes 393224 | tf_op jit(solution)/shard_map/ppermute | solution.py:486
  158.1 11.1 %collective-permute-start.16 = (bf16[128,512]{1,0:T(8,128)(2,1)}, bf16[128,512]{1,0:T(8,128)(2,1)S(1)}, u32[]{:S(2)}, u32[]{:S(2)}) collective-permute-start(bf16[128,512]{1,0:T(8,128)(2,1)} %get-tuple-element.83), channel_id=1, source_target_pairs={{1,0},{2,1},{3,2},{4,3},{5,4},{6,5},{7,6},{8,7},{9,8},{10,9},{11,1... | collective-permute-start | bytes 393224 | tf_op jit(solution)/shard_map/ppermute | solution.py:486
  166.0 0.8 copy-start.19
  166.8 0.9 copy-start.13
  167.7 0.9 copy-start.16
  169.9 1.1 copy-start.11
  171.1 1.1 copy-start.14
  172.2 1.1 copy-start.17
  175.9 34.4 %all-to-all-start.3 = ((bf16[8,1152,128]{2,1,0:T(8,128)(2,1)}), bf16[8,1152,128]{2,1,0:T(8,128)(2,1)}, u32[]{:S(2)}, u32[]{:S(2)}) async-start(bf16[8,1152,128]{2,1,0:T(8,128)(2,1)} %pick_blocks.6), calls=%async_computation.3 | async-start | bytes 4718592 | tf_op jit(solution)/shard_map/all_to_all | solution.py:77
  180.3 25.9 %collective-permute-start.21 = (bf16[512,1024]{1,0:T(8,128)(2,1)}, bf16[512,1024]{1,0:T(8,128)(2,1)S(1)}, u32[]{:S(2)}, u32[]{:S(2)}) collective-permute-start(bf16[512,1024]{1,0:T(8,128)(2,1)} %get-tuple-element.100), channel_id=1, source_target_pairs={{0,192},{64,0},{128,64},{192,128},{1,193},{65,1},{129,65},{193,129... | collective-permute-start | bytes 3145736 | tf_op jit(solution)/shard_map/ppermute | solution.py:29
  183.0 19.7 %collective-permute-start.19 = (bf16[768,512]{1,0:T(8,128)(2,1)}, bf16[768,512]{1,0:T(8,128)(2,1)S(1)}, u32[]{:S(2)}, u32[]{:S(2)}) collective-permute-start(bf16[768,512]{1,0:T(8,128)(2,1)} %copy-done.10), channel_id=1, source_target_pairs={{0,8},{8,16},{16,24},{24,32},{32,40},{40,48},{48,56},{56,0},{1,9},... | collective-permute-start | bytes 2359304 | tf_op jit(solution)/shard_map/ppermute | solution.py:24
  184.4 19.4 %collective-permute-start.20 = (bf16[768,512]{1,0:T(8,128)(2,1)}, bf16[768,512]{1,0:T(8,128)(2,1)S(1)}, u32[]{:S(2)}, u32[]{:S(2)}) collective-permute-start(bf16[768,512]{1,0:T(8,128)(2,1)} %copy-done.7), channel_id=1, source_target_pairs={{0,56},{8,0},{16,8},{24,16},{32,24},{40,32},{48,40},{56,48},{1,57}... | collective-permute-start | bytes 2359304 | tf_op jit(solution)/shard_map/ppermute | solution.py:24
  185.1 1.2 copy-start.9
  186.2 1.1 copy-start.12
  187.4 1.1 copy-start.15
  188.5 1.1 copy-start.18
  189.6 1.0 copy-start.20
  206.2 3.8 %copy-start.4 = (bf16[512,1024]{1,0:T(8,128)(2,1)}, bf16[512,1024]{1,0:T(8,128)(2,1)S(1)}, u32[]{:S(2)}) copy-start(bf16[512,1024]{1,0:T(8,128)(2,1)S(1)} %collective-permute-done.21.refs_6_.refs_10_) | copy-start | bytes 3145732
  210.3 23.0 %all-to-all-start.4 = ((bf16[8,640,128]{2,1,0:T(8,128)(2,1)}), bf16[8,640,128]{2,1,0:T(8,128)(2,1)S(1)}, u32[]{:S(2)}, u32[]{:S(2)}) async-start(bf16[8,640,128]{2,1,0:T(8,128)(2,1)} %pick_blocks.7), calls=%async_computation.4 | async-start | bytes 2621440 | tf_op jit(solution)/shard_map/all_to_all | solution.py:77
  233.3 1.1 copy-start.6
  234.4 1.4 copy-start.23
  235.8 1.4 copy-start.24
  237.2 37.8 %copy-start.3 = (bf16[512,1024]{1,0:T(8,128)(2,1)S(1)}, bf16[512,1024]{1,0:T(8,128)(2,1)}, u32[]{:S(2)}) copy-start(bf16[512,1024]{1,0:T(8,128)(2,1)} %copy-done.2) | copy-start | bytes 3145732
  237.2 37.8 %copy-start.5 = (bf16[512,1024]{1,0:T(8,128)(2,1)S(1)}, bf16[512,1024]{1,0:T(8,128)(2,1)}, u32[]{:S(2)}) copy-start(bf16[512,1024]{1,0:T(8,128)(2,1)} %copy-done.4) | copy-start | bytes 3145732
  246.4 11.6 %collective-permute-start.22 = (bf16[384,512]{1,0:T(8,128)(2,1)S(1)}, bf16[384,512]{1,0:T(8,128)(2,1)S(1)}, u32[]{:S(2)}, u32[]{:S(2)}) collective-permute-start(bf16[384,512]{1,0:T(8,128)(2,1)S(1)} %get-tuple-element.104.refs_0_), channel_id=1, source_target_pairs={{0,64},{64,128},{128,192},{192,0},{1,65},{65,129},{129,193},{193,1... | collective-permute-start | bytes 1179656 | tf_op jit(solution)/shard_map/ppermute | solution.py:29
  246.5 12.8 %collective-permute-start.26 = (bf16[384,512]{1,0:T(8,128)(2,1)S(1)}, bf16[384,512]{1,0:T(8,128)(2,1)S(1)}, u32[]{:S(2)}, u32[]{:S(2)}) collective-permute-start(bf16[384,512]{1,0:T(8,128)(2,1)S(1)} %get-tuple-element.109.refs_0_), channel_id=1, source_target_pairs={{0,192},{64,0},{128,64},{192,128},{1,193},{65,1},{129,65},{193,129... | collective-permute-start | bytes 1179656 | tf_op jit(solution)/shard_map/ppermute | solution.py:29
  249.8 22.0 %collective-permute-start.23 = (bf16[384,512]{1,0:T(8,128)(2,1)S(1)}, bf16[384,512]{1,0:T(8,128)(2,1)S(1)}, u32[]{:S(2)}, u32[]{:S(2)}) collective-permute-start(bf16[384,512]{1,0:T(8,128)(2,1)S(1)} %get-tuple-element.104.refs_0_), channel_id=1, source_target_pairs={{0,192},{64,0},{128,64},{192,128},{1,193},{65,1},{129,65},{193,129... | collective-permute-start | bytes 1179656 | tf_op jit(solution)/shard_map/ppermute | solution.py:29
  258.0 17.0 %collective-permute-start.24 = (bf16[384,512]{1,0:T(8,128)(2,1)S(1)}, bf16[384,512]{1,0:T(8,128)(2,1)S(1)}, u32[]{:S(2)}, u32[]{:S(2)}) collective-permute-start(bf16[384,512]{1,0:T(8,128)(2,1)S(1)} %collective-permute-done.22.refs_1_), channel_id=1, source_target_pairs={{0,64},{64,128},{128,192},{192,0},{1,65},{65,129},{129,193},{193,1... | collective-permute-start | bytes 1179656 | tf_op jit(solution)/shard_map/ppermute | solution.py:29
  258.0 24.8 %collective-permute-start.25 = (bf16[384,512]{1,0:T(8,128)(2,1)S(1)}, bf16[384,512]{1,0:T(8,128)(2,1)S(1)}, u32[]{:S(2)}, u32[]{:S(2)}) collective-permute-start(bf16[384,512]{1,0:T(8,128)(2,1)S(1)} %get-tuple-element.109.refs_0_), channel_id=1, source_target_pairs={{0,64},{64,128},{128,192},{192,0},{1,65},{65,129},{129,193},{193,1... | collective-permute-start | bytes 1179656 | tf_op jit(solution)/shard_map/ppermute | solution.py:29
  259.3 23.5 %collective-permute-start.27 = (bf16[384,512]{1,0:T(8,128)(2,1)S(1)}, bf16[384,512]{1,0:T(8,128)(2,1)S(1)}, u32[]{:S(2)}, u32[]{:S(2)}) collective-permute-start(bf16[384,512]{1,0:T(8,128)(2,1)S(1)} %collective-permute-done.26.refs_2_), channel_id=1, source_target_pairs={{0,192},{64,0},{128,64},{192,128},{1,193},{65,1},{129,65},{193,129... | collective-permute-start | bytes 1179656 | tf_op jit(solution)/shard_map/ppermute | solution.py:29
  271.7 11.1 %copy-start.25 = (s32[4]{0:T(128)S(1)}, s32[4]{0:T(128)}, u32[]{:S(2)}) copy-start(s32[4]{0:T(128)} %pad_add_fusion.refs_1_.place) | copy-start | bytes 52
  271.7 9.5 %collective-permute-start.28 = (bf16[128,512]{1,0:T(8,128)(2,1)S(1)}, bf16[128,512]{1,0:T(8,128)(2,1)S(1)}, u32[]{:S(2)}, u32[]{:S(2)}) collective-permute-start(bf16[128,512]{1,0:T(8,128)(2,1)S(1)} %bitcast.12), channel_id=1, source_target_pairs={{0,64},{64,128},{128,192},{192,0},{1,65},{65,129},{129,193},{193,1... | collective-permute-start | bytes 393224 | tf_op jit(solution)/shard_map/ppermute | solution.py:29
  271.8 9.4 %collective-permute-start.29 = (bf16[128,512]{1,0:T(8,128)(2,1)S(1)}, bf16[128,512]{1,0:T(8,128)(2,1)S(1)}, u32[]{:S(2)}, u32[]{:S(2)}) collective-permute-start(bf16[128,512]{1,0:T(8,128)(2,1)S(1)} %bitcast.13), channel_id=1, source_target_pairs={{0,192},{64,0},{128,64},{192,128},{1,193},{65,1},{129,65},{193,129... | collective-permute-start | bytes 393224 | tf_op jit(solution)/shard_map/ppermute | solution.py:29
  275.0 7.8 %collective-permute-start.30 = (bf16[128,512]{1,0:T(8,128)(2,1)S(1)}, bf16[128,512]{1,0:T(8,128)(2,1)S(1)}, u32[]{:S(2)}, u32[]{:S(2)}) collective-permute-start(bf16[128,512]{1,0:T(8,128)(2,1)S(1)} %bitcast.14), channel_id=1, source_target_pairs={{0,128},{64,192},{128,0},{192,64},{1,129},{65,193},{129,1},{193,65... | collective-permute-start | bytes 393224 | tf_op jit(solution)/shard_map/ppermute | solution.py:29
  (3 other events, 2.1 us)

commit v10 on v9

--- a/solution.py
+++ b/solution.py
@@ -484,9 +484,8 @@
         if step == 3:
             ends, starts, _ = lax.optimization_barrier((ends, starts, held))
             beside += (lax.ppermute(ends, SEQ, ahead), lax.ppermute(starts, SEQ, back))
-        if step == 3:
-            shared, _ = lax.optimization_barrier((shared, held))
-            shared = doubled(doubled(shared, 2), 4)
+        if step < PLANES // 2:
+            shared = doubled(shared, 2 * (step - 1))
         picks = picked(asked, first, held, (shared,) if step == PLANES // 2 else ())
         arrived.append(over_plane(picks))
         first += len(held) // 2
@@ -511,12 +510,13 @@
         slots, place, queries, key_vectors, value_vectors, before, after, arrived[:-1]
     )
     own_t, own_b, gout = finished(late, queries, acc, stats, arrived[-1])
+    gout = over_plane(gout).reshape(heads, GLOBAL * BLOCK, DH)
+    gout = gout.transpose(1, 0, 2).reshape(GLOBAL * BLOCK, features)
     right_t, left_t = across(own_t, 1), across(own_t, -1)
     right_b, left_b = across(own_b, 1), across(own_b, -1)
-    far_t, far_b = across(right_t, 1), across(left_b, -1)
-    gout = over_plane(gout).reshape(heads, GLOBAL * BLOCK, DH)
-    gout = gout.transpose(1, 0, 2).reshape(GLOBAL * BLOCK, features)
+    near_t, near_b, gout, _ = lax.optimization_barrier((right_t, left_b, gout, (left_t, right_b)))
     rows_g = (gout, across(gout, 1), across(gout, -1), across(gout, 2))
+    far_t, far_b = across(near_t, 1), across(near_b, -1)
     top = product((own_t, right_t, left_t, far_t), weights)
     return product((own_b, right_b, left_b, far_b), weights, place, top, rows_g)
 

time: 291 us -> 293 us (level)
  waiting for transfers between devices: 109 us -> 104 us
  local copies, waits for them, and re-layouts: 25.6 us -> 30.2 us
    unnamed x63 -> x77, local copies, waits for them, and re-layouts: 21.3 us -> 25.8 us
    ppermute x3, waiting for transfers between devices: 33.4 us -> 29.2 us  [doubled(): lax.ppermute(own, 'seq_0', [(i, i ^ apart) for i in range(PLANES)])]
  transfers between devices with their start and end apart: 36 -> 36, of which waited for: 19 -> 18; matrix products, arithmetic and copies ran while one was open for 6% -> 7% of each run, Pallas kernels for 11% -> 11%
where the time goes in v10:
time: 293 us; the launch traced here: 290 us
  waiting for transfers between devices  104 us (35%)
  starting transfers between devices  74.2 us (25%)
  Pallas kernels  55.6 us (19%)
  local copies, waits for them, and re-layouts  30.2 us (10%)
  other arithmetic  15.2 us (5%)
  blocking collectives  8.51 us (3%)
    ppermute x14, waiting for transfers between devices, ring_step(): lax.ppermute(shard, 'seq_0', [(i, (i + step) % peers) for i in range(peer...  41.7 us
    ppermute x3, waiting for transfers between devices, doubled(): lax.ppermute(own, 'seq_0', [(i, i ^ apart) for i in range(PLANES)])  29.2 us
    unnamed x77, local copies, waits for them, and re-layouts  25.8 us
    all_to_all x5, starting transfers between devices, over_plane(): return lax.all_to_all(parts, PLANE, split_axis=0, concat_axis=0, tiled=True)  22 us
    ppermute x12, starting transfers between devices, across(): lax.ppermute(shard, 'heads', [(i, (i + step) % peers) for i in range(peer...  19.6 us
    all_to_all x5, waiting for transfers between devices, over_plane(): return lax.all_to_all(parts, PLANE, split_axis=0, concat_axis=0, tiled=True)  17 us
    ppermute x14, starting transfers between devices, ring_step(): lax.ppermute(shard, 'seq_0', [(i, (i + step) % peers) for i in range(peer...  17 us
    ppermute x12, waiting for transfers between devices, across(): lax.ppermute(shard, 'heads', [(i, (i + step) % peers) for i in range(peer...  16.2 us
  transfers between devices with their start and end apart: 36, of which 18 were waited for; matrix products, arithmetic and copies ran while one was open for 7% of the time, Pallas kernels for 11%

profile of v10, /device:TPU:32, one launch (start us, length us, event | category | flops | bytes accessed | tf_op | source)
XLA Modules:
  0.0 289.5 jit_solution(12935677288589433372)
XLA Ops:
  0.0 1.9 collective-permute-start
  6.6 2.2 fusion.14
  8.8 2.1 dynamic-slice_select_fusion.5
  12.2 1.3 fusion.15
  14.4 1.2 fusion.1
  16.3 1.9 constant_dynamic-slice_fusion
  18.2 1.3 collective-permute-done.refs_2_
  19.5 1.9 collective-permute-done.2.refs_6_
  21.4 4.5 %all-to-all-start = ((bf16[8,176,512]{2,1,0:T(8,128)(2,1)}), bf16[8,176,512]{2,1,0:T(8,128)(2,1)}, u32[]{:S(2)}, u32[]{:S(2)}) async-start(bf16[8,176,512]{2,1,0:T(8,128)(2,1)} %fusion.1), calls=%async_computation | async-start | bytes 2883584 | tf_op jit(solution)/shard_map/all_to_all | solution.py:77
  25.9 3.1 %collective-permute-start.4 = (bf16[768,512]{1,0:T(8,128)(2,1)S(1)}, bf16[768,512]{1,0:T(8,128)(2,1)}, u32[]{:S(2)}, u32[]{:S(2)}) collective-permute-start(bf16[768,512]{1,0:T(8,128)(2,1)S(1)} %copy-done.1), channel_id=1, source_target_pairs={{0,8},{8,16},{16,24},{24,32},{32,40},{40,48},{48,56},{56,0},{1,9},... | collective-permute-start | bytes 2359304 | tf_op jit(solution)/shard_map/ppermute | solution.py:24
  29.0 3.0 %collective-permute-start.1 = (bf16[768,512]{1,0:T(8,128)(2,1)S(1)}, bf16[768,512]{1,0:T(8,128)(2,1)}, u32[]{:S(2)}, u32[]{:S(2)}) collective-permute-start(bf16[768,512]{1,0:T(8,128)(2,1)S(1)} %collective-permute-done.refs_2_), channel_id=1, source_target_pairs={{0,8},{8,16},{16,24},{24,32},{32,40},{40,48},{48,56},{56,0},{1,9},... | collective-permute-start | bytes 2359304 | tf_op jit(solution)/shard_map/ppermute | solution.py:24
  32.0 14.2 %all-to-all-done = bf16[8,176,512]{2,1,0:T(8,128)(2,1)} async-done(((bf16[8,176,512]{2,1,0:T(8,128)(2,1)}), bf16[8,176,512]{2,1,0:T(8,128)(2,1)}, u32[]{:S(2)}, u32[]{:S(2)}) %all-to-all-start) | async-done | bytes 1441824 | tf_op jit(solution)/shard_map/all_to_all | solution.py:77
  47.2 2.4 collective-permute-start.9
  50.4 13.7 %collective-permute-done.9 = bf16[32,512]{1,0:T(8,128)(2,1)S(1)} collective-permute-done((bf16[32,512]{1,0:T(8,128)(2,1)S(1)}, bf16[32,512]{1,0:T(8,128)(2,1)S(1)}, u32[]{:S(2)}, u32[]{:S(2)}) %collective-permute-start.9) | collective-permute-done | bytes 32800 | tf_op jit(solution)/shard_map/ppermute | solution.py:459
  64.1 2.8 collective-permute-done.3.refs_4_
  66.9 4.1 %pick_blocks.4 = bf16[8,1536,128]{2,1,0:T(8,128)(2,1)} custom-call(s32[256]{0:T(256)S(1)} %reshape.185.refs_0_, bf16[768,512]{1,0:T(8,128)(2,1)S(1)} %copy-done, bf16[768,512]{1,0:T(8,128)(2,1)S(1)} %collective-permute-done.refs_2_, bf16[768,512]{1,0:T(8,128)(2,1)} %collective-permute-done.5.refs_3_, bf16[768,512]{1,0:T(8,128)(2,1)S(1)} %copy-done.1, ...), custom_call_target="tpu_custom_call" | custom-call | bytes 25165824 | tf_op jit(solution)/shard_map/pick_blocks/pallas_call | solution.py:65
  71.0 4.5 %all-to-all-start.1 = ((bf16[8,1536,128]{2,1,0:T(8,128)(2,1)}), bf16[8,1536,128]{2,1,0:T(8,128)(2,1)}, u32[]{:S(2)}, u32[]{:S(2)}) async-start(bf16[8,1536,128]{2,1,0:T(8,128)(2,1)} %pick_blocks.4), calls=%async_computation.1 | async-start | bytes 6291456 | tf_op jit(solution)/shard_map/all_to_all | solution.py:77
  75.5 3.1 %collective-permute-start.13 = (bf16[512,1024]{1,0:T(8,128)(2,1)}, bf16[512,1024]{1,0:T(8,128)(2,1)S(1)}, u32[]{:S(2)}, u32[]{:S(2)}) collective-permute-start(bf16[512,1024]{1,0:T(8,128)(2,1)} %get-tuple-element.74), channel_id=1, source_target_pairs={{0,128},{64,192},{128,0},{192,64},{1,129},{65,193},{129,1},{193,65... | collective-permute-start | bytes 3145736 | tf_op jit(solution)/shard_map/ppermute | solution.py:29
  78.6 2.8 collective-permute-start.14
  81.4 2.0 collective-permute-start.8
  83.4 2.3 collective-permute-start.12
  86.2 1.4 slice_reduce_fusion.refs_0_
  87.6 4.1 %global_parts.4.refs_5_ = f32[512,256]{1,0:T(8,128)S(1)} custom-call(bf16[128,512]{1,0:T(8,128)(2,1)S(1)} %slice_reduce_fusion.refs_0_, bf16[768,512]{1,0:T(8,128)(2,1)S(1)} %copy-done, bf16[768,512]{1,0:T(8,128)(2,1)S(1)} %collective-permute-done.refs_2_, bf16[768,512]{1,0:T(8,128)(2,1)} %collective-permute-done.5.refs_3_, bf16[768,512]{1,0:T(8,128)(2,1)S(1)} %copy-done.1, ...), custom_call_target="tpu_custom_call" | custom-call | flops 603979776 | bytes 25165824 | tf_op jit(solution)/shard_map/global_parts/pallas_call | solution.py:125
  93.1 8.9 %collective-permute-done.7.refs_3_ = bf16[768,512]{1,0:T(8,128)(2,1)S(1)} collective-permute-done((bf16[768,512]{1,0:T(8,128)(2,1)}, bf16[768,512]{1,0:T(8,128)(2,1)S(1)}, u32[]{:S(2)}, u32[]{:S(2)}) %collective-permute-start.7) | collective-permute-done | bytes 786464 | tf_op jit(solution)/shard_map/ppermute | solution.py:24
  102.0 15.7 %collective-permute-done.12.refs_4_ = bf16[768,512]{1,0:T(8,128)(2,1)S(1)} collective-permute-done((bf16[768,512]{1,0:T(8,128)(2,1)}, bf16[768,512]{1,0:T(8,128)(2,1)S(1)}, u32[]{:S(2)}, u32[]{:S(2)}) %collective-permute-start.12) | collective-permute-done | bytes 786464 | tf_op jit(solution)/shard_map/ppermute | solution.py:24
  120.5 1.1 copy-done.20
  121.7 1.1 copy-done.23
  122.8 3.3 %pick_blocks.5 = bf16[8,1024,128]{2,1,0:T(8,128)(2,1)} custom-call(s32[256]{0:T(256)S(1)} %reshape.185.refs_0_, bf16[768,512]{1,0:T(8,128)(2,1)} %collective-permute-done.1.refs_1_, bf16[768,512]{1,0:T(8,128)(2,1)S(1)} %copy-done.23, bf16[768,512]{1,0:T(8,128)(2,1)S(1)} %copy-done.20, bf16[768,512]{1,0:T(8,128)(2,1)} %collective-permute-done.3.refs_4_), custom_call_target="tpu_custom_call" | custom-call | bytes 25165824 | tf_op jit(solution)/shard_map/pick_blocks/pallas_call | solution.py:65
  126.1 4.6 %all-to-all-start.2 = ((bf16[8,1024,128]{2,1,0:T(8,128)(2,1)}), bf16[8,1024,128]{2,1,0:T(8,128)(2,1)}, u32[]{:S(2)}, u32[]{:S(2)}) async-start(bf16[8,1024,128]{2,1,0:T(8,128)(2,1)} %pick_blocks.5), calls=%async_computation.2 | async-start | bytes 4194304 | tf_op jit(solution)/shard_map/all_to_all | solution.py:77
  131.3 1.7 collective-permute-start.10
  133.3 2.7 collective-permute-start.18
  136.0 1.9 collective-permute-start.16
  137.9 15.5 %collective-permute-done.18 = bf16[32,512]{1,0:T(8,128)(2,1)S(1)} collective-permute-done((bf16[32,512]{1,0:T(8,128)(2,1)}, bf16[32,512]{1,0:T(8,128)(2,1)S(1)}, u32[]{:S(2)}, u32[]{:S(2)}) %collective-permute-start.18) | collective-permute-done | bytes 32800 | tf_op jit(solution)/shard_map/ppermute | solution.py:459
  153.4 5.9 %collective-permute-start.17 = (bf16[128,512]{1,0:T(8,128)(2,1)}, bf16[128,512]{1,0:T(8,128)(2,1)S(1)}, u32[]{:S(2)}, u32[]{:S(2)}) collective-permute-start(bf16[128,512]{1,0:T(8,128)(2,1)} %get-tuple-element.85), channel_id=1, source_target_pairs={{1,0},{2,1},{3,2},{4,3},{5,4},{6,5},{7,6},{8,7},{9,8},{10,9},{11,1... | collective-permute-start | bytes 393224 | tf_op jit(solution)/shard_map/ppermute | solution.py:486
  161.6 3.7 %global_parts.5.refs_5_ = f32[512,256]{1,0:T(8,128)S(1)} custom-call(bf16[128,512]{1,0:T(8,128)(2,1)S(1)} %slice_reduce_fusion.refs_0_, bf16[768,512]{1,0:T(8,128)(2,1)} %collective-permute-done.1.refs_1_, bf16[768,512]{1,0:T(8,128)(2,1)S(1)} %copy-done.24, bf16[768,512]{1,0:T(8,128)(2,1)S(1)} %copy-done.21, ...), custom_call_target="tpu_custom_call" | custom-call | flops 402653184 | bytes 25165824 | tf_op jit(solution)/shard_map/global_parts/pallas_call | solution.py:125
  171.2 1.1 copy-done.14
  173.4 2.6 pick_blocks.6
  176.0 4.4 %all-to-all-start.3 = ((bf16[8,1152,128]{2,1,0:T(8,128)(2,1)}), bf16[8,1152,128]{2,1,0:T(8,128)(2,1)}, u32[]{:S(2)}, u32[]{:S(2)}) async-start(bf16[8,1152,128]{2,1,0:T(8,128)(2,1)} %pick_blocks.6), calls=%async_computation.3 | async-start | bytes 4718592 | tf_op jit(solution)/shard_map/all_to_all | solution.py:77
  180.4 2.7 collective-permute-start.21
  183.1 1.6 collective-permute-start.19
  185.2 1.2 copy-done.9
  190.8 2.4 global_parts.6.refs_3_
  193.1 9.7 %collective-permute-done.19.refs_1_ = bf16[768,512]{1,0:T(8,128)(2,1)S(1)} collective-permute-done((bf16[768,512]{1,0:T(8,128)(2,1)}, bf16[768,512]{1,0:T(8,128)(2,1)S(1)}, u32[]{:S(2)}, u32[]{:S(2)}) %collective-permute-start.19) | collective-permute-done | bytes 786464 | tf_op jit(solution)/shard_map/ppermute | solution.py:24
  202.8 1.5 collective-permute-done.20.refs_2_
  204.4 2.0 collective-permute-done.21.refs_6_.refs_10_
  206.3 1.8 global_parts.7.refs_3_
  208.2 1.9 pick_blocks.7
  210.4 4.2 %all-to-all-start.4 = ((bf16[8,640,128]{2,1,0:T(8,128)(2,1)}), bf16[8,640,128]{2,1,0:T(8,128)(2,1)S(1)}, u32[]{:S(2)}, u32[]{:S(2)}) async-start(bf16[8,640,128]{2,1,0:T(8,128)(2,1)} %pick_blocks.7), calls=%async_computation.4 | async-start | bytes 2621440 | tf_op jit(solution)/shard_map/all_to_all | solution.py:77
  215.4 15.4 %attend.1 = (f32[768,512]{1,0:T(8,128)}, f32[4,768,128]{2,1,0:T(8,128)}) custom-call(s32[144]{0:T(256)} %copy-done.37, s32[4]{0:T(128)} %pad_add_fusion.refs_1_.place, bf16[768,512]{1,0:T(8,128)(2,1)} %q.1, bf16[768,512]{1,0:T(8,128)(2,1)} %refs_3_.1, bf16[768,512]{1,0:T(8,128)(2,1)} %refs_4_.3, bf16[128,512]{1,0:T(8,128)(2,1)} %copy-done.33, ...), custom_call_target="tpu_custom_call" | custom-call | flops 805306368 | bytes 25165824 | tf_op jit(solution)/shard_map/attend/pallas_call | solution.py:294
  230.8 2.5 all-to-all-done.4.blocks_late
  233.4 1.1 copy-done.6
  234.5 1.4 copy-done.29
  235.9 1.4 copy-done.30
  237.3 8.4 %late_blocks.1 = (bf16[384,512]{1,0:T(8,128)(2,1)S(1)}, bf16[384,512]{1,0:T(8,128)(2,1)S(1)}, bf16[8,64,128]{2,1,0:T(8,128)(2,1)S(1)}) custom-call(s32[32]{0:T(128)S(1)} %reshape_squeeze.3.late, bf16[768,512]{1,0:T(8,128)(2,1)S(1)} %copy-done.6, f32[768,512]{1,0:T(8,128)S(1)} %copy-done.29, f32[4,768,128]{2,1,0:T(8,128)S(1)} %copy-done.30, ...), custom_call_target="tpu_custom_call" | custom-call | tf_op jit(solution)/shard_map/late_blocks/pallas_call | solution.py:379
  246.2 3.8 %collective-permute-start.23 = (bf16[384,512]{1,0:T(8,128)(2,1)S(1)}, bf16[384,512]{1,0:T(8,128)(2,1)S(1)}, u32[]{:S(2)}, u32[]{:S(2)}) collective-permute-start(bf16[384,512]{1,0:T(8,128)(2,1)S(1)} %get-tuple-element.105.refs_0_), channel_id=1, source_target_pairs={{0,192},{64,0},{128,64},{192,128},{1,193},{65,1},{129,65},{193,129... | collective-permute-start | bytes 1179656 | tf_op jit(solution)/shard_map/ppermute | solution.py:29
  249.9 1.9 collective-permute-start.24
  252.0 8.5 %all_to_all.30 = bf16[8,64,128]{2,1,0:T(8,128)(2,1)S(1)} all-to-all(bf16[8,64,128]{2,1,0:T(8,128)(2,1)S(1)} %get-tuple-element.107), channel_id=1, replica_groups=mesh['heads'=4,'seq_0'=8,'seq_1'=4,'seq_2'=2] {'seq_1','seq_2'}, dimensions={0} | all-to-all | bytes 262144 | tf_op jit(solution)/shard_map/all_to_all | solution.py:77
  260.6 5.7 %collective-permute-done.24.refs_2_ = bf16[384,512]{1,0:T(8,128)(2,1)S(1)} collective-permute-done((bf16[384,512]{1,0:T(8,128)(2,1)S(1)}, bf16[384,512]{1,0:T(8,128)(2,1)S(1)}, u32[]{:S(2)}, u32[]{:S(2)}) %collective-permute-start.24) | collective-permute-done | bytes 393248 | tf_op jit(solution)/shard_map/ppermute | solution.py:29
  268.0 2.3 collective-permute-start.27
  270.3 3.2 %collective-permute-start.29 = (bf16[128,512]{1,0:T(8,128)(2,1)S(1)}, bf16[128,512]{1,0:T(8,128)(2,1)S(1)}, u32[]{:S(2)}, u32[]{:S(2)}) collective-permute-start(bf16[128,512]{1,0:T(8,128)(2,1)S(1)} %bitcast.13), channel_id=1, source_target_pairs={{0,192},{64,0},{128,64},{192,128},{1,193},{65,1},{129,65},{193,129... | collective-permute-start | bytes 393224 | tf_op jit(solution)/shard_map/ppermute | solution.py:29
  273.8 6.1 %collective-permute-done.26.refs_3_ = bf16[384,512]{1,0:T(8,128)(2,1)S(1)} collective-permute-done((bf16[384,512]{1,0:T(8,128)(2,1)S(1)}, bf16[384,512]{1,0:T(8,128)(2,1)S(1)}, u32[]{:S(2)}, u32[]{:S(2)}) %collective-permute-start.26) | collective-permute-done | bytes 393248 | tf_op jit(solution)/shard_map/ppermute | solution.py:29
  280.0 3.0 %upper_product.1.top = bf16[384,1024]{1,0:T(8,128)(2,1)S(1)} custom-call(bf16[384,512]{1,0:T(8,128)(2,1)S(1)} %get-tuple-element.105.refs_0_, bf16[384,512]{1,0:T(8,128)(2,1)S(1)} %collective-permute-done.22.refs_1_, bf16[384,512]{1,0:T(8,128)(2,1)S(1)} %collective-permute-done.23.refs_2_, bf16[384,512]{1,0:T(8,128)(2,1)S(1)} %collective-permute-done.26.refs_3_, ...), custom_call_target="tpu_custom_call" | custom-call | flops 1610612736 | bytes 8388608 | tf_op jit(solution)/shard_map/upper_product/pallas_call | solution.py:193
  283.1 1.5 collective-permute-done.30.refs_7_
  284.6 4.9 %lower_product.1 = bf16[768,1024]{1,0:T(8,128)(2,1)} custom-call(s32[4]{0:T(128)S(1)} %copy-done.31, bf16[384,1024]{1,0:T(8,128)(2,1)S(1)} %upper_product.1.top, bf16[384,512]{1,0:T(8,128)(2,1)S(1)} %get-tuple-element.106.refs_0_, bf16[384,512]{1,0:T(8,128)(2,1)S(1)} %collective-permute-done.25.refs_1_, ...), custom_call_target="tpu_custom_call" | custom-call | flops 1610612736 | bytes 8388608 | tf_op jit(solution)/shard_map/lower_product/pallas_call | solution.py:193
  (137 shorter events, 31.8 us)
Async XLA Ops:
  0.0 12.2 %copy-start.1 = (bf16[768,512]{1,0:T(8,128)(2,1)S(1)}, bf16[768,512]{1,0:T(8,128)(2,1)}, u32[]{:S(2)}) copy-start(bf16[768,512]{1,0:T(8,128)(2,1)} %refs_4_.3) | copy-start | bytes 2359300
  0.0 19.5 %collective-permute-start = (bf16[768,512]{1,0:T(8,128)(2,1)}, bf16[768,512]{1,0:T(8,128)(2,1)S(1)}, u32[]{:S(2)}, u32[]{:S(2)}) collective-permute-start(bf16[768,512]{1,0:T(8,128)(2,1)} %refs_3_.1), channel_id=1, source_target_pairs={{0,8},{8,16},{16,24},{24,32},{32,40},{40,48},{48,56},{56,0},{1,9},... | collective-permute-start | bytes 2359304 | tf_op jit(solution)/shard_map/ppermute | solution.py:24
  1.9 19.5 %collective-permute-start.2 = (bf16[768,512]{1,0:T(8,128)(2,1)}, bf16[768,512]{1,0:T(8,128)(2,1)}, u32[]{:S(2)}, u32[]{:S(2)}) collective-permute-start(bf16[768,512]{1,0:T(8,128)(2,1)} %refs_4_.3), channel_id=1, source_target_pairs={{0,56},{8,0},{16,8},{24,16},{32,24},{40,32},{48,40},{56,48},{1,57}... | collective-permute-start | bytes 2359304 | tf_op jit(solution)/shard_map/ppermute | solution.py:24
  12.0 3.6 %copy-start.37 = (s32[144]{0:T(256)}, s32[144]{0:T(256)S(1)}, u32[]{:S(2)}) copy-start(s32[144]{0:T(256)S(1)} %multiply_add_fusion.refs_0_) | copy-start | bytes 1732
  13.5 2.8 copy-start.32
  18.2 10.8 %copy-start = (bf16[768,512]{1,0:T(8,128)(2,1)S(1)}, bf16[768,512]{1,0:T(8,128)(2,1)}, u32[]{:S(2)}) copy-start(bf16[768,512]{1,0:T(8,128)(2,1)} %refs_3_.1) | copy-start | bytes 2359300
  21.4 24.8 %all-to-all-start = ((bf16[8,176,512]{2,1,0:T(8,128)(2,1)}), bf16[8,176,512]{2,1,0:T(8,128)(2,1)}, u32[]{:S(2)}, u32[]{:S(2)}) async-start(bf16[8,176,512]{2,1,0:T(8,128)(2,1)} %fusion.1), calls=%async_computation | async-start | bytes 2883584 | tf_op jit(solution)/shard_map/all_to_all | solution.py:77
  25.9 38.2 %collective-permute-start.4 = (bf16[768,512]{1,0:T(8,128)(2,1)S(1)}, bf16[768,512]{1,0:T(8,128)(2,1)}, u32[]{:S(2)}, u32[]{:S(2)}) collective-permute-start(bf16[768,512]{1,0:T(8,128)(2,1)S(1)} %copy-done.1), channel_id=1, source_target_pairs={{0,8},{8,16},{16,24},{24,32},{32,40},{40,48},{48,56},{56,0},{1,9},... | collective-permute-start | bytes 2359304 | tf_op jit(solution)/shard_map/ppermute | solution.py:24
  29.0 35.1 %collective-permute-start.5 = (bf16[768,512]{1,0:T(8,128)(2,1)S(1)}, bf16[768,512]{1,0:T(8,128)(2,1)}, u32[]{:S(2)}, u32[]{:S(2)}) collective-permute-start(bf16[768,512]{1,0:T(8,128)(2,1)S(1)} %copy-done), channel_id=1, source_target_pairs={{0,56},{8,0},{16,8},{24,16},{32,24},{40,32},{48,40},{56,48},{1,57}... | collective-permute-start | bytes 2359304 | tf_op jit(solution)/shard_map/ppermute | solution.py:24
  29.0 35.1 %collective-permute-start.1 = (bf16[768,512]{1,0:T(8,128)(2,1)S(1)}, bf16[768,512]{1,0:T(8,128)(2,1)}, u32[]{:S(2)}, u32[]{:S(2)}) collective-permute-start(bf16[768,512]{1,0:T(8,128)(2,1)S(1)} %collective-permute-done.refs_2_), channel_id=1, source_target_pairs={{0,8},{8,16},{16,24},{24,32},{32,40},{40,48},{48,56},{56,0},{1,9},... | collective-permute-start | bytes 2359304 | tf_op jit(solution)/shard_map/ppermute | solution.py:24
  32.0 34.9 %collective-permute-start.3 = (bf16[768,512]{1,0:T(8,128)(2,1)}, bf16[768,512]{1,0:T(8,128)(2,1)}, u32[]{:S(2)}, u32[]{:S(2)}) collective-permute-start(bf16[768,512]{1,0:T(8,128)(2,1)} %collective-permute-done.2.refs_6_), channel_id=1, source_target_pairs={{0,56},{8,0},{16,8},{24,16},{32,24},{40,32},{48,40},{56,48},{1,57}... | collective-permute-start | bytes 2359304 | tf_op jit(solution)/shard_map/ppermute | solution.py:24
  47.2 16.9 %collective-permute-start.9 = (bf16[32,512]{1,0:T(8,128)(2,1)S(1)}, bf16[32,512]{1,0:T(8,128)(2,1)S(1)}, u32[]{:S(2)}, u32[]{:S(2)}) collective-permute-start(bf16[32,512]{1,0:T(8,128)(2,1)S(1)} %slice_reduce_fusion.1), channel_id=1, source_target_pairs={{0,8},{8,0},{16,24},{24,16},{32,40},{40,32},{48,56},{56,48},{1,9},... | collective-permute-start | bytes 98312 | tf_op jit(solution)/shard_map/ppermute | solution.py:459
  64.1 14.5 %copy-start.35 = (bf16[32,512]{1,0:T(8,128)(2,1)}, bf16[32,512]{1,0:T(8,128)(2,1)S(1)}, u32[]{:S(2)}) copy-start(bf16[32,512]{1,0:T(8,128)(2,1)S(1)} %add.194) | copy-start | bytes 98308
  71.0 49.6 %all-to-all-start.1 = ((bf16[8,1536,128]{2,1,0:T(8,128)(2,1)}), bf16[8,1536,128]{2,1,0:T(8,128)(2,1)}, u32[]{:S(2)}, u32[]{:S(2)}) async-start(bf16[8,1536,128]{2,1,0:T(8,128)(2,1)} %pick_blocks.4), calls=%async_computation.1 | async-start | bytes 6291456 | tf_op jit(solution)/shard_map/all_to_all | solution.py:77
  75.5 44.0 %collective-permute-start.13 = (bf16[512,1024]{1,0:T(8,128)(2,1)}, bf16[512,1024]{1,0:T(8,128)(2,1)S(1)}, u32[]{:S(2)}, u32[]{:S(2)}) collective-permute-start(bf16[512,1024]{1,0:T(8,128)(2,1)} %get-tuple-element.74), channel_id=1, source_target_pairs={{0,128},{64,192},{128,0},{192,64},{1,129},{65,193},{129,1},{193,65... | collective-permute-start | bytes 3145736 | tf_op jit(solution)/shard_map/ppermute | solution.py:29
  78.6 7.1 %collective-permute-start.14 = (bf16[32,512]{1,0:T(8,128)(2,1)S(1)}, bf16[32,512]{1,0:T(8,128)(2,1)S(1)}, u32[]{:S(2)}, u32[]{:S(2)}) collective-permute-start(bf16[32,512]{1,0:T(8,128)(2,1)S(1)} %add.194), channel_id=1, source_target_pairs={{0,16},{8,24},{16,0},{24,8},{32,48},{40,56},{48,32},{56,40},{1,17}... | collective-permute-start | bytes 98312 | tf_op jit(solution)/shard_map/ppermute | solution.py:459
  81.4 20.6 %collective-permute-start.7 = (bf16[768,512]{1,0:T(8,128)(2,1)}, bf16[768,512]{1,0:T(8,128)(2,1)S(1)}, u32[]{:S(2)}, u32[]{:S(2)}) collective-permute-start(bf16[768,512]{1,0:T(8,128)(2,1)} %collective-permute-done.4.refs_5_), channel_id=1, source_target_pairs={{0,8},{8,16},{16,24},{24,32},{32,40},{40,48},{48,56},{56,0},{1,9},... | collective-permute-start | bytes 2359304 | tf_op jit(solution)/shard_map/ppermute | solution.py:24
  81.4 20.6 %collective-permute-start.8 = (bf16[768,512]{1,0:T(8,128)(2,1)}, bf16[768,512]{1,0:T(8,128)(2,1)S(1)}, u32[]{:S(2)}, u32[]{:S(2)}) collective-permute-start(bf16[768,512]{1,0:T(8,128)(2,1)} %collective-permute-done.5.refs_3_), channel_id=1, source_target_pairs={{0,56},{8,0},{16,8},{24,16},{32,24},{40,32},{48,40},{56,48},{1,57}... | collective-permute-start | bytes 2359304 | tf_op jit(solution)/shard_map/ppermute | solution.py:24
  83.4 34.3 %collective-permute-start.12 = (bf16[768,512]{1,0:T(8,128)(2,1)}, bf16[768,512]{1,0:T(8,128)(2,1)S(1)}, u32[]{:S(2)}, u32[]{:S(2)}) collective-permute-start(bf16[768,512]{1,0:T(8,128)(2,1)} %collective-permute-done.3.refs_4_), channel_id=1, source_target_pairs={{0,56},{8,0},{16,8},{24,16},{32,24},{40,32},{48,40},{56,48},{1,57}... | collective-permute-start | bytes 2359304 | tf_op jit(solution)/shard_map/ppermute | solution.py:24
  85.7 32.9 %collective-permute-start.6 = (bf16[768,512]{1,0:T(8,128)(2,1)}, bf16[768,512]{1,0:T(8,128)(2,1)S(1)}, u32[]{:S(2)}, u32[]{:S(2)}) collective-permute-start(bf16[768,512]{1,0:T(8,128)(2,1)} %collective-permute-done.1.refs_1_), channel_id=1, source_target_pairs={{0,8},{8,16},{16,24},{24,32},{32,40},{40,48},{48,56},{56,0},{1,9},... | collective-permute-start | bytes 2359304 | tf_op jit(solution)/shard_map/ppermute | solution.py:24
  87.5 5.0 %copy-start.36 = (bf16[32,512]{1,0:T(8,128)(2,1)S(1)}, bf16[32,512]{1,0:T(8,128)(2,1)}, u32[]{:S(2)}) copy-start(bf16[32,512]{1,0:T(8,128)(2,1)} %copy-done.35) | copy-start | bytes 98308
  102.0 16.6 %copy-start.19 = (bf16[768,512]{1,0:T(8,128)(2,1)}, bf16[768,512]{1,0:T(8,128)(2,1)S(1)}, u32[]{:S(2)}) copy-start(bf16[768,512]{1,0:T(8,128)(2,1)S(1)} %collective-permute-done.7.refs_3_) | copy-start | bytes 2359300
  102.0 16.6 %copy-start.22 = (bf16[768,512]{1,0:T(8,128)(2,1)}, bf16[768,512]{1,0:T(8,128)(2,1)S(1)}, u32[]{:S(2)}) copy-start(bf16[768,512]{1,0:T(8,128)(2,1)S(1)} %collective-permute-done.8.refs_2_) | copy-start | bytes 2359300
  120.5 1.1 copy-start.20
  121.7 1.1 copy-start.23
  126.1 33.3 %copy-start.28 = (f32[512,256]{1,0:T(8,128)S(1)}, f32[512,256]{1,0:T(8,128)}, u32[]{:S(2)}) copy-start(f32[512,256]{1,0:T(8,128)} %copy-done.27) | copy-start | bytes 1572868
  126.1 44.0 %all-to-all-start.2 = ((bf16[8,1024,128]{2,1,0:T(8,128)(2,1)}), bf16[8,1024,128]{2,1,0:T(8,128)(2,1)}, u32[]{:S(2)}, u32[]{:S(2)}) async-start(bf16[8,1024,128]{2,1,0:T(8,128)(2,1)} %pick_blocks.5), calls=%async_computation.2 | async-start | bytes 4194304 | tf_op jit(solution)/shard_map/all_to_all | solution.py:77
  130.6 39.4 %copy-start.8 = (bf16[768,512]{1,0:T(8,128)(2,1)S(1)}, bf16[768,512]{1,0:T(8,128)(2,1)}, u32[]{:S(2)}) copy-start(bf16[768,512]{1,0:T(8,128)(2,1)} %copy-done.7) | copy-start | bytes 2359300
  130.7 39.4 %collective-permute-start.15 = (bf16[512,1024]{1,0:T(8,128)(2,1)}, bf16[512,1024]{1,0:T(8,128)(2,1)S(1)}, u32[]{:S(2)}, u32[]{:S(2)}) collective-permute-start(bf16[512,1024]{1,0:T(8,128)(2,1)} %get-tuple-element.81), channel_id=1, source_target_pairs={{0,64},{64,128},{128,192},{192,0},{1,65},{65,129},{129,193},{193,1... | collective-permute-start | bytes 3145736 | tf_op jit(solution)/shard_map/ppermute | solution.py:29
  131.3 35.6 %collective-permute-start.10 = (bf16[768,512]{1,0:T(8,128)(2,1)}, bf16[768,512]{1,0:T(8,128)(2,1)S(1)}, u32[]{:S(2)}, u32[]{:S(2)}) collective-permute-start(bf16[768,512]{1,0:T(8,128)(2,1)} %copy-done.22), channel_id=1, source_target_pairs={{0,56},{8,0},{16,8},{24,16},{32,24},{40,32},{48,40},{56,48},{1,57}... | collective-permute-start | bytes 2359304 | tf_op jit(solution)/shard_map/ppermute | solution.py:24
  133.1 34.8 %collective-permute-start.11 = (bf16[768,512]{1,0:T(8,128)(2,1)}, bf16[768,512]{1,0:T(8,128)(2,1)S(1)}, u32[]{:S(2)}, u32[]{:S(2)}) collective-permute-start(bf16[768,512]{1,0:T(8,128)(2,1)} %copy-done.19), channel_id=1, source_target_pairs={{0,8},{8,16},{16,24},{24,32},{32,40},{40,48},{48,56},{56,0},{1,9},... | collective-permute-start | bytes 2359304 | tf_op jit(solution)/shard_map/ppermute | solution.py:24
  133.3 20.1 %collective-permute-start.18 = (bf16[32,512]{1,0:T(8,128)(2,1)}, bf16[32,512]{1,0:T(8,128)(2,1)S(1)}, u32[]{:S(2)}, u32[]{:S(2)}) collective-permute-start(bf16[32,512]{1,0:T(8,128)(2,1)} %add.195), channel_id=1, source_target_pairs={{0,32},{8,40},{16,48},{24,56},{32,0},{40,8},{48,16},{56,24},{1,33}... | collective-permute-start | bytes 98312 | tf_op jit(solution)/shard_map/ppermute | solution.py:459
  136.0 32.7 %collective-permute-start.16 = (bf16[128,512]{1,0:T(8,128)(2,1)}, bf16[128,512]{1,0:T(8,128)(2,1)S(1)}, u32[]{:S(2)}, u32[]{:S(2)}) collective-permute-start(bf16[128,512]{1,0:T(8,128)(2,1)} %get-tuple-element.84), channel_id=1, source_target_pairs={{0,1},{1,2},{2,3},{3,4},{4,5},{5,6},{6,7},{7,8},{8,9},{9,10},{10,1... | collective-permute-start | bytes 393224 | tf_op jit(solution)/shard_map/ppermute | solution.py:486
  153.4 15.9 %collective-permute-start.17 = (bf16[128,512]{1,0:T(8,128)(2,1)}, bf16[128,512]{1,0:T(8,128)(2,1)S(1)}, u32[]{:S(2)}, u32[]{:S(2)}) collective-permute-start(bf16[128,512]{1,0:T(8,128)(2,1)} %get-tuple-element.85), channel_id=1, source_target_pairs={{1,0},{2,1},{3,2},{4,3},{5,4},{6,5},{7,6},{8,7},{9,8},{10,9},{11,1... | collective-permute-start | bytes 393224 | tf_op jit(solution)/shard_map/ppermute | solution.py:486
  159.4 1.1 copy-start.21
  160.5 1.1 copy-start.24
  170.0 1.1 copy-start.11
  171.2 1.1 copy-start.14
  172.3 1.1 copy-start.17
  176.0 34.4 %all-to-all-start.3 = ((bf16[8,1152,128]{2,1,0:T(8,128)(2,1)}), bf16[8,1152,128]{2,1,0:T(8,128)(2,1)}, u32[]{:S(2)}, u32[]{:S(2)}) async-start(bf16[8,1152,128]{2,1,0:T(8,128)(2,1)} %pick_blocks.6), calls=%async_computation.3 | async-start | bytes 4718592 | tf_op jit(solution)/shard_map/all_to_all | solution.py:77
  180.4 25.9 %collective-permute-start.21 = (bf16[512,1024]{1,0:T(8,128)(2,1)}, bf16[512,1024]{1,0:T(8,128)(2,1)S(1)}, u32[]{:S(2)}, u32[]{:S(2)}) collective-permute-start(bf16[512,1024]{1,0:T(8,128)(2,1)} %get-tuple-element.101), channel_id=1, source_target_pairs={{0,192},{64,0},{128,64},{192,128},{1,193},{65,1},{129,65},{193,129... | collective-permute-start | bytes 3145736 | tf_op jit(solution)/shard_map/ppermute | solution.py:29
  183.1 19.7 %collective-permute-start.19 = (bf16[768,512]{1,0:T(8,128)(2,1)}, bf16[768,512]{1,0:T(8,128)(2,1)S(1)}, u32[]{:S(2)}, u32[]{:S(2)}) collective-permute-start(bf16[768,512]{1,0:T(8,128)(2,1)} %copy-done.10), channel_id=1, source_target_pairs={{0,8},{8,16},{16,24},{24,32},{32,40},{40,48},{48,56},{56,0},{1,9},... | collective-permute-start | bytes 2359304 | tf_op jit(solution)/shard_map/ppermute | solution.py:24
  184.8 19.6 %collective-permute-start.20 = (bf16[768,512]{1,0:T(8,128)(2,1)}, bf16[768,512]{1,0:T(8,128)(2,1)S(1)}, u32[]{:S(2)}, u32[]{:S(2)}) collective-permute-start(bf16[768,512]{1,0:T(8,128)(2,1)} %copy-done.7), channel_id=1, source_target_pairs={{0,56},{8,0},{16,8},{24,16},{32,24},{40,32},{48,40},{56,48},{1,57}... | collective-permute-start | bytes 2359304 | tf_op jit(solution)/shard_map/ppermute | solution.py:24
  185.2 1.2 copy-start.9
  186.3 1.1 copy-start.12
  187.5 1.1 copy-start.15
  188.6 1.1 copy-start.18
  206.3 3.8 %copy-start.4 = (bf16[512,1024]{1,0:T(8,128)(2,1)}, bf16[512,1024]{1,0:T(8,128)(2,1)S(1)}, u32[]{:S(2)}) copy-start(bf16[512,1024]{1,0:T(8,128)(2,1)S(1)} %collective-permute-done.21.refs_6_.refs_10_) | copy-start | bytes 3145732
  210.4 22.9 %all-to-all-start.4 = ((bf16[8,640,128]{2,1,0:T(8,128)(2,1)}), bf16[8,640,128]{2,1,0:T(8,128)(2,1)S(1)}, u32[]{:S(2)}, u32[]{:S(2)}) async-start(bf16[8,640,128]{2,1,0:T(8,128)(2,1)} %pick_blocks.7), calls=%async_computation.4 | async-start | bytes 2621440 | tf_op jit(solution)/shard_map/all_to_all | solution.py:77
  233.4 1.1 copy-start.6
  234.5 1.4 copy-start.29
  235.9 1.4 copy-start.30
  237.3 42.7 %copy-start.3 = (bf16[512,1024]{1,0:T(8,128)(2,1)S(1)}, bf16[512,1024]{1,0:T(8,128)(2,1)}, u32[]{:S(2)}) copy-start(bf16[512,1024]{1,0:T(8,128)(2,1)} %copy-done.2) | copy-start | bytes 3145732
  237.3 42.7 %copy-start.5 = (bf16[512,1024]{1,0:T(8,128)(2,1)S(1)}, bf16[512,1024]{1,0:T(8,128)(2,1)}, u32[]{:S(2)}) copy-start(bf16[512,1024]{1,0:T(8,128)(2,1)} %copy-done.4) | copy-start | bytes 3145732
  245.7 14.9 %collective-permute-start.22 = (bf16[384,512]{1,0:T(8,128)(2,1)S(1)}, bf16[384,512]{1,0:T(8,128)(2,1)S(1)}, u32[]{:S(2)}, u32[]{:S(2)}) collective-permute-start(bf16[384,512]{1,0:T(8,128)(2,1)S(1)} %get-tuple-element.105.refs_0_), channel_id=1, source_target_pairs={{0,64},{64,128},{128,192},{192,0},{1,65},{65,129},{129,193},{193,1... | collective-permute-start | bytes 1179656 | tf_op jit(solution)/shard_map/ppermute | solution.py:29
  246.2 14.5 %collective-permute-start.23 = (bf16[384,512]{1,0:T(8,128)(2,1)S(1)}, bf16[384,512]{1,0:T(8,128)(2,1)S(1)}, u32[]{:S(2)}, u32[]{:S(2)}) collective-permute-start(bf16[384,512]{1,0:T(8,128)(2,1)S(1)} %get-tuple-element.105.refs_0_), channel_id=1, source_target_pairs={{0,192},{64,0},{128,64},{192,128},{1,193},{65,1},{129,65},{193,129... | collective-permute-start | bytes 1179656 | tf_op jit(solution)/shard_map/ppermute | solution.py:29
  249.9 16.4 %collective-permute-start.24 = (bf16[384,512]{1,0:T(8,128)(2,1)S(1)}, bf16[384,512]{1,0:T(8,128)(2,1)S(1)}, u32[]{:S(2)}, u32[]{:S(2)}) collective-permute-start(bf16[384,512]{1,0:T(8,128)(2,1)S(1)} %get-tuple-element.106.refs_0_), channel_id=1, source_target_pairs={{0,192},{64,0},{128,64},{192,128},{1,193},{65,1},{129,65},{193,129... | collective-permute-start | bytes 1179656 | tf_op jit(solution)/shard_map/ppermute | solution.py:29
  251.9 15.2 %collective-permute-start.25 = (bf16[384,512]{1,0:T(8,128)(2,1)S(1)}, bf16[384,512]{1,0:T(8,128)(2,1)S(1)}, u32[]{:S(2)}, u32[]{:S(2)}) collective-permute-start(bf16[384,512]{1,0:T(8,128)(2,1)S(1)} %get-tuple-element.106.refs_0_), channel_id=1, source_target_pairs={{0,64},{64,128},{128,192},{192,0},{1,65},{65,129},{129,193},{193,1... | collective-permute-start | bytes 1179656 | tf_op jit(solution)/shard_map/ppermute | solution.py:29
  267.1 17.6 %copy-start.31 = (s32[4]{0:T(128)S(1)}, s32[4]{0:T(128)}, u32[]{:S(2)}) copy-start(s32[4]{0:T(128)} %pad_add_fusion.refs_1_.place) | copy-start | bytes 52
  267.1 12.9 %collective-permute-start.26 = (bf16[384,512]{1,0:T(8,128)(2,1)S(1)}, bf16[384,512]{1,0:T(8,128)(2,1)S(1)}, u32[]{:S(2)}, u32[]{:S(2)}) collective-permute-start(bf16[384,512]{1,0:T(8,128)(2,1)S(1)} %collective-permute-done.22.refs_1_), channel_id=1, source_target_pairs={{0,64},{64,128},{128,192},{192,0},{1,65},{65,129},{129,193},{193,1... | collective-permute-start | bytes 1179656 | tf_op jit(solution)/shard_map/ppermute | solution.py:29
  268.0 16.6 %collective-permute-start.27 = (bf16[384,512]{1,0:T(8,128)(2,1)S(1)}, bf16[384,512]{1,0:T(8,128)(2,1)S(1)}, u32[]{:S(2)}, u32[]{:S(2)}) collective-permute-start(bf16[384,512]{1,0:T(8,128)(2,1)S(1)} %collective-permute-done.24.refs_2_), channel_id=1, source_target_pairs={{0,192},{64,0},{128,64},{192,128},{1,193},{65,1},{129,65},{193,129... | collective-permute-start | bytes 1179656 | tf_op jit(solution)/shard_map/ppermute | solution.py:29
  270.3 12.6 %collective-permute-start.28 = (bf16[128,512]{1,0:T(8,128)(2,1)S(1)}, bf16[128,512]{1,0:T(8,128)(2,1)S(1)}, u32[]{:S(2)}, u32[]{:S(2)}) collective-permute-start(bf16[128,512]{1,0:T(8,128)(2,1)S(1)} %bitcast.12), channel_id=1, source_target_pairs={{0,64},{64,128},{128,192},{192,0},{1,65},{65,129},{129,193},{193,1... | collective-permute-start | bytes 393224 | tf_op jit(solution)/shard_map/ppermute | solution.py:29
  270.3 12.8 %collective-permute-start.29 = (bf16[128,512]{1,0:T(8,128)(2,1)S(1)}, bf16[128,512]{1,0:T(8,128)(2,1)S(1)}, u32[]{:S(2)}, u32[]{:S(2)}) collective-permute-start(bf16[128,512]{1,0:T(8,128)(2,1)S(1)} %bitcast.13), channel_id=1, source_target_pairs={{0,192},{64,0},{128,64},{192,128},{1,193},{65,1},{129,65},{193,129... | collective-permute-start | bytes 393224 | tf_op jit(solution)/shard_map/ppermute | solution.py:29
  273.5 11.1 %collective-permute-start.30 = (bf16[128,512]{1,0:T(8,128)(2,1)S(1)}, bf16[128,512]{1,0:T(8,128)(2,1)S(1)}, u32[]{:S(2)}, u32[]{:S(2)}) collective-permute-start(bf16[128,512]{1,0:T(8,128)(2,1)S(1)} %bitcast.14), channel_id=1, source_target_pairs={{0,128},{64,192},{128,0},{192,64},{1,129},{65,193},{129,1},{193,65... | collective-permute-start | bytes 393224 | tf_op jit(solution)/shard_map/ppermute | solution.py:29
  (10 other events, 8.6 us)

commit v11 on v9

--- a/solution.py
+++ b/solution.py
@@ -471,9 +471,10 @@
         if step < PLANES // 2:
             up_v, down_k, _ = lax.optimization_barrier((up_v, down_k, picks))
         gate = (up_k, down_v) if step < PLANES // 2 else ()
-        held, _, _, tied, parts, shared = lax.optimization_barrier(
-            (held, gate, arrived[-1:], beside if step > 2 else (), parts, shared)
+        held, _, _, tied, early, shared = lax.optimization_barrier(
+            (held, gate, arrived[-1:], beside if step > 2 else (), parts if step < 4 else (), shared)
         )
+        parts = early if step < 4 else parts
         if step > 2:
             weights[turn] = tied[0]
         if step > 3:

time: 291 us -> 290 us (level)
    ppermute x14, waiting for transfers between devices: 44.4 us -> 36.3 us  [ring_step(): lax.ppermute(shard, 'seq_0', [(i, (i + step) % peers) for i in range(peer...]
    ppermute x12, waiting for transfers between devices: 14.1 us -> 18 us  [across(): lax.ppermute(shard, 'heads', [(i, (i + step) % peers) for i in range(peer...]
    ppermute x3, waiting for transfers between devices: 33.4 us -> 36.5 us  [doubled(): lax.ppermute(own, 'seq_0', [(i, i ^ apart) for i in range(PLANES)])]
    unnamed x63 -> x73, local copies, waits for them, and re-layouts: 21.3 us -> 19.8 us
  transfers between devices with their start and end apart: 36 -> 36, of which waited for: 19 -> 18; matrix products, arithmetic and copies ran while one was open for 6% -> 7% of each run, Pallas kernels for 11% -> 11%
where the time goes in v11:
time: 290 us; the launch traced here: 289 us
  waiting for transfers between devices  108 us (37%)
  starting transfers between devices  73.8 us (25%)
  Pallas kernels  56 us (19%)
  local copies, waits for them, and re-layouts  24.2 us (8%)
  other arithmetic  14.5 us (5%)
  blocking collectives  10 us (3%)
    ppermute x3, waiting for transfers between devices, doubled(): lax.ppermute(own, 'seq_0', [(i, i ^ apart) for i in range(PLANES)])  36.5 us
    ppermute x14, waiting for transfers between devices, ring_step(): lax.ppermute(shard, 'seq_0', [(i, (i + step) % peers) for i in range(peer...  36.3 us
    all_to_all x5, starting transfers between devices, over_plane(): return lax.all_to_all(parts, PLANE, split_axis=0, concat_axis=0, tiled=True)  24.5 us
    unnamed x73, local copies, waits for them, and re-layouts  19.8 us
    ppermute x14, starting transfers between devices, ring_step(): lax.ppermute(shard, 'seq_0', [(i, (i + step) % peers) for i in range(peer...  18.2 us
    ppermute x12, waiting for transfers between devices, across(): lax.ppermute(shard, 'heads', [(i, (i + step) % peers) for i in range(peer...  18 us
    ppermute x12, starting transfers between devices, across(): lax.ppermute(shard, 'heads', [(i, (i + step) % peers) for i in range(peer...  17.7 us
    all_to_all x5, waiting for transfers between devices, over_plane(): return lax.all_to_all(parts, PLANE, split_axis=0, concat_axis=0, tiled=True)  16.7 us
  transfers between devices with their start and end apart: 36, of which 18 were waited for; matrix products, arithmetic and copies ran while one was open for 7% of the time, Pallas kernels for 11%

profile of v11, /device:TPU:32, one launch (start us, length us, event | category | flops | bytes accessed | tf_op | source)
XLA Modules:
  0.0 288.5 jit_solution(11125589825226861298)
XLA Ops:
  0.0 1.9 collective-permute-start
  7.9 2.2 fusion.14
  10.1 2.2 dynamic-slice_select_fusion.5
  12.4 1.3 fusion.15
  14.5 1.2 fusion.1
  15.8 1.3 copy-done.30
  17.1 1.8 constant_dynamic-slice_fusion
  19.5 1.9 collective-permute-done.2.refs_6_
  21.4 4.5 %all-to-all-start = ((bf16[8,176,512]{2,1,0:T(8,128)(2,1)}), bf16[8,176,512]{2,1,0:T(8,128)(2,1)}, u32[]{:S(2)}, u32[]{:S(2)}) async-start(bf16[8,176,512]{2,1,0:T(8,128)(2,1)} %fusion.1), calls=%async_computation | async-start | bytes 2883584 | tf_op jit(solution)/shard_map/all_to_all | solution.py:77
  25.9 2.4 collective-permute-start.5
  29.2 3.0 %collective-permute-start.1 = (bf16[768,512]{1,0:T(8,128)(2,1)S(1)}, bf16[768,512]{1,0:T(8,128)(2,1)}, u32[]{:S(2)}, u32[]{:S(2)}) collective-permute-start(bf16[768,512]{1,0:T(8,128)(2,1)S(1)} %collective-permute-done.refs_2_), channel_id=1, source_target_pairs={{0,8},{8,16},{16,24},{24,32},{32,40},{40,48},{48,56},{56,0},{1,9},... | collective-permute-start | bytes 2359304 | tf_op jit(solution)/shard_map/ppermute | solution.py:24
  32.1 14.0 %all-to-all-done = bf16[8,176,512]{2,1,0:T(8,128)(2,1)} async-done(((bf16[8,176,512]{2,1,0:T(8,128)(2,1)}), bf16[8,176,512]{2,1,0:T(8,128)(2,1)}, u32[]{:S(2)}, u32[]{:S(2)}) %all-to-all-start) | async-done | bytes 1441824 | tf_op jit(solution)/shard_map/all_to_all | solution.py:77
  47.2 2.4 collective-permute-start.9
  50.4 16.5 %collective-permute-done.9 = bf16[32,512]{1,0:T(8,128)(2,1)S(1)} collective-permute-done((bf16[32,512]{1,0:T(8,128)(2,1)S(1)}, bf16[32,512]{1,0:T(8,128)(2,1)S(1)}, u32[]{:S(2)}, u32[]{:S(2)}) %collective-permute-start.9) | collective-permute-done | bytes 32800 | tf_op jit(solution)/shard_map/ppermute | solution.py:459
  67.5 4.1 %pick_blocks.4 = bf16[8,1536,128]{2,1,0:T(8,128)(2,1)} custom-call(s32[256]{0:T(256)S(1)} %reshape.185.refs_0_, bf16[768,512]{1,0:T(8,128)(2,1)S(1)} %copy-done, bf16[768,512]{1,0:T(8,128)(2,1)S(1)} %collective-permute-done.refs_2_, bf16[768,512]{1,0:T(8,128)(2,1)} %collective-permute-done.5.refs_3_, bf16[768,512]{1,0:T(8,128)(2,1)S(1)} %copy-done.1, ...), custom_call_target="tpu_custom_call" | custom-call | bytes 25165824 | tf_op jit(solution)/shard_map/pick_blocks/pallas_call | solution.py:65
  71.6 4.4 %all-to-all-start.1 = ((bf16[8,1536,128]{2,1,0:T(8,128)(2,1)}), bf16[8,1536,128]{2,1,0:T(8,128)(2,1)}, u32[]{:S(2)}, u32[]{:S(2)}) async-start(bf16[8,1536,128]{2,1,0:T(8,128)(2,1)} %pick_blocks.4), calls=%async_computation.1 | async-start | bytes 6291456 | tf_op jit(solution)/shard_map/all_to_all | solution.py:77
  76.0 3.1 %collective-permute-start.13 = (bf16[512,1024]{1,0:T(8,128)(2,1)}, bf16[512,1024]{1,0:T(8,128)(2,1)S(1)}, u32[]{:S(2)}, u32[]{:S(2)}) collective-permute-start(bf16[512,1024]{1,0:T(8,128)(2,1)} %get-tuple-element.71), channel_id=1, source_target_pairs={{0,128},{64,192},{128,0},{192,64},{1,129},{65,193},{129,1},{193,65... | collective-permute-start | bytes 3145736 | tf_op jit(solution)/shard_map/ppermute | solution.py:29
  80.0 1.1 collective-permute-start.8
  82.1 2.1 collective-permute-start.12
  84.1 1.4 slice_reduce_fusion.refs_0_
  85.5 4.1 %global_parts.4.refs_5_ = f32[512,256]{1,0:T(8,128)S(1)} custom-call(bf16[128,512]{1,0:T(8,128)(2,1)S(1)} %slice_reduce_fusion.refs_0_, bf16[768,512]{1,0:T(8,128)(2,1)S(1)} %copy-done, bf16[768,512]{1,0:T(8,128)(2,1)S(1)} %collective-permute-done.refs_2_, bf16[768,512]{1,0:T(8,128)(2,1)} %collective-permute-done.5.refs_3_, bf16[768,512]{1,0:T(8,128)(2,1)S(1)} %copy-done.1, ...), custom_call_target="tpu_custom_call" | custom-call | flops 603979776 | bytes 25165824 | tf_op jit(solution)/shard_map/global_parts/pallas_call | solution.py:125
  90.5 9.3 %collective-permute-done.7.refs_3_ = bf16[768,512]{1,0:T(8,128)(2,1)S(1)} collective-permute-done((bf16[768,512]{1,0:T(8,128)(2,1)}, bf16[768,512]{1,0:T(8,128)(2,1)S(1)}, u32[]{:S(2)}, u32[]{:S(2)}) %collective-permute-start.7) | collective-permute-done | bytes 786464 | tf_op jit(solution)/shard_map/ppermute | solution.py:24
  100.7 15.1 %collective-permute-done.6.refs_1_ = bf16[768,512]{1,0:T(8,128)(2,1)S(1)} collective-permute-done((bf16[768,512]{1,0:T(8,128)(2,1)}, bf16[768,512]{1,0:T(8,128)(2,1)S(1)}, u32[]{:S(2)}, u32[]{:S(2)}) %collective-permute-start.6) | collective-permute-done | bytes 786464 | tf_op jit(solution)/shard_map/ppermute | solution.py:24
  118.6 1.1 copy-done.20
  119.7 1.1 copy-done.23
  120.8 3.2 %pick_blocks.5 = bf16[8,1024,128]{2,1,0:T(8,128)(2,1)} custom-call(s32[256]{0:T(256)S(1)} %reshape.185.refs_0_, bf16[768,512]{1,0:T(8,128)(2,1)} %collective-permute-done.1.refs_1_, bf16[768,512]{1,0:T(8,128)(2,1)S(1)} %copy-done.23, bf16[768,512]{1,0:T(8,128)(2,1)S(1)} %copy-done.20, bf16[768,512]{1,0:T(8,128)(2,1)} %collective-permute-done.3.refs_4_), custom_call_target="tpu_custom_call" | custom-call | bytes 25165824 | tf_op jit(solution)/shard_map/pick_blocks/pallas_call | solution.py:65
  124.1 4.6 %all-to-all-start.2 = ((bf16[8,1024,128]{2,1,0:T(8,128)(2,1)}), bf16[8,1024,128]{2,1,0:T(8,128)(2,1)}, u32[]{:S(2)}, u32[]{:S(2)}) async-start(bf16[8,1024,128]{2,1,0:T(8,128)(2,1)} %pick_blocks.5), calls=%async_computation.2 | async-start | bytes 4194304 | tf_op jit(solution)/shard_map/all_to_all | solution.py:77
  129.3 2.9 %collective-permute-start.10 = (bf16[768,512]{1,0:T(8,128)(2,1)}, bf16[768,512]{1,0:T(8,128)(2,1)S(1)}, u32[]{:S(2)}, u32[]{:S(2)}) collective-permute-start(bf16[768,512]{1,0:T(8,128)(2,1)} %copy-done.22), channel_id=1, source_target_pairs={{0,56},{8,0},{16,8},{24,16},{32,24},{40,32},{48,40},{56,48},{1,57}... | collective-permute-start | bytes 2359304 | tf_op jit(solution)/shard_map/ppermute | solution.py:24
  132.2 5.4 %collective-permute-start.17 = (bf16[32,512]{1,0:T(8,128)(2,1)S(1)}, bf16[32,512]{1,0:T(8,128)(2,1)S(1)}, u32[]{:S(2)}, u32[]{:S(2)}) collective-permute-start(bf16[32,512]{1,0:T(8,128)(2,1)S(1)} %copy-done.33), channel_id=1, source_target_pairs={{0,16},{8,24},{16,0},{24,8},{32,48},{40,56},{48,32},{56,40},{1,17}... | collective-permute-start | bytes 98312 | tf_op jit(solution)/shard_map/ppermute | solution.py:459
  137.6 15.6 %collective-permute-done.17 = bf16[32,512]{1,0:T(8,128)(2,1)S(1)} collective-permute-done((bf16[32,512]{1,0:T(8,128)(2,1)S(1)}, bf16[32,512]{1,0:T(8,128)(2,1)S(1)}, u32[]{:S(2)}, u32[]{:S(2)}) %collective-permute-start.17) | collective-permute-done | bytes 32800 | tf_op jit(solution)/shard_map/ppermute | solution.py:459
  153.2 1.8 collective-permute-start.18
  155.0 1.9 collective-permute-start.15
  156.9 4.5 %collective-permute-done.18 = bf16[32,512]{1,0:T(8,128)(2,1)S(1)} collective-permute-done((bf16[32,512]{1,0:T(8,128)(2,1)S(1)}, bf16[32,512]{1,0:T(8,128)(2,1)S(1)}, u32[]{:S(2)}, u32[]{:S(2)}) %collective-permute-start.18) | collective-permute-done | bytes 32800 | tf_op jit(solution)/shard_map/ppermute | solution.py:459
  161.5 1.9 collective-permute-start.16
  165.9 1.2 copy-done.11
  167.1 1.1 copy-done.14
  168.2 1.1 copy-done.17
  169.3 2.6 pick_blocks.6
  171.9 6.7 %all-to-all-start.3 = ((bf16[8,1152,128]{2,1,0:T(8,128)(2,1)}), bf16[8,1152,128]{2,1,0:T(8,128)(2,1)}, u32[]{:S(2)}, u32[]{:S(2)}) async-start(bf16[8,1152,128]{2,1,0:T(8,128)(2,1)} %pick_blocks.6), calls=%async_computation.3 | async-start | bytes 4718592 | tf_op jit(solution)/shard_map/all_to_all | solution.py:77
  178.7 2.7 collective-permute-start.21
  182.0 1.4 collective-permute-start.20
  186.7 3.7 %global_parts.5.refs_5_ = f32[512,256]{1,0:T(8,128)S(1)} custom-call(bf16[128,512]{1,0:T(8,128)(2,1)S(1)} %slice_reduce_fusion.refs_0_, bf16[768,512]{1,0:T(8,128)(2,1)} %collective-permute-done.1.refs_1_, bf16[768,512]{1,0:T(8,128)(2,1)S(1)} %copy-done.24, bf16[768,512]{1,0:T(8,128)(2,1)S(1)} %copy-done.21, ...), custom_call_target="tpu_custom_call" | custom-call | flops 402653184 | bytes 25165824 | tf_op jit(solution)/shard_map/global_parts/pallas_call | solution.py:125
  190.5 2.4 global_parts.6.refs_3_
  192.8 8.4 %collective-permute-done.19.refs_1_ = bf16[768,512]{1,0:T(8,128)(2,1)S(1)} collective-permute-done((bf16[768,512]{1,0:T(8,128)(2,1)}, bf16[768,512]{1,0:T(8,128)(2,1)S(1)}, u32[]{:S(2)}, u32[]{:S(2)}) %collective-permute-start.19) | collective-permute-done | bytes 786464 | tf_op jit(solution)/shard_map/ppermute | solution.py:24
  201.4 3.3 %collective-permute-done.21.refs_6_.refs_10_ = bf16[512,1024]{1,0:T(8,128)(2,1)S(1)} collective-permute-done((bf16[512,1024]{1,0:T(8,128)(2,1)}, bf16[512,1024]{1,0:T(8,128)(2,1)S(1)}, u32[]{:S(2)}, u32[]{:S(2)}) %collective-permute-start.21) | collective-permute-done | bytes 1048608 | tf_op jit(solution)/shard_map/ppermute | solution.py:29
  204.8 1.8 global_parts.7.refs_3_
  206.6 2.0 pick_blocks.7
  208.7 4.3 %all-to-all-start.4 = ((bf16[8,640,128]{2,1,0:T(8,128)(2,1)}), bf16[8,640,128]{2,1,0:T(8,128)(2,1)S(1)}, u32[]{:S(2)}, u32[]{:S(2)}) async-start(bf16[8,640,128]{2,1,0:T(8,128)(2,1)} %pick_blocks.7), calls=%async_computation.4 | async-start | bytes 2621440 | tf_op jit(solution)/shard_map/all_to_all | solution.py:77
  213.9 15.4 %attend.1 = (f32[768,512]{1,0:T(8,128)}, f32[4,768,128]{2,1,0:T(8,128)}) custom-call(s32[144]{0:T(256)} %copy-done.35, s32[4]{0:T(128)} %pad_add_fusion.refs_1_.place, bf16[768,512]{1,0:T(8,128)(2,1)} %q.1, bf16[768,512]{1,0:T(8,128)(2,1)} %refs_3_.1, bf16[768,512]{1,0:T(8,128)(2,1)} %refs_4_.3, bf16[128,512]{1,0:T(8,128)(2,1)} %copy-done.31, ...), custom_call_target="tpu_custom_call" | custom-call | flops 805306368 | bytes 25165824 | tf_op jit(solution)/shard_map/attend/pallas_call | solution.py:294
  229.3 2.5 all-to-all-done.4.blocks_late
  231.8 1.1 copy-done.6
  233.0 1.4 copy-done.27
  234.4 1.4 copy-done.28
  235.8 8.9 %late_blocks.1 = (bf16[384,512]{1,0:T(8,128)(2,1)S(1)}, bf16[384,512]{1,0:T(8,128)(2,1)S(1)}, bf16[8,64,128]{2,1,0:T(8,128)(2,1)S(1)}) custom-call(s32[32]{0:T(128)S(1)} %reshape_squeeze.3.late, bf16[768,512]{1,0:T(8,128)(2,1)S(1)} %copy-done.6, f32[768,512]{1,0:T(8,128)S(1)} %copy-done.27, f32[4,768,128]{2,1,0:T(8,128)S(1)} %copy-done.28, ...), custom_call_target="tpu_custom_call" | custom-call | tf_op jit(solution)/shard_map/late_blocks/pallas_call | solution.py:379
  244.7 3.2 %collective-permute-start.26 = (bf16[384,512]{1,0:T(8,128)(2,1)S(1)}, bf16[384,512]{1,0:T(8,128)(2,1)S(1)}, u32[]{:S(2)}, u32[]{:S(2)}) collective-permute-start(bf16[384,512]{1,0:T(8,128)(2,1)S(1)} %get-tuple-element.107.refs_0_), channel_id=1, source_target_pairs={{0,192},{64,0},{128,64},{192,128},{1,193},{65,1},{129,65},{193,129... | collective-permute-start | bytes 1179656 | tf_op jit(solution)/shard_map/ppermute | solution.py:29
  248.0 1.7 collective-permute-start.23
  249.7 7.9 %collective-permute-done.22.refs_1_ = bf16[384,512]{1,0:T(8,128)(2,1)S(1)} collective-permute-done((bf16[384,512]{1,0:T(8,128)(2,1)S(1)}, bf16[384,512]{1,0:T(8,128)(2,1)S(1)}, u32[]{:S(2)}, u32[]{:S(2)}) %collective-permute-start.22) | collective-permute-done | bytes 393248 | tf_op jit(solution)/shard_map/ppermute | solution.py:29
  258.3 2.8 collective-permute-start.27
  261.1 10.0 %all_to_all.30 = bf16[8,64,128]{2,1,0:T(8,128)(2,1)S(1)} all-to-all(bf16[8,64,128]{2,1,0:T(8,128)(2,1)S(1)} %get-tuple-element.108), channel_id=1, replica_groups=mesh['heads'=4,'seq_0'=8,'seq_1'=4,'seq_2'=2] {'seq_1','seq_2'}, dimensions={0} | all-to-all | bytes 262144 | tf_op jit(solution)/shard_map/all_to_all | solution.py:77
  272.4 1.4 collective-permute-start.28
  273.9 3.0 %upper_product.1.top = bf16[384,1024]{1,0:T(8,128)(2,1)S(1)} custom-call(bf16[384,512]{1,0:T(8,128)(2,1)S(1)} %get-tuple-element.102.refs_0_, bf16[384,512]{1,0:T(8,128)(2,1)S(1)} %collective-permute-done.22.refs_1_, bf16[384,512]{1,0:T(8,128)(2,1)S(1)} %collective-permute-done.23.refs_2_, bf16[384,512]{1,0:T(8,128)(2,1)S(1)} %collective-permute-done.24.refs_3_, ...), custom_call_target="tpu_custom_call" | custom-call | flops 1610612736 | bytes 8388608 | tf_op jit(solution)/shard_map/upper_product/pallas_call | solution.py:193
  276.8 5.2 %collective-permute-done.30.refs_7_ = bf16[128,512]{1,0:T(8,128)(2,1)S(1)} collective-permute-done((bf16[128,512]{1,0:T(8,128)(2,1)S(1)}, bf16[128,512]{1,0:T(8,128)(2,1)S(1)}, u32[]{:S(2)}, u32[]{:S(2)}) %collective-permute-start.30) | collective-permute-done | bytes 131104 | tf_op jit(solution)/shard_map/ppermute | solution.py:29
  282.0 1.6 collective-permute-done.28.refs_5_
  283.6 4.9 %lower_product.1 = bf16[768,1024]{1,0:T(8,128)(2,1)} custom-call(s32[4]{0:T(128)S(1)} %copy-done.29, bf16[384,1024]{1,0:T(8,128)(2,1)S(1)} %upper_product.1.top, bf16[384,512]{1,0:T(8,128)(2,1)S(1)} %get-tuple-element.107.refs_0_, bf16[384,512]{1,0:T(8,128)(2,1)S(1)} %collective-permute-done.25.refs_1_, ...), custom_call_target="tpu_custom_call" | custom-call | flops 1610612736 | bytes 8388608 | tf_op jit(solution)/shard_map/lower_product/pallas_call | solution.py:193
  (133 shorter events, 26.1 us)
Async XLA Ops:
  0.0 12.4 %copy-start.1 = (bf16[768,512]{1,0:T(8,128)(2,1)S(1)}, bf16[768,512]{1,0:T(8,128)(2,1)}, u32[]{:S(2)}) copy-start(bf16[768,512]{1,0:T(8,128)(2,1)} %refs_4_.3) | copy-start | bytes 2359300
  0.0 19.5 %collective-permute-start = (bf16[768,512]{1,0:T(8,128)(2,1)}, bf16[768,512]{1,0:T(8,128)(2,1)S(1)}, u32[]{:S(2)}, u32[]{:S(2)}) collective-permute-start(bf16[768,512]{1,0:T(8,128)(2,1)} %refs_3_.1), channel_id=1, source_target_pairs={{0,8},{8,16},{16,24},{24,32},{32,40},{40,48},{48,56},{56,0},{1,9},... | collective-permute-start | bytes 2359304 | tf_op jit(solution)/shard_map/ppermute | solution.py:24
  1.9 19.5 %collective-permute-start.2 = (bf16[768,512]{1,0:T(8,128)(2,1)}, bf16[768,512]{1,0:T(8,128)(2,1)}, u32[]{:S(2)}, u32[]{:S(2)}) collective-permute-start(bf16[768,512]{1,0:T(8,128)(2,1)} %refs_4_.3), channel_id=1, source_target_pairs={{0,56},{8,0},{16,8},{24,16},{32,24},{40,32},{48,40},{56,48},{1,57}... | collective-permute-start | bytes 2359304 | tf_op jit(solution)/shard_map/ppermute | solution.py:24
  7.7 6.9 %copy-start.35 = (s32[144]{0:T(256)}, s32[144]{0:T(256)S(1)}, u32[]{:S(2)}) copy-start(s32[144]{0:T(256)S(1)} %multiply_add_fusion.refs_0_) | copy-start | bytes 1732
  14.4 2.7 copy-start.30
  19.0 6.9 %copy-start = (bf16[768,512]{1,0:T(8,128)(2,1)S(1)}, bf16[768,512]{1,0:T(8,128)(2,1)}, u32[]{:S(2)}) copy-start(bf16[768,512]{1,0:T(8,128)(2,1)} %refs_3_.1) | copy-start | bytes 2359300
  21.4 24.8 %all-to-all-start = ((bf16[8,176,512]{2,1,0:T(8,128)(2,1)}), bf16[8,176,512]{2,1,0:T(8,128)(2,1)}, u32[]{:S(2)}, u32[]{:S(2)}) async-start(bf16[8,176,512]{2,1,0:T(8,128)(2,1)} %fusion.1), calls=%async_computation | async-start | bytes 2883584 | tf_op jit(solution)/shard_map/all_to_all | solution.py:77
  25.9 41.6 %collective-permute-start.5 = (bf16[768,512]{1,0:T(8,128)(2,1)S(1)}, bf16[768,512]{1,0:T(8,128)(2,1)}, u32[]{:S(2)}, u32[]{:S(2)}) collective-permute-start(bf16[768,512]{1,0:T(8,128)(2,1)S(1)} %copy-done), channel_id=1, source_target_pairs={{0,56},{8,0},{16,8},{24,16},{32,24},{40,32},{48,40},{56,48},{1,57}... | collective-permute-start | bytes 2359304 | tf_op jit(solution)/shard_map/ppermute | solution.py:24
  28.3 39.2 %collective-permute-start.4 = (bf16[768,512]{1,0:T(8,128)(2,1)S(1)}, bf16[768,512]{1,0:T(8,128)(2,1)}, u32[]{:S(2)}, u32[]{:S(2)}) collective-permute-start(bf16[768,512]{1,0:T(8,128)(2,1)S(1)} %copy-done.1), channel_id=1, source_target_pairs={{0,8},{8,16},{16,24},{24,32},{32,40},{40,48},{48,56},{56,0},{1,9},... | collective-permute-start | bytes 2359304 | tf_op jit(solution)/shard_map/ppermute | solution.py:24
  29.2 38.3 %collective-permute-start.1 = (bf16[768,512]{1,0:T(8,128)(2,1)S(1)}, bf16[768,512]{1,0:T(8,128)(2,1)}, u32[]{:S(2)}, u32[]{:S(2)}) collective-permute-start(bf16[768,512]{1,0:T(8,128)(2,1)S(1)} %collective-permute-done.refs_2_), channel_id=1, source_target_pairs={{0,8},{8,16},{16,24},{24,32},{32,40},{40,48},{48,56},{56,0},{1,9},... | collective-permute-start | bytes 2359304 | tf_op jit(solution)/shard_map/ppermute | solution.py:24
  32.1 35.3 %collective-permute-start.3 = (bf16[768,512]{1,0:T(8,128)(2,1)}, bf16[768,512]{1,0:T(8,128)(2,1)}, u32[]{:S(2)}, u32[]{:S(2)}) collective-permute-start(bf16[768,512]{1,0:T(8,128)(2,1)} %collective-permute-done.2.refs_6_), channel_id=1, source_target_pairs={{0,56},{8,0},{16,8},{24,16},{32,24},{40,32},{48,40},{56,48},{1,57}... | collective-permute-start | bytes 2359304 | tf_op jit(solution)/shard_map/ppermute | solution.py:24
  47.2 19.7 %collective-permute-start.9 = (bf16[32,512]{1,0:T(8,128)(2,1)S(1)}, bf16[32,512]{1,0:T(8,128)(2,1)S(1)}, u32[]{:S(2)}, u32[]{:S(2)}) collective-permute-start(bf16[32,512]{1,0:T(8,128)(2,1)S(1)} %slice_reduce_fusion.1), channel_id=1, source_target_pairs={{0,8},{8,0},{16,24},{24,16},{32,40},{40,32},{48,56},{56,48},{1,9},... | collective-permute-start | bytes 98312 | tf_op jit(solution)/shard_map/ppermute | solution.py:459
  71.6 47.0 %all-to-all-start.1 = ((bf16[8,1536,128]{2,1,0:T(8,128)(2,1)}), bf16[8,1536,128]{2,1,0:T(8,128)(2,1)}, u32[]{:S(2)}, u32[]{:S(2)}) async-start(bf16[8,1536,128]{2,1,0:T(8,128)(2,1)} %pick_blocks.4), calls=%async_computation.1 | async-start | bytes 6291456 | tf_op jit(solution)/shard_map/all_to_all | solution.py:77
  76.0 41.5 %collective-permute-start.13 = (bf16[512,1024]{1,0:T(8,128)(2,1)}, bf16[512,1024]{1,0:T(8,128)(2,1)S(1)}, u32[]{:S(2)}, u32[]{:S(2)}) collective-permute-start(bf16[512,1024]{1,0:T(8,128)(2,1)} %get-tuple-element.71), channel_id=1, source_target_pairs={{0,128},{64,192},{128,0},{192,64},{1,129},{65,193},{129,1},{193,65... | collective-permute-start | bytes 3145736 | tf_op jit(solution)/shard_map/ppermute | solution.py:29
  79.2 20.6 %collective-permute-start.7 = (bf16[768,512]{1,0:T(8,128)(2,1)}, bf16[768,512]{1,0:T(8,128)(2,1)S(1)}, u32[]{:S(2)}, u32[]{:S(2)}) collective-permute-start(bf16[768,512]{1,0:T(8,128)(2,1)} %collective-permute-done.4.refs_5_), channel_id=1, source_target_pairs={{0,8},{8,16},{16,24},{24,32},{32,40},{40,48},{48,56},{56,0},{1,9},... | collective-permute-start | bytes 2359304 | tf_op jit(solution)/shard_map/ppermute | solution.py:24
  80.0 20.6 %collective-permute-start.8 = (bf16[768,512]{1,0:T(8,128)(2,1)}, bf16[768,512]{1,0:T(8,128)(2,1)S(1)}, u32[]{:S(2)}, u32[]{:S(2)}) collective-permute-start(bf16[768,512]{1,0:T(8,128)(2,1)} %collective-permute-done.5.refs_3_), channel_id=1, source_target_pairs={{0,56},{8,0},{16,8},{24,16},{32,24},{40,32},{48,40},{56,48},{1,57}... | collective-permute-start | bytes 2359304 | tf_op jit(solution)/shard_map/ppermute | solution.py:24
  81.2 34.6 %collective-permute-start.6 = (bf16[768,512]{1,0:T(8,128)(2,1)}, bf16[768,512]{1,0:T(8,128)(2,1)S(1)}, u32[]{:S(2)}, u32[]{:S(2)}) collective-permute-start(bf16[768,512]{1,0:T(8,128)(2,1)} %collective-permute-done.1.refs_1_), channel_id=1, source_target_pairs={{0,8},{8,16},{16,24},{24,32},{32,40},{40,48},{48,56},{56,0},{1,9},... | collective-permute-start | bytes 2359304 | tf_op jit(solution)/shard_map/ppermute | solution.py:24
  82.1 34.6 %collective-permute-start.12 = (bf16[768,512]{1,0:T(8,128)(2,1)}, bf16[768,512]{1,0:T(8,128)(2,1)S(1)}, u32[]{:S(2)}, u32[]{:S(2)}) collective-permute-start(bf16[768,512]{1,0:T(8,128)(2,1)} %collective-permute-done.3.refs_4_), channel_id=1, source_target_pairs={{0,56},{8,0},{16,8},{24,16},{32,24},{40,32},{48,40},{56,48},{1,57}... | collective-permute-start | bytes 2359304 | tf_op jit(solution)/shard_map/ppermute | solution.py:24
  99.8 16.9 %copy-start.19 = (bf16[768,512]{1,0:T(8,128)(2,1)}, bf16[768,512]{1,0:T(8,128)(2,1)S(1)}, u32[]{:S(2)}) copy-start(bf16[768,512]{1,0:T(8,128)(2,1)S(1)} %collective-permute-done.7.refs_3_) | copy-start | bytes 2359300
  100.7 16.0 %copy-start.22 = (bf16[768,512]{1,0:T(8,128)(2,1)}, bf16[768,512]{1,0:T(8,128)(2,1)S(1)}, u32[]{:S(2)}) copy-start(bf16[768,512]{1,0:T(8,128)(2,1)S(1)} %collective-permute-done.8.refs_2_) | copy-start | bytes 2359300
  118.6 1.1 copy-start.20
  119.7 1.1 copy-start.23
  124.1 8.2 %copy-start.33 = (bf16[32,512]{1,0:T(8,128)(2,1)S(1)}, bf16[32,512]{1,0:T(8,128)(2,1)}, u32[]{:S(2)}) copy-start(bf16[32,512]{1,0:T(8,128)(2,1)} %add.194) | copy-start | bytes 98308
  124.1 37.4 %copy-start.34 = (bf16[128,512]{1,0:T(8,128)(2,1)S(1)}, bf16[128,512]{1,0:T(8,128)(2,1)}, u32[]{:S(2)}) copy-start(bf16[128,512]{1,0:T(8,128)(2,1)} %get-tuple-element.82) | copy-start | bytes 393220
  124.1 41.8 %copy-start.8 = (bf16[768,512]{1,0:T(8,128)(2,1)S(1)}, bf16[768,512]{1,0:T(8,128)(2,1)}, u32[]{:S(2)}) copy-start(bf16[768,512]{1,0:T(8,128)(2,1)} %copy-done.7) | copy-start | bytes 2359300
  124.1 41.8 %all-to-all-start.2 = ((bf16[8,1024,128]{2,1,0:T(8,128)(2,1)}), bf16[8,1024,128]{2,1,0:T(8,128)(2,1)}, u32[]{:S(2)}, u32[]{:S(2)}) async-start(bf16[8,1024,128]{2,1,0:T(8,128)(2,1)} %pick_blocks.5), calls=%async_computation.2 | async-start | bytes 4194304 | tf_op jit(solution)/shard_map/all_to_all | solution.py:77
  128.7 37.2 %collective-permute-start.14 = (bf16[512,1024]{1,0:T(8,128)(2,1)}, bf16[512,1024]{1,0:T(8,128)(2,1)S(1)}, u32[]{:S(2)}, u32[]{:S(2)}) collective-permute-start(bf16[512,1024]{1,0:T(8,128)(2,1)} %get-tuple-element.78), channel_id=1, source_target_pairs={{0,64},{64,128},{128,192},{192,0},{1,65},{65,129},{129,193},{193,1... | collective-permute-start | bytes 3145736 | tf_op jit(solution)/shard_map/ppermute | solution.py:29
  129.3 34.1 %collective-permute-start.10 = (bf16[768,512]{1,0:T(8,128)(2,1)}, bf16[768,512]{1,0:T(8,128)(2,1)S(1)}, u32[]{:S(2)}, u32[]{:S(2)}) collective-permute-start(bf16[768,512]{1,0:T(8,128)(2,1)} %copy-done.22), channel_id=1, source_target_pairs={{0,56},{8,0},{16,8},{24,16},{32,24},{40,32},{48,40},{56,48},{1,57}... | collective-permute-start | bytes 2359304 | tf_op jit(solution)/shard_map/ppermute | solution.py:24
  132.2 32.1 %collective-permute-start.11 = (bf16[768,512]{1,0:T(8,128)(2,1)}, bf16[768,512]{1,0:T(8,128)(2,1)S(1)}, u32[]{:S(2)}, u32[]{:S(2)}) collective-permute-start(bf16[768,512]{1,0:T(8,128)(2,1)} %copy-done.19), channel_id=1, source_target_pairs={{0,8},{8,16},{16,24},{24,32},{32,40},{40,48},{48,56},{56,0},{1,9},... | collective-permute-start | bytes 2359304 | tf_op jit(solution)/shard_map/ppermute | solution.py:24
  132.2 21.0 %collective-permute-start.17 = (bf16[32,512]{1,0:T(8,128)(2,1)S(1)}, bf16[32,512]{1,0:T(8,128)(2,1)S(1)}, u32[]{:S(2)}, u32[]{:S(2)}) collective-permute-start(bf16[32,512]{1,0:T(8,128)(2,1)S(1)} %copy-done.33), channel_id=1, source_target_pairs={{0,16},{8,24},{16,0},{24,8},{32,48},{40,56},{48,32},{56,40},{1,17}... | collective-permute-start | bytes 98312 | tf_op jit(solution)/shard_map/ppermute | solution.py:459
  153.2 8.3 %collective-permute-start.18 = (bf16[32,512]{1,0:T(8,128)(2,1)S(1)}, bf16[32,512]{1,0:T(8,128)(2,1)S(1)}, u32[]{:S(2)}, u32[]{:S(2)}) collective-permute-start(bf16[32,512]{1,0:T(8,128)(2,1)S(1)} %add.195), channel_id=1, source_target_pairs={{0,32},{8,40},{16,48},{24,56},{32,0},{40,8},{48,16},{56,24},{1,33}... | collective-permute-start | bytes 98312 | tf_op jit(solution)/shard_map/ppermute | solution.py:459
  155.0 10.2 %collective-permute-start.15 = (bf16[128,512]{1,0:T(8,128)(2,1)}, bf16[128,512]{1,0:T(8,128)(2,1)S(1)}, u32[]{:S(2)}, u32[]{:S(2)}) collective-permute-start(bf16[128,512]{1,0:T(8,128)(2,1)} %get-tuple-element.81), channel_id=1, source_target_pairs={{0,1},{1,2},{2,3},{3,4},{4,5},{5,6},{6,7},{7,8},{8,9},{9,10},{10,1... | collective-permute-start | bytes 393224 | tf_op jit(solution)/shard_map/ppermute | solution.py:487
  161.5 4.4 %collective-permute-start.16 = (bf16[128,512]{1,0:T(8,128)(2,1)S(1)}, bf16[128,512]{1,0:T(8,128)(2,1)S(1)}, u32[]{:S(2)}, u32[]{:S(2)}) collective-permute-start(bf16[128,512]{1,0:T(8,128)(2,1)S(1)} %copy-done.34), channel_id=1, source_target_pairs={{1,0},{2,1},{3,2},{4,3},{5,4},{6,5},{7,6},{8,7},{9,8},{10,9},{11,1... | collective-permute-start | bytes 393224 | tf_op jit(solution)/shard_map/ppermute | solution.py:487
  165.2 6.7 %copy-start.31 = (bf16[128,512]{1,0:T(8,128)(2,1)}, bf16[128,512]{1,0:T(8,128)(2,1)S(1)}, u32[]{:S(2)}) copy-start(bf16[128,512]{1,0:T(8,128)(2,1)S(1)} %collective-permute-done.15.refs_5_) | copy-start | bytes 393220
  165.9 6.0 %copy-start.32 = (bf16[128,512]{1,0:T(8,128)(2,1)}, bf16[128,512]{1,0:T(8,128)(2,1)S(1)}, u32[]{:S(2)}) copy-start(bf16[128,512]{1,0:T(8,128)(2,1)S(1)} %collective-permute-done.16.refs_6_) | copy-start | bytes 393220
  165.9 1.2 copy-start.11
  167.1 1.1 copy-start.14
  168.2 1.1 copy-start.17
  171.9 36.8 %all-to-all-start.3 = ((bf16[8,1152,128]{2,1,0:T(8,128)(2,1)}), bf16[8,1152,128]{2,1,0:T(8,128)(2,1)}, u32[]{:S(2)}, u32[]{:S(2)}) async-start(bf16[8,1152,128]{2,1,0:T(8,128)(2,1)} %pick_blocks.6), calls=%async_computation.3 | async-start | bytes 4718592 | tf_op jit(solution)/shard_map/all_to_all | solution.py:77
  178.6 11.8 %copy-start.9 = (bf16[768,512]{1,0:T(8,128)(2,1)S(1)}, bf16[768,512]{1,0:T(8,128)(2,1)}, u32[]{:S(2)}) copy-start(bf16[768,512]{1,0:T(8,128)(2,1)} %copy-done.7) | copy-start | bytes 2359300
  178.6 11.8 %copy-start.12 = (bf16[768,512]{1,0:T(8,128)(2,1)S(1)}, bf16[768,512]{1,0:T(8,128)(2,1)}, u32[]{:S(2)}) copy-start(bf16[768,512]{1,0:T(8,128)(2,1)} %copy-done.10) | copy-start | bytes 2359300
  178.6 11.8 %copy-start.15 = (bf16[768,512]{1,0:T(8,128)(2,1)S(1)}, bf16[768,512]{1,0:T(8,128)(2,1)}, u32[]{:S(2)}) copy-start(bf16[768,512]{1,0:T(8,128)(2,1)} %copy-done.13) | copy-start | bytes 2359300
  178.7 11.8 %copy-start.18 = (bf16[768,512]{1,0:T(8,128)(2,1)S(1)}, bf16[768,512]{1,0:T(8,128)(2,1)}, u32[]{:S(2)}) copy-start(bf16[768,512]{1,0:T(8,128)(2,1)} %copy-done.16) | copy-start | bytes 2359300
  178.7 26.1 %collective-permute-start.21 = (bf16[512,1024]{1,0:T(8,128)(2,1)}, bf16[512,1024]{1,0:T(8,128)(2,1)S(1)}, u32[]{:S(2)}, u32[]{:S(2)}) collective-permute-start(bf16[512,1024]{1,0:T(8,128)(2,1)} %get-tuple-element.98), channel_id=1, source_target_pairs={{0,192},{64,0},{128,64},{192,128},{1,193},{65,1},{129,65},{193,129... | collective-permute-start | bytes 3145736 | tf_op jit(solution)/shard_map/ppermute | solution.py:29
  181.4 19.9 %collective-permute-start.19 = (bf16[768,512]{1,0:T(8,128)(2,1)}, bf16[768,512]{1,0:T(8,128)(2,1)S(1)}, u32[]{:S(2)}, u32[]{:S(2)}) collective-permute-start(bf16[768,512]{1,0:T(8,128)(2,1)} %copy-done.7), channel_id=1, source_target_pairs={{0,8},{8,16},{16,24},{24,32},{32,40},{40,48},{48,56},{56,0},{1,9},... | collective-permute-start | bytes 2359304 | tf_op jit(solution)/shard_map/ppermute | solution.py:24
  182.0 19.4 %collective-permute-start.20 = (bf16[768,512]{1,0:T(8,128)(2,1)}, bf16[768,512]{1,0:T(8,128)(2,1)S(1)}, u32[]{:S(2)}, u32[]{:S(2)}) collective-permute-start(bf16[768,512]{1,0:T(8,128)(2,1)} %copy-done.10), channel_id=1, source_target_pairs={{0,56},{8,0},{16,8},{24,16},{32,24},{40,32},{48,40},{56,48},{1,57}... | collective-permute-start | bytes 2359304 | tf_op jit(solution)/shard_map/ppermute | solution.py:24
  183.4 1.1 copy-start.21
  204.8 3.8 %copy-start.4 = (bf16[512,1024]{1,0:T(8,128)(2,1)}, bf16[512,1024]{1,0:T(8,128)(2,1)S(1)}, u32[]{:S(2)}) copy-start(bf16[512,1024]{1,0:T(8,128)(2,1)S(1)} %collective-permute-done.21.refs_6_.refs_10_) | copy-start | bytes 3145732
  208.7 23.1 %all-to-all-start.4 = ((bf16[8,640,128]{2,1,0:T(8,128)(2,1)}), bf16[8,640,128]{2,1,0:T(8,128)(2,1)S(1)}, u32[]{:S(2)}, u32[]{:S(2)}) async-start(bf16[8,640,128]{2,1,0:T(8,128)(2,1)} %pick_blocks.7), calls=%async_computation.4 | async-start | bytes 2621440 | tf_op jit(solution)/shard_map/all_to_all | solution.py:77
  231.8 1.1 copy-start.6
  233.0 1.4 copy-start.27
  234.4 1.4 copy-start.28
  235.8 38.1 %copy-start.3 = (bf16[512,1024]{1,0:T(8,128)(2,1)S(1)}, bf16[512,1024]{1,0:T(8,128)(2,1)}, u32[]{:S(2)}) copy-start(bf16[512,1024]{1,0:T(8,128)(2,1)} %copy-done.2) | copy-start | bytes 3145732
  235.8 38.1 %copy-start.5 = (bf16[512,1024]{1,0:T(8,128)(2,1)S(1)}, bf16[512,1024]{1,0:T(8,128)(2,1)}, u32[]{:S(2)}) copy-start(bf16[512,1024]{1,0:T(8,128)(2,1)} %copy-done.4) | copy-start | bytes 3145732
  244.6 12.9 %collective-permute-start.22 = (bf16[384,512]{1,0:T(8,128)(2,1)S(1)}, bf16[384,512]{1,0:T(8,128)(2,1)S(1)}, u32[]{:S(2)}, u32[]{:S(2)}) collective-permute-start(bf16[384,512]{1,0:T(8,128)(2,1)S(1)} %get-tuple-element.102.refs_0_), channel_id=1, source_target_pairs={{0,64},{64,128},{128,192},{192,0},{1,65},{65,129},{129,193},{193,1... | collective-permute-start | bytes 1179656 | tf_op jit(solution)/shard_map/ppermute | solution.py:29
  244.7 13.5 %collective-permute-start.26 = (bf16[384,512]{1,0:T(8,128)(2,1)S(1)}, bf16[384,512]{1,0:T(8,128)(2,1)S(1)}, u32[]{:S(2)}, u32[]{:S(2)}) collective-permute-start(bf16[384,512]{1,0:T(8,128)(2,1)S(1)} %get-tuple-element.107.refs_0_), channel_id=1, source_target_pairs={{0,192},{64,0},{128,64},{192,128},{1,193},{65,1},{129,65},{193,129... | collective-permute-start | bytes 1179656 | tf_op jit(solution)/shard_map/ppermute | solution.py:29
  248.0 23.9 %collective-permute-start.23 = (bf16[384,512]{1,0:T(8,128)(2,1)S(1)}, bf16[384,512]{1,0:T(8,128)(2,1)S(1)}, u32[]{:S(2)}, u32[]{:S(2)}) collective-permute-start(bf16[384,512]{1,0:T(8,128)(2,1)S(1)} %get-tuple-element.102.refs_0_), channel_id=1, source_target_pairs={{0,192},{64,0},{128,64},{192,128},{1,193},{65,1},{129,65},{193,129... | collective-permute-start | bytes 1179656 | tf_op jit(solution)/shard_map/ppermute | solution.py:29
  257.6 14.9 %collective-permute-start.24 = (bf16[384,512]{1,0:T(8,128)(2,1)S(1)}, bf16[384,512]{1,0:T(8,128)(2,1)S(1)}, u32[]{:S(2)}, u32[]{:S(2)}) collective-permute-start(bf16[384,512]{1,0:T(8,128)(2,1)S(1)} %collective-permute-done.22.refs_1_), channel_id=1, source_target_pairs={{0,64},{64,128},{128,192},{192,0},{1,65},{65,129},{129,193},{193,1... | collective-permute-start | bytes 1179656 | tf_op jit(solution)/shard_map/ppermute | solution.py:29
  257.6 26.0 %collective-permute-start.25 = (bf16[384,512]{1,0:T(8,128)(2,1)S(1)}, bf16[384,512]{1,0:T(8,128)(2,1)S(1)}, u32[]{:S(2)}, u32[]{:S(2)}) collective-permute-start(bf16[384,512]{1,0:T(8,128)(2,1)S(1)} %get-tuple-element.107.refs_0_), channel_id=1, source_target_pairs={{0,64},{64,128},{128,192},{192,0},{1,65},{65,129},{129,193},{193,1... | collective-permute-start | bytes 1179656 | tf_op jit(solution)/shard_map/ppermute | solution.py:29
  258.3 25.4 %collective-permute-start.27 = (bf16[384,512]{1,0:T(8,128)(2,1)S(1)}, bf16[384,512]{1,0:T(8,128)(2,1)S(1)}, u32[]{:S(2)}, u32[]{:S(2)}) collective-permute-start(bf16[384,512]{1,0:T(8,128)(2,1)S(1)} %collective-permute-done.26.refs_2_), channel_id=1, source_target_pairs={{0,192},{64,0},{128,64},{192,128},{1,193},{65,1},{129,65},{193,129... | collective-permute-start | bytes 1179656 | tf_op jit(solution)/shard_map/ppermute | solution.py:29
  271.2 12.4 %copy-start.29 = (s32[4]{0:T(128)S(1)}, s32[4]{0:T(128)}, u32[]{:S(2)}) copy-start(s32[4]{0:T(128)} %pad_add_fusion.refs_1_.place) | copy-start | bytes 52
  271.2 10.8 %collective-permute-start.30 = (bf16[128,512]{1,0:T(8,128)(2,1)S(1)}, bf16[128,512]{1,0:T(8,128)(2,1)S(1)}, u32[]{:S(2)}, u32[]{:S(2)}) collective-permute-start(bf16[128,512]{1,0:T(8,128)(2,1)S(1)} %bitcast.12), channel_id=1, source_target_pairs={{0,128},{64,192},{128,0},{192,64},{1,129},{65,193},{129,1},{193,65... | collective-permute-start | bytes 393224 | tf_op jit(solution)/shard_map/ppermute | solution.py:29
  271.8 10.2 %collective-permute-start.29 = (bf16[128,512]{1,0:T(8,128)(2,1)S(1)}, bf16[128,512]{1,0:T(8,128)(2,1)S(1)}, u32[]{:S(2)}, u32[]{:S(2)}) collective-permute-start(bf16[128,512]{1,0:T(8,128)(2,1)S(1)} %bitcast.13), channel_id=1, source_target_pairs={{0,192},{64,0},{128,64},{192,128},{1,193},{65,1},{129,65},{193,129... | collective-permute-start | bytes 393224 | tf_op jit(solution)/shard_map/ppermute | solution.py:29
  272.4 11.2 %collective-permute-start.28 = (bf16[128,512]{1,0:T(8,128)(2,1)S(1)}, bf16[128,512]{1,0:T(8,128)(2,1)S(1)}, u32[]{:S(2)}, u32[]{:S(2)}) collective-permute-start(bf16[128,512]{1,0:T(8,128)(2,1)S(1)} %bitcast.14), channel_id=1, source_target_pairs={{0,64},{64,128},{128,192},{192,0},{1,65},{65,129},{129,193},{193,1... | collective-permute-start | bytes 393224 | tf_op jit(solution)/shard_map/ppermute | solution.py:29
  (8 other events, 7.6 us)
